TPU v7x, 128 devices: a whole 4x4x4 slice. The times are simulated.
128 devices in a mesh: node: 8 (over y, core), fsdp: 16 (over z, x).
Axes of the slice: x: 4, y: 4, z: 4, core: 2. Of those that a mesh axis runs over, the one named last changes fastest.
Arguments:
- activations: bfloat16 [131072, 2560], P(('node', 'fsdp'))
- grad_out: bfloat16 [131072, 2560], P(('node', 'fsdp'))
Outputs:
- combined: float32 [2560, 2560], P('fsdp', 'node')
All inputs are finite; a program needn't handle non-finite values.
Results may differ from a plain program's by a relative error of at most 0.0003.
Values may be sent and summed in bfloat16 or wider, within the bound.
No kernel may reach another device: no remote copies, remote signals or barrier semaphores. Data moves between devices by JAX's collectives and lax.ppermute only.
A program may use at most 256 MiB of HBM per device.

v0:
```python
import jax
import jax.numpy as jnp
from jax import lax
from jax.sharding import PartitionSpec as P

EPS = 1e-06


def partner(array, axis, distance):
    return lax.ppermute(array, axis, [(i, i ^ 1 << distance) for i in range(lax.axis_size(axis))])


def group_totals(sums, node_index, bit, node_count):
    slot = node_index % 2**bit
    selector = (jnp.arange(node_count) == slot).astype(jnp.float32)
    spread = sums[:, None] * selector[None, :]
    totals = lax.psum(spread, ("node", "fsdp"))
    return jnp.sum(totals * selector[None, :], axis=1)


def local(activations, grad_out):
    node_count = lax.axis_size("node")
    current = lax.psum_scatter(
        lax.dot_general(
            activations, grad_out, (((0,), (0,)), ((), ())), preferred_element_type=jnp.float32
        ),
        "fsdp",
        scatter_dimension=0,
        tiled=True,
    )
    node_index = lax.axis_index("node")
    levels = node_count.bit_length() - 1
    for level in range(levels):
        bit = levels - 1 - level
        upper = node_index // 2**bit % 2
        half = current.shape[1] // 2
        lower_part = current[:, :half]
        upper_part = current[:, half:]
        keep = jnp.where(upper == 0, lower_part, upper_part)
        give = jnp.where(upper == 0, upper_part, lower_part)
        arrived = partner(give, "node", bit)
        first = jnp.where(upper == 0, keep, arrived)
        second = jnp.where(upper == 0, arrived, keep)
        sums = jnp.stack(
            [jnp.sum(first * second), jnp.sum(first * first), jnp.sum(second * second)]
        )
        totals = group_totals(sums, node_index, bit, node_count)
        coef_first = 1.0 - totals[0] / (2.0 * (totals[1] + EPS))
        coef_second = 1.0 - totals[0] / (2.0 * (totals[2] + EPS))
        current = coef_first * first + coef_second * second
    return current


def solution(mesh):
    in_specs = (P(("node", "fsdp"), None), P(("node", "fsdp"), None))
    out_specs = P("fsdp", "node")
    return jax.shard_map(local, mesh=mesh, in_specs=in_specs, out_specs=out_specs, check_vma=False)
```

profile of v0, /device:TPU:1, one launch (start us, length us, event | category | flops | bytes accessed | tf_op | source)
XLA Modules:
  0.0 445.0 jit_solution(4860127070176561867)
XLA Ops:
  6.5 0.0 reduce-scatter.2.cloned.1.call-start
  6.5 22.2 %fusion.3 = f32[2560,2560]{1,0:T(8,128)} fusion(bf16[1024,2560]{1,0:T(8,128)(2,1)} %param.2, bf16[1024,2560]{1,0:T(8,128)(2,1)} %param.3), kind=kOutput, calls=%fused_computation.39 | convolution fusion | flops 13421772800 | bytes 36700160 | tf_op jit(solution)/shard_map/dot_general | solution.py:24
  28.8 0.0 reduce-scatter.2.cloned.1.call-update
  28.8 162.0 %reduce-scatter.2.cloned.1.call-done = f32[160,2560]{1,0:T(8,128)} async-done(((f32[2560,2560]{1,0:T(8,128)}), f32[160,2560]{1,0:T(8,128)}) %reduce-scatter.2.cloned.1.call-update) | async-done | bytes 1638416 | tf_op jit(solution)/shard_map/reduce_scatter | solution.py:23
  190.8 1.5 slice_select_fusion
  192.3 2.8 collective-permute-start
  195.1 17.9 %collective-permute-done = f32[160,1280]{1,0:T(8,128)S(1)} collective-permute-done((f32[160,1280]{1,0:T(8,128)S(1)}, f32[160,1280]{1,0:T(8,128)S(1)}, u32[]{:S(2)}, u32[]{:S(2)}) %collective-permute-start) | collective-permute-done | bytes 819232 | tf_op jit(solution)/shard_map/ppermute | solution.py:10
  213.0 2.3 multiply_reduce_fusion.2
  215.4 2.0 pad_maximum_fusion
  217.3 0.1 broadcast_multiply_fusion.2
  217.4 65.4 %psum.21 = f32[3,8]{1,0:T(4,128)S(1)} all-reduce(f32[3,8]{1,0:T(4,128)S(1)} %broadcast_multiply_fusion.2), channel_id=1, replica_groups=mesh['node'=8,'fsdp'=16] {'node','fsdp'}, use_global_device_ids=true, to_apply=%region_4.5 | all-reduce | flops 24 | bytes 192 | tf_op jit(solution)/shard_map/psum | solution.py:17
  282.8 0.1 multiply_reduce_fusion.11
  282.9 0.7 fusion.2
  286.0 0.1 multiply_add_fusion
  286.2 0.1 collective-permute-start.1
  286.3 10.3 %collective-permute-done.1 = f32[160,640]{1,0:T(8,128)S(1)} collective-permute-done((f32[160,640]{1,0:T(8,128)S(1)}, f32[160,640]{1,0:T(8,128)S(1)}, u32[]{:S(2)}, u32[]{:S(2)}) %collective-permute-start.1) | collective-permute-done | bytes 409632 | tf_op jit(solution)/shard_map/ppermute | solution.py:10
  296.6 0.9 multiply_reduce_fusion.5
  297.5 2.0 pad_maximum_fusion.1
  299.5 0.1 broadcast_multiply_fusion.1
  299.5 63.1 %psum.22 = f32[3,8]{1,0:T(4,128)S(1)} all-reduce(f32[3,8]{1,0:T(4,128)S(1)} %broadcast_multiply_fusion.1), channel_id=1, replica_groups=mesh['node'=8,'fsdp'=16] {'node','fsdp'}, use_global_device_ids=true, to_apply=%region_9.10 | all-reduce | flops 24 | bytes 192 | tf_op jit(solution)/shard_map/psum | solution.py:17
  362.6 0.1 multiply_reduce_fusion.10
  362.7 0.7 fusion.1
  366.1 0.1 slice_select_fusion.4
  366.2 0.7 collective-permute-start.2
  366.9 1.1 collective-permute-done.2
  368.1 0.8 multiply_reduce_fusion.8
  368.9 2.0 pad_maximum_fusion.2
  370.9 0.1 broadcast_multiply_fusion
  370.9 63.1 %psum.23 = f32[3,8]{1,0:T(4,128)S(1)} all-reduce(f32[3,8]{1,0:T(4,128)S(1)} %broadcast_multiply_fusion), channel_id=1, replica_groups=mesh['node'=8,'fsdp'=16] {'node','fsdp'}, use_global_device_ids=true, to_apply=%region_14.15 | all-reduce | flops 24 | bytes 192 | tf_op jit(solution)/shard_map/psum | solution.py:17
  434.0 0.1 multiply_reduce_fusion.9
  434.1 0.7 fusion
  437.4 0.7 multiply_add_fusion.2
  (5 shorter events, 0.1 us)
Async XLA Ops:
  6.5 184.3 %reduce-scatter.2.cloned.1.call-start = ((), (), s32[]{:S(2)}) async-start(), calls=%async_computation.1 | async-start | bytes 27852800 | tf_op jit(solution)/shard_map/reduce_scatter | solution.py:23
  192.3 20.7 %collective-permute-start = (f32[160,1280]{1,0:T(8,128)S(1)}, f32[160,1280]{1,0:T(8,128)S(1)}, u32[]{:S(2)}, u32[]{:S(2)}) collective-permute-start(f32[160,1280]{1,0:T(8,128)S(1)} %slice_select_fusion), channel_id=1, source_target_pairs={{0,64},{16,80},{32,96},{48,112},{64,0},{80,16},{96,32},{112,48},{1... | collective-permute-start | bytes 2457608 | tf_op jit(solution)/shard_map/ppermute | solution.py:10
  286.2 10.5 %collective-permute-start.1 = (f32[160,640]{1,0:T(8,128)S(1)}, f32[160,640]{1,0:T(8,128)S(1)}, u32[]{:S(2)}, u32[]{:S(2)}) collective-permute-start(f32[160,640]{1,0:T(8,128)S(1)} %slice_select_fusion.2), channel_id=1, source_target_pairs={{0,32},{16,48},{32,0},{48,16},{64,96},{80,112},{96,64},{112,80},{1... | collective-permute-start | bytes 1228808 | tf_op jit(solution)/shard_map/ppermute | solution.py:10
  366.2 1.9 collective-permute-start.2
Sparse Core Ops, SparseCore 0:
  28.9 161.8 reduce-scatter.1
where the time goes:
time: 446 us; the launch traced here: 445 us
  blocking collectives  192 us (43%)
  waiting for transfers between devices  191 us (43%)
  matrix products  22.2 us (5%)
  between operations  21.2 us (5%)
  other arithmetic  13 us (3%)
    psum x3, blocking collectives, group_totals(): totals = lax.psum(spread, ('node', 'fsdp'))  192 us
    reduce_scatter x1, waiting for transfers between devices, local(): lax.psum_scatter(lax.dot_general(activations, grad_out, (((0,), (0,)), ((...  162 us
    ppermute x3, waiting for transfers between devices, partner(): lax.ppermute(array, axis, [(i, i ^ 1 << distance) for i in range(lax.axis...  29.4 us
    dot_general x1, matrix products, local(): lax.dot_general(activations, grad_out, (((0,), (0,)), ((), ())), preferre...  22.2 us
  transfers between devices with their start and end apart: 4, of which 4 were waited for; matrix products, arithmetic and copies ran while one was open for 0% of the time, Pallas kernels for 0%

commit v1 on v0

v1 whole, which is shorter than its diff:
```python
import functools

import jax
import jax.numpy as jnp
from jax import lax
from jax.experimental import pallas as pl
from jax.experimental.pallas import tpu as pltpu
from jax.sharding import PartitionSpec as P

EPS = 1e-06
POWER = 17
TOP = 2.0 ** (124 / POWER)
TINY = 2.0**-126
PAD = 16
SIDE = 4
VMEM_BYTES = 60 * 2**20
BF16, F32 = jnp.bfloat16, jnp.float32


def encode(values):
    peak = jnp.max(jnp.abs(values), axis=0, keepdims=True).astype(BF16)
    x = values * (TOP / jnp.maximum(peak.astype(F32), TINY))
    x2 = x * x
    x4 = x2 * x2
    x8 = x4 * x4
    return (x8 * x8 * x).astype(BF16), peak


def decode(code, peak):
    code = code.astype(F32)
    size = jnp.exp(jnp.log(jnp.abs(code)) * (1.0 / POWER))
    return jnp.where(code < 0, -size, size) * (peak.astype(F32) * (1.0 / TOP))


def coordinates():
    node, fsdp = lax.axis_index("node"), lax.axis_index("fsdp")
    return lax.rem(fsdp, SIDE), node // 2, fsdp // SIDE, lax.rem(node, 2)


def masks(core):
    return 1 + 2 * core, 3 - 2 * core


def pairing(axis, first):
    pairs = []
    for y in range(SIDE):
        for core in range(2):
            mask = masks(core)[0 if first else 1]
            for z in range(SIDE):
                for x in range(SIDE):
                    at = dict(x=x, y=y, z=z)
                    to = dict(at)
                    to[axis] ^= mask
                    index = lambda p: (p["y"] * 2 + core) * SIDE * SIDE + p["z"] * SIDE + p["x"]
                    pairs.append((index(at), index(to)))
    return pairs


def exchange(array, axis, first):
    return lax.ppermute(array, ("node", "fsdp"), pairing(axis, first))


def block_offset(stream, p, q, rows):
    owner = jnp.where(stream == 0, q * SIDE + p, p * SIDE + q)
    return pl.multiple_of((owner * 2 + stream) * rows, 16)


def wanted(which, rows):
    x, _, z, core = coordinates()
    m1, m2 = masks(core)
    offsets = []
    for stream in range(2):
        p, q = (x, z) if stream == 0 else (z, x)
        everything = [q ^ 2, q ^ m1, q ^ m2, q]
        ps, qs = {
            "p1a": (p ^ 2, everything),
            "p1b": (p ^ m1, everything),
            "p2": (p ^ m2, everything),
            "q1": (p, everything[:2]),
            "q2": (p, everything[2:3]),
            "last": (p, everything[3:]),
        }[which]
        offsets.append([block_offset(stream, ps, each, rows) for each in qs])
    return offsets


def first_kernel(rows, x_ref, dy_ref, xt_ref, out0, out1, lhs):
    offsets = wanted("p1a", rows)
    count = len(offsets[0])

    @pl.when(pl.program_id(0) == 0)
    def _():
        for t in range(x_ref.shape[1] // 256):
            xt_ref[t * 256 : (t + 1) * 256, :] = x_ref[:, t * 256 : (t + 1) * 256].T
        for s in range(2):
            for b in range(count):
                at = (s * count + b) * rows
                lhs[at : at + rows, :] = xt_ref[pl.ds(offsets[s][b], rows), :]

    total = jnp.dot(lhs[...], dy_ref[...], preferred_element_type=F32)
    for s, out in enumerate((out0, out1)):
        code, peak = encode(total[s * count * rows : (s + 1) * count * rows])
        out[: count * rows, :] = code
        out[count * rows :, :] = jnp.broadcast_to(peak, (PAD, peak.shape[1]))


def fetch(xt_ref, lhs, sems, offsets, rows):
    copies = []
    for s in range(2):
        for b, offset in enumerate(offsets[s]):
            at = s * len(offsets[s]) + b
            copies.append(
                pltpu.make_async_copy(
                    xt_ref.at[pl.ds(offset, rows), :], lhs.at[pl.ds(at * rows, rows), :], sems.at[at]
                )
            )
    for copy in copies:
        copy.start()
    for copy in copies:
        copy.wait()


def step_kernel(which, rows, picks, xt_ref, dy_ref, *rest):
    arrivals, (out0, out1, lhs, sems) = rest[:-4], rest[-4:]
    offsets = wanted(which, rows)
    size = len(offsets[0]) * rows

    @pl.when(pl.program_id(0) == 0)
    def _():
        fetch(xt_ref, lhs, sems, offsets, rows)

    total = jnp.dot(lhs[...], dy_ref[...], preferred_element_type=F32)
    for s, out in enumerate((out0, out1)):
        part = total[s * size : (s + 1) * size]
        for k, pick in enumerate(picks):
            ref = arrivals[2 * k + s]
            scale = ref.shape[0] - PAD
            part += decode(ref[pick * rows : pick * rows + size, :], ref[scale : scale + 1, :])
        code, peak = encode(part)
        out[:size, :] = code
        out[size:, :] = jnp.broadcast_to(peak, (PAD, peak.shape[1]))


def step(which, rows, tile, xt, dy, arrivals, picks, count):
    tokens, cols = dy.shape
    size = count * rows
    message = jax.ShapeDtypeStruct((size + PAD, cols), BF16)
    column = lambda i: (0, i)
    return pl.pallas_call(
        functools.partial(step_kernel, which, rows, picks),
        grid=(cols // tile,),
        out_shape=[message, message],
        in_specs=[pl.BlockSpec(memory_space=pl.ANY), pl.BlockSpec((tokens, tile), column)]
        + [pl.BlockSpec((a.shape[0], tile), column) for a in arrivals],
        out_specs=[pl.BlockSpec((size + PAD, tile), column)] * 2,
        scratch_shapes=[pltpu.VMEM((2 * size, tokens), BF16), pltpu.SemaphoreType.DMA((2 * count,))],
        compiler_params=pltpu.CompilerParams(vmem_limit_bytes=VMEM_BYTES),
        name=which,
    )(xt, dy, *arrivals)


def first(rows, tile, x, dy):
    tokens, cols = dy.shape
    size = SIDE * rows
    message = jax.ShapeDtypeStruct((size + PAD, cols), BF16)
    column = lambda i: (0, i)
    return pl.pallas_call(
        functools.partial(first_kernel, rows),
        grid=(cols // tile,),
        out_shape=[jax.ShapeDtypeStruct((x.shape[1], tokens), BF16), message, message],
        in_specs=[pl.BlockSpec(x.shape, lambda i: (0, 0)), pl.BlockSpec((tokens, tile), column)],
        out_specs=[pl.BlockSpec((x.shape[1], tokens), lambda i: (0, 0))]
        + [pl.BlockSpec((size + PAD, tile), column)] * 2,
        scratch_shapes=[pltpu.VMEM((2 * size, tokens), BF16)],
        compiler_params=pltpu.CompilerParams(vmem_limit_bytes=VMEM_BYTES),
        name="p1a",
    )(x, dy)


def last_kernel(rows, picks, place, xt_ref, dy_ref, *rest):
    arrivals, (out0, out1, lhs, sems) = rest[:-4], rest[-4:]

    @pl.when(pl.program_id(0) == 0)
    def _():
        fetch(xt_ref, lhs, sems, wanted("last", rows), rows)

    total = jnp.dot(lhs[...], dy_ref[...], preferred_element_type=F32)
    parts = []
    for s in range(2):
        part = total[s * rows : (s + 1) * rows]
        for k, pick in enumerate(picks):
            ref = arrivals[2 * k + s]
            scale = ref.shape[0] - PAD
            part += decode(ref[pick * rows : (pick + 1) * rows, :], ref[scale : scale + 1, :])
        parts.append(part)
    code, peak = encode(jnp.concatenate(parts))

    def put(out):
        out[0, : 2 * rows, :] = code
        out[0, 2 * rows :, :] = jnp.broadcast_to(peak, (PAD, peak.shape[1]))

    pl.when(pl.program_id(0) < 2)(lambda: put(out0))
    pl.when(pl.program_id(0) >= 2)(lambda: put(out1))


def last(rows, place, xt, dy, arrivals, picks):
    tokens, cols = dy.shape
    tile = cols // SIDE
    message = jax.ShapeDtypeStruct((2, 2 * rows + PAD, tile), BF16)
    column = lambda i, place: (0, place[i])
    return pl.pallas_call(
        functools.partial(last_kernel, rows, picks),
        grid_spec=pltpu.PrefetchScalarGridSpec(
            num_scalar_prefetch=1,
            grid=(SIDE,),
            in_specs=[pl.BlockSpec(memory_space=pl.ANY), pl.BlockSpec((tokens, tile), column)]
            + [pl.BlockSpec((a.shape[0], tile), column) for a in arrivals],
            out_specs=[
                pl.BlockSpec((1, 2 * rows + PAD, tile), lambda i, place: (jnp.minimum(i, 1), 0, 0)),
                pl.BlockSpec((1, 2 * rows + PAD, tile), lambda i, place: (jnp.maximum(i, 2) - 2, 0, 0)),
            ],
            scratch_shapes=[pltpu.VMEM((2 * rows, tokens), BF16), pltpu.SemaphoreType.DMA((2,))],
        ),
        out_shape=[message, message],
        compiler_params=pltpu.CompilerParams(vmem_limit_bytes=VMEM_BYTES),
        name="last",
    )(place, xt, dy, *arrivals)


def gram_kernel(rows, half, y2own, y1arr, y2arr, carr, g_ref, gram_ref):
    _, y, _, core = coordinates()
    m1, m2 = masks(core)
    wide = g_ref.shape[2]
    lane = lax.broadcasted_iota(jnp.int32, (1, wide), 1)
    start = (wide - half) * core
    valid = (lane >= start) & (lane < start + half)
    at = pl.ds(pl.multiple_of((y2own.shape[2] - wide) * core, 128), wide)
    sources = [(y2own, 1, 0, 0), (y1arr, 1, m1, m2), (y2arr, 0, m2, m1), (y2arr, 1, 2, 2)]
    for k, (ref, index, mask, mask_other) in enumerate(sources):
        own = decode(ref[index, :rows, at], ref[index, rows : rows + 1, at])
        g_ref[(y ^ mask) * 2 + core] = jnp.where(valid, own, 0.0)
        other = decode(carr[k, :rows, :], carr[k, rows : rows + 1, :])
        g_ref[(y ^ mask_other) * 2 + 1 - core] = jnp.where(valid, other, 0.0)
    nodes = g_ref.shape[0]
    pairs = [(i, j) for i in range(nodes) for j in range(i, nodes)]

    def body(r, sums):
        blocks = [g_ref[n, pl.ds(r * 8, 8), :] for n in range(nodes)]
        out = []
        for total, (i, j) in zip(sums, pairs):
            product = blocks[i] * blocks[j]
            for t in range(wide // 128):
                total = total + product[:, t * 128 : (t + 1) * 128]
            out.append(total)
        return tuple(out)

    sums = lax.fori_loop(0, rows // 8, body, tuple(jnp.zeros((8, 128), F32) for _ in pairs))
    filled = [jnp.sum(total, axis=0, keepdims=True) for total in sums]
    filled += [jnp.zeros((1, 128), F32)] * (-len(pairs) % 8)
    stacked = jnp.sum(jnp.concatenate(filled), axis=1, keepdims=True)
    shape = (len(filled), 128)
    on = lax.broadcasted_iota(jnp.int32, shape, 0) == lax.broadcasted_iota(jnp.int32, shape, 1)
    row = jnp.sum(jnp.where(on, jnp.broadcast_to(stacked, shape), 0.0), axis=0, keepdims=True)
    gram_ref[...] = jnp.broadcast_to(row, gram_ref.shape)


def combine_kernel(half, g_ref, sums_ref, out_ref):
    nodes, rows, wide = g_ref.shape
    sums = jnp.sum(sums_ref[...], axis=0, keepdims=True)
    pairs = [(i, j) for i in range(nodes) for j in range(i, nodes)]
    gram = {}
    for k, (i, j) in enumerate(pairs):
        gram[i, j] = gram[j, i] = sums[:, k : k + 1]

    def inner(u, v):
        total = None
        for i, a in u.items():
            row = None
            for j, b in v.items():
                term = gram[i, j] * b
                row = term if row is None else row + term
            total = a * row if total is None else total + a * row
        return total

    one = jnp.ones((1, 1), F32)
    vectors = [{n: one} for n in range(nodes)]
    while len(vectors) > 1:
        middle = len(vectors) // 2
        merged = []
        for u, v in zip(vectors[:middle], vectors[middle:]):
            dot = inner(u, v)
            cu = 1.0 - dot / (2.0 * (inner(u, u) + EPS))
            cv = 1.0 - dot / (2.0 * (inner(v, v) + EPS))
            merged.append({**{n: cu * a for n, a in u.items()}, **{n: cv * a for n, a in v.items()}})
        vectors = merged
    total = None
    for n, coefficient in vectors[0].items():
        term = coefficient * g_ref[n]
        total = term if total is None else total + term
    core = lax.rem(lax.axis_index("node"), 2)
    moved = pltpu.roll(total, half, 1)
    out_ref[...] = jnp.where(core == 0, total[:, :half], moved[:, :half])


def local(x, dy):
    cols = dy.shape[1]
    rows = x.shape[1] // (2 * SIDE * SIDE)
    tile = cols // 5
    half = cols // (2 * SIDE)
    wide = -(-half // 128) * 128
    axes = ("x", "z")
    _, y, _, core = coordinates()
    m1, m2 = masks(core)
    place = jnp.stack([y ^ 2, y ^ m1, y ^ m2, y]).astype(jnp.int32)

    def send(pair, primary, is_first):
        return [exchange(m, axes[s] if primary else axes[1 - s], is_first) for s, m in enumerate(pair)]

    xt, *p1a = first(rows, tile, x, dy)
    p1a = send(p1a, True, True)
    p1b = send(step("p1b", rows, tile, xt, dy, [], [], 4), True, True)
    p2 = send(step("p2", rows, tile, xt, dy, p1a, [0], 4), True, False)
    q1 = send(step("q1", rows, tile, xt, dy, p1b + p2, [0, 0], 2), False, True)
    q2 = send(step("q2", rows, tile, xt, dy, p1b + p2 + q1, [2, 2, 0], 1), False, False)
    y1, y2 = last(rows, place, xt, dy, p1b + p2 + q1 + q2, [3, 3, 1, 0])
    y1arr = exchange(y1, "y", True)
    y2arr = exchange(jnp.stack([y2[0], y1arr[0]]), "y", False)
    across = jnp.stack([y2[1], y1arr[1], y2arr[0], y2arr[1]])
    start = (cols // SIDE - wide) * (1 - core)
    across = lax.dynamic_slice_in_dim(across, start, wide, axis=2)
    carr = lax.ppermute(across, "node", [(i, i ^ 1) for i in range(2 * SIDE)])
    params = pltpu.CompilerParams(vmem_limit_bytes=VMEM_BYTES)
    count = 2 * SIDE * SIDE * SIDE
    g, gram = pl.pallas_call(
        functools.partial(gram_kernel, 2 * rows, half),
        out_shape=[
            jax.ShapeDtypeStruct((2 * SIDE, 2 * rows, wide), F32),
            jax.ShapeDtypeStruct((count, 128), F32),
        ],
        compiler_params=params,
        name="gram",
    )(y2, y1arr, y2arr, carr)
    sums = lax.all_to_all(gram, ("node", "fsdp"), 0, 0, tiled=True)
    return pl.pallas_call(
        functools.partial(combine_kernel, half),
        out_shape=jax.ShapeDtypeStruct((2 * rows, half), F32),
        compiler_params=params,
        name="combine",
    )(g, sums)


def solution(mesh):
    in_specs = (P(("node", "fsdp"), None), P(("node", "fsdp"), None))
    out_specs = P("fsdp", "node")
    return jax.shard_map(local, mesh=mesh, in_specs=in_specs, out_specs=out_specs, check_vma=False)
```

time: 446 us -> 183 us (0.41)
  blocking collectives: 192 us -> 14.7 us
  waiting for transfers between devices: 191 us -> 64.4 us
  Pallas kernels: 0 us -> 74.2 us
  matrix products: 22.2 us -> 0 us
  between operations: 21.2 us -> 0.13 us
  starting transfers between devices: 3.62 us -> 23.5 us
  other arithmetic: 13 us -> 0.78 us
    psum x3 -> x0, blocking collectives: 192 us -> none  [group_totals(): totals = lax.psum(spread, ('node', 'fsdp'))]
    reduce_scatter x1 -> x0, waiting for transfers between devices: 162 us -> none  [local(): lax.psum_scatter(lax.dot_general(activations, grad_out, (((0,), (0,)), ((...]
    pallas_call x0 -> x8, Pallas kernels: none -> 74.2 us  [the longest x4 42.9 us: step(): pl.pallas_call(functools.partial(step_kernel, which, rows, picks), grid=(...]
    ppermute x3 -> x13, waiting for transfers between devices: 29.4 us -> 64.4 us  [the longest x12 62.8 us: exchange(): return lax.ppermute(array, ('node', 'fsdp'), pairing(axis, first))]
    dot_general x1 -> x0, matrix products: 22.2 us -> none  [local(): lax.dot_general(activations, grad_out, (((0,), (0,)), ((), ())), preferre...]
    ppermute x3 -> x13, starting transfers between devices: 3.61 us -> 23.5 us  [the longest x12 16.7 us: exchange(): return lax.ppermute(array, ('node', 'fsdp'), pairing(axis, first))]
    all_to_all x0 -> x1, blocking collectives: none -> 14.7 us  [local(): sums = lax.all_to_all(gram, ('node', 'fsdp'), 0, 0, tiled=True)]
    another operation x3, other arithmetic: 5.9 us -> 0.78 us  [the longest x1 0.67 us: local(): place = jnp.stack([y ^ 2, y ^ m1, y ^ m2, y]).astype(jnp.int32)]
  transfers between devices with their start and end apart: 4 -> 13, of which waited for: 4 -> 13; matrix products, arithmetic and copies ran while one was open for 0% -> 1% of each run, Pallas kernels for 0% -> 13%
where the time goes in v1:
time: 183 us; the launch traced here: 182 us
  Pallas kernels  74.2 us (41%)
  waiting for transfers between devices  64.4 us (35%)
  starting transfers between devices  23.5 us (13%)
  blocking collectives  14.7 us (8%)
  local copies, waits for them, and re-layouts  4.33 us (2%)
    ppermute x12, waiting for transfers between devices, exchange(): return lax.ppermute(array, ('node', 'fsdp'), pairing(axis, first))  62.8 us
    pallas_call x4, Pallas kernels, step(): pl.pallas_call(functools.partial(step_kernel, which, rows, picks), grid=(...  42.9 us
    ppermute x12, starting transfers between devices, exchange(): return lax.ppermute(array, ('node', 'fsdp'), pairing(axis, first))  16.7 us
    all_to_all x1, blocking collectives, local(): sums = lax.all_to_all(gram, ('node', 'fsdp'), 0, 0, tiled=True)  14.7 us
    pallas_call x1, Pallas kernels, first(): pl.pallas_call(functools.partial(first_kernel, rows), grid=(cols // tile,...  13.1 us
    pallas_call x1, Pallas kernels, last(): pl.pallas_call(functools.partial(last_kernel, rows, picks), grid_spec=plt...  10.7 us
    ppermute x1, starting transfers between devices, local(): carr = lax.ppermute(across, 'node', [(i, i ^ 1) for i in range(2 * SIDE)])  6.74 us
    pallas_call x1, Pallas kernels, local(): pl.pallas_call(functools.partial(gram_kernel, 2 * rows, half), out_shape=...  4.28 us
  transfers between devices with their start and end apart: 13, of which 13 were waited for; matrix products, arithmetic and copies ran while one was open for 1% of the time, Pallas kernels for 13%

profile of v1, /device:TPU:1, one launch (start us, length us, event | category | flops | bytes accessed | tf_op | source)
XLA Modules:
  0.0 182.0 jit_solution(5439019040943111254)
XLA Ops:
  0.0 13.1 %p1a.1 = (bf16[2560,1024]{1,0:T(8,128)(2,1)}, bf16[336,2560]{1,0:T(8,128)(2,1)}, bf16[336,2560]{1,0:T(8,128)(2,1)}) custom-call(bf16[1024,2560]{1,0:T(8,128)(2,1)} %x_ref.1, bf16[1024,2560]{1,0:T(8,128)(2,1)} %dy_ref.11), custom_call_target="tpu_custom_call" | custom-call | tf_op jit(solution)/shard_map/p1a/pallas_call | solution.py:167
  13.1 3.3 %collective-permute-start.2 = (bf16[336,2560]{1,0:T(8,128)(2,1)}, bf16[336,2560]{1,0:T(8,128)(2,1)}, u32[]{:S(2)}, u32[]{:S(2)}) collective-permute-start(bf16[336,2560]{1,0:T(8,128)(2,1)} %get-tuple-element.23), channel_id=1, source_target_pairs={{0,1},{1,0},{2,3},{3,2},{4,5},{5,4},{6,7},{7,6},{8,9},{9,8},{10,11... | collective-permute-start | bytes 5160968 | tf_op jit(solution)/shard_map/ppermute | solution.py:60
  16.4 3.8 %collective-permute-start.3 = (bf16[336,2560]{1,0:T(8,128)(2,1)}, bf16[336,2560]{1,0:T(8,128)(2,1)}, u32[]{:S(2)}, u32[]{:S(2)}) collective-permute-start(bf16[336,2560]{1,0:T(8,128)(2,1)} %get-tuple-element.24), channel_id=1, source_target_pairs={{0,4},{1,5},{2,6},{3,7},{4,0},{5,1},{6,2},{7,3},{8,12},{9,13},{10,... | collective-permute-start | bytes 5160968 | tf_op jit(solution)/shard_map/ppermute | solution.py:60
  20.2 10.5 %p1b.1 = (bf16[336,2560]{1,0:T(8,128)(2,1)}, bf16[336,2560]{1,0:T(8,128)(2,1)}) custom-call(bf16[2560,1024]{1,0:T(8,128)(2,1)} %get-tuple-element.20.xt_ref, bf16[1024,2560]{1,0:T(8,128)(2,1)} %dy_ref.11), custom_call_target="tpu_custom_call" | custom-call | tf_op jit(solution)/shard_map/p1b/pallas_call | solution.py:149
  30.6 0.3 collective-permute-start
  30.9 0.0 collective-permute-start.1
  30.9 5.2 %collective-permute-done.2.rest_0_ = bf16[336,2560]{1,0:T(8,128)(2,1)} collective-permute-done((bf16[336,2560]{1,0:T(8,128)(2,1)}, bf16[336,2560]{1,0:T(8,128)(2,1)}, u32[]{:S(2)}, u32[]{:S(2)}) %collective-permute-start.2) | collective-permute-done | bytes 1720352 | tf_op jit(solution)/shard_map/ppermute | solution.py:60
  36.1 3.8 %collective-permute-done.3.rest_1_ = bf16[336,2560]{1,0:T(8,128)(2,1)} collective-permute-done((bf16[336,2560]{1,0:T(8,128)(2,1)}, bf16[336,2560]{1,0:T(8,128)(2,1)}, u32[]{:S(2)}, u32[]{:S(2)}) %collective-permute-start.3) | collective-permute-done | bytes 1720352 | tf_op jit(solution)/shard_map/ppermute | solution.py:60
  39.9 12.6 %p2.1 = (bf16[336,2560]{1,0:T(8,128)(2,1)}, bf16[336,2560]{1,0:T(8,128)(2,1)}) custom-call(bf16[2560,1024]{1,0:T(8,128)(2,1)} %get-tuple-element.20.xt_ref, bf16[1024,2560]{1,0:T(8,128)(2,1)} %dy_ref.11, bf16[336,2560]{1,0:T(8,128)(2,1)} %collective-permute-done.2.rest_0_, bf16[336,2560]{1,0:T(8,128)(2,1)} %collective-permute-done.3.rest_1_), custom_call_target="tpu_custom_call" | custom-call | tf_op jit(solution)/shard_map/p2/pallas_call | solution.py:149
  52.4 0.1 collective-permute-start.4
  52.5 0.1 collective-permute-start.5
  52.6 1.8 collective-permute-done.rest_0_
  54.4 4.2 %collective-permute-done.1.rest_1_ = bf16[336,2560]{1,0:T(8,128)(2,1)S(1)} collective-permute-done((bf16[336,2560]{1,0:T(8,128)(2,1)}, bf16[336,2560]{1,0:T(8,128)(2,1)S(1)}, u32[]{:S(2)}, u32[]{:S(2)}) %collective-permute-start.1) | collective-permute-done | bytes 1720352 | tf_op jit(solution)/shard_map/ppermute | solution.py:60
  58.6 15.4 %collective-permute-done.4.rest_2_ = bf16[336,2560]{1,0:T(8,128)(2,1)} collective-permute-done((bf16[336,2560]{1,0:T(8,128)(2,1)}, bf16[336,2560]{1,0:T(8,128)(2,1)}, u32[]{:S(2)}, u32[]{:S(2)}) %collective-permute-start.4) | collective-permute-done | bytes 1720352 | tf_op jit(solution)/shard_map/ppermute | solution.py:60
  74.0 0.9 collective-permute-done.5.rest_3_
  74.9 0.0 copy-done
  74.9 0.0 copy-done.1
  74.9 10.3 %q1.1 = (bf16[176,2560]{1,0:T(8,128)(2,1)}, bf16[176,2560]{1,0:T(8,128)(2,1)}) custom-call(bf16[2560,1024]{1,0:T(8,128)(2,1)} %get-tuple-element.20.xt_ref, bf16[1024,2560]{1,0:T(8,128)(2,1)} %dy_ref.11, bf16[336,2560]{1,0:T(8,128)(2,1)} %copy-done, bf16[336,2560]{1,0:T(8,128)(2,1)} %copy-done.1, bf16[336,2560]{1,0:T(8,128)(2,1)} %collective-permute-done.4.rest_2_, ...), custom_call_target="tpu_custom_call" | custom-call | tf_op jit(solution)/shard_map/q1/pallas_call | solution.py:149
  85.2 3.8 %collective-permute-start.6 = (bf16[176,2560]{1,0:T(8,128)(2,1)}, bf16[176,2560]{1,0:T(8,128)(2,1)S(1)}, u32[]{:S(2)}, u32[]{:S(2)}) collective-permute-start(bf16[176,2560]{1,0:T(8,128)(2,1)} %get-tuple-element.27), channel_id=1, source_target_pairs={{0,4},{1,5},{2,6},{3,7},{4,0},{5,1},{6,2},{7,3},{8,12},{9,13},{10,... | collective-permute-start | bytes 2703368 | tf_op jit(solution)/shard_map/ppermute | solution.py:60
  89.1 1.8 %collective-permute-start.7 = (bf16[176,2560]{1,0:T(8,128)(2,1)}, bf16[176,2560]{1,0:T(8,128)(2,1)S(1)}, u32[]{:S(2)}, u32[]{:S(2)}) collective-permute-start(bf16[176,2560]{1,0:T(8,128)(2,1)} %get-tuple-element.28), channel_id=1, source_target_pairs={{0,1},{1,0},{2,3},{3,2},{4,5},{5,4},{6,7},{7,6},{8,9},{9,8},{10,11... | collective-permute-start | bytes 2703368 | tf_op jit(solution)/shard_map/ppermute | solution.py:60
  90.9 9.0 %collective-permute-done.6.rest_4_ = bf16[176,2560]{1,0:T(8,128)(2,1)S(1)} collective-permute-done((bf16[176,2560]{1,0:T(8,128)(2,1)}, bf16[176,2560]{1,0:T(8,128)(2,1)S(1)}, u32[]{:S(2)}, u32[]{:S(2)}) %collective-permute-start.6) | collective-permute-done | bytes 901152 | tf_op jit(solution)/shard_map/ppermute | solution.py:60
  99.9 2.7 %collective-permute-done.7.rest_5_ = bf16[176,2560]{1,0:T(8,128)(2,1)S(1)} collective-permute-done((bf16[176,2560]{1,0:T(8,128)(2,1)}, bf16[176,2560]{1,0:T(8,128)(2,1)S(1)}, u32[]{:S(2)}, u32[]{:S(2)}) %collective-permute-start.7) | collective-permute-done | bytes 901152 | tf_op jit(solution)/shard_map/ppermute | solution.py:60
  102.5 0.0 copy-done.2
  102.6 0.9 copy-done.3
  103.5 9.5 %q2.1 = (bf16[96,2560]{1,0:T(8,128)(2,1)}, bf16[96,2560]{1,0:T(8,128)(2,1)}) custom-call(bf16[2560,1024]{1,0:T(8,128)(2,1)} %get-tuple-element.20.xt_ref, bf16[1024,2560]{1,0:T(8,128)(2,1)} %dy_ref.11, bf16[336,2560]{1,0:T(8,128)(2,1)} %copy-done, bf16[336,2560]{1,0:T(8,128)(2,1)} %copy-done.1, bf16[336,2560]{1,0:T(8,128)(2,1)} %collective-permute-done.4.rest_2_, ...), custom_call_target="tpu_custom_call" | custom-call | tf_op jit(solution)/shard_map/q2/pallas_call | solution.py:149
  113.0 0.1 collective-permute-start.8
  113.1 0.1 collective-permute-start.9
  113.2 0.7 pad_add_fusion.place
  113.9 7.4 %collective-permute-done.8.rest_6_ = bf16[96,2560]{1,0:T(8,128)(2,1)S(1)} collective-permute-done((bf16[96,2560]{1,0:T(8,128)(2,1)}, bf16[96,2560]{1,0:T(8,128)(2,1)S(1)}, u32[]{:S(2)}, u32[]{:S(2)}) %collective-permute-start.8) | collective-permute-done | bytes 491552 | tf_op jit(solution)/shard_map/ppermute | solution.py:60
  121.3 0.1 collective-permute-done.9.rest_7_
  121.3 0.7 copy-done.7
  122.0 0.8 copy-done.8
  122.8 10.7 %last.1 = (bf16[2,176,640]{2,1,0:T(8,128)(2,1)}, bf16[2,176,640]{2,1,0:T(8,128)(2,1)}) custom-call(s32[4]{0:T(128)} %pad_add_fusion.place, bf16[2560,1024]{1,0:T(8,128)(2,1)} %get-tuple-element.20.xt_ref, bf16[1024,2560]{1,0:T(8,128)(2,1)} %dy_ref.11, bf16[336,2560]{1,0:T(8,128)(2,1)} %copy-done, bf16[336,2560]{1,0:T(8,128)(2,1)} %copy-done.1, ...), custom_call_target="tpu_custom_call" | custom-call | tf_op jit(solution)/shard_map/last/pallas_call | solution.py:211
  133.5 2.8 %collective-permute-start.10 = (bf16[2,176,640]{2,1,0:T(8,128)(2,1)}, bf16[2,176,640]{2,1,0:T(8,128)(2,1)S(1)}, u32[]{:S(2)}, u32[]{:S(2)}) collective-permute-start(bf16[2,176,640]{2,1,0:T(8,128)(2,1)} %get-tuple-element.32), channel_id=1, source_target_pairs={{0,32},{1,33},{2,34},{3,35},{4,36},{5,37},{6,38},{7,39},{8,40},{9,... | collective-permute-start | bytes 1351688 | tf_op jit(solution)/shard_map/ppermute | solution.py:60
  136.4 1.1 fusion.3
  137.4 4.9 %collective-permute-done.10.y1arr = bf16[2,176,640]{2,1,0:T(8,128)(2,1)S(1)} collective-permute-done((bf16[2,176,640]{2,1,0:T(8,128)(2,1)}, bf16[2,176,640]{2,1,0:T(8,128)(2,1)S(1)}, u32[]{:S(2)}, u32[]{:S(2)}) %collective-permute-start.10) | collective-permute-done | bytes 450592 | tf_op jit(solution)/shard_map/ppermute | solution.py:60
  142.4 0.1 pad_maximum_fusion
  142.5 0.6 collective-permute-start.11
  143.0 7.6 %collective-permute-done.11.y2arr = bf16[2,176,640]{2,1,0:T(8,128)(2,1)S(1)} collective-permute-done((bf16[2,176,640]{2,1,0:T(8,128)(2,1)S(1)}, bf16[2,176,640]{2,1,0:T(8,128)(2,1)S(1)}, u32[]{:S(2)}, u32[]{:S(2)}) %collective-permute-start.11) | collective-permute-done | bytes 450592 | tf_op jit(solution)/shard_map/ppermute | solution.py:60
  150.7 0.1 fusion.1
  150.7 6.7 %collective-permute-start.12 = (bf16[4,176,384]{2,1,0:T(8,128)(2,1)S(1)}, bf16[4,176,384]{2,1,0:T(8,128)(2,1)S(1)}, u32[]{:S(2)}, u32[]{:S(2)}) collective-permute-start(bf16[4,176,384]{2,1,0:T(8,128)(2,1)S(1)} %fusion.1), channel_id=1, source_target_pairs={{0,16},{16,0},{32,48},{48,32},{64,80},{80,64},{96,112},{112,96},{1... | collective-permute-start | bytes 1622024 | tf_op jit(solution)/shard_map/ppermute | solution.py:331
  157.5 1.6 collective-permute-done.12.carr
  159.0 0.0 copy-done.4
  159.0 0.0 copy-done.5
  159.0 0.8 copy-done.6
  159.8 4.3 %gram.1 = (f32[8,160,384]{2,1,0:T(8,128)}, f32[128,128]{1,0:T(8,128)}) custom-call(bf16[2,176,640]{2,1,0:T(8,128)(2,1)} %get-tuple-element.31.y2own, bf16[2,176,640]{2,1,0:T(8,128)(2,1)} %copy-done.4, bf16[2,176,640]{2,1,0:T(8,128)(2,1)} %copy-done.5, bf16[4,176,384]{2,1,0:T(8,128)(2,1)} %copy-done.6), custom_call_target="tpu_custom_call" | custom-call | tf_op jit(solution)/shard_map/gram/pallas_call | solution.py:334
  164.1 14.7 %all_to_all.11 = f32[128,1,128]{2,1,0:T(1,128)} all-to-all(f32[128,1,128]{2,1,0:T(1,128)} %bitcast.9), channel_id=1, replica_groups=mesh['node'=8,'fsdp'=16] {'node','fsdp'}, dimensions={0} | all-to-all | bytes 131072 | tf_op jit(solution)/shard_map/all_to_all | solution.py:343
  178.8 3.2 %combine.1 = f32[160,320]{1,0:T(8,128)} custom-call(f32[8,160,384]{2,1,0:T(8,128)} %get-tuple-element.33.g_ref, f32[128,128]{1,0:T(8,128)} %bitcast.8), custom_call_target="tpu_custom_call" | custom-call | tf_op jit(solution)/shard_map/combine/pallas_call | solution.py:344
  (10 shorter events, 0.1 us)
Async XLA Ops:
  13.1 23.0 %collective-permute-start.2 = (bf16[336,2560]{1,0:T(8,128)(2,1)}, bf16[336,2560]{1,0:T(8,128)(2,1)}, u32[]{:S(2)}, u32[]{:S(2)}) collective-permute-start(bf16[336,2560]{1,0:T(8,128)(2,1)} %get-tuple-element.23), channel_id=1, source_target_pairs={{0,1},{1,0},{2,3},{3,2},{4,5},{5,4},{6,7},{7,6},{8,9},{9,8},{10,11... | collective-permute-start | bytes 5160968 | tf_op jit(solution)/shard_map/ppermute | solution.py:60
  16.4 23.5 %collective-permute-start.3 = (bf16[336,2560]{1,0:T(8,128)(2,1)}, bf16[336,2560]{1,0:T(8,128)(2,1)}, u32[]{:S(2)}, u32[]{:S(2)}) collective-permute-start(bf16[336,2560]{1,0:T(8,128)(2,1)} %get-tuple-element.24), channel_id=1, source_target_pairs={{0,4},{1,5},{2,6},{3,7},{4,0},{5,1},{6,2},{7,3},{8,12},{9,13},{10,... | collective-permute-start | bytes 5160968 | tf_op jit(solution)/shard_map/ppermute | solution.py:60
  30.6 23.8 %collective-permute-start = (bf16[336,2560]{1,0:T(8,128)(2,1)}, bf16[336,2560]{1,0:T(8,128)(2,1)S(1)}, u32[]{:S(2)}, u32[]{:S(2)}) collective-permute-start(bf16[336,2560]{1,0:T(8,128)(2,1)} %get-tuple-element.21), channel_id=1, source_target_pairs={{0,1},{1,0},{2,3},{3,2},{4,5},{5,4},{6,7},{7,6},{8,9},{9,8},{10,11... | collective-permute-start | bytes 5160968 | tf_op jit(solution)/shard_map/ppermute | solution.py:60
  30.9 27.7 %collective-permute-start.1 = (bf16[336,2560]{1,0:T(8,128)(2,1)}, bf16[336,2560]{1,0:T(8,128)(2,1)S(1)}, u32[]{:S(2)}, u32[]{:S(2)}) collective-permute-start(bf16[336,2560]{1,0:T(8,128)(2,1)} %get-tuple-element.22), channel_id=1, source_target_pairs={{0,4},{1,5},{2,6},{3,7},{4,0},{5,1},{6,2},{7,3},{8,12},{9,13},{10,... | collective-permute-start | bytes 5160968 | tf_op jit(solution)/shard_map/ppermute | solution.py:60
  52.4 21.5 %collective-permute-start.4 = (bf16[336,2560]{1,0:T(8,128)(2,1)}, bf16[336,2560]{1,0:T(8,128)(2,1)}, u32[]{:S(2)}, u32[]{:S(2)}) collective-permute-start(bf16[336,2560]{1,0:T(8,128)(2,1)} %get-tuple-element.25), channel_id=1, source_target_pairs={{0,3},{1,2},{2,1},{3,0},{4,7},{5,6},{6,5},{7,4},{8,11},{9,10},{10,... | collective-permute-start | bytes 5160968 | tf_op jit(solution)/shard_map/ppermute | solution.py:60
  52.5 22.3 %collective-permute-start.5 = (bf16[336,2560]{1,0:T(8,128)(2,1)}, bf16[336,2560]{1,0:T(8,128)(2,1)}, u32[]{:S(2)}, u32[]{:S(2)}) collective-permute-start(bf16[336,2560]{1,0:T(8,128)(2,1)} %get-tuple-element.26), channel_id=1, source_target_pairs={{0,12},{1,13},{2,14},{3,15},{4,8},{5,9},{6,10},{7,11},{8,4},{9,5},... | collective-permute-start | bytes 5160968 | tf_op jit(solution)/shard_map/ppermute | solution.py:60
  54.4 20.4 %copy-start = (bf16[336,2560]{1,0:T(8,128)(2,1)}, bf16[336,2560]{1,0:T(8,128)(2,1)S(1)}, u32[]{:S(2)}) copy-start(bf16[336,2560]{1,0:T(8,128)(2,1)S(1)} %collective-permute-done.rest_0_) | copy-start | bytes 5160964
  58.6 16.3 %copy-start.1 = (bf16[336,2560]{1,0:T(8,128)(2,1)}, bf16[336,2560]{1,0:T(8,128)(2,1)S(1)}, u32[]{:S(2)}) copy-start(bf16[336,2560]{1,0:T(8,128)(2,1)S(1)} %collective-permute-done.1.rest_1_) | copy-start | bytes 5160964
  85.2 14.7 %collective-permute-start.6 = (bf16[176,2560]{1,0:T(8,128)(2,1)}, bf16[176,2560]{1,0:T(8,128)(2,1)S(1)}, u32[]{:S(2)}, u32[]{:S(2)}) collective-permute-start(bf16[176,2560]{1,0:T(8,128)(2,1)} %get-tuple-element.27), channel_id=1, source_target_pairs={{0,4},{1,5},{2,6},{3,7},{4,0},{5,1},{6,2},{7,3},{8,12},{9,13},{10,... | collective-permute-start | bytes 2703368 | tf_op jit(solution)/shard_map/ppermute | solution.py:60
  89.1 13.5 %collective-permute-start.7 = (bf16[176,2560]{1,0:T(8,128)(2,1)}, bf16[176,2560]{1,0:T(8,128)(2,1)S(1)}, u32[]{:S(2)}, u32[]{:S(2)}) collective-permute-start(bf16[176,2560]{1,0:T(8,128)(2,1)} %get-tuple-element.28), channel_id=1, source_target_pairs={{0,1},{1,0},{2,3},{3,2},{4,5},{5,4},{6,7},{7,6},{8,9},{9,8},{10,11... | collective-permute-start | bytes 2703368 | tf_op jit(solution)/shard_map/ppermute | solution.py:60
  99.9 2.7 %copy-start.2 = (bf16[176,2560]{1,0:T(8,128)(2,1)}, bf16[176,2560]{1,0:T(8,128)(2,1)S(1)}, u32[]{:S(2)}) copy-start(bf16[176,2560]{1,0:T(8,128)(2,1)S(1)} %collective-permute-done.6.rest_4_) | copy-start | bytes 2703364
  102.5 0.9 copy-start.3
  113.0 8.3 %collective-permute-start.8 = (bf16[96,2560]{1,0:T(8,128)(2,1)}, bf16[96,2560]{1,0:T(8,128)(2,1)S(1)}, u32[]{:S(2)}, u32[]{:S(2)}) collective-permute-start(bf16[96,2560]{1,0:T(8,128)(2,1)} %get-tuple-element.29), channel_id=1, source_target_pairs={{0,12},{1,13},{2,14},{3,15},{4,8},{5,9},{6,10},{7,11},{8,4},{9,5},... | collective-permute-start | bytes 1474568 | tf_op jit(solution)/shard_map/ppermute | solution.py:60
  113.1 8.3 %collective-permute-start.9 = (bf16[96,2560]{1,0:T(8,128)(2,1)}, bf16[96,2560]{1,0:T(8,128)(2,1)S(1)}, u32[]{:S(2)}, u32[]{:S(2)}) collective-permute-start(bf16[96,2560]{1,0:T(8,128)(2,1)} %get-tuple-element.30), channel_id=1, source_target_pairs={{0,3},{1,2},{2,1},{3,0},{4,7},{5,6},{6,5},{7,4},{8,11},{9,10},{10,... | collective-permute-start | bytes 1474568 | tf_op jit(solution)/shard_map/ppermute | solution.py:60
  121.3 0.8 copy-start.7
  122.0 0.8 copy-start.8
  133.5 8.8 %collective-permute-start.10 = (bf16[2,176,640]{2,1,0:T(8,128)(2,1)}, bf16[2,176,640]{2,1,0:T(8,128)(2,1)S(1)}, u32[]{:S(2)}, u32[]{:S(2)}) collective-permute-start(bf16[2,176,640]{2,1,0:T(8,128)(2,1)} %get-tuple-element.32), channel_id=1, source_target_pairs={{0,32},{1,33},{2,34},{3,35},{4,36},{5,37},{6,38},{7,39},{8,40},{9,... | collective-permute-start | bytes 1351688 | tf_op jit(solution)/shard_map/ppermute | solution.py:60
  142.3 16.7 %copy-start.4 = (bf16[2,176,640]{2,1,0:T(8,128)(2,1)}, bf16[2,176,640]{2,1,0:T(8,128)(2,1)S(1)}, u32[]{:S(2)}) copy-start(bf16[2,176,640]{2,1,0:T(8,128)(2,1)S(1)} %collective-permute-done.10.y1arr) | copy-start | bytes 1351684
  142.5 8.2 %collective-permute-start.11 = (bf16[2,176,640]{2,1,0:T(8,128)(2,1)S(1)}, bf16[2,176,640]{2,1,0:T(8,128)(2,1)S(1)}, u32[]{:S(2)}, u32[]{:S(2)}) collective-permute-start(bf16[2,176,640]{2,1,0:T(8,128)(2,1)S(1)} %pad_maximum_fusion), channel_id=1, source_target_pairs={{0,96},{1,97},{2,98},{3,99},{4,100},{5,101},{6,102},{7,103},{8,104... | collective-permute-start | bytes 1351688 | tf_op jit(solution)/shard_map/ppermute | solution.py:60
  150.7 8.4 %copy-start.5 = (bf16[2,176,640]{2,1,0:T(8,128)(2,1)}, bf16[2,176,640]{2,1,0:T(8,128)(2,1)S(1)}, u32[]{:S(2)}) copy-start(bf16[2,176,640]{2,1,0:T(8,128)(2,1)S(1)} %collective-permute-done.11.y2arr) | copy-start | bytes 1351684
  150.7 8.3 %collective-permute-start.12 = (bf16[4,176,384]{2,1,0:T(8,128)(2,1)S(1)}, bf16[4,176,384]{2,1,0:T(8,128)(2,1)S(1)}, u32[]{:S(2)}, u32[]{:S(2)}) collective-permute-start(bf16[4,176,384]{2,1,0:T(8,128)(2,1)S(1)} %fusion.1), channel_id=1, source_target_pairs={{0,16},{16,0},{32,48},{48,32},{64,80},{80,64},{96,112},{112,96},{1... | collective-permute-start | bytes 1622024 | tf_op jit(solution)/shard_map/ppermute | solution.py:331
  159.0 0.8 copy-start.6

commit v2 on v1

v2 whole, which is shorter than its diff:
```python
import functools

import jax
import jax.numpy as jnp
from jax import lax
from jax.experimental import pallas as pl
from jax.experimental.pallas import tpu as pltpu
from jax.sharding import PartitionSpec as P

EPS = 1e-06
POWER = 17
TOP = 2.0 ** (124 / POWER)
TINY = 2.0**-126
PAD = 8
SIDE = 4
BF16, F32 = jnp.bfloat16, jnp.float32


def encode(values):
    peak = jnp.max(jnp.abs(values), axis=0, keepdims=True).astype(BF16)
    x = values * (TOP / jnp.maximum(peak.astype(F32), TINY))
    x2 = x * x
    x4 = x2 * x2
    x8 = x4 * x4
    return (x8 * x8 * x).astype(BF16), peak


def decode(code, peak):
    code = code.astype(F32)
    size = jnp.exp(jnp.log(jnp.abs(code)) * (1.0 / POWER))
    return jnp.where(code < 0, -size, size) * (peak.astype(F32) * (1.0 / TOP))


def coordinates():
    node, fsdp = lax.axis_index("node"), lax.axis_index("fsdp")
    return lax.rem(fsdp, SIDE), node // 2, fsdp // SIDE, lax.rem(node, 2)


def masks(core):
    return 1 + 2 * core, 3 - 2 * core


def pairing(axis, first):
    pairs = []
    for y in range(SIDE):
        for core in range(2):
            mask = masks(core)[0 if first else 1]
            for z in range(SIDE):
                for x in range(SIDE):
                    at = dict(x=x, y=y, z=z)
                    to = dict(at)
                    to[axis] ^= mask
                    index = lambda p: (p["y"] * 2 + core) * SIDE * SIDE + p["z"] * SIDE + p["x"]
                    pairs.append((index(at), index(to)))
    return pairs


def exchange(array, axis, first):
    return lax.ppermute(array, ("node", "fsdp"), pairing(axis, first))


def block_offset(stream, p, q, rows):
    owner = jnp.where(stream == 0, q * SIDE + p, p * SIDE + q)
    return pl.multiple_of((owner * 2 + stream) * rows, 16)


def wanted(which, rows):
    x, _, z, core = coordinates()
    m1, m2 = masks(core)
    offsets = []
    for stream in range(2):
        p, q = (x, z) if stream == 0 else (z, x)
        everything = [q ^ 2, q ^ m1, q ^ m2, q]
        ps, qs = {
            "p1a_near": (p ^ 2, everything[:2]),
            "p1a_far": (p ^ 2, everything[2:]),
            "p1b_near": (p ^ m1, everything[:2]),
            "p1b_far": (p ^ m1, everything[2:]),
            "p2_near": (p ^ m2, everything[:2]),
            "p2_far": (p ^ m2, everything[2:]),
            "kept_near": (p, everything[:2]),
            "kept_far": (p, everything[2:]),
        }[which]
        offsets.append([block_offset(stream, ps, each, rows) for each in qs])
    return offsets


def gather(xt_ref, lhs, offsets, rows):
    for s in range(2):
        for b, offset in enumerate(offsets[s]):
            at = (s * len(offsets[s]) + b) * rows
            lhs[at : at + rows, :] = xt_ref[pl.ds(offset, rows), :]


def first_kernel(rows, tile, x_ref, dy_ref, xt_ref, dy_vmem, out0, out1, x_vmem, lhs, x_sems, dy_sems):
    x_cols, dy_cols = list(parts_of(x_ref, tile)), list(parts_of(dy_ref, tile))

    def bring(source, target, sems, cols):
        return [
            pltpu.make_async_copy(source.at[:, pl.ds(c.start, tile)], target.at[:, pl.ds(c.start, tile)], sems.at[t])
            for t, c in enumerate(cols)
        ]

    x_copies, dy_copies = bring(x_ref, x_vmem, x_sems, x_cols), bring(dy_ref, dy_vmem, dy_sems, dy_cols)
    for copy in x_copies + dy_copies:
        copy.start()
    for cols, copy in zip(x_cols, x_copies):
        copy.wait()
        xt_ref[cols, :] = x_vmem[:, cols].T
    gather(xt_ref, lhs, wanted("p1a_near", rows), rows)
    size = 2 * rows
    for cols, copy in zip(dy_cols, dy_copies):
        copy.wait()
        total = jnp.dot(lhs[...], dy_vmem[:, cols], preferred_element_type=F32)
        for s, out in enumerate((out0, out1)):
            write(out, total[s * size : (s + 1) * size], cols)


def product_kernel(which, rows, tile, coded, xt_ref, dy_ref, *rest):
    arrivals, (_, _, out0, out1, lhs) = rest[:-5], rest[-5:]
    offsets = wanted(which, rows)
    count = len(offsets[0])
    size = count * rows
    gather(xt_ref, lhs, offsets, rows)
    for cols in parts_of(dy_ref, tile):
        total = jnp.dot(lhs[...], dy_ref[:, cols], preferred_element_type=F32)
        for s, out in enumerate((out0, out1)):
            part = total[s * size : (s + 1) * size]
            for ref in arrivals[s::2]:
                part += read(ref, rows, 0, count, cols)
            if coded:
                write(out, part, cols)
            else:
                out[:, cols] = part


def params(mib):
    return pltpu.CompilerParams(vmem_limit_bytes=mib * 2**20)


def column(i):
    return (0, i)


VMEM = pl.BlockSpec(memory_space=pltpu.VMEM)


def product(which, rows, tile, count, xt, dy, arrivals, after, coded=True):
    tokens, cols = dy.shape
    size = count * rows
    message = jax.ShapeDtypeStruct((size + PAD if coded else size, cols), BF16 if coded else F32)
    return pl.pallas_call(
        functools.partial(product_kernel, which, rows, tile, coded),
        out_shape=[message, message],
        in_specs=[VMEM] * (2 + len(arrivals)) + [pl.BlockSpec(memory_space=pl.ANY)] * 2,
        out_specs=[VMEM] * 2,
        scratch_shapes=[pltpu.VMEM((2 * size, tokens), BF16)],
        compiler_params=params(12),
        name=which,
    )(xt, dy, *arrivals, *after)


def first(rows, tile, x, dy):
    tokens, cols = dy.shape
    size = 2 * rows
    message = jax.ShapeDtypeStruct((size + PAD, cols), BF16)
    xt = jax.ShapeDtypeStruct((x.shape[1], tokens), BF16)
    return pl.pallas_call(
        functools.partial(first_kernel, rows, tile),
        out_shape=[xt, jax.ShapeDtypeStruct(dy.shape, BF16), message, message],
        in_specs=[pl.BlockSpec(memory_space=pltpu.HBM)] * 2,
        out_specs=[VMEM] * 4,
        scratch_shapes=[
            pltpu.VMEM(x.shape, BF16),
            pltpu.VMEM((2 * size, tokens), BF16),
            pltpu.SemaphoreType.DMA((x.shape[1] // tile,)),
            pltpu.SemaphoreType.DMA((cols // tile,)),
        ],
        compiler_params=params(40),
        name="p1a_near",
    )(x, dy)


def parts_of(ref, tile):
    for at in range(0, ref.shape[1], tile):
        yield slice(at, at + tile)


def read(ref, rows, at, count, cols=slice(None)):
    scale = ref.shape[0] - PAD
    return decode(ref[at * rows : (at + count) * rows, cols], ref[scale : scale + 1, cols])


def write(out, values, cols=slice(None)):
    code, peak = encode(values)
    size = values.shape[0]
    out[:size, cols] = code
    out[size:, cols] = jnp.broadcast_to(peak, (PAD, peak.shape[1]))


def near_kernel(rows, tile, kept0, kept1, arr0, arr1, *rest):
    for kept, arr, out in ((kept0, arr0, rest[-2]), (kept1, arr1, rest[-1])):
        for cols in parts_of(kept, tile):
            write(out, kept[:rows, cols] + read(arr, rows, 0, 1, cols), cols)


def far_kernel(rows, tile, kept0, kept1, arr0, arr1, *rest):
    for kept, arr, out in ((kept0, arr0, rest[-2]), (kept1, arr1, rest[-1])):
        for cols in parts_of(kept, tile):
            write(out, kept[rows:, cols] + read(arr, rows, 1, 1, cols), cols)


def add_kernel(rows, tile, kept0, kept1, arr0, arr1, out0, out1):
    for kept, arr, out in ((kept0, arr0, out0), (kept1, arr1, out1)):
        for cols in parts_of(kept, tile):
            out[:, cols] = kept[:, cols] + read(arr, rows, 0, 2, cols)


def own_kernel(rows, tile, kept0, kept1, arr0, arr1, out):
    for s, (kept, arr) in enumerate(((kept0, arr0), (kept1, arr1))):
        for cols in parts_of(kept, tile):
            out[s * rows : (s + 1) * rows, cols] = kept[rows:, cols] + read(arr, rows, 0, 1, cols)


def merge(name, kernel, rows, tile, ins, heights, outs, after=()):
    cols = ins[0].shape[1]
    return pl.pallas_call(
        functools.partial(kernel, rows, tile),
        out_shape=[jax.ShapeDtypeStruct((h, cols), dtype) for h, dtype in zip(heights, outs)],
        in_specs=[VMEM] * len(ins) + [pl.BlockSpec(memory_space=pl.ANY)] * len(after),
        out_specs=[VMEM] * len(outs),
        compiler_params=params(12),
        name=name,
    )(*ins, *after)


def last_kernel(rows, place, own, arr0, arr1, out0, out1, out2, out3):
    values = jnp.concatenate([own[s * rows : (s + 1) * rows, :] + read(a, rows, 0, 1) for s, a in enumerate((arr0, arr1))])
    for k, out in enumerate((out0, out1, out2, out3)):
        pl.when(pl.program_id(0) == k)(functools.partial(write, out, values))


def last(rows, place, own, arrivals):
    cols = own.shape[1]
    tile = cols // SIDE
    height = 2 * rows + PAD
    at = lambda i, place: (0, place[i])
    return pl.pallas_call(
        functools.partial(last_kernel, rows),
        grid_spec=pltpu.PrefetchScalarGridSpec(
            num_scalar_prefetch=1,
            grid=(SIDE,),
            in_specs=[pl.BlockSpec((2 * rows, tile), at)] + [pl.BlockSpec((a.shape[0], tile), at) for a in arrivals],
            out_specs=[pl.BlockSpec((height, tile), lambda i, place: (0, 0))] * SIDE,
        ),
        out_shape=[jax.ShapeDtypeStruct((height, tile), BF16)] * SIDE,
        compiler_params=params(12),
        name="last",
    )(place, own, *arrivals)


def gram_kernel(rows, half, own0, own1, own2, own3, carr, g_ref, gram_ref):
    _, y, _, core = coordinates()
    m1, m2 = masks(core)
    wide = g_ref.shape[2]
    lane = lax.broadcasted_iota(jnp.int32, (1, wide), 1)
    start = (wide - half) * core
    valid = (lane >= start) & (lane < start + half)
    at = pl.ds(pl.multiple_of((own0.shape[1] - wide) * core, 128), wide)
    sources = [(own0, 0, 0), (own1, m1, m2), (own2, m2, m1), (own3, 2, 2)]
    for k, (ref, mask, mask_other) in enumerate(sources):
        own = decode(ref[:rows, at], ref[rows : rows + 1, at])
        g_ref[(y ^ mask) * 2 + core] = jnp.where(valid, own, 0.0)
        other = decode(carr[k, :rows, :], carr[k, rows : rows + 1, :])
        g_ref[(y ^ mask_other) * 2 + 1 - core] = jnp.where(valid, other, 0.0)
    nodes = g_ref.shape[0]
    pairs = [(i, j) for i in range(nodes) for j in range(i, nodes)]

    def body(r, sums):
        blocks = [g_ref[n, pl.ds(r * 8, 8), :] for n in range(nodes)]
        out = []
        for total, (i, j) in zip(sums, pairs):
            product = blocks[i] * blocks[j]
            for t in range(wide // 128):
                total = total + product[:, t * 128 : (t + 1) * 128]
            out.append(total)
        return tuple(out)

    sums = lax.fori_loop(0, rows // 8, body, tuple(jnp.zeros((8, 128), F32) for _ in pairs))
    filled = [jnp.sum(total, axis=0, keepdims=True) for total in sums]
    filled += [jnp.zeros((1, 128), F32)] * (-len(pairs) % 8)
    stacked = jnp.sum(jnp.concatenate(filled), axis=1, keepdims=True)
    shape = (len(filled), 128)
    on = lax.broadcasted_iota(jnp.int32, shape, 0) == lax.broadcasted_iota(jnp.int32, shape, 1)
    row = jnp.sum(jnp.where(on, jnp.broadcast_to(stacked, shape), 0.0), axis=0, keepdims=True)
    gram_ref[...] = jnp.broadcast_to(row, gram_ref.shape)


def combine_kernel(half, g_ref, sums_ref, out_ref):
    nodes, rows, wide = g_ref.shape
    sums = jnp.sum(sums_ref[...], axis=0, keepdims=True)
    pairs = [(i, j) for i in range(nodes) for j in range(i, nodes)]
    gram = {}
    for k, (i, j) in enumerate(pairs):
        gram[i, j] = gram[j, i] = sums[:, k : k + 1]

    def inner(u, v):
        total = None
        for i, a in u.items():
            row = None
            for j, b in v.items():
                term = gram[i, j] * b
                row = term if row is None else row + term
            total = a * row if total is None else total + a * row
        return total

    one = jnp.ones((1, 1), F32)
    vectors = [{n: one} for n in range(nodes)]
    while len(vectors) > 1:
        middle = len(vectors) // 2
        merged = []
        for u, v in zip(vectors[:middle], vectors[middle:]):
            dot = inner(u, v)
            cu = 1.0 - dot / (2.0 * (inner(u, u) + EPS))
            cv = 1.0 - dot / (2.0 * (inner(v, v) + EPS))
            merged.append({**{n: cu * a for n, a in u.items()}, **{n: cv * a for n, a in v.items()}})
        vectors = merged
    total = None
    for n, coefficient in vectors[0].items():
        term = coefficient * g_ref[n]
        total = term if total is None else total + term
    core = lax.rem(lax.axis_index("node"), 2)
    moved = pltpu.roll(total, half, 1)
    out_ref[...] = jnp.where(core == 0, total[:, :half], moved[:, :half])


def local(x, dy):
    cols = dy.shape[1]
    rows = x.shape[1] // (2 * SIDE * SIDE)
    half = cols // (2 * SIDE)
    wide = -(-half // 128) * 128
    axes = ("x", "z")
    _, y, _, core = coordinates()
    m1, m2 = masks(core)
    place = jnp.stack([y ^ 2, y ^ m1, y ^ m2, y]).astype(jnp.int32)

    def send(pair, primary, is_first):
        return [exchange(m, axes[s] if primary else axes[1 - s], is_first) for s, m in enumerate(pair)]

    make = functools.partial(product, rows=rows, tile=256, count=2)
    xt, dyv, *m1 = first(rows, 256, x, dy)
    p1a_near = send(m1, True, True)
    p1a_far = send(make("p1a_far", xt=xt, dy=dyv, arrivals=[], after=m1), True, True)
    p1b_near = send(make("p1b_near", xt=xt, dy=dyv, arrivals=[], after=p1a_near), True, True)
    p2_near = send(make("p2_near", xt=xt, dy=dyv, arrivals=p1a_near, after=p1a_far), True, False)
    p1b_far = send(make("p1b_far", xt=xt, dy=dyv, arrivals=[], after=p1b_near), True, True)
    p2_far = send(make("p2_far", xt=xt, dy=dyv, arrivals=p1a_far, after=p2_near), True, False)
    kept_near = make("kept_near", xt=xt, dy=dyv, arrivals=p1b_near, after=p1b_near, coded=False)
    kept_far = make("kept_far", xt=xt, dy=dyv, arrivals=p1b_far, after=p1b_far, coded=False)
    one = [rows + PAD] * 2
    two = [2 * rows] * 2
    q1_near = send(merge("q1_near", near_kernel, rows, 256, [*kept_near, *p2_near], one, [BF16] * 2, p1b_far), False, True)
    q1_far = send(merge("q1_far", far_kernel, rows, 256, [*kept_near, *p2_near], one, [BF16] * 2, p2_far), False, True)
    rest = merge("rest", add_kernel, rows, 256, [*kept_far, *p2_far], two, [F32] * 2)
    q2 = send(merge("q2", near_kernel, rows, 256, [*rest, *q1_near], one, [BF16] * 2), False, False)
    own = merge("own", own_kernel, rows, 256, [*rest, *q1_far], two[:1], [F32])
    far, near1, near2, mine = last(rows, place, own[0], q2)
    far = lax.ppermute(far, "node", [(i, i ^ 4) for i in range(2 * SIDE)])
    near1 = exchange(near1, "y", True)
    near2 = exchange(near2, "y", False)
    blocks = [mine, near1, near2, far]
    start = (cols // SIDE - wide) * (1 - core)
    across = jnp.stack([lax.dynamic_slice_in_dim(b, start, wide, axis=1) for b in blocks])
    carr = lax.ppermute(across, "node", [(i, i ^ 1) for i in range(2 * SIDE)])
    count = 2 * SIDE * SIDE * SIDE
    g, gram = pl.pallas_call(
        functools.partial(gram_kernel, 2 * rows, half),
        out_shape=[
            jax.ShapeDtypeStruct((2 * SIDE, 2 * rows, wide), F32),
            jax.ShapeDtypeStruct((count, 128), F32),
        ],
        compiler_params=params(12),
        name="gram",
    )(*blocks, carr)
    sums = lax.all_to_all(gram, ("node", "fsdp"), 0, 0, tiled=True)
    return pl.pallas_call(
        functools.partial(combine_kernel, half),
        out_shape=jax.ShapeDtypeStruct((2 * rows, half), F32),
        compiler_params=params(12),
        name="combine",
    )(g, sums)


def solution(mesh):
    in_specs = (P(("node", "fsdp"), None), P(("node", "fsdp"), None))
    out_specs = P("fsdp", "node")
    return jax.shard_map(local, mesh=mesh, in_specs=in_specs, out_specs=out_specs, check_vma=False)
```

time: 183 us -> 140 us (0.77)
  Pallas kernels: 74.2 us -> 43.1 us
  waiting for transfers between devices: 64.4 us -> 41.1 us
  starting transfers between devices: 23.5 us -> 37.1 us
  local copies, waits for them, and re-layouts: 4.33 us -> 0.05 us
  blocking collectives: 14.7 us -> 18.1 us
    pallas_call x6 -> x14, Pallas kernels: 66.7 us -> 39.8 us  [the longest x7 17.8 us: product(): pl.pallas_call(functools.partial(product_kernel, which, rows, tile, coded...]
    ppermute x12 -> x20, waiting for transfers between devices: 62.8 us -> 37.5 us  [exchange(): return lax.ppermute(array, ('node', 'fsdp'), pairing(axis, first))]
    ppermute x12 -> x20, starting transfers between devices: 16.7 us -> 28.1 us  [exchange(): return lax.ppermute(array, ('node', 'fsdp'), pairing(axis, first))]
    all_to_all x1, blocking collectives: 14.7 us -> 18.1 us  [local(): sums = lax.all_to_all(gram, ('node', 'fsdp'), 0, 0, tiled=True)]
    unnamed x18 -> x0, local copies, waits for them, and re-layouts: 3.2 us -> none
    pallas_call x1, Pallas kernels: 4.28 us -> 1.71 us  [local(): pl.pallas_call(functools.partial(gram_kernel, 2 * rows, half), out_shape=...]
    ppermute x0 -> x1, waiting for transfers between devices: none -> 2.1 us  [local(): far = lax.ppermute(far, 'node', [(i, i ^ 4) for i in range(2 * SIDE)])]
  transfers between devices with their start and end apart: 13 -> 22, of which waited for: 13 -> 18; matrix products, arithmetic and copies ran while one was open for 1% -> 0% of each run, Pallas kernels for 13% -> 19%
where the time goes in v2:
time: 140 us
  Pallas kernels  43.1 us (31%)
  waiting for transfers between devices  41.1 us (29%)
  starting transfers between devices  37.1 us (26%)
  blocking collectives  18.1 us (13%)
    ppermute x20, waiting for transfers between devices, exchange(): return lax.ppermute(array, ('node', 'fsdp'), pairing(axis, first))  37.5 us
    ppermute x20, starting transfers between devices, exchange(): return lax.ppermute(array, ('node', 'fsdp'), pairing(axis, first))  28.1 us
    all_to_all x1, blocking collectives, local(): sums = lax.all_to_all(gram, ('node', 'fsdp'), 0, 0, tiled=True)  18.1 us
    pallas_call x7, Pallas kernels, product(): pl.pallas_call(functools.partial(product_kernel, which, rows, tile, coded...  17.8 us
    pallas_call x1, Pallas kernels, first(): pl.pallas_call(functools.partial(first_kernel, rows, tile), out_shape=[xt...  9.98 us
    pallas_call x5, Pallas kernels, merge(): pl.pallas_call(functools.partial(kernel, rows, tile), out_shape=[jax.Shap...  8.19 us
    ppermute x1, starting transfers between devices, local(): carr = lax.ppermute(across, 'node', [(i, i ^ 1) for i in range(2 * SIDE)])  7.68 us
    pallas_call x1, Pallas kernels, last(): pl.pallas_call(functools.partial(last_kernel, rows), grid_spec=pltpu.Pref...  3.79 us
  transfers between devices with their start and end apart: 22, of which 18 were waited for; matrix products, arithmetic and copies ran while one was open for 0% of the time, Pallas kernels for 19%

profile of v2, /device:TPU:1, one launch (start us, length us, event | category | flops | bytes accessed | tf_op | source)
XLA Modules:
  0.0 139.8 jit_solution(17032344495664989396)
XLA Ops:
  0.0 10.0 %p1a_near.1 = (bf16[2560,1024]{1,0:T(8,128)(2,1)S(1)}, bf16[1024,2560]{1,0:T(8,128)(2,1)S(1)}, bf16[168,2560]{1,0:T(8,128)(2,1)S(1)}, bf16[168,2560]{1,0:T(8,128)(2,1)S(1)}) custom-call(bf16[1024,2560]{1,0:T(8,128)(2,1)} %x_ref.1, bf16[1024,2560]{1,0:T(8,128)(2,1)} %dy_ref.1), custom_call_target="tpu_custom_call" | custom-call | tf_op jit(solution)/shard_map/p1a_near/pallas_call | solution.py:168
  10.0 3.4 %collective-permute-start = (bf16[168,2560]{1,0:T(8,128)(2,1)S(1)}, bf16[168,2560]{1,0:T(8,128)(2,1)S(1)}, u32[]{:S(2)}, u32[]{:S(2)}) collective-permute-start(bf16[168,2560]{1,0:T(8,128)(2,1)S(1)} %get-tuple-element.39.rest_0_), channel_id=1, source_target_pairs={{0,1},{1,0},{2,3},{3,2},{4,5},{5,4},{6,7},{7,6},{8,9},{9,8},{10,11... | collective-permute-start | bytes 2580488 | tf_op jit(solution)/shard_map/ppermute | solution.py:59
  13.4 3.8 %collective-permute-start.1 = (bf16[168,2560]{1,0:T(8,128)(2,1)S(1)}, bf16[168,2560]{1,0:T(8,128)(2,1)S(1)}, u32[]{:S(2)}, u32[]{:S(2)}) collective-permute-start(bf16[168,2560]{1,0:T(8,128)(2,1)S(1)} %get-tuple-element.40.rest_1_), channel_id=1, source_target_pairs={{0,4},{1,5},{2,6},{3,7},{4,0},{5,1},{6,2},{7,3},{8,12},{9,13},{10,... | collective-permute-start | bytes 2580488 | tf_op jit(solution)/shard_map/ppermute | solution.py:59
  17.1 2.3 %p1a_far.1 = (bf16[168,2560]{1,0:T(8,128)(2,1)S(1)}, bf16[168,2560]{1,0:T(8,128)(2,1)S(1)}) custom-call(bf16[2560,1024]{1,0:T(8,128)(2,1)S(1)} %get-tuple-element.37.xt_ref, bf16[1024,2560]{1,0:T(8,128)(2,1)S(1)} %get-tuple-element.38.dy_ref, bf16[168,2560]{1,0:T(8,128)(2,1)S(1)} %get-tuple-element.39.rest_0_, bf16[168,2560]{1,0:T(8,128)(2,1)S(1)} %get-tuple-element.40.rest_1_), custom_call_target="tpu_custom_call" | custom-call | tf_op jit(solution)/shard_map/p1a_far/pallas_call | solution.py:152
  19.8 3.8 %collective-permute-done.rest_0_ = bf16[168,2560]{1,0:T(8,128)(2,1)S(1)} collective-permute-done((bf16[168,2560]{1,0:T(8,128)(2,1)S(1)}, bf16[168,2560]{1,0:T(8,128)(2,1)S(1)}, u32[]{:S(2)}, u32[]{:S(2)}) %collective-permute-start) | collective-permute-done | bytes 860192 | tf_op jit(solution)/shard_map/ppermute | solution.py:59
  23.5 3.8 %collective-permute-done.1.rest_1_ = bf16[168,2560]{1,0:T(8,128)(2,1)S(1)} collective-permute-done((bf16[168,2560]{1,0:T(8,128)(2,1)S(1)}, bf16[168,2560]{1,0:T(8,128)(2,1)S(1)}, u32[]{:S(2)}, u32[]{:S(2)}) %collective-permute-start.1) | collective-permute-done | bytes 860192 | tf_op jit(solution)/shard_map/ppermute | solution.py:59
  27.3 2.3 %p1b_near.1 = (bf16[168,2560]{1,0:T(8,128)(2,1)S(1)}, bf16[168,2560]{1,0:T(8,128)(2,1)S(1)}) custom-call(bf16[2560,1024]{1,0:T(8,128)(2,1)S(1)} %get-tuple-element.37.xt_ref, bf16[1024,2560]{1,0:T(8,128)(2,1)S(1)} %get-tuple-element.38.dy_ref, bf16[168,2560]{1,0:T(8,128)(2,1)S(1)} %collective-permute-done.rest_0_, ...), custom_call_target="tpu_custom_call" | custom-call | tf_op jit(solution)/shard_map/p1b_near/pallas_call | solution.py:152
  29.6 0.3 collective-permute-start.2
  29.9 2.7 %collective-permute-start.3 = (bf16[168,2560]{1,0:T(8,128)(2,1)S(1)}, bf16[168,2560]{1,0:T(8,128)(2,1)S(1)}, u32[]{:S(2)}, u32[]{:S(2)}) collective-permute-start(bf16[168,2560]{1,0:T(8,128)(2,1)S(1)} %get-tuple-element.42), channel_id=1, source_target_pairs={{0,4},{1,5},{2,6},{3,7},{4,0},{5,1},{6,2},{7,3},{8,12},{9,13},{10,... | collective-permute-start | bytes 2580488 | tf_op jit(solution)/shard_map/ppermute | solution.py:59
  32.8 3.8 %collective-permute-done.7.rest_3_.rest_1_ = bf16[168,2560]{1,0:T(8,128)(2,1)S(1)} collective-permute-done((bf16[168,2560]{1,0:T(8,128)(2,1)S(1)}, bf16[168,2560]{1,0:T(8,128)(2,1)S(1)}, u32[]{:S(2)}, u32[]{:S(2)}) %collective-permute-start.7) | collective-permute-done | bytes 860192 | tf_op jit(solution)/shard_map/ppermute | solution.py:59
  36.5 3.2 %p2_near.1 = (bf16[168,2560]{1,0:T(8,128)(2,1)S(1)}, bf16[168,2560]{1,0:T(8,128)(2,1)S(1)}) custom-call(bf16[2560,1024]{1,0:T(8,128)(2,1)S(1)} %get-tuple-element.37.xt_ref, bf16[1024,2560]{1,0:T(8,128)(2,1)S(1)} %get-tuple-element.38.dy_ref, bf16[168,2560]{1,0:T(8,128)(2,1)S(1)} %collective-permute-done.rest_0_, ...), custom_call_target="tpu_custom_call" | custom-call | tf_op jit(solution)/shard_map/p2_near/pallas_call | solution.py:152
  39.9 2.9 %collective-permute-done.2.rest_0_.rest_2_ = bf16[168,2560]{1,0:T(8,128)(2,1)S(1)} collective-permute-done((bf16[168,2560]{1,0:T(8,128)(2,1)S(1)}, bf16[168,2560]{1,0:T(8,128)(2,1)S(1)}, u32[]{:S(2)}, u32[]{:S(2)}) %collective-permute-start.2) | collective-permute-done | bytes 860192 | tf_op jit(solution)/shard_map/ppermute | solution.py:59
  42.9 3.4 %collective-permute-done.3.rest_1_.rest_3_ = bf16[168,2560]{1,0:T(8,128)(2,1)S(1)} collective-permute-done((bf16[168,2560]{1,0:T(8,128)(2,1)S(1)}, bf16[168,2560]{1,0:T(8,128)(2,1)S(1)}, u32[]{:S(2)}, u32[]{:S(2)}) %collective-permute-start.3) | collective-permute-done | bytes 860192 | tf_op jit(solution)/shard_map/ppermute | solution.py:59
  46.3 2.3 %p1b_far.1 = (bf16[168,2560]{1,0:T(8,128)(2,1)S(1)}, bf16[168,2560]{1,0:T(8,128)(2,1)S(1)}) custom-call(bf16[2560,1024]{1,0:T(8,128)(2,1)S(1)} %get-tuple-element.37.xt_ref, bf16[1024,2560]{1,0:T(8,128)(2,1)S(1)} %get-tuple-element.38.dy_ref, bf16[168,2560]{1,0:T(8,128)(2,1)S(1)} %collective-permute-done.2.rest_0_.rest_2_, ...), custom_call_target="tpu_custom_call" | custom-call | tf_op jit(solution)/shard_map/p1b_far/pallas_call | solution.py:152
  48.8 2.7 %collective-permute-start.5 = (bf16[168,2560]{1,0:T(8,128)(2,1)S(1)}, bf16[168,2560]{1,0:T(8,128)(2,1)S(1)}, u32[]{:S(2)}, u32[]{:S(2)}) collective-permute-start(bf16[168,2560]{1,0:T(8,128)(2,1)S(1)} %get-tuple-element.44), channel_id=1, source_target_pairs={{0,4},{1,5},{2,6},{3,7},{4,0},{5,1},{6,2},{7,3},{8,12},{9,13},{10,... | collective-permute-start | bytes 2580488 | tf_op jit(solution)/shard_map/ppermute | solution.py:59
  51.4 0.3 collective-permute-done.8.rest_2_.arr0
  51.8 1.7 %collective-permute-done.9.rest_3_.arr1 = bf16[168,2560]{1,0:T(8,128)(2,1)S(1)} collective-permute-done((bf16[168,2560]{1,0:T(8,128)(2,1)S(1)}, bf16[168,2560]{1,0:T(8,128)(2,1)S(1)}, u32[]{:S(2)}, u32[]{:S(2)}) %collective-permute-start.9) | collective-permute-done | bytes 860192 | tf_op jit(solution)/shard_map/ppermute | solution.py:59
  53.5 3.2 %p2_far.1 = (bf16[168,2560]{1,0:T(8,128)(2,1)S(1)}, bf16[168,2560]{1,0:T(8,128)(2,1)S(1)}) custom-call(bf16[2560,1024]{1,0:T(8,128)(2,1)S(1)} %get-tuple-element.37.xt_ref, bf16[1024,2560]{1,0:T(8,128)(2,1)S(1)} %get-tuple-element.38.dy_ref, bf16[168,2560]{1,0:T(8,128)(2,1)S(1)} %collective-permute-done.6.rest_2_.rest_0_, ...), custom_call_target="tpu_custom_call" | custom-call | tf_op jit(solution)/shard_map/p2_far/pallas_call | solution.py:152
  56.7 0.4 collective-permute-start.10
  57.1 1.6 %collective-permute-start.11 = (bf16[168,2560]{1,0:T(8,128)(2,1)S(1)}, bf16[168,2560]{1,0:T(8,128)(2,1)S(1)}, u32[]{:S(2)}, u32[]{:S(2)}) collective-permute-start(bf16[168,2560]{1,0:T(8,128)(2,1)S(1)} %get-tuple-element.52), channel_id=1, source_target_pairs={{0,12},{1,13},{2,14},{3,15},{4,8},{5,9},{6,10},{7,11},{8,4},{9,5},... | collective-permute-start | bytes 2580488 | tf_op jit(solution)/shard_map/ppermute | solution.py:59
  58.6 2.2 %kept_near.1 = (f32[160,2560]{1,0:T(8,128)S(1)}, f32[160,2560]{1,0:T(8,128)S(1)}) custom-call(bf16[2560,1024]{1,0:T(8,128)(2,1)S(1)} %get-tuple-element.37.xt_ref, bf16[1024,2560]{1,0:T(8,128)(2,1)S(1)} %get-tuple-element.38.dy_ref, bf16[168,2560]{1,0:T(8,128)(2,1)S(1)} %collective-permute-done.2.rest_0_.rest_2_, ...), custom_call_target="tpu_custom_call" | custom-call | tf_op jit(solution)/shard_map/kept_near/pallas_call | solution.py:152
  60.8 0.8 collective-permute-done.4.rest_0_.rest_2_
  61.6 2.6 %collective-permute-done.5.rest_1_.rest_3_ = bf16[168,2560]{1,0:T(8,128)(2,1)S(1)} collective-permute-done((bf16[168,2560]{1,0:T(8,128)(2,1)S(1)}, bf16[168,2560]{1,0:T(8,128)(2,1)S(1)}, u32[]{:S(2)}, u32[]{:S(2)}) %collective-permute-start.5) | collective-permute-done | bytes 860192 | tf_op jit(solution)/shard_map/ppermute | solution.py:59
  64.2 1.2 q1_near.1
  65.3 2.8 %collective-permute-start.14 = (bf16[88,2560]{1,0:T(8,128)(2,1)S(1)}, bf16[88,2560]{1,0:T(8,128)(2,1)S(1)}, u32[]{:S(2)}, u32[]{:S(2)}) collective-permute-start(bf16[88,2560]{1,0:T(8,128)(2,1)S(1)} %get-tuple-element.59), channel_id=1, source_target_pairs={{0,4},{1,5},{2,6},{3,7},{4,0},{5,1},{6,2},{7,3},{8,12},{9,13},{10,... | collective-permute-start | bytes 1351688 | tf_op jit(solution)/shard_map/ppermute | solution.py:59
  68.1 0.8 collective-permute-start.15
  68.9 1.7 %collective-permute-done.10.arr0.rest_0_ = bf16[168,2560]{1,0:T(8,128)(2,1)S(1)} collective-permute-done((bf16[168,2560]{1,0:T(8,128)(2,1)S(1)}, bf16[168,2560]{1,0:T(8,128)(2,1)S(1)}, u32[]{:S(2)}, u32[]{:S(2)}) %collective-permute-start.10) | collective-permute-done | bytes 860192 | tf_op jit(solution)/shard_map/ppermute | solution.py:59
  70.6 2.2 %collective-permute-done.11.arr1.rest_1_ = bf16[168,2560]{1,0:T(8,128)(2,1)S(1)} collective-permute-done((bf16[168,2560]{1,0:T(8,128)(2,1)S(1)}, bf16[168,2560]{1,0:T(8,128)(2,1)S(1)}, u32[]{:S(2)}, u32[]{:S(2)}) %collective-permute-start.11) | collective-permute-done | bytes 860192 | tf_op jit(solution)/shard_map/ppermute | solution.py:59
  72.8 2.0 %q1_far.1 = (bf16[88,2560]{1,0:T(8,128)(2,1)}, bf16[88,2560]{1,0:T(8,128)(2,1)}) custom-call(f32[160,2560]{1,0:T(8,128)S(1)} %get-tuple-element.55.kept0, f32[160,2560]{1,0:T(8,128)S(1)} %get-tuple-element.56.kept1, bf16[168,2560]{1,0:T(8,128)(2,1)S(1)} %collective-permute-done.8.rest_2_.arr0, bf16[168,2560]{1,0:T(8,128)(2,1)S(1)} %collective-permute-done.9.rest_3_.arr1, ...), custom_call_target="tpu_custom_call" | custom-call | tf_op jit(solution)/shard_map/q1_far/pallas_call | solution.py:227
  74.7 4.9 %collective-permute-start.12 = (bf16[88,2560]{1,0:T(8,128)(2,1)}, bf16[88,2560]{1,0:T(8,128)(2,1)}, u32[]{:S(2)}, u32[]{:S(2)}) collective-permute-start(bf16[88,2560]{1,0:T(8,128)(2,1)} %get-tuple-element.57), channel_id=1, source_target_pairs={{0,4},{1,5},{2,6},{3,7},{4,0},{5,1},{6,2},{7,3},{8,12},{9,13},{10,... | collective-permute-start | bytes 1351688 | tf_op jit(solution)/shard_map/ppermute | solution.py:59
  79.6 1.6 %collective-permute-start.13 = (bf16[88,2560]{1,0:T(8,128)(2,1)}, bf16[88,2560]{1,0:T(8,128)(2,1)}, u32[]{:S(2)}, u32[]{:S(2)}) collective-permute-start(bf16[88,2560]{1,0:T(8,128)(2,1)} %get-tuple-element.58), channel_id=1, source_target_pairs={{0,1},{1,0},{2,3},{3,2},{4,5},{5,4},{6,7},{7,6},{8,9},{9,8},{10,11... | collective-permute-start | bytes 1351688 | tf_op jit(solution)/shard_map/ppermute | solution.py:59
  81.2 2.2 %kept_far.1 = (f32[160,2560]{1,0:T(8,128)S(1)}, f32[160,2560]{1,0:T(8,128)S(1)}) custom-call(bf16[2560,1024]{1,0:T(8,128)(2,1)S(1)} %get-tuple-element.37.xt_ref, bf16[1024,2560]{1,0:T(8,128)(2,1)S(1)} %get-tuple-element.38.dy_ref, bf16[168,2560]{1,0:T(8,128)(2,1)S(1)} %collective-permute-done.4.rest_0_.rest_2_, ...), custom_call_target="tpu_custom_call" | custom-call | tf_op jit(solution)/shard_map/kept_far/pallas_call | solution.py:152
  83.4 1.3 rest.1
  84.7 1.9 %q2.1 = (bf16[88,2560]{1,0:T(8,128)(2,1)}, bf16[88,2560]{1,0:T(8,128)(2,1)}) custom-call(f32[160,2560]{1,0:T(8,128)S(1)} %get-tuple-element.53.kept0, f32[160,2560]{1,0:T(8,128)S(1)} %get-tuple-element.54.kept1, bf16[88,2560]{1,0:T(8,128)(2,1)S(1)} %collective-permute-done.14.arr0, bf16[88,2560]{1,0:T(8,128)(2,1)S(1)} %collective-permute-done.15.arr1), custom_call_target="tpu_custom_call" | custom-call | tf_op jit(solution)/shard_map/q2/pallas_call | solution.py:227
  86.7 1.6 %collective-permute-done.13.arr1 = bf16[88,2560]{1,0:T(8,128)(2,1)} collective-permute-done((bf16[88,2560]{1,0:T(8,128)(2,1)}, bf16[88,2560]{1,0:T(8,128)(2,1)}, u32[]{:S(2)}, u32[]{:S(2)}) %collective-permute-start.13) | collective-permute-done | bytes 450592 | tf_op jit(solution)/shard_map/ppermute | solution.py:59
  88.3 1.8 %own.1 = f32[160,2560]{1,0:T(8,128)S(1)} custom-call(f32[160,2560]{1,0:T(8,128)S(1)} %get-tuple-element.53.kept0, f32[160,2560]{1,0:T(8,128)S(1)} %get-tuple-element.54.kept1, bf16[88,2560]{1,0:T(8,128)(2,1)} %collective-permute-done.12.arr0, bf16[88,2560]{1,0:T(8,128)(2,1)} %collective-permute-done.13.arr1), custom_call_target="tpu_custom_call" | custom-call | tf_op jit(solution)/shard_map/own/pallas_call | solution.py:227
  90.2 5.5 %collective-permute-done.16.arr0 = bf16[88,2560]{1,0:T(8,128)(2,1)} collective-permute-done((bf16[88,2560]{1,0:T(8,128)(2,1)}, bf16[88,2560]{1,0:T(8,128)(2,1)}, u32[]{:S(2)}, u32[]{:S(2)}) %collective-permute-start.16) | collective-permute-done | bytes 450592 | tf_op jit(solution)/shard_map/ppermute | solution.py:59
  95.6 3.8 %last.1 = (bf16[168,640]{1,0:T(8,128)(2,1)S(1)}, bf16[168,640]{1,0:T(8,128)(2,1)S(1)}, bf16[168,640]{1,0:T(8,128)(2,1)S(1)}, bf16[168,640]{1,0:T(8,128)(2,1)S(1)}) custom-call(s32[4]{0:T(128)S(1)} %pad_add_fusion.place, f32[160,2560]{1,0:T(8,128)S(1)} %own.1, bf16[88,2560]{1,0:T(8,128)(2,1)} %collective-permute-done.16.arr0, ...), custom_call_target="tpu_custom_call" | custom-call | tf_op jit(solution)/shard_map/last/pallas_call | solution.py:248
  99.4 2.8 %collective-permute-start.18 = (bf16[168,640]{1,0:T(8,128)(2,1)S(1)}, bf16[168,640]{1,0:T(8,128)(2,1)S(1)}, u32[]{:S(2)}, u32[]{:S(2)}) collective-permute-start(bf16[168,640]{1,0:T(8,128)(2,1)S(1)} %get-tuple-element.64), channel_id=1, source_target_pairs={{0,32},{1,33},{2,34},{3,35},{4,36},{5,37},{6,38},{7,39},{8,40},{9,... | collective-permute-start | bytes 645128 | tf_op jit(solution)/shard_map/ppermute | solution.py:59
  102.2 1.3 collective-permute-start.20
  103.5 2.0 %collective-permute-done.18.own1 = bf16[168,640]{1,0:T(8,128)(2,1)S(1)} collective-permute-done((bf16[168,640]{1,0:T(8,128)(2,1)S(1)}, bf16[168,640]{1,0:T(8,128)(2,1)S(1)}, u32[]{:S(2)}, u32[]{:S(2)}) %collective-permute-start.18) | collective-permute-done | bytes 215072 | tf_op jit(solution)/shard_map/ppermute | solution.py:59
  105.5 1.4 %collective-permute-done.19.own2 = bf16[168,640]{1,0:T(8,128)(2,1)S(1)} collective-permute-done((bf16[168,640]{1,0:T(8,128)(2,1)S(1)}, bf16[168,640]{1,0:T(8,128)(2,1)S(1)}, u32[]{:S(2)}, u32[]{:S(2)}) %collective-permute-start.19) | collective-permute-done | bytes 215072 | tf_op jit(solution)/shard_map/ppermute | solution.py:59
  107.0 2.1 %collective-permute-done.20.own3 = bf16[168,640]{1,0:T(8,128)(2,1)S(1)} collective-permute-done((bf16[168,640]{1,0:T(8,128)(2,1)S(1)}, bf16[168,640]{1,0:T(8,128)(2,1)S(1)}, u32[]{:S(2)}, u32[]{:S(2)}) %collective-permute-start.20) | collective-permute-done | bytes 215072 | tf_op jit(solution)/shard_map/ppermute | solution.py:368
  109.2 7.7 %collective-permute-start.21 = (bf16[4,168,384]{2,1,0:T(8,128)(2,1)S(1)}, bf16[4,168,384]{2,1,0:T(8,128)(2,1)S(1)}, u32[]{:S(2)}, u32[]{:S(2)}) collective-permute-start(bf16[4,168,384]{2,1,0:T(8,128)(2,1)S(1)} %pad_maximum_fusion), channel_id=1, source_target_pairs={{0,16},{16,0},{32,48},{48,32},{64,80},{80,64},{96,112},{112,96},{1... | collective-permute-start | bytes 1548296 | tf_op jit(solution)/shard_map/ppermute | solution.py:374
  116.8 1.5 %collective-permute-done.21.carr = bf16[4,168,384]{2,1,0:T(8,128)(2,1)S(1)} collective-permute-done((bf16[4,168,384]{2,1,0:T(8,128)(2,1)S(1)}, bf16[4,168,384]{2,1,0:T(8,128)(2,1)S(1)}, u32[]{:S(2)}, u32[]{:S(2)}) %collective-permute-start.21) | collective-permute-done | bytes 516128 | tf_op jit(solution)/shard_map/ppermute | solution.py:374
  118.4 1.7 %gram.1 = (f32[8,160,384]{2,1,0:T(8,128)S(1)}, f32[128,128]{1,0:T(8,128)S(1)}) custom-call(bf16[168,640]{1,0:T(8,128)(2,1)S(1)} %get-tuple-element.63.own0, bf16[168,640]{1,0:T(8,128)(2,1)S(1)} %collective-permute-done.18.own1, bf16[168,640]{1,0:T(8,128)(2,1)S(1)} %collective-permute-done.19.own2, bf16[168,640]{1,0:T(8,128)(2,1)S(1)} %collective-permute-done.20.own3, ...), custom_call_target="tpu_custom_call" | custom-call | tf_op jit(solution)/shard_map/gram/pallas_call | solution.py:376
  120.1 18.1 %all_to_all.11 = f32[128,1,128]{2,1,0:T(1,128)S(1)} all-to-all(f32[128,1,128]{2,1,0:T(1,128)S(1)} %bitcast.17), channel_id=1, replica_groups=mesh['node'=8,'fsdp'=16] {'node','fsdp'}, dimensions={0} | all-to-all | bytes 131072 | tf_op jit(solution)/shard_map/all_to_all | solution.py:385
  138.2 1.6 %combine.1 = f32[160,320]{1,0:T(8,128)} custom-call(f32[8,160,384]{2,1,0:T(8,128)S(1)} %get-tuple-element.67.g_ref, f32[128,128]{1,0:T(8,128)S(1)} %bitcast.16), custom_call_target="tpu_custom_call" | custom-call | tf_op jit(solution)/shard_map/combine/pallas_call | solution.py:386
  (19 shorter events, 0.9 us)
Async XLA Ops:
  10.0 13.6 %collective-permute-start = (bf16[168,2560]{1,0:T(8,128)(2,1)S(1)}, bf16[168,2560]{1,0:T(8,128)(2,1)S(1)}, u32[]{:S(2)}, u32[]{:S(2)}) collective-permute-start(bf16[168,2560]{1,0:T(8,128)(2,1)S(1)} %get-tuple-element.39.rest_0_), channel_id=1, source_target_pairs={{0,1},{1,0},{2,3},{3,2},{4,5},{5,4},{6,7},{7,6},{8,9},{9,8},{10,11... | collective-permute-start | bytes 2580488 | tf_op jit(solution)/shard_map/ppermute | solution.py:59
  13.4 13.9 %collective-permute-start.1 = (bf16[168,2560]{1,0:T(8,128)(2,1)S(1)}, bf16[168,2560]{1,0:T(8,128)(2,1)S(1)}, u32[]{:S(2)}, u32[]{:S(2)}) collective-permute-start(bf16[168,2560]{1,0:T(8,128)(2,1)S(1)} %get-tuple-element.40.rest_1_), channel_id=1, source_target_pairs={{0,4},{1,5},{2,6},{3,7},{4,0},{5,1},{6,2},{7,3},{8,12},{9,13},{10,... | collective-permute-start | bytes 2580488 | tf_op jit(solution)/shard_map/ppermute | solution.py:59
  19.5 13.3 %collective-permute-start.6 = (bf16[168,2560]{1,0:T(8,128)(2,1)S(1)}, bf16[168,2560]{1,0:T(8,128)(2,1)S(1)}, u32[]{:S(2)}, u32[]{:S(2)}) collective-permute-start(bf16[168,2560]{1,0:T(8,128)(2,1)S(1)} %get-tuple-element.47), channel_id=1, source_target_pairs={{0,1},{1,0},{2,3},{3,2},{4,5},{5,4},{6,7},{7,6},{8,9},{9,8},{10,11... | collective-permute-start | bytes 2580488 | tf_op jit(solution)/shard_map/ppermute | solution.py:59
  19.8 16.8 %collective-permute-start.7 = (bf16[168,2560]{1,0:T(8,128)(2,1)S(1)}, bf16[168,2560]{1,0:T(8,128)(2,1)S(1)}, u32[]{:S(2)}, u32[]{:S(2)}) collective-permute-start(bf16[168,2560]{1,0:T(8,128)(2,1)S(1)} %get-tuple-element.48), channel_id=1, source_target_pairs={{0,4},{1,5},{2,6},{3,7},{4,0},{5,1},{6,2},{7,3},{8,12},{9,13},{10,... | collective-permute-start | bytes 2580488 | tf_op jit(solution)/shard_map/ppermute | solution.py:59
  29.6 13.2 %collective-permute-start.2 = (bf16[168,2560]{1,0:T(8,128)(2,1)S(1)}, bf16[168,2560]{1,0:T(8,128)(2,1)S(1)}, u32[]{:S(2)}, u32[]{:S(2)}) collective-permute-start(bf16[168,2560]{1,0:T(8,128)(2,1)S(1)} %get-tuple-element.41), channel_id=1, source_target_pairs={{0,1},{1,0},{2,3},{3,2},{4,5},{5,4},{6,7},{7,6},{8,9},{9,8},{10,11... | collective-permute-start | bytes 2580488 | tf_op jit(solution)/shard_map/ppermute | solution.py:59
  29.9 16.4 %collective-permute-start.3 = (bf16[168,2560]{1,0:T(8,128)(2,1)S(1)}, bf16[168,2560]{1,0:T(8,128)(2,1)S(1)}, u32[]{:S(2)}, u32[]{:S(2)}) collective-permute-start(bf16[168,2560]{1,0:T(8,128)(2,1)S(1)} %get-tuple-element.42), channel_id=1, source_target_pairs={{0,4},{1,5},{2,6},{3,7},{4,0},{5,1},{6,2},{7,3},{8,12},{9,13},{10,... | collective-permute-start | bytes 2580488 | tf_op jit(solution)/shard_map/ppermute | solution.py:59
  39.8 12.0 %collective-permute-start.8 = (bf16[168,2560]{1,0:T(8,128)(2,1)S(1)}, bf16[168,2560]{1,0:T(8,128)(2,1)S(1)}, u32[]{:S(2)}, u32[]{:S(2)}) collective-permute-start(bf16[168,2560]{1,0:T(8,128)(2,1)S(1)} %get-tuple-element.49), channel_id=1, source_target_pairs={{0,3},{1,2},{2,1},{3,0},{4,7},{5,6},{6,5},{7,4},{8,11},{9,10},{10,... | collective-permute-start | bytes 2580488 | tf_op jit(solution)/shard_map/ppermute | solution.py:59
  39.9 13.6 %collective-permute-start.9 = (bf16[168,2560]{1,0:T(8,128)(2,1)S(1)}, bf16[168,2560]{1,0:T(8,128)(2,1)S(1)}, u32[]{:S(2)}, u32[]{:S(2)}) collective-permute-start(bf16[168,2560]{1,0:T(8,128)(2,1)S(1)} %get-tuple-element.50), channel_id=1, source_target_pairs={{0,12},{1,13},{2,14},{3,15},{4,8},{5,9},{6,10},{7,11},{8,4},{9,5},... | collective-permute-start | bytes 2580488 | tf_op jit(solution)/shard_map/ppermute | solution.py:59
  48.7 12.9 %collective-permute-start.4 = (bf16[168,2560]{1,0:T(8,128)(2,1)S(1)}, bf16[168,2560]{1,0:T(8,128)(2,1)S(1)}, u32[]{:S(2)}, u32[]{:S(2)}) collective-permute-start(bf16[168,2560]{1,0:T(8,128)(2,1)S(1)} %get-tuple-element.43), channel_id=1, source_target_pairs={{0,1},{1,0},{2,3},{3,2},{4,5},{5,4},{6,7},{7,6},{8,9},{9,8},{10,11... | collective-permute-start | bytes 2580488 | tf_op jit(solution)/shard_map/ppermute | solution.py:59
  48.8 15.4 %collective-permute-start.5 = (bf16[168,2560]{1,0:T(8,128)(2,1)S(1)}, bf16[168,2560]{1,0:T(8,128)(2,1)S(1)}, u32[]{:S(2)}, u32[]{:S(2)}) collective-permute-start(bf16[168,2560]{1,0:T(8,128)(2,1)S(1)} %get-tuple-element.44), channel_id=1, source_target_pairs={{0,4},{1,5},{2,6},{3,7},{4,0},{5,1},{6,2},{7,3},{8,12},{9,13},{10,... | collective-permute-start | bytes 2580488 | tf_op jit(solution)/shard_map/ppermute | solution.py:59
  56.7 13.9 %collective-permute-start.10 = (bf16[168,2560]{1,0:T(8,128)(2,1)S(1)}, bf16[168,2560]{1,0:T(8,128)(2,1)S(1)}, u32[]{:S(2)}, u32[]{:S(2)}) collective-permute-start(bf16[168,2560]{1,0:T(8,128)(2,1)S(1)} %get-tuple-element.51), channel_id=1, source_target_pairs={{0,3},{1,2},{2,1},{3,0},{4,7},{5,6},{6,5},{7,4},{8,11},{9,10},{10,... | collective-permute-start | bytes 2580488 | tf_op jit(solution)/shard_map/ppermute | solution.py:59
  57.1 15.7 %collective-permute-start.11 = (bf16[168,2560]{1,0:T(8,128)(2,1)S(1)}, bf16[168,2560]{1,0:T(8,128)(2,1)S(1)}, u32[]{:S(2)}, u32[]{:S(2)}) collective-permute-start(bf16[168,2560]{1,0:T(8,128)(2,1)S(1)} %get-tuple-element.52), channel_id=1, source_target_pairs={{0,12},{1,13},{2,14},{3,15},{4,8},{5,9},{6,10},{7,11},{8,4},{9,5},... | collective-permute-start | bytes 2580488 | tf_op jit(solution)/shard_map/ppermute | solution.py:59
  65.3 19.3 %collective-permute-start.14 = (bf16[88,2560]{1,0:T(8,128)(2,1)S(1)}, bf16[88,2560]{1,0:T(8,128)(2,1)S(1)}, u32[]{:S(2)}, u32[]{:S(2)}) collective-permute-start(bf16[88,2560]{1,0:T(8,128)(2,1)S(1)} %get-tuple-element.59), channel_id=1, source_target_pairs={{0,4},{1,5},{2,6},{3,7},{4,0},{5,1},{6,2},{7,3},{8,12},{9,13},{10,... | collective-permute-start | bytes 1351688 | tf_op jit(solution)/shard_map/ppermute | solution.py:59
  68.1 16.6 %collective-permute-start.15 = (bf16[88,2560]{1,0:T(8,128)(2,1)S(1)}, bf16[88,2560]{1,0:T(8,128)(2,1)S(1)}, u32[]{:S(2)}, u32[]{:S(2)}) collective-permute-start(bf16[88,2560]{1,0:T(8,128)(2,1)S(1)} %get-tuple-element.60), channel_id=1, source_target_pairs={{0,1},{1,0},{2,3},{3,2},{4,5},{5,4},{6,7},{7,6},{8,9},{9,8},{10,11... | collective-permute-start | bytes 1351688 | tf_op jit(solution)/shard_map/ppermute | solution.py:59
  74.7 12.0 %collective-permute-start.12 = (bf16[88,2560]{1,0:T(8,128)(2,1)}, bf16[88,2560]{1,0:T(8,128)(2,1)}, u32[]{:S(2)}, u32[]{:S(2)}) collective-permute-start(bf16[88,2560]{1,0:T(8,128)(2,1)} %get-tuple-element.57), channel_id=1, source_target_pairs={{0,4},{1,5},{2,6},{3,7},{4,0},{5,1},{6,2},{7,3},{8,12},{9,13},{10,... | collective-permute-start | bytes 1351688 | tf_op jit(solution)/shard_map/ppermute | solution.py:59
  79.6 8.8 %collective-permute-start.13 = (bf16[88,2560]{1,0:T(8,128)(2,1)}, bf16[88,2560]{1,0:T(8,128)(2,1)}, u32[]{:S(2)}, u32[]{:S(2)}) collective-permute-start(bf16[88,2560]{1,0:T(8,128)(2,1)} %get-tuple-element.58), channel_id=1, source_target_pairs={{0,1},{1,0},{2,3},{3,2},{4,5},{5,4},{6,7},{7,6},{8,9},{9,8},{10,11... | collective-permute-start | bytes 1351688 | tf_op jit(solution)/shard_map/ppermute | solution.py:59
  86.7 9.0 %collective-permute-start.16 = (bf16[88,2560]{1,0:T(8,128)(2,1)}, bf16[88,2560]{1,0:T(8,128)(2,1)}, u32[]{:S(2)}, u32[]{:S(2)}) collective-permute-start(bf16[88,2560]{1,0:T(8,128)(2,1)} %get-tuple-element.61), channel_id=1, source_target_pairs={{0,12},{1,13},{2,14},{3,15},{4,8},{5,9},{6,10},{7,11},{8,4},{9,5},... | collective-permute-start | bytes 1351688 | tf_op jit(solution)/shard_map/ppermute | solution.py:59
  86.7 9.0 %collective-permute-start.17 = (bf16[88,2560]{1,0:T(8,128)(2,1)}, bf16[88,2560]{1,0:T(8,128)(2,1)}, u32[]{:S(2)}, u32[]{:S(2)}) collective-permute-start(bf16[88,2560]{1,0:T(8,128)(2,1)} %get-tuple-element.62), channel_id=1, source_target_pairs={{0,3},{1,2},{2,1},{3,0},{4,7},{5,6},{6,5},{7,4},{8,11},{9,10},{10,... | collective-permute-start | bytes 1351688 | tf_op jit(solution)/shard_map/ppermute | solution.py:59
  99.4 6.1 %collective-permute-start.18 = (bf16[168,640]{1,0:T(8,128)(2,1)S(1)}, bf16[168,640]{1,0:T(8,128)(2,1)S(1)}, u32[]{:S(2)}, u32[]{:S(2)}) collective-permute-start(bf16[168,640]{1,0:T(8,128)(2,1)S(1)} %get-tuple-element.64), channel_id=1, source_target_pairs={{0,32},{1,33},{2,34},{3,35},{4,36},{5,37},{6,38},{7,39},{8,40},{9,... | collective-permute-start | bytes 645128 | tf_op jit(solution)/shard_map/ppermute | solution.py:59
  102.2 4.7 %collective-permute-start.19 = (bf16[168,640]{1,0:T(8,128)(2,1)S(1)}, bf16[168,640]{1,0:T(8,128)(2,1)S(1)}, u32[]{:S(2)}, u32[]{:S(2)}) collective-permute-start(bf16[168,640]{1,0:T(8,128)(2,1)S(1)} %get-tuple-element.65), channel_id=1, source_target_pairs={{0,96},{1,97},{2,98},{3,99},{4,100},{5,101},{6,102},{7,103},{8,104... | collective-permute-start | bytes 645128 | tf_op jit(solution)/shard_map/ppermute | solution.py:59
  102.2 6.8 %collective-permute-start.20 = (bf16[168,640]{1,0:T(8,128)(2,1)S(1)}, bf16[168,640]{1,0:T(8,128)(2,1)S(1)}, u32[]{:S(2)}, u32[]{:S(2)}) collective-permute-start(bf16[168,640]{1,0:T(8,128)(2,1)S(1)} %get-tuple-element.66), channel_id=1, source_target_pairs={{0,64},{16,80},{32,96},{48,112},{64,0},{80,16},{96,32},{112,48},{1... | collective-permute-start | bytes 645128 | tf_op jit(solution)/shard_map/ppermute | solution.py:368
  109.2 9.2 %collective-permute-start.21 = (bf16[4,168,384]{2,1,0:T(8,128)(2,1)S(1)}, bf16[4,168,384]{2,1,0:T(8,128)(2,1)S(1)}, u32[]{:S(2)}, u32[]{:S(2)}) collective-permute-start(bf16[4,168,384]{2,1,0:T(8,128)(2,1)S(1)} %pad_maximum_fusion), channel_id=1, source_target_pairs={{0,16},{16,0},{32,48},{48,32},{64,80},{80,64},{96,112},{112,96},{1... | collective-permute-start | bytes 1548296 | tf_op jit(solution)/shard_map/ppermute | solution.py:374

commit v3 on v2

--- a/solution.py
+++ b/solution.py
@@ -93,27 +93,24 @@
 
 
 def first_kernel(rows, tile, x_ref, dy_ref, xt_ref, dy_vmem, out0, out1, x_vmem, lhs, x_sems, dy_sems):
-    x_cols, dy_cols = list(parts_of(x_ref, tile)), list(parts_of(dy_ref, tile))
-
-    def bring(source, target, sems, cols):
-        return [
-            pltpu.make_async_copy(source.at[:, pl.ds(c.start, tile)], target.at[:, pl.ds(c.start, tile)], sems.at[t])
-            for t, c in enumerate(cols)
-        ]
-
-    x_copies, dy_copies = bring(x_ref, x_vmem, x_sems, x_cols), bring(dy_ref, dy_vmem, dy_sems, dy_cols)
+    x_rows = [pl.ds(at, tile) for at in range(0, x_ref.shape[0], tile)]
+    dy_cols = [pl.ds(at, 2 * tile) for at in range(0, dy_ref.shape[1], 2 * tile)]
+    x_copies = [pltpu.make_async_copy(x_ref.at[r, :], x_vmem.at[r, :], x_sems.at[t]) for t, r in enumerate(x_rows)]
+    dy_copies = [pltpu.make_async_copy(dy_ref.at[:, c], dy_vmem.at[:, c], dy_sems.at[t]) for t, c in enumerate(dy_cols)]
     for copy in x_copies + dy_copies:
         copy.start()
-    for cols, copy in zip(x_cols, x_copies):
+    for at, copy in zip(range(0, x_ref.shape[0], tile), x_copies):
         copy.wait()
-        xt_ref[cols, :] = x_vmem[:, cols].T
+        for cols in parts_of(x_ref, tile):
+            xt_ref[cols, at : at + tile] = x_vmem[at : at + tile, cols].T
     gather(xt_ref, lhs, wanted("p1a_near", rows), rows)
     size = 2 * rows
-    for cols, copy in zip(dy_cols, dy_copies):
+    for t, copy in enumerate(dy_copies):
         copy.wait()
-        total = jnp.dot(lhs[...], dy_vmem[:, cols], preferred_element_type=F32)
-        for s, out in enumerate((out0, out1)):
-            write(out, total[s * size : (s + 1) * size], cols)
+        for cols in (slice(2 * t * tile, (2 * t + 1) * tile), slice((2 * t + 1) * tile, (2 * t + 2) * tile)):
+            total = jnp.dot(lhs[...], dy_vmem[:, cols], preferred_element_type=F32)
+            for s, out in enumerate((out0, out1)):
+                write(out, total[s * size : (s + 1) * size], cols)
 
 
 def product_kernel(which, rows, tile, coded, xt_ref, dy_ref, *rest):
@@ -173,8 +170,8 @@
         scratch_shapes=[
             pltpu.VMEM(x.shape, BF16),
             pltpu.VMEM((2 * size, tokens), BF16),
-            pltpu.SemaphoreType.DMA((x.shape[1] // tile,)),
-            pltpu.SemaphoreType.DMA((cols // tile,)),
+            pltpu.SemaphoreType.DMA((tokens // tile,)),
+            pltpu.SemaphoreType.DMA((cols // (2 * tile),)),
         ],
         compiler_params=params(40),
         name="p1a_near",
@@ -234,29 +231,26 @@
     )(*ins, *after)
 
 
-def last_kernel(rows, place, own, arr0, arr1, out0, out1, out2, out3):
-    values = jnp.concatenate([own[s * rows : (s + 1) * rows, :] + read(a, rows, 0, 1) for s, a in enumerate((arr0, arr1))])
-    for k, out in enumerate((out0, out1, out2, out3)):
-        pl.when(pl.program_id(0) == k)(functools.partial(write, out, values))
-
-
-def last(rows, place, own, arrivals):
-    cols = own.shape[1]
-    tile = cols // SIDE
-    height = 2 * rows + PAD
-    at = lambda i, place: (0, place[i])
+def last_kernel(rows, own, arr0, arr1, *outs):
+    _, y, _, core = coordinates()
+    m1, m2 = masks(core)
+    width = own.shape[1] // SIDE
+    for out, at in zip(outs, (y ^ 2, y ^ m1, y ^ m2, y)):
+        cols = pl.ds(pl.multiple_of(at * width, 128), width)
+        parts = [own[s * rows : (s + 1) * rows, cols] + read(a, rows, 0, 1, cols) for s, a in enumerate((arr0, arr1))]
+        write(out, jnp.concatenate(parts))
+
+
+def last(rows, own, arrivals):
+    message = jax.ShapeDtypeStruct((2 * rows + PAD, own.shape[1] // SIDE), BF16)
     return pl.pallas_call(
         functools.partial(last_kernel, rows),
-        grid_spec=pltpu.PrefetchScalarGridSpec(
-            num_scalar_prefetch=1,
-            grid=(SIDE,),
-            in_specs=[pl.BlockSpec((2 * rows, tile), at)] + [pl.BlockSpec((a.shape[0], tile), at) for a in arrivals],
-            out_specs=[pl.BlockSpec((height, tile), lambda i, place: (0, 0))] * SIDE,
-        ),
-        out_shape=[jax.ShapeDtypeStruct((height, tile), BF16)] * SIDE,
+        out_shape=[message] * SIDE,
+        in_specs=[VMEM] * 3,
+        out_specs=[VMEM] * SIDE,
         compiler_params=params(12),
         name="last",
-    )(place, own, *arrivals)
+    )(own, *arrivals)
 
 
 def gram_kernel(rows, half, own0, own1, own2, own3, carr, g_ref, gram_ref):
@@ -340,9 +334,7 @@
     half = cols // (2 * SIDE)
     wide = -(-half // 128) * 128
     axes = ("x", "z")
-    _, y, _, core = coordinates()
-    m1, m2 = masks(core)
-    place = jnp.stack([y ^ 2, y ^ m1, y ^ m2, y]).astype(jnp.int32)
+    core = coordinates()[3]
 
     def send(pair, primary, is_first):
         return [exchange(m, axes[s] if primary else axes[1 - s], is_first) for s, m in enumerate(pair)]
@@ -350,21 +342,22 @@
     make = functools.partial(product, rows=rows, tile=256, count=2)
     xt, dyv, *m1 = first(rows, 256, x, dy)
     p1a_near = send(m1, True, True)
-    p1a_far = send(make("p1a_far", xt=xt, dy=dyv, arrivals=[], after=m1), True, True)
-    p1b_near = send(make("p1b_near", xt=xt, dy=dyv, arrivals=[], after=p1a_near), True, True)
-    p2_near = send(make("p2_near", xt=xt, dy=dyv, arrivals=p1a_near, after=p1a_far), True, False)
-    p1b_far = send(make("p1b_far", xt=xt, dy=dyv, arrivals=[], after=p1b_near), True, True)
-    p2_far = send(make("p2_far", xt=xt, dy=dyv, arrivals=p1a_far, after=p2_near), True, False)
+    m2 = make("p1a_far", xt=xt, dy=dyv, arrivals=[], after=m1)
+    p1a_far = send(m2, True, True)
+    p1b_near = send(make("p1b_near", xt=xt, dy=dyv, arrivals=[], after=m2), True, True)
+    p2_near = send(make("p2_near", xt=xt, dy=dyv, arrivals=p1a_near, after=p1a_near), True, False)
+    p1b_far = send(make("p1b_far", xt=xt, dy=dyv, arrivals=[], after=p1a_far), True, True)
+    p2_far = send(make("p2_far", xt=xt, dy=dyv, arrivals=p1a_far, after=p1b_near), True, False)
     kept_near = make("kept_near", xt=xt, dy=dyv, arrivals=p1b_near, after=p1b_near, coded=False)
     kept_far = make("kept_far", xt=xt, dy=dyv, arrivals=p1b_far, after=p1b_far, coded=False)
     one = [rows + PAD] * 2
     two = [2 * rows] * 2
-    q1_near = send(merge("q1_near", near_kernel, rows, 256, [*kept_near, *p2_near], one, [BF16] * 2, p1b_far), False, True)
-    q1_far = send(merge("q1_far", far_kernel, rows, 256, [*kept_near, *p2_near], one, [BF16] * 2, p2_far), False, True)
+    q1_near = send(merge("q1_near", near_kernel, rows, 256, [*kept_near, *p2_near], one, [BF16] * 2), False, True)
+    q1_far = send(merge("q1_far", far_kernel, rows, 256, [*kept_near, *p2_near], one, [BF16] * 2, p1b_far), False, True)
     rest = merge("rest", add_kernel, rows, 256, [*kept_far, *p2_far], two, [F32] * 2)
     q2 = send(merge("q2", near_kernel, rows, 256, [*rest, *q1_near], one, [BF16] * 2), False, False)
     own = merge("own", own_kernel, rows, 256, [*rest, *q1_far], two[:1], [F32])
-    far, near1, near2, mine = last(rows, place, own[0], q2)
+    far, near1, near2, mine = last(rows, own[0], q2)
     far = lax.ppermute(far, "node", [(i, i ^ 4) for i in range(2 * SIDE)])
     near1 = exchange(near1, "y", True)
     near2 = exchange(near2, "y", False)

time: 140 us -> 128 us (0.914)
  waiting for transfers between devices: 41.1 us -> 28.1 us
  starting transfers between devices: 37.1 us -> 49.2 us
  Pallas kernels: 43.1 us -> 35.4 us
  blocking collectives: 18.1 us -> 14.7 us
    ppermute x20, waiting for transfers between devices: 37.5 us -> 24.5 us  [exchange(): return lax.ppermute(array, ('node', 'fsdp'), pairing(axis, first))]
    ppermute x20, starting transfers between devices: 28.1 us -> 38.1 us  [exchange(): return lax.ppermute(array, ('node', 'fsdp'), pairing(axis, first))]
    all_to_all x1, blocking collectives: 18.1 us -> 14.7 us  [local(): sums = lax.all_to_all(gram, ('node', 'fsdp'), 0, 0, tiled=True)]
    pallas_call x5, Pallas kernels: 8.19 us -> 5.48 us  [merge(): pl.pallas_call(functools.partial(kernel, rows, tile), out_shape=[jax.Shap...]
    pallas_call x1, Pallas kernels: 3.79 us -> 1.15 us  [last(): pl.pallas_call(functools.partial(last_kernel, rows), out_shape=[message]...]
    pallas_call x1, Pallas kernels: 9.98 us -> 7.56 us  [first(): pl.pallas_call(functools.partial(first_kernel, rows, tile), out_shape=[xt...]
    ppermute x1, starting transfers between devices: 7.68 us -> 9.82 us  [local(): carr = lax.ppermute(across, 'node', [(i, i ^ 1) for i in range(2 * SIDE)])]
  transfers between devices with their start and end apart: 22 -> 22, of which waited for: 18 -> 12; matrix products, arithmetic and copies ran while one was open for 0% -> 0% of each run, Pallas kernels for 19% -> 18%
where the time goes in v3:
time: 128 us
  starting transfers between devices  49.2 us (38%)
  Pallas kernels  35.4 us (28%)
  waiting for transfers between devices  28.1 us (22%)
  blocking collectives  14.7 us (11%)
    ppermute x20, starting transfers between devices, exchange(): return lax.ppermute(array, ('node', 'fsdp'), pairing(axis, first))  38.1 us
    ppermute x20, waiting for transfers between devices, exchange(): return lax.ppermute(array, ('node', 'fsdp'), pairing(axis, first))  24.5 us
    pallas_call x7, Pallas kernels, product(): pl.pallas_call(functools.partial(product_kernel, which, rows, tile, coded...  17.9 us
    all_to_all x1, blocking collectives, local(): sums = lax.all_to_all(gram, ('node', 'fsdp'), 0, 0, tiled=True)  14.7 us
    ppermute x1, starting transfers between devices, local(): carr = lax.ppermute(across, 'node', [(i, i ^ 1) for i in range(2 * SIDE)])  9.82 us
    pallas_call x1, Pallas kernels, first(): pl.pallas_call(functools.partial(first_kernel, rows, tile), out_shape=[xt...  7.56 us
    pallas_call x5, Pallas kernels, merge(): pl.pallas_call(functools.partial(kernel, rows, tile), out_shape=[jax.Shap...  5.48 us
  transfers between devices with their start and end apart: 22, of which 12 were waited for; matrix products, arithmetic and copies ran while one was open for 0% of the time, Pallas kernels for 18%

profile of v3, /device:TPU:1, one launch (start us, length us, event | category | flops | bytes accessed | tf_op | source)
XLA Modules:
  0.0 127.6 jit_solution(3466912726134624447)
XLA Ops:
  0.0 7.6 %p1a_near.1 = (bf16[2560,1024]{1,0:T(8,128)(2,1)S(1)}, bf16[1024,2560]{1,0:T(8,128)(2,1)S(1)}, bf16[168,2560]{1,0:T(8,128)(2,1)S(1)}, bf16[168,2560]{1,0:T(8,128)(2,1)S(1)}) custom-call(bf16[1024,2560]{1,0:T(8,128)(2,1)} %x_ref.1, bf16[1024,2560]{1,0:T(8,128)(2,1)} %dy_ref.1), custom_call_target="tpu_custom_call" | custom-call | tf_op jit(solution)/shard_map/p1a_near/pallas_call | solution.py:165
  7.6 3.4 %collective-permute-start.8 = (bf16[168,2560]{1,0:T(8,128)(2,1)S(1)}, bf16[168,2560]{1,0:T(8,128)(2,1)S(1)}, u32[]{:S(2)}, u32[]{:S(2)}) collective-permute-start(bf16[168,2560]{1,0:T(8,128)(2,1)S(1)} %get-tuple-element.39.rest_0_), channel_id=1, source_target_pairs={{0,1},{1,0},{2,3},{3,2},{4,5},{5,4},{6,7},{7,6},{8,9},{9,8},{10,11... | collective-permute-start | bytes 2580488 | tf_op jit(solution)/shard_map/ppermute | solution.py:59
  11.0 3.8 %collective-permute-start.9 = (bf16[168,2560]{1,0:T(8,128)(2,1)S(1)}, bf16[168,2560]{1,0:T(8,128)(2,1)S(1)}, u32[]{:S(2)}, u32[]{:S(2)}) collective-permute-start(bf16[168,2560]{1,0:T(8,128)(2,1)S(1)} %get-tuple-element.40.rest_1_), channel_id=1, source_target_pairs={{0,4},{1,5},{2,6},{3,7},{4,0},{5,1},{6,2},{7,3},{8,12},{9,13},{10,... | collective-permute-start | bytes 2580488 | tf_op jit(solution)/shard_map/ppermute | solution.py:59
  14.7 2.3 %p1a_far.1 = (bf16[168,2560]{1,0:T(8,128)(2,1)S(1)}, bf16[168,2560]{1,0:T(8,128)(2,1)S(1)}) custom-call(bf16[2560,1024]{1,0:T(8,128)(2,1)S(1)} %get-tuple-element.37.xt_ref, bf16[1024,2560]{1,0:T(8,128)(2,1)S(1)} %get-tuple-element.38.dy_ref, bf16[168,2560]{1,0:T(8,128)(2,1)S(1)} %get-tuple-element.39.rest_0_, bf16[168,2560]{1,0:T(8,128)(2,1)S(1)} %get-tuple-element.40.rest_1_), custom_call_target="tpu_custom_call" | custom-call | tf_op jit(solution)/shard_map/p1a_far/pallas_call | solution.py:149
  17.1 0.3 collective-permute-start
  17.3 2.3 %p1b_near.1 = (bf16[168,2560]{1,0:T(8,128)(2,1)S(1)}, bf16[168,2560]{1,0:T(8,128)(2,1)S(1)}) custom-call(bf16[2560,1024]{1,0:T(8,128)(2,1)S(1)} %get-tuple-element.37.xt_ref, bf16[1024,2560]{1,0:T(8,128)(2,1)S(1)} %get-tuple-element.38.dy_ref, bf16[168,2560]{1,0:T(8,128)(2,1)S(1)} %get-tuple-element.41.rest_0_, bf16[168,2560]{1,0:T(8,128)(2,1)S(1)} %get-tuple-element.42.rest_1_), custom_call_target="tpu_custom_call" | custom-call | tf_op jit(solution)/shard_map/p1b_near/pallas_call | solution.py:149
  19.7 2.6 %collective-permute-start.4 = (bf16[168,2560]{1,0:T(8,128)(2,1)S(1)}, bf16[168,2560]{1,0:T(8,128)(2,1)S(1)}, u32[]{:S(2)}, u32[]{:S(2)}) collective-permute-start(bf16[168,2560]{1,0:T(8,128)(2,1)S(1)} %get-tuple-element.47), channel_id=1, source_target_pairs={{0,1},{1,0},{2,3},{3,2},{4,5},{5,4},{6,7},{7,6},{8,9},{9,8},{10,11... | collective-permute-start | bytes 2580488 | tf_op jit(solution)/shard_map/ppermute | solution.py:59
  22.2 2.8 %collective-permute-start.5 = (bf16[168,2560]{1,0:T(8,128)(2,1)S(1)}, bf16[168,2560]{1,0:T(8,128)(2,1)S(1)}, u32[]{:S(2)}, u32[]{:S(2)}) collective-permute-start(bf16[168,2560]{1,0:T(8,128)(2,1)S(1)} %get-tuple-element.48), channel_id=1, source_target_pairs={{0,4},{1,5},{2,6},{3,7},{4,0},{5,1},{6,2},{7,3},{8,12},{9,13},{10,... | collective-permute-start | bytes 2580488 | tf_op jit(solution)/shard_map/ppermute | solution.py:59
  25.1 3.2 %p2_near.1 = (bf16[168,2560]{1,0:T(8,128)(2,1)S(1)}, bf16[168,2560]{1,0:T(8,128)(2,1)S(1)}) custom-call(bf16[2560,1024]{1,0:T(8,128)(2,1)S(1)} %get-tuple-element.37.xt_ref, bf16[1024,2560]{1,0:T(8,128)(2,1)S(1)} %get-tuple-element.38.dy_ref, bf16[168,2560]{1,0:T(8,128)(2,1)S(1)} %collective-permute-done.8.rest_0_.rest_2_, ...), custom_call_target="tpu_custom_call" | custom-call | tf_op jit(solution)/shard_map/p2_near/pallas_call | solution.py:149
  28.3 0.6 collective-permute-start.10
  28.9 1.5 %collective-permute-done.rest_0_ = bf16[168,2560]{1,0:T(8,128)(2,1)S(1)} collective-permute-done((bf16[168,2560]{1,0:T(8,128)(2,1)S(1)}, bf16[168,2560]{1,0:T(8,128)(2,1)S(1)}, u32[]{:S(2)}, u32[]{:S(2)}) %collective-permute-start) | collective-permute-done | bytes 860192 | tf_op jit(solution)/shard_map/ppermute | solution.py:59
  30.3 1.8 %collective-permute-start.11 = (bf16[168,2560]{1,0:T(8,128)(2,1)S(1)}, bf16[168,2560]{1,0:T(8,128)(2,1)S(1)}, u32[]{:S(2)}, u32[]{:S(2)}) collective-permute-start(bf16[168,2560]{1,0:T(8,128)(2,1)S(1)} %get-tuple-element.56), channel_id=1, source_target_pairs={{0,12},{1,13},{2,14},{3,15},{4,8},{5,9},{6,10},{7,11},{8,4},{9,5},... | collective-permute-start | bytes 2580488 | tf_op jit(solution)/shard_map/ppermute | solution.py:59
  32.2 2.2 %collective-permute-done.1.rest_1_ = bf16[168,2560]{1,0:T(8,128)(2,1)S(1)} collective-permute-done((bf16[168,2560]{1,0:T(8,128)(2,1)S(1)}, bf16[168,2560]{1,0:T(8,128)(2,1)S(1)}, u32[]{:S(2)}, u32[]{:S(2)}) %collective-permute-start.1) | collective-permute-done | bytes 860192 | tf_op jit(solution)/shard_map/ppermute | solution.py:59
  34.4 2.3 %p1b_far.1 = (bf16[168,2560]{1,0:T(8,128)(2,1)S(1)}, bf16[168,2560]{1,0:T(8,128)(2,1)S(1)}) custom-call(bf16[2560,1024]{1,0:T(8,128)(2,1)S(1)} %get-tuple-element.37.xt_ref, bf16[1024,2560]{1,0:T(8,128)(2,1)S(1)} %get-tuple-element.38.dy_ref, bf16[168,2560]{1,0:T(8,128)(2,1)S(1)} %collective-permute-done.rest_0_, ...), custom_call_target="tpu_custom_call" | custom-call | tf_op jit(solution)/shard_map/p1b_far/pallas_call | solution.py:149
  36.7 0.8 collective-permute-start.2
  37.5 10.4 %collective-permute-done.4.rest_2_.rest_0_ = bf16[168,2560]{1,0:T(8,128)(2,1)S(1)} collective-permute-done((bf16[168,2560]{1,0:T(8,128)(2,1)S(1)}, bf16[168,2560]{1,0:T(8,128)(2,1)S(1)}, u32[]{:S(2)}, u32[]{:S(2)}) %collective-permute-start.4) | collective-permute-done | bytes 860192 | tf_op jit(solution)/shard_map/ppermute | solution.py:59
  47.9 4.6 %collective-permute-start.3 = (bf16[168,2560]{1,0:T(8,128)(2,1)S(1)}, bf16[168,2560]{1,0:T(8,128)(2,1)S(1)}, u32[]{:S(2)}, u32[]{:S(2)}) collective-permute-start(bf16[168,2560]{1,0:T(8,128)(2,1)S(1)} %get-tuple-element.44), channel_id=1, source_target_pairs={{0,4},{1,5},{2,6},{3,7},{4,0},{5,1},{6,2},{7,3},{8,12},{9,13},{10,... | collective-permute-start | bytes 2580488 | tf_op jit(solution)/shard_map/ppermute | solution.py:59
  52.5 3.2 %p2_far.1 = (bf16[168,2560]{1,0:T(8,128)(2,1)S(1)}, bf16[168,2560]{1,0:T(8,128)(2,1)S(1)}) custom-call(bf16[2560,1024]{1,0:T(8,128)(2,1)S(1)} %get-tuple-element.37.xt_ref, bf16[1024,2560]{1,0:T(8,128)(2,1)S(1)} %get-tuple-element.38.dy_ref, bf16[168,2560]{1,0:T(8,128)(2,1)S(1)} %collective-permute-done.rest_0_, ...), custom_call_target="tpu_custom_call" | custom-call | tf_op jit(solution)/shard_map/p2_far/pallas_call | solution.py:149
  55.7 0.6 collective-permute-start.6
  56.4 2.2 %kept_near.1 = (f32[160,2560]{1,0:T(8,128)S(1)}, f32[160,2560]{1,0:T(8,128)S(1)}) custom-call(bf16[2560,1024]{1,0:T(8,128)(2,1)S(1)} %get-tuple-element.37.xt_ref, bf16[1024,2560]{1,0:T(8,128)(2,1)S(1)} %get-tuple-element.38.dy_ref, bf16[168,2560]{1,0:T(8,128)(2,1)S(1)} %collective-permute-done.4.rest_2_.rest_0_, ...), custom_call_target="tpu_custom_call" | custom-call | tf_op jit(solution)/shard_map/kept_near/pallas_call | solution.py:149
  58.6 1.2 q1_near.1
  59.7 0.1 collective-permute-start.14
  59.8 2.7 %collective-permute-start.15 = (bf16[88,2560]{1,0:T(8,128)(2,1)S(1)}, bf16[88,2560]{1,0:T(8,128)(2,1)S(1)}, u32[]{:S(2)}, u32[]{:S(2)}) collective-permute-start(bf16[88,2560]{1,0:T(8,128)(2,1)S(1)} %get-tuple-element.60), channel_id=1, source_target_pairs={{0,1},{1,0},{2,3},{3,2},{4,5},{5,4},{6,7},{7,6},{8,9},{9,8},{10,11... | collective-permute-start | bytes 1351688 | tf_op jit(solution)/shard_map/ppermute | solution.py:59
  62.5 1.3 %collective-permute-done.3.rest_1_.rest_3_ = bf16[168,2560]{1,0:T(8,128)(2,1)S(1)} collective-permute-done((bf16[168,2560]{1,0:T(8,128)(2,1)S(1)}, bf16[168,2560]{1,0:T(8,128)(2,1)S(1)}, u32[]{:S(2)}, u32[]{:S(2)}) %collective-permute-start.3) | collective-permute-done | bytes 860192 | tf_op jit(solution)/shard_map/ppermute | solution.py:59
  63.8 1.2 q1_far.1
  65.0 3.4 %collective-permute-start.12 = (bf16[88,2560]{1,0:T(8,128)(2,1)S(1)}, bf16[88,2560]{1,0:T(8,128)(2,1)S(1)}, u32[]{:S(2)}, u32[]{:S(2)}) collective-permute-start(bf16[88,2560]{1,0:T(8,128)(2,1)S(1)} %get-tuple-element.57), channel_id=1, source_target_pairs={{0,4},{1,5},{2,6},{3,7},{4,0},{5,1},{6,2},{7,3},{8,12},{9,13},{10,... | collective-permute-start | bytes 1351688 | tf_op jit(solution)/shard_map/ppermute | solution.py:59
  68.4 2.2 %kept_far.1 = (f32[160,2560]{1,0:T(8,128)S(1)}, f32[160,2560]{1,0:T(8,128)S(1)}) custom-call(bf16[2560,1024]{1,0:T(8,128)(2,1)S(1)} %get-tuple-element.37.xt_ref, bf16[1024,2560]{1,0:T(8,128)(2,1)S(1)} %get-tuple-element.38.dy_ref, bf16[168,2560]{1,0:T(8,128)(2,1)S(1)} %collective-permute-done.2.rest_0_.rest_2_, ...), custom_call_target="tpu_custom_call" | custom-call | tf_op jit(solution)/shard_map/kept_far/pallas_call | solution.py:149
  70.7 5.9 %collective-permute-start.13 = (bf16[88,2560]{1,0:T(8,128)(2,1)S(1)}, bf16[88,2560]{1,0:T(8,128)(2,1)S(1)}, u32[]{:S(2)}, u32[]{:S(2)}) collective-permute-start(bf16[88,2560]{1,0:T(8,128)(2,1)S(1)} %get-tuple-element.58), channel_id=1, source_target_pairs={{0,1},{1,0},{2,3},{3,2},{4,5},{5,4},{6,7},{7,6},{8,9},{9,8},{10,11... | collective-permute-start | bytes 1351688 | tf_op jit(solution)/shard_map/ppermute | solution.py:59
  76.6 1.3 %rest.1 = (f32[160,2560]{1,0:T(8,128)S(1)}, f32[160,2560]{1,0:T(8,128)S(1)}) custom-call(f32[160,2560]{1,0:T(8,128)S(1)} %get-tuple-element.45.kept0, f32[160,2560]{1,0:T(8,128)S(1)} %get-tuple-element.46.kept1, bf16[168,2560]{1,0:T(8,128)(2,1)S(1)} %collective-permute-done.6.arr0, bf16[168,2560]{1,0:T(8,128)(2,1)S(1)} %collective-permute-done.7.arr1), custom_call_target="tpu_custom_call" | custom-call | tf_op jit(solution)/shard_map/rest/pallas_call | solution.py:224
  77.9 1.2 q2.1
  79.1 1.1 collective-permute-start.16
  80.1 0.9 collective-permute-start.17
  81.1 0.5 collective-permute-done.12.arr0
  81.5 0.8 collective-permute-done.13.arr1
  82.3 0.7 own.1
  83.0 3.4 %collective-permute-done.16.arr0 = bf16[88,2560]{1,0:T(8,128)(2,1)S(1)} collective-permute-done((bf16[88,2560]{1,0:T(8,128)(2,1)S(1)}, bf16[88,2560]{1,0:T(8,128)(2,1)S(1)}, u32[]{:S(2)}, u32[]{:S(2)}) %collective-permute-start.16) | collective-permute-done | bytes 450592 | tf_op jit(solution)/shard_map/ppermute | solution.py:59
  86.4 1.0 collective-permute-done.17.arr1
  87.4 1.1 last.1
  88.5 2.8 %collective-permute-start.18 = (bf16[168,640]{1,0:T(8,128)(2,1)S(1)}, bf16[168,640]{1,0:T(8,128)(2,1)S(1)}, u32[]{:S(2)}, u32[]{:S(2)}) collective-permute-start(bf16[168,640]{1,0:T(8,128)(2,1)S(1)} %get-tuple-element.64), channel_id=1, source_target_pairs={{0,32},{1,33},{2,34},{3,35},{4,36},{5,37},{6,38},{7,39},{8,40},{9,... | collective-permute-start | bytes 645128 | tf_op jit(solution)/shard_map/ppermute | solution.py:59
  91.4 1.3 %collective-permute-start.20 = (bf16[168,640]{1,0:T(8,128)(2,1)S(1)}, bf16[168,640]{1,0:T(8,128)(2,1)S(1)}, u32[]{:S(2)}, u32[]{:S(2)}) collective-permute-start(bf16[168,640]{1,0:T(8,128)(2,1)S(1)} %get-tuple-element.66), channel_id=1, source_target_pairs={{0,64},{16,80},{32,96},{48,112},{64,0},{80,16},{96,32},{112,48},{1... | collective-permute-start | bytes 645128 | tf_op jit(solution)/shard_map/ppermute | solution.py:361
  92.6 2.3 %collective-permute-done.18.own1 = bf16[168,640]{1,0:T(8,128)(2,1)S(1)} collective-permute-done((bf16[168,640]{1,0:T(8,128)(2,1)S(1)}, bf16[168,640]{1,0:T(8,128)(2,1)S(1)}, u32[]{:S(2)}, u32[]{:S(2)}) %collective-permute-start.18) | collective-permute-done | bytes 215072 | tf_op jit(solution)/shard_map/ppermute | solution.py:59
  94.9 1.1 collective-permute-done.19.own2
  96.1 2.1 %collective-permute-done.20.own3 = bf16[168,640]{1,0:T(8,128)(2,1)S(1)} collective-permute-done((bf16[168,640]{1,0:T(8,128)(2,1)S(1)}, bf16[168,640]{1,0:T(8,128)(2,1)S(1)}, u32[]{:S(2)}, u32[]{:S(2)}) %collective-permute-start.20) | collective-permute-done | bytes 215072 | tf_op jit(solution)/shard_map/ppermute | solution.py:361
  98.3 9.8 %collective-permute-start.21 = (bf16[4,168,384]{2,1,0:T(8,128)(2,1)S(1)}, bf16[4,168,384]{2,1,0:T(8,128)(2,1)S(1)}, u32[]{:S(2)}, u32[]{:S(2)}) collective-permute-start(bf16[4,168,384]{2,1,0:T(8,128)(2,1)S(1)} %pad_maximum_fusion), channel_id=1, source_target_pairs={{0,16},{16,0},{32,48},{48,32},{64,80},{80,64},{96,112},{112,96},{1... | collective-permute-start | bytes 1548296 | tf_op jit(solution)/shard_map/ppermute | solution.py:367
  108.1 1.5 %collective-permute-done.21.carr = bf16[4,168,384]{2,1,0:T(8,128)(2,1)S(1)} collective-permute-done((bf16[4,168,384]{2,1,0:T(8,128)(2,1)S(1)}, bf16[4,168,384]{2,1,0:T(8,128)(2,1)S(1)}, u32[]{:S(2)}, u32[]{:S(2)}) %collective-permute-start.21) | collective-permute-done | bytes 516128 | tf_op jit(solution)/shard_map/ppermute | solution.py:367
  109.6 1.7 %gram.1 = (f32[8,160,384]{2,1,0:T(8,128)S(1)}, f32[128,128]{1,0:T(8,128)S(1)}) custom-call(bf16[168,640]{1,0:T(8,128)(2,1)S(1)} %get-tuple-element.63.own0, bf16[168,640]{1,0:T(8,128)(2,1)S(1)} %collective-permute-done.18.own1, bf16[168,640]{1,0:T(8,128)(2,1)S(1)} %collective-permute-done.19.own2, bf16[168,640]{1,0:T(8,128)(2,1)S(1)} %collective-permute-done.20.own3, ...), custom_call_target="tpu_custom_call" | custom-call | tf_op jit(solution)/shard_map/gram/pallas_call | solution.py:369
  111.3 14.7 %all_to_all.11 = f32[128,1,128]{2,1,0:T(1,128)S(1)} all-to-all(f32[128,1,128]{2,1,0:T(1,128)S(1)} %bitcast.13), channel_id=1, replica_groups=mesh['node'=8,'fsdp'=16] {'node','fsdp'}, dimensions={0} | all-to-all | bytes 131072 | tf_op jit(solution)/shard_map/all_to_all | solution.py:378
  126.0 1.6 %combine.1 = f32[160,320]{1,0:T(8,128)} custom-call(f32[8,160,384]{2,1,0:T(8,128)S(1)} %get-tuple-element.67.g_ref, f32[128,128]{1,0:T(8,128)S(1)} %bitcast.12), custom_call_target="tpu_custom_call" | custom-call | tf_op jit(solution)/shard_map/combine/pallas_call | solution.py:379
  (18 shorter events, 0.2 us)
Async XLA Ops:
  7.6 14.7 %collective-permute-start.8 = (bf16[168,2560]{1,0:T(8,128)(2,1)S(1)}, bf16[168,2560]{1,0:T(8,128)(2,1)S(1)}, u32[]{:S(2)}, u32[]{:S(2)}) collective-permute-start(bf16[168,2560]{1,0:T(8,128)(2,1)S(1)} %get-tuple-element.39.rest_0_), channel_id=1, source_target_pairs={{0,1},{1,0},{2,3},{3,2},{4,5},{5,4},{6,7},{7,6},{8,9},{9,8},{10,11... | collective-permute-start | bytes 2580488 | tf_op jit(solution)/shard_map/ppermute | solution.py:59
  11.0 14.1 %collective-permute-start.9 = (bf16[168,2560]{1,0:T(8,128)(2,1)S(1)}, bf16[168,2560]{1,0:T(8,128)(2,1)S(1)}, u32[]{:S(2)}, u32[]{:S(2)}) collective-permute-start(bf16[168,2560]{1,0:T(8,128)(2,1)S(1)} %get-tuple-element.40.rest_1_), channel_id=1, source_target_pairs={{0,4},{1,5},{2,6},{3,7},{4,0},{5,1},{6,2},{7,3},{8,12},{9,13},{10,... | collective-permute-start | bytes 2580488 | tf_op jit(solution)/shard_map/ppermute | solution.py:59
  17.1 13.3 %collective-permute-start = (bf16[168,2560]{1,0:T(8,128)(2,1)S(1)}, bf16[168,2560]{1,0:T(8,128)(2,1)S(1)}, u32[]{:S(2)}, u32[]{:S(2)}) collective-permute-start(bf16[168,2560]{1,0:T(8,128)(2,1)S(1)} %get-tuple-element.41.rest_0_), channel_id=1, source_target_pairs={{0,1},{1,0},{2,3},{3,2},{4,5},{5,4},{6,7},{7,6},{8,9},{9,8},{10,11... | collective-permute-start | bytes 2580488 | tf_op jit(solution)/shard_map/ppermute | solution.py:59
  17.3 17.1 %collective-permute-start.1 = (bf16[168,2560]{1,0:T(8,128)(2,1)S(1)}, bf16[168,2560]{1,0:T(8,128)(2,1)S(1)}, u32[]{:S(2)}, u32[]{:S(2)}) collective-permute-start(bf16[168,2560]{1,0:T(8,128)(2,1)S(1)} %get-tuple-element.42.rest_1_), channel_id=1, source_target_pairs={{0,4},{1,5},{2,6},{3,7},{4,0},{5,1},{6,2},{7,3},{8,12},{9,13},{10,... | collective-permute-start | bytes 2580488 | tf_op jit(solution)/shard_map/ppermute | solution.py:59
  19.7 28.2 %collective-permute-start.4 = (bf16[168,2560]{1,0:T(8,128)(2,1)S(1)}, bf16[168,2560]{1,0:T(8,128)(2,1)S(1)}, u32[]{:S(2)}, u32[]{:S(2)}) collective-permute-start(bf16[168,2560]{1,0:T(8,128)(2,1)S(1)} %get-tuple-element.47), channel_id=1, source_target_pairs={{0,1},{1,0},{2,3},{3,2},{4,5},{5,4},{6,7},{7,6},{8,9},{9,8},{10,11... | collective-permute-start | bytes 2580488 | tf_op jit(solution)/shard_map/ppermute | solution.py:59
  22.2 30.2 %collective-permute-start.5 = (bf16[168,2560]{1,0:T(8,128)(2,1)S(1)}, bf16[168,2560]{1,0:T(8,128)(2,1)S(1)}, u32[]{:S(2)}, u32[]{:S(2)}) collective-permute-start(bf16[168,2560]{1,0:T(8,128)(2,1)S(1)} %get-tuple-element.48), channel_id=1, source_target_pairs={{0,4},{1,5},{2,6},{3,7},{4,0},{5,1},{6,2},{7,3},{8,12},{9,13},{10,... | collective-permute-start | bytes 2580488 | tf_op jit(solution)/shard_map/ppermute | solution.py:59
  28.3 28.0 %collective-permute-start.10 = (bf16[168,2560]{1,0:T(8,128)(2,1)S(1)}, bf16[168,2560]{1,0:T(8,128)(2,1)S(1)}, u32[]{:S(2)}, u32[]{:S(2)}) collective-permute-start(bf16[168,2560]{1,0:T(8,128)(2,1)S(1)} %get-tuple-element.55), channel_id=1, source_target_pairs={{0,3},{1,2},{2,1},{3,0},{4,7},{5,6},{6,5},{7,4},{8,11},{9,10},{10,... | collective-permute-start | bytes 2580488 | tf_op jit(solution)/shard_map/ppermute | solution.py:59
  30.3 28.2 %collective-permute-start.11 = (bf16[168,2560]{1,0:T(8,128)(2,1)S(1)}, bf16[168,2560]{1,0:T(8,128)(2,1)S(1)}, u32[]{:S(2)}, u32[]{:S(2)}) collective-permute-start(bf16[168,2560]{1,0:T(8,128)(2,1)S(1)} %get-tuple-element.56), channel_id=1, source_target_pairs={{0,12},{1,13},{2,14},{3,15},{4,8},{5,9},{6,10},{7,11},{8,4},{9,5},... | collective-permute-start | bytes 2580488 | tf_op jit(solution)/shard_map/ppermute | solution.py:59
  36.7 23.1 %collective-permute-start.2 = (bf16[168,2560]{1,0:T(8,128)(2,1)S(1)}, bf16[168,2560]{1,0:T(8,128)(2,1)S(1)}, u32[]{:S(2)}, u32[]{:S(2)}) collective-permute-start(bf16[168,2560]{1,0:T(8,128)(2,1)S(1)} %get-tuple-element.43), channel_id=1, source_target_pairs={{0,1},{1,0},{2,3},{3,2},{4,5},{5,4},{6,7},{7,6},{8,9},{9,8},{10,11... | collective-permute-start | bytes 2580488 | tf_op jit(solution)/shard_map/ppermute | solution.py:59
  47.9 15.9 %collective-permute-start.3 = (bf16[168,2560]{1,0:T(8,128)(2,1)S(1)}, bf16[168,2560]{1,0:T(8,128)(2,1)S(1)}, u32[]{:S(2)}, u32[]{:S(2)}) collective-permute-start(bf16[168,2560]{1,0:T(8,128)(2,1)S(1)} %get-tuple-element.44), channel_id=1, source_target_pairs={{0,4},{1,5},{2,6},{3,7},{4,0},{5,1},{6,2},{7,3},{8,12},{9,13},{10,... | collective-permute-start | bytes 2580488 | tf_op jit(solution)/shard_map/ppermute | solution.py:59
  55.7 14.9 %collective-permute-start.6 = (bf16[168,2560]{1,0:T(8,128)(2,1)S(1)}, bf16[168,2560]{1,0:T(8,128)(2,1)S(1)}, u32[]{:S(2)}, u32[]{:S(2)}) collective-permute-start(bf16[168,2560]{1,0:T(8,128)(2,1)S(1)} %get-tuple-element.49), channel_id=1, source_target_pairs={{0,3},{1,2},{2,1},{3,0},{4,7},{5,6},{6,5},{7,4},{8,11},{9,10},{10,... | collective-permute-start | bytes 2580488 | tf_op jit(solution)/shard_map/ppermute | solution.py:59
  56.4 20.2 %collective-permute-start.7 = (bf16[168,2560]{1,0:T(8,128)(2,1)S(1)}, bf16[168,2560]{1,0:T(8,128)(2,1)S(1)}, u32[]{:S(2)}, u32[]{:S(2)}) collective-permute-start(bf16[168,2560]{1,0:T(8,128)(2,1)S(1)} %get-tuple-element.50), channel_id=1, source_target_pairs={{0,12},{1,13},{2,14},{3,15},{4,8},{5,9},{6,10},{7,11},{8,4},{9,5},... | collective-permute-start | bytes 2580488 | tf_op jit(solution)/shard_map/ppermute | solution.py:59
  59.7 18.1 %collective-permute-start.14 = (bf16[88,2560]{1,0:T(8,128)(2,1)S(1)}, bf16[88,2560]{1,0:T(8,128)(2,1)S(1)}, u32[]{:S(2)}, u32[]{:S(2)}) collective-permute-start(bf16[88,2560]{1,0:T(8,128)(2,1)S(1)} %get-tuple-element.59), channel_id=1, source_target_pairs={{0,4},{1,5},{2,6},{3,7},{4,0},{5,1},{6,2},{7,3},{8,12},{9,13},{10,... | collective-permute-start | bytes 1351688 | tf_op jit(solution)/shard_map/ppermute | solution.py:59
  59.8 18.0 %collective-permute-start.15 = (bf16[88,2560]{1,0:T(8,128)(2,1)S(1)}, bf16[88,2560]{1,0:T(8,128)(2,1)S(1)}, u32[]{:S(2)}, u32[]{:S(2)}) collective-permute-start(bf16[88,2560]{1,0:T(8,128)(2,1)S(1)} %get-tuple-element.60), channel_id=1, source_target_pairs={{0,1},{1,0},{2,3},{3,2},{4,5},{5,4},{6,7},{7,6},{8,9},{9,8},{10,11... | collective-permute-start | bytes 1351688 | tf_op jit(solution)/shard_map/ppermute | solution.py:59
  65.0 16.5 %collective-permute-start.12 = (bf16[88,2560]{1,0:T(8,128)(2,1)S(1)}, bf16[88,2560]{1,0:T(8,128)(2,1)S(1)}, u32[]{:S(2)}, u32[]{:S(2)}) collective-permute-start(bf16[88,2560]{1,0:T(8,128)(2,1)S(1)} %get-tuple-element.57), channel_id=1, source_target_pairs={{0,4},{1,5},{2,6},{3,7},{4,0},{5,1},{6,2},{7,3},{8,12},{9,13},{10,... | collective-permute-start | bytes 1351688 | tf_op jit(solution)/shard_map/ppermute | solution.py:59
  70.7 11.7 %collective-permute-start.13 = (bf16[88,2560]{1,0:T(8,128)(2,1)S(1)}, bf16[88,2560]{1,0:T(8,128)(2,1)S(1)}, u32[]{:S(2)}, u32[]{:S(2)}) collective-permute-start(bf16[88,2560]{1,0:T(8,128)(2,1)S(1)} %get-tuple-element.58), channel_id=1, source_target_pairs={{0,1},{1,0},{2,3},{3,2},{4,5},{5,4},{6,7},{7,6},{8,9},{9,8},{10,11... | collective-permute-start | bytes 1351688 | tf_op jit(solution)/shard_map/ppermute | solution.py:59
  79.1 7.3 %collective-permute-start.16 = (bf16[88,2560]{1,0:T(8,128)(2,1)S(1)}, bf16[88,2560]{1,0:T(8,128)(2,1)S(1)}, u32[]{:S(2)}, u32[]{:S(2)}) collective-permute-start(bf16[88,2560]{1,0:T(8,128)(2,1)S(1)} %get-tuple-element.61), channel_id=1, source_target_pairs={{0,12},{1,13},{2,14},{3,15},{4,8},{5,9},{6,10},{7,11},{8,4},{9,5},... | collective-permute-start | bytes 1351688 | tf_op jit(solution)/shard_map/ppermute | solution.py:59
  80.1 7.2 %collective-permute-start.17 = (bf16[88,2560]{1,0:T(8,128)(2,1)S(1)}, bf16[88,2560]{1,0:T(8,128)(2,1)S(1)}, u32[]{:S(2)}, u32[]{:S(2)}) collective-permute-start(bf16[88,2560]{1,0:T(8,128)(2,1)S(1)} %get-tuple-element.62), channel_id=1, source_target_pairs={{0,3},{1,2},{2,1},{3,0},{4,7},{5,6},{6,5},{7,4},{8,11},{9,10},{10,... | collective-permute-start | bytes 1351688 | tf_op jit(solution)/shard_map/ppermute | solution.py:59
  88.5 6.4 %collective-permute-start.18 = (bf16[168,640]{1,0:T(8,128)(2,1)S(1)}, bf16[168,640]{1,0:T(8,128)(2,1)S(1)}, u32[]{:S(2)}, u32[]{:S(2)}) collective-permute-start(bf16[168,640]{1,0:T(8,128)(2,1)S(1)} %get-tuple-element.64), channel_id=1, source_target_pairs={{0,32},{1,33},{2,34},{3,35},{4,36},{5,37},{6,38},{7,39},{8,40},{9,... | collective-permute-start | bytes 645128 | tf_op jit(solution)/shard_map/ppermute | solution.py:59
  91.3 4.7 %collective-permute-start.19 = (bf16[168,640]{1,0:T(8,128)(2,1)S(1)}, bf16[168,640]{1,0:T(8,128)(2,1)S(1)}, u32[]{:S(2)}, u32[]{:S(2)}) collective-permute-start(bf16[168,640]{1,0:T(8,128)(2,1)S(1)} %get-tuple-element.65), channel_id=1, source_target_pairs={{0,96},{1,97},{2,98},{3,99},{4,100},{5,101},{6,102},{7,103},{8,104... | collective-permute-start | bytes 645128 | tf_op jit(solution)/shard_map/ppermute | solution.py:59
  91.4 6.8 %collective-permute-start.20 = (bf16[168,640]{1,0:T(8,128)(2,1)S(1)}, bf16[168,640]{1,0:T(8,128)(2,1)S(1)}, u32[]{:S(2)}, u32[]{:S(2)}) collective-permute-start(bf16[168,640]{1,0:T(8,128)(2,1)S(1)} %get-tuple-element.66), channel_id=1, source_target_pairs={{0,64},{16,80},{32,96},{48,112},{64,0},{80,16},{96,32},{112,48},{1... | collective-permute-start | bytes 645128 | tf_op jit(solution)/shard_map/ppermute | solution.py:361
  98.3 11.3 %collective-permute-start.21 = (bf16[4,168,384]{2,1,0:T(8,128)(2,1)S(1)}, bf16[4,168,384]{2,1,0:T(8,128)(2,1)S(1)}, u32[]{:S(2)}, u32[]{:S(2)}) collective-permute-start(bf16[4,168,384]{2,1,0:T(8,128)(2,1)S(1)} %pad_maximum_fusion), channel_id=1, source_target_pairs={{0,16},{16,0},{32,48},{48,32},{64,80},{80,64},{96,112},{112,96},{1... | collective-permute-start | bytes 1548296 | tf_op jit(solution)/shard_map/ppermute | solution.py:367

commit v4 on v3

--- a/solution.py
+++ b/solution.py
@@ -11,14 +11,16 @@
 POWER = 17
 TOP = 2.0 ** (124 / POWER)
 TINY = 2.0**-126
-PAD = 8
+LANES = 128
+WIDE_ROWS = 8
+GROUP = 16
 SIDE = 4
 BF16, F32 = jnp.bfloat16, jnp.float32
 
 
 def encode(values):
-    peak = jnp.max(jnp.abs(values), axis=0, keepdims=True).astype(BF16)
-    x = values * (TOP / jnp.maximum(peak.astype(F32), TINY))
+    peak = jnp.max(jnp.abs(values), axis=0, keepdims=True).astype(BF16).astype(F32)
+    x = values * (TOP / jnp.maximum(peak, TINY))
     x2 = x * x
     x4 = x2 * x2
     x8 = x4 * x4
@@ -28,7 +30,74 @@
 def decode(code, peak):
     code = code.astype(F32)
     size = jnp.exp(jnp.log(jnp.abs(code)) * (1.0 / POWER))
-    return jnp.where(code < 0, -size, size) * (peak.astype(F32) * (1.0 / TOP))
+    return jnp.where(code < 0, -size, size) * (peak * (1.0 / TOP))
+
+
+def scale_rows(tiles):
+    return -(-tiles // GROUP) * GROUP
+
+
+def message(rows, cols, wide=False):
+    tiles = cols // LANES
+    if wide:
+        return jax.ShapeDtypeStruct((rows + WIDE_ROWS, cols), BF16)
+    return jax.ShapeDtypeStruct((tiles * rows + scale_rows(tiles), LANES), BF16)
+
+
+class Reader:
+    def __init__(self, ref, cols, rows):
+        self.ref, self.rows = ref, rows
+        tiles = cols // LANES
+        self.wide = ref.shape[1] == cols
+        if self.wide:
+            self.height = ref.shape[0] - WIDE_ROWS
+            return
+        self.height = (ref.shape[0] - scale_rows(tiles)) // tiles
+        self.scales = ref[tiles * self.height :, :].astype(F32)
+
+    def __call__(self, at, count, cols):
+        if self.wide:
+            values = self.ref[at * self.rows : (at + count) * self.rows, cols]
+            return decode(values, self.ref[self.height : self.height + 1, cols].astype(F32))
+        out = []
+        for t in range(cols.start // LANES, cols.stop // LANES):
+            first = t * self.height + at * self.rows
+            out.append(decode(self.ref[first : first + count * self.rows, :], self.scales[t : t + 1]))
+        return jnp.concatenate(out, axis=1)
+
+    def dynamic(self, tile):
+        if self.wide:
+            cols = pl.ds(pl.multiple_of(tile * LANES, LANES), LANES)
+            return decode(self.ref[: self.height, cols], self.ref[self.height : self.height + 1, cols].astype(F32))
+        on = lax.broadcasted_iota(jnp.int32, self.scales.shape, 0) == tile
+        peak = jnp.sum(jnp.where(on, self.scales, 0.0), axis=0, keepdims=True)
+        first = pl.multiple_of(tile * self.height, GROUP)
+        return decode(self.ref[pl.ds(first, self.height), :], peak)
+
+
+class Writer:
+    def __init__(self, out):
+        self.out, self.at, self.peaks = out, 0, []
+
+    def __call__(self, values):
+        code, peak = encode(values)
+        rows, width = values.shape
+        if self.out.shape[1] > LANES:
+            cols = slice(self.at, self.at + width)
+            self.out[:rows, cols] = code
+            self.out[rows:, cols] = jnp.broadcast_to(peak, (WIDE_ROWS, width)).astype(BF16)
+            self.at += width
+            return
+        for t in range(0, values.shape[1], LANES):
+            self.out[self.at : self.at + rows, :] = code[:, t : t + LANES]
+            self.at += rows
+            self.peaks.append(peak[:, t : t + LANES])
+
+    def close(self):
+        if self.out.shape[1] > LANES:
+            return
+        spare = [jnp.zeros((1, LANES), F32)] * (scale_rows(len(self.peaks)) - len(self.peaks))
+        self.out[self.at :, :] = jnp.concatenate(self.peaks + spare).astype(BF16)
 
 
 def coordinates():
@@ -97,38 +166,50 @@
     dy_cols = [pl.ds(at, 2 * tile) for at in range(0, dy_ref.shape[1], 2 * tile)]
     x_copies = [pltpu.make_async_copy(x_ref.at[r, :], x_vmem.at[r, :], x_sems.at[t]) for t, r in enumerate(x_rows)]
     dy_copies = [pltpu.make_async_copy(dy_ref.at[:, c], dy_vmem.at[:, c], dy_sems.at[t]) for t, c in enumerate(dy_cols)]
-    for copy in x_copies + dy_copies:
+    for copy in x_copies:
         copy.start()
-    for at, copy in zip(range(0, x_ref.shape[0], tile), x_copies):
+    for t, (at, copy) in enumerate(zip(range(0, x_ref.shape[0], tile), x_copies)):
         copy.wait()
+        if t == len(x_copies) // 2 - 1:
+            dy_copies[0].start()
+        if t == len(x_copies) - 1:
+            for other in dy_copies[1:]:
+                other.start()
         for cols in parts_of(x_ref, tile):
             xt_ref[cols, at : at + tile] = x_vmem[at : at + tile, cols].T
     gather(xt_ref, lhs, wanted("p1a_near", rows), rows)
     size = 2 * rows
+    writers = [Writer(out0), Writer(out1)]
     for t, copy in enumerate(dy_copies):
         copy.wait()
         for cols in (slice(2 * t * tile, (2 * t + 1) * tile), slice((2 * t + 1) * tile, (2 * t + 2) * tile)):
             total = jnp.dot(lhs[...], dy_vmem[:, cols], preferred_element_type=F32)
-            for s, out in enumerate((out0, out1)):
-                write(out, total[s * size : (s + 1) * size], cols)
-
-
-def product_kernel(which, rows, tile, coded, xt_ref, dy_ref, *rest):
+            for s, put in enumerate(writers):
+                put(total[s * size : (s + 1) * size])
+    for put in writers:
+        put.close()
+
+
+def product_kernel(which, rows, tile, coded, pieces, xt_ref, dy_ref, *rest):
     arrivals, (_, _, out0, out1, lhs) = rest[:-5], rest[-5:]
     offsets = wanted(which, rows)
-    count = len(offsets[0])
-    size = count * rows
+    size = len(offsets[0]) * rows
     gather(xt_ref, lhs, offsets, rows)
+    readers = [Reader(ref, dy_ref.shape[1], rows) for ref in arrivals]
+    writers = [Writer(out0), Writer(out1)]
     for cols in parts_of(dy_ref, tile):
         total = jnp.dot(lhs[...], dy_ref[:, cols], preferred_element_type=F32)
         for s, out in enumerate((out0, out1)):
             part = total[s * size : (s + 1) * size]
-            for ref in arrivals[s::2]:
-                part += read(ref, rows, 0, count, cols)
+            if pieces:
+                part += jnp.concatenate([readers[2 * k + s](at, count, cols) for k, at, count in pieces])
             if coded:
-                write(out, part, cols)
+                writers[s](part)
             else:
                 out[:, cols] = part
+    if coded:
+        for put in writers:
+            put.close()
 
 
 def params(mib):
@@ -142,13 +223,13 @@
 VMEM = pl.BlockSpec(memory_space=pltpu.VMEM)
 
 
-def product(which, rows, tile, count, xt, dy, arrivals, after, coded=True):
+def product(which, rows, tile, xt, dy, arrivals, after, count=2, pieces=(), coded=True):
     tokens, cols = dy.shape
     size = count * rows
-    message = jax.ShapeDtypeStruct((size + PAD if coded else size, cols), BF16 if coded else F32)
+    shape = message(size, cols, False) if coded else jax.ShapeDtypeStruct((size, cols), F32)
     return pl.pallas_call(
-        functools.partial(product_kernel, which, rows, tile, coded),
-        out_shape=[message, message],
+        functools.partial(product_kernel, which, rows, tile, coded, pieces),
+        out_shape=[shape, shape],
         in_specs=[VMEM] * (2 + len(arrivals)) + [pl.BlockSpec(memory_space=pl.ANY)] * 2,
         out_specs=[VMEM] * 2,
         scratch_shapes=[pltpu.VMEM((2 * size, tokens), BF16)],
@@ -159,17 +240,15 @@
 
 def first(rows, tile, x, dy):
     tokens, cols = dy.shape
-    size = 2 * rows
-    message = jax.ShapeDtypeStruct((size + PAD, cols), BF16)
     xt = jax.ShapeDtypeStruct((x.shape[1], tokens), BF16)
     return pl.pallas_call(
         functools.partial(first_kernel, rows, tile),
-        out_shape=[xt, jax.ShapeDtypeStruct(dy.shape, BF16), message, message],
+        out_shape=[xt, jax.ShapeDtypeStruct(dy.shape, BF16)] + [message(2 * rows, cols, False)] * 2,
         in_specs=[pl.BlockSpec(memory_space=pltpu.HBM)] * 2,
         out_specs=[VMEM] * 4,
         scratch_shapes=[
             pltpu.VMEM(x.shape, BF16),
-            pltpu.VMEM((2 * size, tokens), BF16),
+            pltpu.VMEM((4 * rows, tokens), BF16),
             pltpu.SemaphoreType.DMA((tokens // tile,)),
             pltpu.SemaphoreType.DMA((cols // (2 * tile),)),
         ],
@@ -183,47 +262,40 @@
         yield slice(at, at + tile)
 
 
-def read(ref, rows, at, count, cols=slice(None)):
-    scale = ref.shape[0] - PAD
-    return decode(ref[at * rows : (at + count) * rows, cols], ref[scale : scale + 1, cols])
-
-
-def write(out, values, cols=slice(None)):
-    code, peak = encode(values)
-    size = values.shape[0]
-    out[:size, cols] = code
-    out[size:, cols] = jnp.broadcast_to(peak, (PAD, peak.shape[1]))
-
-
 def near_kernel(rows, tile, kept0, kept1, arr0, arr1, *rest):
     for kept, arr, out in ((kept0, arr0, rest[-2]), (kept1, arr1, rest[-1])):
+        read, put = Reader(arr, kept.shape[1], rows), Writer(out)
         for cols in parts_of(kept, tile):
-            write(out, kept[:rows, cols] + read(arr, rows, 0, 1, cols), cols)
+            put(kept[:rows, cols] + read(0, 1, cols))
+        put.close()
 
 
 def far_kernel(rows, tile, kept0, kept1, arr0, arr1, *rest):
     for kept, arr, out in ((kept0, arr0, rest[-2]), (kept1, arr1, rest[-1])):
+        read, put = Reader(arr, kept.shape[1], rows), Writer(out)
         for cols in parts_of(kept, tile):
-            write(out, kept[rows:, cols] + read(arr, rows, 1, 1, cols), cols)
+            put(kept[rows:, cols] + read(1, 1, cols))
+        put.close()
 
 
 def add_kernel(rows, tile, kept0, kept1, arr0, arr1, out0, out1):
     for kept, arr, out in ((kept0, arr0, out0), (kept1, arr1, out1)):
+        read = Reader(arr, kept.shape[1], rows)
         for cols in parts_of(kept, tile):
-            out[:, cols] = kept[:, cols] + read(arr, rows, 0, 2, cols)
+            out[:, cols] = kept[:, cols] + read(0, 2, cols)
 
 
 def own_kernel(rows, tile, kept0, kept1, arr0, arr1, out):
     for s, (kept, arr) in enumerate(((kept0, arr0), (kept1, arr1))):
+        read = Reader(arr, kept.shape[1], rows)
         for cols in parts_of(kept, tile):
-            out[s * rows : (s + 1) * rows, cols] = kept[rows:, cols] + read(arr, rows, 0, 1, cols)
-
-
-def merge(name, kernel, rows, tile, ins, heights, outs, after=()):
-    cols = ins[0].shape[1]
+            out[s * rows : (s + 1) * rows, cols] = kept[rows:, cols] + read(0, 1, cols)
+
+
+def merge(name, kernel, rows, tile, ins, outs, after=()):
     return pl.pallas_call(
         functools.partial(kernel, rows, tile),
-        out_shape=[jax.ShapeDtypeStruct((h, cols), dtype) for h, dtype in zip(heights, outs)],
+        out_shape=outs,
         in_specs=[VMEM] * len(ins) + [pl.BlockSpec(memory_space=pl.ANY)] * len(after),
         out_specs=[VMEM] * len(outs),
         compiler_params=params(12),
@@ -231,41 +303,46 @@
     )(*ins, *after)
 
 
-def last_kernel(rows, own, arr0, arr1, *outs):
+def last_kernel(rows, far, own, arr0, arr1, *rest):
     _, y, _, core = coordinates()
     m1, m2 = masks(core)
-    width = own.shape[1] // SIDE
-    for out, at in zip(outs, (y ^ 2, y ^ m1, y ^ m2, y)):
-        cols = pl.ds(pl.multiple_of(at * width, 128), width)
-        parts = [own[s * rows : (s + 1) * rows, cols] + read(a, rows, 0, 1, cols) for s, a in enumerate((arr0, arr1))]
-        write(out, jnp.concatenate(parts))
-
-
-def last(rows, own, arrivals):
-    message = jax.ShapeDtypeStruct((2 * rows + PAD, own.shape[1] // SIDE), BF16)
+    tiles = own.shape[1] // SIDE // LANES
+    targets, outs = ((y ^ 2,), rest) if far else ((y ^ m1, y ^ m2, y), rest[1:])
+    readers = [Reader(a, own.shape[1], rows) for a in (arr0, arr1)]
+    for out, at in zip(outs, targets):
+        put = Writer(out)
+        for t in range(tiles):
+            tile = at * tiles + t
+            added = jnp.concatenate([read.dynamic(tile) for read in readers])
+            put(own[:, pl.ds(pl.multiple_of(tile * LANES, LANES), LANES)] + added)
+        put.close()
+
+
+def last(rows, own, arrivals, after=()):
+    count = 3 if after else 1
     return pl.pallas_call(
-        functools.partial(last_kernel, rows),
-        out_shape=[message] * SIDE,
-        in_specs=[VMEM] * 3,
-        out_specs=[VMEM] * SIDE,
+        functools.partial(last_kernel, rows, not after),
+        out_shape=[message(2 * rows, own.shape[1] // SIDE, True)] * count,
+        in_specs=[VMEM] * 3 + [pl.BlockSpec(memory_space=pl.ANY)] * len(after),
+        out_specs=[VMEM] * count,
         compiler_params=params(12),
-        name="last",
-    )(own, *arrivals)
+        name="last_near" if after else "last_far",
+    )(own, *arrivals, *after)
 
 
 def gram_kernel(rows, half, own0, own1, own2, own3, carr, g_ref, gram_ref):
     _, y, _, core = coordinates()
     m1, m2 = masks(core)
     wide = g_ref.shape[2]
+    start = (wide - half) * core
     lane = lax.broadcasted_iota(jnp.int32, (1, wide), 1)
-    start = (wide - half) * core
     valid = (lane >= start) & (lane < start + half)
-    at = pl.ds(pl.multiple_of((own0.shape[1] - wide) * core, 128), wide)
+    at = pl.ds(pl.multiple_of((own0.shape[1] - wide) * core, LANES), wide)
     sources = [(own0, 0, 0), (own1, m1, m2), (own2, m2, m1), (own3, 2, 2)]
     for k, (ref, mask, mask_other) in enumerate(sources):
-        own = decode(ref[:rows, at], ref[rows : rows + 1, at])
+        own = decode(ref[:rows, at], ref[rows : rows + 1, at].astype(F32))
         g_ref[(y ^ mask) * 2 + core] = jnp.where(valid, own, 0.0)
-        other = decode(carr[k, :rows, :], carr[k, rows : rows + 1, :])
+        other = decode(carr[k, :rows, :], carr[k, rows : rows + 1, :].astype(F32))
         g_ref[(y ^ mask_other) * 2 + 1 - core] = jnp.where(valid, other, 0.0)
     nodes = g_ref.shape[0]
     pairs = [(i, j) for i in range(nodes) for j in range(i, nodes)]
@@ -339,25 +416,29 @@
     def send(pair, primary, is_first):
         return [exchange(m, axes[s] if primary else axes[1 - s], is_first) for s, m in enumerate(pair)]
 
-    make = functools.partial(product, rows=rows, tile=256, count=2)
+    make = functools.partial(product, rows=rows, tile=256)
     xt, dyv, *m1 = first(rows, 256, x, dy)
     p1a_near = send(m1, True, True)
     m2 = make("p1a_far", xt=xt, dy=dyv, arrivals=[], after=m1)
     p1a_far = send(m2, True, True)
     p1b_near = send(make("p1b_near", xt=xt, dy=dyv, arrivals=[], after=m2), True, True)
-    p2_near = send(make("p2_near", xt=xt, dy=dyv, arrivals=p1a_near, after=p1a_near), True, False)
-    p1b_far = send(make("p1b_far", xt=xt, dy=dyv, arrivals=[], after=p1a_far), True, True)
-    p2_far = send(make("p2_far", xt=xt, dy=dyv, arrivals=p1a_far, after=p1b_near), True, False)
-    kept_near = make("kept_near", xt=xt, dy=dyv, arrivals=p1b_near, after=p1b_near, coded=False)
-    kept_far = make("kept_far", xt=xt, dy=dyv, arrivals=p1b_far, after=p1b_far, coded=False)
-    one = [rows + PAD] * 2
-    two = [2 * rows] * 2
-    q1_near = send(merge("q1_near", near_kernel, rows, 256, [*kept_near, *p2_near], one, [BF16] * 2), False, True)
-    q1_far = send(merge("q1_far", far_kernel, rows, 256, [*kept_near, *p2_near], one, [BF16] * 2, p1b_far), False, True)
-    rest = merge("rest", add_kernel, rows, 256, [*kept_far, *p2_far], two, [F32] * 2)
-    q2 = send(merge("q2", near_kernel, rows, 256, [*rest, *q1_near], one, [BF16] * 2), False, False)
-    own = merge("own", own_kernel, rows, 256, [*rest, *q1_far], two[:1], [F32])
-    far, near1, near2, mine = last(rows, own[0], q2)
+    whole = ((0, 0, 2),)
+    p2_near = send(make("p2_near", xt=xt, dy=dyv, arrivals=p1a_near, after=p1a_near, pieces=whole), True, False)
+    m5 = make("p1b_far", xt=xt, dy=dyv, arrivals=[], after=p1a_far)
+    p1b_far = send(m5, True, True)
+    p2_far = send(make("p2_far", xt=xt, dy=dyv, arrivals=p1a_far, after=m5, pieces=whole), True, False)
+    kept_near = make("kept_near", xt=xt, dy=dyv, arrivals=p1b_near, after=p1b_near, pieces=whole, coded=False)
+    kept_far = make("kept_far", xt=xt, dy=dyv, arrivals=p1b_far, after=p1b_far, pieces=whole, coded=False)
+    one = [message(rows, cols, False)] * 2
+    two = [jax.ShapeDtypeStruct((2 * rows, cols), F32)] * 2
+    q1_near = send(merge("q1_near", near_kernel, rows, 256, [*kept_near, *p2_near], one), False, True)
+    q1_far = send(merge("q1_far", far_kernel, rows, 256, [*kept_near, *p2_near], one, p1b_far), False, True)
+    rest = merge("rest", add_kernel, rows, 256, [*kept_far, *p2_far], two)
+    q2 = send(merge("q2", near_kernel, rows, 256, [*rest, *q1_near], one), False, False)
+    own = merge("own", own_kernel, rows, 256, [*rest, *q1_far], two[:1])
+    far = last(rows, own[0], q2)
+    near1, near2, mine = last(rows, own[0], q2, far)
+    far = far[0]
     far = lax.ppermute(far, "node", [(i, i ^ 4) for i in range(2 * SIDE)])
     near1 = exchange(near1, "y", True)
     near2 = exchange(near2, "y", False)

time: 128 us -> 125 us (0.977)
  waiting for transfers between devices: 28.1 us -> 26.3 us
  blocking collectives: 14.7 us -> 13.1 us
  starting transfers between devices: 49.2 us -> 50.5 us
    ppermute x1, starting transfers between devices: 9.82 us -> 12 us  [local(): carr = lax.ppermute(across, 'node', [(i, i ^ 1) for i in range(2 * SIDE)])]
    ppermute x1, waiting for transfers between devices: 2.1 us -> 0.01 us  [local(): far = lax.ppermute(far, 'node', [(i, i ^ 4) for i in range(2 * SIDE)])]
    all_to_all x1, blocking collectives: 14.7 us -> 13.1 us  [local(): sums = lax.all_to_all(gram, ('node', 'fsdp'), 0, 0, tiled=True)]
    pallas_call x6 -> x7, Pallas kernels: 6.63 us -> 6.71 us  [the longest x5 5.39 us: merge(): pl.pallas_call(functools.partial(kernel, rows, tile), out_shape=outs, in_...]
  transfers between devices with their start and end apart: 22 -> 22, of which waited for: 12 -> 10; matrix products, arithmetic and copies ran while one was open for 0% -> 0% of each run, Pallas kernels for 18% -> 19%
where the time goes in v4:
time: 125 us
  starting transfers between devices  50.5 us (40%)
  Pallas kernels  34.3 us (27%)
  waiting for transfers between devices  26.3 us (21%)
  blocking collectives  13.1 us (10%)
    ppermute x20, starting transfers between devices, exchange(): return lax.ppermute(array, ('node', 'fsdp'), pairing(axis, first))  38.2 us
    ppermute x20, waiting for transfers between devices, exchange(): return lax.ppermute(array, ('node', 'fsdp'), pairing(axis, first))  24.8 us
    pallas_call x7, Pallas kernels, product(): pl.pallas_call(functools.partial(product_kernel, which, rows, tile, coded...  17.7 us
    all_to_all x1, blocking collectives, local(): sums = lax.all_to_all(gram, ('node', 'fsdp'), 0, 0, tiled=True)  13.1 us
    ppermute x1, starting transfers between devices, local(): carr = lax.ppermute(across, 'node', [(i, i ^ 1) for i in range(2 * SIDE)])  12 us
    pallas_call x1, Pallas kernels, first(): pl.pallas_call(functools.partial(first_kernel, rows, tile), out_shape=[xt...  6.57 us
    pallas_call x5, Pallas kernels, merge(): pl.pallas_call(functools.partial(kernel, rows, tile), out_shape=outs, in_...  5.39 us
  transfers between devices with their start and end apart: 22, of which 10 were waited for; matrix products, arithmetic and copies ran while one was open for 0% of the time, Pallas kernels for 19%

profile of v4, /device:TPU:1, one launch (start us, length us, event | category | flops | bytes accessed | tf_op | source)
XLA Modules:
  0.0 124.6 jit_solution(6136854772755433632)
XLA Ops:
  0.0 6.6 %p1a_near.1 = (bf16[2560,1024]{1,0:T(8,128)(2,1)S(1)}, bf16[1024,2560]{1,0:T(8,128)(2,1)S(1)}, bf16[3232,128]{1,0:T(8,128)(2,1)S(1)}, bf16[3232,128]{1,0:T(8,128)(2,1)S(1)}) custom-call(bf16[1024,2560]{1,0:T(8,128)(2,1)} %x_ref.1, bf16[1024,2560]{1,0:T(8,128)(2,1)} %dy_ref.1), custom_call_target="tpu_custom_call" | custom-call | tf_op jit(solution)/shard_map/p1a_near/pallas_call | solution.py:244
  6.6 3.4 %collective-permute-start.8 = (bf16[3232,128]{1,0:T(8,128)(2,1)S(1)}, bf16[3232,128]{1,0:T(8,128)(2,1)S(1)}, u32[]{:S(2)}, u32[]{:S(2)}) collective-permute-start(bf16[3232,128]{1,0:T(8,128)(2,1)S(1)} %get-tuple-element.38.rest_0_), channel_id=1, source_target_pairs={{0,1},{1,0},{2,3},{3,2},{4,5},{5,4},{6,7},{7,6},{8,9},{9,8},{10,11... | collective-permute-start | bytes 2482184 | tf_op jit(solution)/shard_map/ppermute | solution.py:128
  10.0 3.8 %collective-permute-start.9 = (bf16[3232,128]{1,0:T(8,128)(2,1)S(1)}, bf16[3232,128]{1,0:T(8,128)(2,1)S(1)}, u32[]{:S(2)}, u32[]{:S(2)}) collective-permute-start(bf16[3232,128]{1,0:T(8,128)(2,1)S(1)} %get-tuple-element.39.rest_1_), channel_id=1, source_target_pairs={{0,4},{1,5},{2,6},{3,7},{4,0},{5,1},{6,2},{7,3},{8,12},{9,13},{10,... | collective-permute-start | bytes 2482184 | tf_op jit(solution)/shard_map/ppermute | solution.py:128
  13.7 2.3 %p1a_far.1 = (bf16[3232,128]{1,0:T(8,128)(2,1)S(1)}, bf16[3232,128]{1,0:T(8,128)(2,1)S(1)}) custom-call(bf16[2560,1024]{1,0:T(8,128)(2,1)S(1)} %get-tuple-element.36.xt_ref, bf16[1024,2560]{1,0:T(8,128)(2,1)S(1)} %get-tuple-element.37.dy_ref, bf16[3232,128]{1,0:T(8,128)(2,1)S(1)} %get-tuple-element.38.rest_0_, bf16[3232,128]{1,0:T(8,128)(2,1)S(1)} %get-tuple-element.39.rest_1_), custom_call_target="tpu_custom_call" | custom-call | tf_op jit(solution)/shard_map/p1a_far/pallas_call | solution.py:230
  16.0 0.3 collective-permute-start
  16.3 2.3 %p1b_near.1 = (bf16[3232,128]{1,0:T(8,128)(2,1)S(1)}, bf16[3232,128]{1,0:T(8,128)(2,1)S(1)}) custom-call(bf16[2560,1024]{1,0:T(8,128)(2,1)S(1)} %get-tuple-element.36.xt_ref, bf16[1024,2560]{1,0:T(8,128)(2,1)S(1)} %get-tuple-element.37.dy_ref, bf16[3232,128]{1,0:T(8,128)(2,1)S(1)} %get-tuple-element.40.rest_0_, bf16[3232,128]{1,0:T(8,128)(2,1)S(1)} %get-tuple-element.41.rest_1_), custom_call_target="tpu_custom_call" | custom-call | tf_op jit(solution)/shard_map/p1b_near/pallas_call | solution.py:230
  18.6 2.5 %collective-permute-start.6 = (bf16[3232,128]{1,0:T(8,128)(2,1)S(1)}, bf16[3232,128]{1,0:T(8,128)(2,1)S(1)}, u32[]{:S(2)}, u32[]{:S(2)}) collective-permute-start(bf16[3232,128]{1,0:T(8,128)(2,1)S(1)} %get-tuple-element.50), channel_id=1, source_target_pairs={{0,1},{1,0},{2,3},{3,2},{4,5},{5,4},{6,7},{7,6},{8,9},{9,8},{10,11... | collective-permute-start | bytes 2482184 | tf_op jit(solution)/shard_map/ppermute | solution.py:128
  21.2 2.7 %collective-permute-start.7 = (bf16[3232,128]{1,0:T(8,128)(2,1)S(1)}, bf16[3232,128]{1,0:T(8,128)(2,1)S(1)}, u32[]{:S(2)}, u32[]{:S(2)}) collective-permute-start(bf16[3232,128]{1,0:T(8,128)(2,1)S(1)} %get-tuple-element.51), channel_id=1, source_target_pairs={{0,4},{1,5},{2,6},{3,7},{4,0},{5,1},{6,2},{7,3},{8,12},{9,13},{10,... | collective-permute-start | bytes 2482184 | tf_op jit(solution)/shard_map/ppermute | solution.py:128
  23.8 3.2 %p2_near.1 = (bf16[3232,128]{1,0:T(8,128)(2,1)S(1)}, bf16[3232,128]{1,0:T(8,128)(2,1)S(1)}) custom-call(bf16[2560,1024]{1,0:T(8,128)(2,1)S(1)} %get-tuple-element.36.xt_ref, bf16[1024,2560]{1,0:T(8,128)(2,1)S(1)} %get-tuple-element.37.dy_ref, bf16[3232,128]{1,0:T(8,128)(2,1)S(1)} %collective-permute-done.8.rest_0_.rest_2_, ...), custom_call_target="tpu_custom_call" | custom-call | tf_op jit(solution)/shard_map/p2_near/pallas_call | solution.py:230
  27.1 0.4 collective-permute-start.10
  27.5 1.1 collective-permute-done.rest_0_
  28.6 1.8 %collective-permute-start.11 = (bf16[3232,128]{1,0:T(8,128)(2,1)S(1)}, bf16[3232,128]{1,0:T(8,128)(2,1)S(1)}, u32[]{:S(2)}, u32[]{:S(2)}) collective-permute-start(bf16[3232,128]{1,0:T(8,128)(2,1)S(1)} %get-tuple-element.55), channel_id=1, source_target_pairs={{0,12},{1,13},{2,14},{3,15},{4,8},{5,9},{6,10},{7,11},{8,4},{9,5},... | collective-permute-start | bytes 2482184 | tf_op jit(solution)/shard_map/ppermute | solution.py:128
  30.5 2.2 %collective-permute-done.1.rest_1_ = bf16[3232,128]{1,0:T(8,128)(2,1)S(1)} collective-permute-done((bf16[3232,128]{1,0:T(8,128)(2,1)S(1)}, bf16[3232,128]{1,0:T(8,128)(2,1)S(1)}, u32[]{:S(2)}, u32[]{:S(2)}) %collective-permute-start.1) | collective-permute-done | bytes 827424 | tf_op jit(solution)/shard_map/ppermute | solution.py:128
  32.7 2.3 %p1b_far.1 = (bf16[3232,128]{1,0:T(8,128)(2,1)S(1)}, bf16[3232,128]{1,0:T(8,128)(2,1)S(1)}) custom-call(bf16[2560,1024]{1,0:T(8,128)(2,1)S(1)} %get-tuple-element.36.xt_ref, bf16[1024,2560]{1,0:T(8,128)(2,1)S(1)} %get-tuple-element.37.dy_ref, bf16[3232,128]{1,0:T(8,128)(2,1)S(1)} %collective-permute-done.rest_0_, ...), custom_call_target="tpu_custom_call" | custom-call | tf_op jit(solution)/shard_map/p1b_far/pallas_call | solution.py:230
  35.0 0.4 collective-permute-start.2
  35.4 9.8 %collective-permute-done.6.rest_0_.rest_2_ = bf16[3232,128]{1,0:T(8,128)(2,1)S(1)} collective-permute-done((bf16[3232,128]{1,0:T(8,128)(2,1)S(1)}, bf16[3232,128]{1,0:T(8,128)(2,1)S(1)}, u32[]{:S(2)}, u32[]{:S(2)}) %collective-permute-start.6) | collective-permute-done | bytes 827424 | tf_op jit(solution)/shard_map/ppermute | solution.py:128
  45.2 4.6 %collective-permute-start.3 = (bf16[3232,128]{1,0:T(8,128)(2,1)S(1)}, bf16[3232,128]{1,0:T(8,128)(2,1)S(1)}, u32[]{:S(2)}, u32[]{:S(2)}) collective-permute-start(bf16[3232,128]{1,0:T(8,128)(2,1)S(1)} %get-tuple-element.43.rest_3_), channel_id=1, source_target_pairs={{0,4},{1,5},{2,6},{3,7},{4,0},{5,1},{6,2},{7,3},{8,12},{9,13},{10,... | collective-permute-start | bytes 2482184 | tf_op jit(solution)/shard_map/ppermute | solution.py:128
  49.7 3.2 %p2_far.1 = (bf16[3232,128]{1,0:T(8,128)(2,1)S(1)}, bf16[3232,128]{1,0:T(8,128)(2,1)S(1)}) custom-call(bf16[2560,1024]{1,0:T(8,128)(2,1)S(1)} %get-tuple-element.36.xt_ref, bf16[1024,2560]{1,0:T(8,128)(2,1)S(1)} %get-tuple-element.37.dy_ref, bf16[3232,128]{1,0:T(8,128)(2,1)S(1)} %collective-permute-done.rest_0_, ...), custom_call_target="tpu_custom_call" | custom-call | tf_op jit(solution)/shard_map/p2_far/pallas_call | solution.py:230
  53.0 0.9 collective-permute-start.4
  53.9 2.2 %kept_near.1 = (f32[160,2560]{1,0:T(8,128)S(1)}, f32[160,2560]{1,0:T(8,128)S(1)}) custom-call(bf16[2560,1024]{1,0:T(8,128)(2,1)S(1)} %get-tuple-element.36.xt_ref, bf16[1024,2560]{1,0:T(8,128)(2,1)S(1)} %get-tuple-element.37.dy_ref, bf16[3232,128]{1,0:T(8,128)(2,1)S(1)} %collective-permute-done.6.rest_0_.rest_2_, ...), custom_call_target="tpu_custom_call" | custom-call | tf_op jit(solution)/shard_map/kept_near/pallas_call | solution.py:230
  56.1 1.1 q1_near.1
  57.3 0.1 collective-permute-start.14
  57.4 2.5 %collective-permute-start.15 = (bf16[1632,128]{1,0:T(8,128)(2,1)S(1)}, bf16[1632,128]{1,0:T(8,128)(2,1)S(1)}, u32[]{:S(2)}, u32[]{:S(2)}) collective-permute-start(bf16[1632,128]{1,0:T(8,128)(2,1)S(1)} %get-tuple-element.59), channel_id=1, source_target_pairs={{0,1},{1,0},{2,3},{3,2},{4,5},{5,4},{6,7},{7,6},{8,9},{9,8},{10,11... | collective-permute-start | bytes 1253384 | tf_op jit(solution)/shard_map/ppermute | solution.py:128
  59.9 0.2 collective-permute-done.3.rest_1_.rest_3_
  60.1 1.1 q1_far.1
  61.2 3.4 %collective-permute-start.12 = (bf16[1632,128]{1,0:T(8,128)(2,1)S(1)}, bf16[1632,128]{1,0:T(8,128)(2,1)S(1)}, u32[]{:S(2)}, u32[]{:S(2)}) collective-permute-start(bf16[1632,128]{1,0:T(8,128)(2,1)S(1)} %get-tuple-element.56), channel_id=1, source_target_pairs={{0,4},{1,5},{2,6},{3,7},{4,0},{5,1},{6,2},{7,3},{8,12},{9,13},{10,... | collective-permute-start | bytes 1253384 | tf_op jit(solution)/shard_map/ppermute | solution.py:128
  64.6 2.2 %kept_far.1 = (f32[160,2560]{1,0:T(8,128)S(1)}, f32[160,2560]{1,0:T(8,128)S(1)}) custom-call(bf16[2560,1024]{1,0:T(8,128)(2,1)S(1)} %get-tuple-element.36.xt_ref, bf16[1024,2560]{1,0:T(8,128)(2,1)S(1)} %get-tuple-element.37.dy_ref, bf16[3232,128]{1,0:T(8,128)(2,1)S(1)} %collective-permute-done.2.rest_0_.rest_2_, ...), custom_call_target="tpu_custom_call" | custom-call | tf_op jit(solution)/shard_map/kept_far/pallas_call | solution.py:230
  66.8 6.2 %collective-permute-start.13 = (bf16[1632,128]{1,0:T(8,128)(2,1)S(1)}, bf16[1632,128]{1,0:T(8,128)(2,1)S(1)}, u32[]{:S(2)}, u32[]{:S(2)}) collective-permute-start(bf16[1632,128]{1,0:T(8,128)(2,1)S(1)} %get-tuple-element.57), channel_id=1, source_target_pairs={{0,1},{1,0},{2,3},{3,2},{4,5},{5,4},{6,7},{7,6},{8,9},{9,8},{10,11... | collective-permute-start | bytes 1253384 | tf_op jit(solution)/shard_map/ppermute | solution.py:128
  73.0 1.3 %rest.1 = (f32[160,2560]{1,0:T(8,128)S(1)}, f32[160,2560]{1,0:T(8,128)S(1)}) custom-call(f32[160,2560]{1,0:T(8,128)S(1)} %get-tuple-element.44.kept0, f32[160,2560]{1,0:T(8,128)S(1)} %get-tuple-element.45.kept1, bf16[3232,128]{1,0:T(8,128)(2,1)S(1)} %collective-permute-done.4.arr0, bf16[3232,128]{1,0:T(8,128)(2,1)S(1)} %collective-permute-done.5.arr1), custom_call_target="tpu_custom_call" | custom-call | tf_op jit(solution)/shard_map/rest/pallas_call | solution.py:296
  74.3 1.2 q2.1
  75.5 1.4 %collective-permute-start.16 = (bf16[1632,128]{1,0:T(8,128)(2,1)S(1)}, bf16[1632,128]{1,0:T(8,128)(2,1)S(1)}, u32[]{:S(2)}, u32[]{:S(2)}) collective-permute-start(bf16[1632,128]{1,0:T(8,128)(2,1)S(1)} %get-tuple-element.60), channel_id=1, source_target_pairs={{0,12},{1,13},{2,14},{3,15},{4,8},{5,9},{6,10},{7,11},{8,4},{9,5},... | collective-permute-start | bytes 1253384 | tf_op jit(solution)/shard_map/ppermute | solution.py:128
  76.9 0.7 collective-permute-start.17
  77.6 0.8 collective-permute-done.13.arr1
  78.4 0.7 own.1
  79.1 3.4 %collective-permute-done.16.arr0 = bf16[1632,128]{1,0:T(8,128)(2,1)S(1)} collective-permute-done((bf16[1632,128]{1,0:T(8,128)(2,1)S(1)}, bf16[1632,128]{1,0:T(8,128)(2,1)S(1)}, u32[]{:S(2)}, u32[]{:S(2)}) %collective-permute-start.16) | collective-permute-done | bytes 417824 | tf_op jit(solution)/shard_map/ppermute | solution.py:128
  82.4 1.6 %collective-permute-done.17.arr1 = bf16[1632,128]{1,0:T(8,128)(2,1)S(1)} collective-permute-done((bf16[1632,128]{1,0:T(8,128)(2,1)S(1)}, bf16[1632,128]{1,0:T(8,128)(2,1)S(1)}, u32[]{:S(2)}, u32[]{:S(2)}) %collective-permute-start.17) | collective-permute-done | bytes 417824 | tf_op jit(solution)/shard_map/ppermute | solution.py:128
  84.1 0.3 last_far.1.rest_0_
  84.4 1.0 last_near.1
  85.4 2.8 %collective-permute-start.18 = (bf16[168,640]{1,0:T(8,128)(2,1)S(1)}, bf16[168,640]{1,0:T(8,128)(2,1)S(1)}, u32[]{:S(2)}, u32[]{:S(2)}) collective-permute-start(bf16[168,640]{1,0:T(8,128)(2,1)S(1)} %get-tuple-element.63), channel_id=1, source_target_pairs={{0,32},{1,33},{2,34},{3,35},{4,36},{5,37},{6,38},{7,39},{8,40},{9,... | collective-permute-start | bytes 645128 | tf_op jit(solution)/shard_map/ppermute | solution.py:128
  88.2 0.3 collective-permute-start.20
  88.6 0.3 collective-permute-start.19
  88.9 4.4 %collective-permute-done.18.own1 = bf16[168,640]{1,0:T(8,128)(2,1)S(1)} collective-permute-done((bf16[168,640]{1,0:T(8,128)(2,1)S(1)}, bf16[168,640]{1,0:T(8,128)(2,1)S(1)}, u32[]{:S(2)}, u32[]{:S(2)}) %collective-permute-start.18) | collective-permute-done | bytes 215072 | tf_op jit(solution)/shard_map/ppermute | solution.py:128
  93.4 1.1 collective-permute-done.19.own2
  94.6 12.0 %collective-permute-start.21 = (bf16[4,168,384]{2,1,0:T(8,128)(2,1)S(1)}, bf16[4,168,384]{2,1,0:T(8,128)(2,1)S(1)}, u32[]{:S(2)}, u32[]{:S(2)}) collective-permute-start(bf16[4,168,384]{2,1,0:T(8,128)(2,1)S(1)} %pad_maximum_fusion), channel_id=1, source_target_pairs={{0,16},{16,0},{32,48},{48,32},{64,80},{80,64},{96,112},{112,96},{1... | collective-permute-start | bytes 1548296 | tf_op jit(solution)/shard_map/ppermute | solution.py:448
  106.7 1.5 %collective-permute-done.21.carr = bf16[4,168,384]{2,1,0:T(8,128)(2,1)S(1)} collective-permute-done((bf16[4,168,384]{2,1,0:T(8,128)(2,1)S(1)}, bf16[4,168,384]{2,1,0:T(8,128)(2,1)S(1)}, u32[]{:S(2)}, u32[]{:S(2)}) %collective-permute-start.21) | collective-permute-done | bytes 516128 | tf_op jit(solution)/shard_map/ppermute | solution.py:448
  108.2 1.7 %gram.1 = (f32[8,160,384]{2,1,0:T(8,128)S(1)}, f32[128,128]{1,0:T(8,128)S(1)}) custom-call(bf16[168,640]{1,0:T(8,128)(2,1)S(1)} %get-tuple-element.62.own0, bf16[168,640]{1,0:T(8,128)(2,1)S(1)} %collective-permute-done.18.own1, bf16[168,640]{1,0:T(8,128)(2,1)S(1)} %collective-permute-done.19.own2, bf16[168,640]{1,0:T(8,128)(2,1)S(1)} %collective-permute-done.20.own3, ...), custom_call_target="tpu_custom_call" | custom-call | tf_op jit(solution)/shard_map/gram/pallas_call | solution.py:450
  109.9 13.1 %all_to_all.11 = f32[128,1,128]{2,1,0:T(1,128)S(1)} all-to-all(f32[128,1,128]{2,1,0:T(1,128)S(1)} %bitcast.13), channel_id=1, replica_groups=mesh['node'=8,'fsdp'=16] {'node','fsdp'}, dimensions={0} | all-to-all | bytes 131072 | tf_op jit(solution)/shard_map/all_to_all | solution.py:459
  122.9 1.6 %combine.1 = f32[160,320]{1,0:T(8,128)} custom-call(f32[8,160,384]{2,1,0:T(8,128)S(1)} %get-tuple-element.65.g_ref, f32[128,128]{1,0:T(8,128)S(1)} %bitcast.12), custom_call_target="tpu_custom_call" | custom-call | tf_op jit(solution)/shard_map/combine/pallas_call | solution.py:460
  (19 shorter events, 0.2 us)
Async XLA Ops:
  6.6 14.6 %collective-permute-start.8 = (bf16[3232,128]{1,0:T(8,128)(2,1)S(1)}, bf16[3232,128]{1,0:T(8,128)(2,1)S(1)}, u32[]{:S(2)}, u32[]{:S(2)}) collective-permute-start(bf16[3232,128]{1,0:T(8,128)(2,1)S(1)} %get-tuple-element.38.rest_0_), channel_id=1, source_target_pairs={{0,1},{1,0},{2,3},{3,2},{4,5},{5,4},{6,7},{7,6},{8,9},{9,8},{10,11... | collective-permute-start | bytes 2482184 | tf_op jit(solution)/shard_map/ppermute | solution.py:128
  10.0 13.9 %collective-permute-start.9 = (bf16[3232,128]{1,0:T(8,128)(2,1)S(1)}, bf16[3232,128]{1,0:T(8,128)(2,1)S(1)}, u32[]{:S(2)}, u32[]{:S(2)}) collective-permute-start(bf16[3232,128]{1,0:T(8,128)(2,1)S(1)} %get-tuple-element.39.rest_1_), channel_id=1, source_target_pairs={{0,4},{1,5},{2,6},{3,7},{4,0},{5,1},{6,2},{7,3},{8,12},{9,13},{10,... | collective-permute-start | bytes 2482184 | tf_op jit(solution)/shard_map/ppermute | solution.py:128
  16.0 12.6 %collective-permute-start = (bf16[3232,128]{1,0:T(8,128)(2,1)S(1)}, bf16[3232,128]{1,0:T(8,128)(2,1)S(1)}, u32[]{:S(2)}, u32[]{:S(2)}) collective-permute-start(bf16[3232,128]{1,0:T(8,128)(2,1)S(1)} %get-tuple-element.40.rest_0_), channel_id=1, source_target_pairs={{0,1},{1,0},{2,3},{3,2},{4,5},{5,4},{6,7},{7,6},{8,9},{9,8},{10,11... | collective-permute-start | bytes 2482184 | tf_op jit(solution)/shard_map/ppermute | solution.py:128
  16.3 16.4 %collective-permute-start.1 = (bf16[3232,128]{1,0:T(8,128)(2,1)S(1)}, bf16[3232,128]{1,0:T(8,128)(2,1)S(1)}, u32[]{:S(2)}, u32[]{:S(2)}) collective-permute-start(bf16[3232,128]{1,0:T(8,128)(2,1)S(1)} %get-tuple-element.41.rest_1_), channel_id=1, source_target_pairs={{0,4},{1,5},{2,6},{3,7},{4,0},{5,1},{6,2},{7,3},{8,12},{9,13},{10,... | collective-permute-start | bytes 2482184 | tf_op jit(solution)/shard_map/ppermute | solution.py:128
  18.6 26.5 %collective-permute-start.6 = (bf16[3232,128]{1,0:T(8,128)(2,1)S(1)}, bf16[3232,128]{1,0:T(8,128)(2,1)S(1)}, u32[]{:S(2)}, u32[]{:S(2)}) collective-permute-start(bf16[3232,128]{1,0:T(8,128)(2,1)S(1)} %get-tuple-element.50), channel_id=1, source_target_pairs={{0,1},{1,0},{2,3},{3,2},{4,5},{5,4},{6,7},{7,6},{8,9},{9,8},{10,11... | collective-permute-start | bytes 2482184 | tf_op jit(solution)/shard_map/ppermute | solution.py:128
  21.2 31.8 %collective-permute-start.7 = (bf16[3232,128]{1,0:T(8,128)(2,1)S(1)}, bf16[3232,128]{1,0:T(8,128)(2,1)S(1)}, u32[]{:S(2)}, u32[]{:S(2)}) collective-permute-start(bf16[3232,128]{1,0:T(8,128)(2,1)S(1)} %get-tuple-element.51), channel_id=1, source_target_pairs={{0,4},{1,5},{2,6},{3,7},{4,0},{5,1},{6,2},{7,3},{8,12},{9,13},{10,... | collective-permute-start | bytes 2482184 | tf_op jit(solution)/shard_map/ppermute | solution.py:128
  27.1 26.8 %collective-permute-start.10 = (bf16[3232,128]{1,0:T(8,128)(2,1)S(1)}, bf16[3232,128]{1,0:T(8,128)(2,1)S(1)}, u32[]{:S(2)}, u32[]{:S(2)}) collective-permute-start(bf16[3232,128]{1,0:T(8,128)(2,1)S(1)} %get-tuple-element.54), channel_id=1, source_target_pairs={{0,3},{1,2},{2,1},{3,0},{4,7},{5,6},{6,5},{7,4},{8,11},{9,10},{10,... | collective-permute-start | bytes 2482184 | tf_op jit(solution)/shard_map/ppermute | solution.py:128
  28.6 27.4 %collective-permute-start.11 = (bf16[3232,128]{1,0:T(8,128)(2,1)S(1)}, bf16[3232,128]{1,0:T(8,128)(2,1)S(1)}, u32[]{:S(2)}, u32[]{:S(2)}) collective-permute-start(bf16[3232,128]{1,0:T(8,128)(2,1)S(1)} %get-tuple-element.55), channel_id=1, source_target_pairs={{0,12},{1,13},{2,14},{3,15},{4,8},{5,9},{6,10},{7,11},{8,4},{9,5},... | collective-permute-start | bytes 2482184 | tf_op jit(solution)/shard_map/ppermute | solution.py:128
  35.0 22.4 %collective-permute-start.2 = (bf16[3232,128]{1,0:T(8,128)(2,1)S(1)}, bf16[3232,128]{1,0:T(8,128)(2,1)S(1)}, u32[]{:S(2)}, u32[]{:S(2)}) collective-permute-start(bf16[3232,128]{1,0:T(8,128)(2,1)S(1)} %get-tuple-element.42.rest_2_), channel_id=1, source_target_pairs={{0,1},{1,0},{2,3},{3,2},{4,5},{5,4},{6,7},{7,6},{8,9},{9,8},{10,11... | collective-permute-start | bytes 2482184 | tf_op jit(solution)/shard_map/ppermute | solution.py:128
  45.2 14.9 %collective-permute-start.3 = (bf16[3232,128]{1,0:T(8,128)(2,1)S(1)}, bf16[3232,128]{1,0:T(8,128)(2,1)S(1)}, u32[]{:S(2)}, u32[]{:S(2)}) collective-permute-start(bf16[3232,128]{1,0:T(8,128)(2,1)S(1)} %get-tuple-element.43.rest_3_), channel_id=1, source_target_pairs={{0,4},{1,5},{2,6},{3,7},{4,0},{5,1},{6,2},{7,3},{8,12},{9,13},{10,... | collective-permute-start | bytes 2482184 | tf_op jit(solution)/shard_map/ppermute | solution.py:128
  53.0 13.8 %collective-permute-start.4 = (bf16[3232,128]{1,0:T(8,128)(2,1)S(1)}, bf16[3232,128]{1,0:T(8,128)(2,1)S(1)}, u32[]{:S(2)}, u32[]{:S(2)}) collective-permute-start(bf16[3232,128]{1,0:T(8,128)(2,1)S(1)} %get-tuple-element.46), channel_id=1, source_target_pairs={{0,3},{1,2},{2,1},{3,0},{4,7},{5,6},{6,5},{7,4},{8,11},{9,10},{10,... | collective-permute-start | bytes 2482184 | tf_op jit(solution)/shard_map/ppermute | solution.py:128
  53.9 19.1 %collective-permute-start.5 = (bf16[3232,128]{1,0:T(8,128)(2,1)S(1)}, bf16[3232,128]{1,0:T(8,128)(2,1)S(1)}, u32[]{:S(2)}, u32[]{:S(2)}) collective-permute-start(bf16[3232,128]{1,0:T(8,128)(2,1)S(1)} %get-tuple-element.47), channel_id=1, source_target_pairs={{0,12},{1,13},{2,14},{3,15},{4,8},{5,9},{6,10},{7,11},{8,4},{9,5},... | collective-permute-start | bytes 2482184 | tf_op jit(solution)/shard_map/ppermute | solution.py:128
  57.3 17.0 %collective-permute-start.14 = (bf16[1632,128]{1,0:T(8,128)(2,1)S(1)}, bf16[1632,128]{1,0:T(8,128)(2,1)S(1)}, u32[]{:S(2)}, u32[]{:S(2)}) collective-permute-start(bf16[1632,128]{1,0:T(8,128)(2,1)S(1)} %get-tuple-element.58), channel_id=1, source_target_pairs={{0,4},{1,5},{2,6},{3,7},{4,0},{5,1},{6,2},{7,3},{8,12},{9,13},{10,... | collective-permute-start | bytes 1253384 | tf_op jit(solution)/shard_map/ppermute | solution.py:128
  57.4 16.9 %collective-permute-start.15 = (bf16[1632,128]{1,0:T(8,128)(2,1)S(1)}, bf16[1632,128]{1,0:T(8,128)(2,1)S(1)}, u32[]{:S(2)}, u32[]{:S(2)}) collective-permute-start(bf16[1632,128]{1,0:T(8,128)(2,1)S(1)} %get-tuple-element.59), channel_id=1, source_target_pairs={{0,1},{1,0},{2,3},{3,2},{4,5},{5,4},{6,7},{7,6},{8,9},{9,8},{10,11... | collective-permute-start | bytes 1253384 | tf_op jit(solution)/shard_map/ppermute | solution.py:128
  61.2 16.4 %collective-permute-start.12 = (bf16[1632,128]{1,0:T(8,128)(2,1)S(1)}, bf16[1632,128]{1,0:T(8,128)(2,1)S(1)}, u32[]{:S(2)}, u32[]{:S(2)}) collective-permute-start(bf16[1632,128]{1,0:T(8,128)(2,1)S(1)} %get-tuple-element.56), channel_id=1, source_target_pairs={{0,4},{1,5},{2,6},{3,7},{4,0},{5,1},{6,2},{7,3},{8,12},{9,13},{10,... | collective-permute-start | bytes 1253384 | tf_op jit(solution)/shard_map/ppermute | solution.py:128
  66.8 11.6 %collective-permute-start.13 = (bf16[1632,128]{1,0:T(8,128)(2,1)S(1)}, bf16[1632,128]{1,0:T(8,128)(2,1)S(1)}, u32[]{:S(2)}, u32[]{:S(2)}) collective-permute-start(bf16[1632,128]{1,0:T(8,128)(2,1)S(1)} %get-tuple-element.57), channel_id=1, source_target_pairs={{0,1},{1,0},{2,3},{3,2},{4,5},{5,4},{6,7},{7,6},{8,9},{9,8},{10,11... | collective-permute-start | bytes 1253384 | tf_op jit(solution)/shard_map/ppermute | solution.py:128
  75.5 7.0 %collective-permute-start.16 = (bf16[1632,128]{1,0:T(8,128)(2,1)S(1)}, bf16[1632,128]{1,0:T(8,128)(2,1)S(1)}, u32[]{:S(2)}, u32[]{:S(2)}) collective-permute-start(bf16[1632,128]{1,0:T(8,128)(2,1)S(1)} %get-tuple-element.60), channel_id=1, source_target_pairs={{0,12},{1,13},{2,14},{3,15},{4,8},{5,9},{6,10},{7,11},{8,4},{9,5},... | collective-permute-start | bytes 1253384 | tf_op jit(solution)/shard_map/ppermute | solution.py:128
  76.9 7.2 %collective-permute-start.17 = (bf16[1632,128]{1,0:T(8,128)(2,1)S(1)}, bf16[1632,128]{1,0:T(8,128)(2,1)S(1)}, u32[]{:S(2)}, u32[]{:S(2)}) collective-permute-start(bf16[1632,128]{1,0:T(8,128)(2,1)S(1)} %get-tuple-element.61), channel_id=1, source_target_pairs={{0,3},{1,2},{2,1},{3,0},{4,7},{5,6},{6,5},{7,4},{8,11},{9,10},{10,... | collective-permute-start | bytes 1253384 | tf_op jit(solution)/shard_map/ppermute | solution.py:128
  85.4 7.9 %collective-permute-start.18 = (bf16[168,640]{1,0:T(8,128)(2,1)S(1)}, bf16[168,640]{1,0:T(8,128)(2,1)S(1)}, u32[]{:S(2)}, u32[]{:S(2)}) collective-permute-start(bf16[168,640]{1,0:T(8,128)(2,1)S(1)} %get-tuple-element.63), channel_id=1, source_target_pairs={{0,32},{1,33},{2,34},{3,35},{4,36},{5,37},{6,38},{7,39},{8,40},{9,... | collective-permute-start | bytes 645128 | tf_op jit(solution)/shard_map/ppermute | solution.py:128
  88.2 6.3 %collective-permute-start.20 = (bf16[168,640]{1,0:T(8,128)(2,1)S(1)}, bf16[168,640]{1,0:T(8,128)(2,1)S(1)}, u32[]{:S(2)}, u32[]{:S(2)}) collective-permute-start(bf16[168,640]{1,0:T(8,128)(2,1)S(1)} %last_far.1.rest_0_), channel_id=1, source_target_pairs={{0,64},{16,80},{32,96},{48,112},{64,0},{80,16},{96,32},{112,48},{1... | collective-permute-start | bytes 645128 | tf_op jit(solution)/shard_map/ppermute | solution.py:442
  88.6 5.9 %collective-permute-start.19 = (bf16[168,640]{1,0:T(8,128)(2,1)S(1)}, bf16[168,640]{1,0:T(8,128)(2,1)S(1)}, u32[]{:S(2)}, u32[]{:S(2)}) collective-permute-start(bf16[168,640]{1,0:T(8,128)(2,1)S(1)} %get-tuple-element.64), channel_id=1, source_target_pairs={{0,96},{1,97},{2,98},{3,99},{4,100},{5,101},{6,102},{7,103},{8,104... | collective-permute-start | bytes 645128 | tf_op jit(solution)/shard_map/ppermute | solution.py:128
  94.6 13.5 %collective-permute-start.21 = (bf16[4,168,384]{2,1,0:T(8,128)(2,1)S(1)}, bf16[4,168,384]{2,1,0:T(8,128)(2,1)S(1)}, u32[]{:S(2)}, u32[]{:S(2)}) collective-permute-start(bf16[4,168,384]{2,1,0:T(8,128)(2,1)S(1)} %pad_maximum_fusion), channel_id=1, source_target_pairs={{0,16},{16,0},{32,48},{48,32},{64,80},{80,64},{96,112},{112,96},{1... | collective-permute-start | bytes 1548296 | tf_op jit(solution)/shard_map/ppermute | solution.py:448

commit v5 on v4

--- a/solution.py
+++ b/solution.py
@@ -278,18 +278,19 @@
         put.close()
 
 
-def add_kernel(rows, tile, kept0, kept1, arr0, arr1, out0, out1):
-    for kept, arr, out in ((kept0, arr0, out0), (kept1, arr1, out1)):
-        read = Reader(arr, kept.shape[1], rows)
+def q2_kernel(rows, tile, kept0, kept1, p0, p1, q0, q1, out0, out1):
+    for kept, p, q, out in ((kept0, p0, q0, out0), (kept1, p1, q1, out1)):
+        far, near, put = Reader(p, kept.shape[1], rows), Reader(q, kept.shape[1], rows), Writer(out)
         for cols in parts_of(kept, tile):
-            out[:, cols] = kept[:, cols] + read(0, 2, cols)
-
-
-def own_kernel(rows, tile, kept0, kept1, arr0, arr1, out):
-    for s, (kept, arr) in enumerate(((kept0, arr0), (kept1, arr1))):
-        read = Reader(arr, kept.shape[1], rows)
+            put(kept[:rows, cols] + far(0, 1, cols) + near(0, 1, cols))
+        put.close()
+
+
+def own_kernel(rows, tile, kept0, kept1, p0, p1, q0, q1, out):
+    for s, (kept, p, q) in enumerate(((kept0, p0, q0), (kept1, p1, q1))):
+        far, near = Reader(p, kept.shape[1], rows), Reader(q, kept.shape[1], rows)
         for cols in parts_of(kept, tile):
-            out[s * rows : (s + 1) * rows, cols] = kept[rows:, cols] + read(0, 1, cols)
+            out[s * rows : (s + 1) * rows, cols] = kept[rows:, cols] + far(1, 1, cols) + near(0, 1, cols)
 
 
 def merge(name, kernel, rows, tile, ins, outs, after=()):
@@ -303,11 +304,12 @@
     )(*ins, *after)
 
 
-def last_kernel(rows, far, own, arr0, arr1, *rest):
+def last_kernel(rows, which, own, arr0, arr1, *rest):
     _, y, _, core = coordinates()
     m1, m2 = masks(core)
     tiles = own.shape[1] // SIDE // LANES
-    targets, outs = ((y ^ 2,), rest) if far else ((y ^ m1, y ^ m2, y), rest[1:])
+    targets = dict(far=(y ^ 2,), near=(y ^ m1, y ^ m2), mine=(y,))[which]
+    outs = rest[-len(targets) :]
     readers = [Reader(a, own.shape[1], rows) for a in (arr0, arr1)]
     for out, at in zip(outs, targets):
         put = Writer(out)
@@ -318,15 +320,15 @@
         put.close()
 
 
-def last(rows, own, arrivals, after=()):
-    count = 3 if after else 1
+def last(which, rows, own, arrivals, after=()):
+    count = 2 if which == "near" else 1
     return pl.pallas_call(
-        functools.partial(last_kernel, rows, not after),
+        functools.partial(last_kernel, rows, which),
         out_shape=[message(2 * rows, own.shape[1] // SIDE, True)] * count,
         in_specs=[VMEM] * 3 + [pl.BlockSpec(memory_space=pl.ANY)] * len(after),
         out_specs=[VMEM] * count,
         compiler_params=params(12),
-        name="last_near" if after else "last_far",
+        name="last_" + which,
     )(own, *arrivals, *after)
 
 
@@ -430,15 +432,14 @@
     kept_near = make("kept_near", xt=xt, dy=dyv, arrivals=p1b_near, after=p1b_near, pieces=whole, coded=False)
     kept_far = make("kept_far", xt=xt, dy=dyv, arrivals=p1b_far, after=p1b_far, pieces=whole, coded=False)
     one = [message(rows, cols, False)] * 2
-    two = [jax.ShapeDtypeStruct((2 * rows, cols), F32)] * 2
     q1_near = send(merge("q1_near", near_kernel, rows, 256, [*kept_near, *p2_near], one), False, True)
     q1_far = send(merge("q1_far", far_kernel, rows, 256, [*kept_near, *p2_near], one, p1b_far), False, True)
-    rest = merge("rest", add_kernel, rows, 256, [*kept_far, *p2_far], two)
-    q2 = send(merge("q2", near_kernel, rows, 256, [*rest, *q1_near], one), False, False)
-    own = merge("own", own_kernel, rows, 256, [*rest, *q1_far], two[:1])
-    far = last(rows, own[0], q2)
-    near1, near2, mine = last(rows, own[0], q2, far)
-    far = far[0]
+    q2 = send(merge("q2", q2_kernel, rows, 256, [*kept_far, *p2_far, *q1_near], one), False, False)
+    own = merge("own", own_kernel, rows, 256, [*kept_far, *p2_far, *q1_far], [jax.ShapeDtypeStruct((2 * rows, cols), F32)])
+    far = last("far", rows, own[0], q2)
+    near = last("near", rows, own[0], q2, far)
+    mine = last("mine", rows, own[0], q2, near)[0]
+    far, (near1, near2) = far[0], near
     far = lax.ppermute(far, "node", [(i, i ^ 4) for i in range(2 * SIDE)])
     near1 = exchange(near1, "y", True)
     near2 = exchange(near2, "y", False)

time: 125 us -> 122 us (0.976)
  waiting for transfers between devices: 26.3 us -> 24.9 us
  starting transfers between devices: 50.5 us -> 49.1 us
    ppermute x20, waiting for transfers between devices: 24.8 us -> 21.9 us  [exchange(): return lax.ppermute(array, ('node', 'fsdp'), pairing(axis, first))]
    ppermute x1, starting transfers between devices: 0.34 us -> 3 us  [local(): far = lax.ppermute(far, 'node', [(i, i ^ 4) for i in range(2 * SIDE)])]
    ppermute x20, starting transfers between devices: 38.2 us -> 35.9 us  [exchange(): return lax.ppermute(array, ('node', 'fsdp'), pairing(axis, first))]
    ppermute x1, starting transfers between devices: 12 us -> 10.2 us  [local(): carr = lax.ppermute(across, 'node', [(i, i ^ 1) for i in range(2 * SIDE)])]
    ppermute x1, waiting for transfers between devices: 0.01 us -> 1.42 us  [local(): far = lax.ppermute(far, 'node', [(i, i ^ 4) for i in range(2 * SIDE)])]
    pallas_call x5 -> x4, Pallas kernels: 5.39 us -> 5.44 us  [merge(): pl.pallas_call(functools.partial(kernel, rows, tile), out_shape=outs, in_...]
  transfers between devices with their start and end apart: 22 -> 22, of which waited for: 10 -> 11; matrix products, arithmetic and copies ran while one was open for 0% -> 0% of each run, Pallas kernels for 19% -> 20%
where the time goes in v5:
time: 122 us
  starting transfers between devices  49.1 us (40%)
  Pallas kernels  34.4 us (28%)
  waiting for transfers between devices  24.9 us (20%)
  blocking collectives  13.6 us (11%)
    ppermute x20, starting transfers between devices, exchange(): return lax.ppermute(array, ('node', 'fsdp'), pairing(axis, first))  35.9 us
    ppermute x20, waiting for transfers between devices, exchange(): return lax.ppermute(array, ('node', 'fsdp'), pairing(axis, first))  21.9 us
    pallas_call x7, Pallas kernels, product(): pl.pallas_call(functools.partial(product_kernel, which, rows, tile, coded...  17.7 us
    all_to_all x1, blocking collectives, local(): sums = lax.all_to_all(gram, ('node', 'fsdp'), 0, 0, tiled=True)  13.6 us
    ppermute x1, starting transfers between devices, local(): carr = lax.ppermute(across, 'node', [(i, i ^ 1) for i in range(2 * SIDE)])  10.2 us
    pallas_call x1, Pallas kernels, first(): pl.pallas_call(functools.partial(first_kernel, rows, tile), out_shape=[xt...  6.57 us
    pallas_call x4, Pallas kernels, merge(): pl.pallas_call(functools.partial(kernel, rows, tile), out_shape=outs, in_...  5.44 us
    ppermute x1, starting transfers between devices, local(): far = lax.ppermute(far, 'node', [(i, i ^ 4) for i in range(2 * SIDE)])  3 us
  transfers between devices with their start and end apart: 22, of which 11 were waited for; matrix products, arithmetic and copies ran while one was open for 0% of the time, Pallas kernels for 20%

profile of v5, /device:TPU:1, one launch (start us, length us, event | category | flops | bytes accessed | tf_op | source)
XLA Modules:
  0.0 122.2 jit_solution(13453776221851247508)
XLA Ops:
  0.0 6.6 %p1a_near.1 = (bf16[2560,1024]{1,0:T(8,128)(2,1)S(1)}, bf16[1024,2560]{1,0:T(8,128)(2,1)S(1)}, bf16[3232,128]{1,0:T(8,128)(2,1)S(1)}, bf16[3232,128]{1,0:T(8,128)(2,1)S(1)}) custom-call(bf16[1024,2560]{1,0:T(8,128)(2,1)} %x_ref.1, bf16[1024,2560]{1,0:T(8,128)(2,1)} %dy_ref.1), custom_call_target="tpu_custom_call" | custom-call | tf_op jit(solution)/shard_map/p1a_near/pallas_call | solution.py:244
  6.6 3.4 %collective-permute-start.8 = (bf16[3232,128]{1,0:T(8,128)(2,1)S(1)}, bf16[3232,128]{1,0:T(8,128)(2,1)S(1)}, u32[]{:S(2)}, u32[]{:S(2)}) collective-permute-start(bf16[3232,128]{1,0:T(8,128)(2,1)S(1)} %get-tuple-element.35.rest_0_), channel_id=1, source_target_pairs={{0,1},{1,0},{2,3},{3,2},{4,5},{5,4},{6,7},{7,6},{8,9},{9,8},{10,11... | collective-permute-start | bytes 2482184 | tf_op jit(solution)/shard_map/ppermute | solution.py:128
  10.0 3.8 %collective-permute-start.9 = (bf16[3232,128]{1,0:T(8,128)(2,1)S(1)}, bf16[3232,128]{1,0:T(8,128)(2,1)S(1)}, u32[]{:S(2)}, u32[]{:S(2)}) collective-permute-start(bf16[3232,128]{1,0:T(8,128)(2,1)S(1)} %get-tuple-element.36.rest_1_), channel_id=1, source_target_pairs={{0,4},{1,5},{2,6},{3,7},{4,0},{5,1},{6,2},{7,3},{8,12},{9,13},{10,... | collective-permute-start | bytes 2482184 | tf_op jit(solution)/shard_map/ppermute | solution.py:128
  13.7 2.3 %p1a_far.1 = (bf16[3232,128]{1,0:T(8,128)(2,1)S(1)}, bf16[3232,128]{1,0:T(8,128)(2,1)S(1)}) custom-call(bf16[2560,1024]{1,0:T(8,128)(2,1)S(1)} %get-tuple-element.33.xt_ref, bf16[1024,2560]{1,0:T(8,128)(2,1)S(1)} %get-tuple-element.34.dy_ref, bf16[3232,128]{1,0:T(8,128)(2,1)S(1)} %get-tuple-element.35.rest_0_, bf16[3232,128]{1,0:T(8,128)(2,1)S(1)} %get-tuple-element.36.rest_1_), custom_call_target="tpu_custom_call" | custom-call | tf_op jit(solution)/shard_map/p1a_far/pallas_call | solution.py:230
  16.0 0.3 collective-permute-start
  16.3 2.3 %p1b_near.1 = (bf16[3232,128]{1,0:T(8,128)(2,1)S(1)}, bf16[3232,128]{1,0:T(8,128)(2,1)S(1)}) custom-call(bf16[2560,1024]{1,0:T(8,128)(2,1)S(1)} %get-tuple-element.33.xt_ref, bf16[1024,2560]{1,0:T(8,128)(2,1)S(1)} %get-tuple-element.34.dy_ref, bf16[3232,128]{1,0:T(8,128)(2,1)S(1)} %get-tuple-element.37.rest_0_, bf16[3232,128]{1,0:T(8,128)(2,1)S(1)} %get-tuple-element.38.rest_1_), custom_call_target="tpu_custom_call" | custom-call | tf_op jit(solution)/shard_map/p1b_near/pallas_call | solution.py:230
  18.6 2.5 %collective-permute-start.6 = (bf16[3232,128]{1,0:T(8,128)(2,1)S(1)}, bf16[3232,128]{1,0:T(8,128)(2,1)S(1)}, u32[]{:S(2)}, u32[]{:S(2)}) collective-permute-start(bf16[3232,128]{1,0:T(8,128)(2,1)S(1)} %get-tuple-element.45), channel_id=1, source_target_pairs={{0,1},{1,0},{2,3},{3,2},{4,5},{5,4},{6,7},{7,6},{8,9},{9,8},{10,11... | collective-permute-start | bytes 2482184 | tf_op jit(solution)/shard_map/ppermute | solution.py:128
  21.2 2.7 %collective-permute-start.7 = (bf16[3232,128]{1,0:T(8,128)(2,1)S(1)}, bf16[3232,128]{1,0:T(8,128)(2,1)S(1)}, u32[]{:S(2)}, u32[]{:S(2)}) collective-permute-start(bf16[3232,128]{1,0:T(8,128)(2,1)S(1)} %get-tuple-element.46), channel_id=1, source_target_pairs={{0,4},{1,5},{2,6},{3,7},{4,0},{5,1},{6,2},{7,3},{8,12},{9,13},{10,... | collective-permute-start | bytes 2482184 | tf_op jit(solution)/shard_map/ppermute | solution.py:128
  23.8 3.2 %p2_near.1 = (bf16[3232,128]{1,0:T(8,128)(2,1)S(1)}, bf16[3232,128]{1,0:T(8,128)(2,1)S(1)}) custom-call(bf16[2560,1024]{1,0:T(8,128)(2,1)S(1)} %get-tuple-element.33.xt_ref, bf16[1024,2560]{1,0:T(8,128)(2,1)S(1)} %get-tuple-element.34.dy_ref, bf16[3232,128]{1,0:T(8,128)(2,1)S(1)} %collective-permute-done.8.rest_0_.rest_2_, ...), custom_call_target="tpu_custom_call" | custom-call | tf_op jit(solution)/shard_map/p2_near/pallas_call | solution.py:230
  27.1 0.4 collective-permute-start.10
  27.5 1.1 collective-permute-done.rest_0_
  28.6 1.8 %collective-permute-start.11 = (bf16[3232,128]{1,0:T(8,128)(2,1)S(1)}, bf16[3232,128]{1,0:T(8,128)(2,1)S(1)}, u32[]{:S(2)}, u32[]{:S(2)}) collective-permute-start(bf16[3232,128]{1,0:T(8,128)(2,1)S(1)} %get-tuple-element.50), channel_id=1, source_target_pairs={{0,12},{1,13},{2,14},{3,15},{4,8},{5,9},{6,10},{7,11},{8,4},{9,5},... | collective-permute-start | bytes 2482184 | tf_op jit(solution)/shard_map/ppermute | solution.py:128
  30.5 2.2 %collective-permute-done.1.rest_1_ = bf16[3232,128]{1,0:T(8,128)(2,1)S(1)} collective-permute-done((bf16[3232,128]{1,0:T(8,128)(2,1)S(1)}, bf16[3232,128]{1,0:T(8,128)(2,1)S(1)}, u32[]{:S(2)}, u32[]{:S(2)}) %collective-permute-start.1) | collective-permute-done | bytes 827424 | tf_op jit(solution)/shard_map/ppermute | solution.py:128
  32.7 2.3 %p1b_far.1 = (bf16[3232,128]{1,0:T(8,128)(2,1)S(1)}, bf16[3232,128]{1,0:T(8,128)(2,1)S(1)}) custom-call(bf16[2560,1024]{1,0:T(8,128)(2,1)S(1)} %get-tuple-element.33.xt_ref, bf16[1024,2560]{1,0:T(8,128)(2,1)S(1)} %get-tuple-element.34.dy_ref, bf16[3232,128]{1,0:T(8,128)(2,1)S(1)} %collective-permute-done.rest_0_, ...), custom_call_target="tpu_custom_call" | custom-call | tf_op jit(solution)/shard_map/p1b_far/pallas_call | solution.py:230
  35.0 0.4 collective-permute-start.2
  35.4 9.8 %collective-permute-done.6.rest_0_.rest_2_ = bf16[3232,128]{1,0:T(8,128)(2,1)S(1)} collective-permute-done((bf16[3232,128]{1,0:T(8,128)(2,1)S(1)}, bf16[3232,128]{1,0:T(8,128)(2,1)S(1)}, u32[]{:S(2)}, u32[]{:S(2)}) %collective-permute-start.6) | collective-permute-done | bytes 827424 | tf_op jit(solution)/shard_map/ppermute | solution.py:128
  45.2 4.6 %collective-permute-start.3 = (bf16[3232,128]{1,0:T(8,128)(2,1)S(1)}, bf16[3232,128]{1,0:T(8,128)(2,1)S(1)}, u32[]{:S(2)}, u32[]{:S(2)}) collective-permute-start(bf16[3232,128]{1,0:T(8,128)(2,1)S(1)} %get-tuple-element.40.rest_3_), channel_id=1, source_target_pairs={{0,4},{1,5},{2,6},{3,7},{4,0},{5,1},{6,2},{7,3},{8,12},{9,13},{10,... | collective-permute-start | bytes 2482184 | tf_op jit(solution)/shard_map/ppermute | solution.py:128
  49.7 3.2 %p2_far.1 = (bf16[3232,128]{1,0:T(8,128)(2,1)S(1)}, bf16[3232,128]{1,0:T(8,128)(2,1)S(1)}) custom-call(bf16[2560,1024]{1,0:T(8,128)(2,1)S(1)} %get-tuple-element.33.xt_ref, bf16[1024,2560]{1,0:T(8,128)(2,1)S(1)} %get-tuple-element.34.dy_ref, bf16[3232,128]{1,0:T(8,128)(2,1)S(1)} %collective-permute-done.rest_0_, ...), custom_call_target="tpu_custom_call" | custom-call | tf_op jit(solution)/shard_map/p2_far/pallas_call | solution.py:230
  53.0 0.9 collective-permute-start.4
  53.9 2.2 %kept_near.1 = (f32[160,2560]{1,0:T(8,128)S(1)}, f32[160,2560]{1,0:T(8,128)S(1)}) custom-call(bf16[2560,1024]{1,0:T(8,128)(2,1)S(1)} %get-tuple-element.33.xt_ref, bf16[1024,2560]{1,0:T(8,128)(2,1)S(1)} %get-tuple-element.34.dy_ref, bf16[3232,128]{1,0:T(8,128)(2,1)S(1)} %collective-permute-done.6.rest_0_.rest_2_, ...), custom_call_target="tpu_custom_call" | custom-call | tf_op jit(solution)/shard_map/kept_near/pallas_call | solution.py:230
  56.1 1.1 q1_near.1
  57.3 0.1 collective-permute-start.14
  57.4 2.5 %collective-permute-start.15 = (bf16[1632,128]{1,0:T(8,128)(2,1)S(1)}, bf16[1632,128]{1,0:T(8,128)(2,1)S(1)}, u32[]{:S(2)}, u32[]{:S(2)}) collective-permute-start(bf16[1632,128]{1,0:T(8,128)(2,1)S(1)} %get-tuple-element.54), channel_id=1, source_target_pairs={{0,1},{1,0},{2,3},{3,2},{4,5},{5,4},{6,7},{7,6},{8,9},{9,8},{10,11... | collective-permute-start | bytes 1253384 | tf_op jit(solution)/shard_map/ppermute | solution.py:128
  59.9 0.2 collective-permute-done.3.rest_1_.rest_3_
  60.1 1.1 q1_far.1
  61.2 3.4 %collective-permute-start.12 = (bf16[1632,128]{1,0:T(8,128)(2,1)S(1)}, bf16[1632,128]{1,0:T(8,128)(2,1)S(1)}, u32[]{:S(2)}, u32[]{:S(2)}) collective-permute-start(bf16[1632,128]{1,0:T(8,128)(2,1)S(1)} %get-tuple-element.51), channel_id=1, source_target_pairs={{0,4},{1,5},{2,6},{3,7},{4,0},{5,1},{6,2},{7,3},{8,12},{9,13},{10,... | collective-permute-start | bytes 1253384 | tf_op jit(solution)/shard_map/ppermute | solution.py:128
  64.6 2.2 %kept_far.1 = (f32[160,2560]{1,0:T(8,128)S(1)}, f32[160,2560]{1,0:T(8,128)S(1)}) custom-call(bf16[2560,1024]{1,0:T(8,128)(2,1)S(1)} %get-tuple-element.33.xt_ref, bf16[1024,2560]{1,0:T(8,128)(2,1)S(1)} %get-tuple-element.34.dy_ref, bf16[3232,128]{1,0:T(8,128)(2,1)S(1)} %collective-permute-done.2.rest_0_.rest_2_, ...), custom_call_target="tpu_custom_call" | custom-call | tf_op jit(solution)/shard_map/kept_far/pallas_call | solution.py:230
  66.8 6.2 %collective-permute-start.13 = (bf16[1632,128]{1,0:T(8,128)(2,1)S(1)}, bf16[1632,128]{1,0:T(8,128)(2,1)S(1)}, u32[]{:S(2)}, u32[]{:S(2)}) collective-permute-start(bf16[1632,128]{1,0:T(8,128)(2,1)S(1)} %get-tuple-element.52), channel_id=1, source_target_pairs={{0,1},{1,0},{2,3},{3,2},{4,5},{5,4},{6,7},{7,6},{8,9},{9,8},{10,11... | collective-permute-start | bytes 1253384 | tf_op jit(solution)/shard_map/ppermute | solution.py:128
  73.0 1.9 %q2.1 = (bf16[1632,128]{1,0:T(8,128)(2,1)S(1)}, bf16[1632,128]{1,0:T(8,128)(2,1)S(1)}) custom-call(f32[160,2560]{1,0:T(8,128)S(1)} %get-tuple-element.41.kept0, f32[160,2560]{1,0:T(8,128)S(1)} %get-tuple-element.42.kept1, bf16[3232,128]{1,0:T(8,128)(2,1)S(1)} %collective-permute-done.4.p0, bf16[3232,128]{1,0:T(8,128)(2,1)S(1)} %collective-permute-done.5.p1, ...), custom_call_target="tpu_custom_call" | custom-call | tf_op jit(solution)/shard_map/q2/pallas_call | solution.py:297
  74.9 1.4 %collective-permute-start.16 = (bf16[1632,128]{1,0:T(8,128)(2,1)S(1)}, bf16[1632,128]{1,0:T(8,128)(2,1)S(1)}, u32[]{:S(2)}, u32[]{:S(2)}) collective-permute-start(bf16[1632,128]{1,0:T(8,128)(2,1)S(1)} %get-tuple-element.55), channel_id=1, source_target_pairs={{0,12},{1,13},{2,14},{3,15},{4,8},{5,9},{6,10},{7,11},{8,4},{9,5},... | collective-permute-start | bytes 1253384 | tf_op jit(solution)/shard_map/ppermute | solution.py:128
  76.3 0.7 collective-permute-start.17
  77.0 0.4 collective-permute-done.12.q0
  77.4 1.0 collective-permute-done.13.q1
  78.4 1.3 %own.1 = f32[160,2560]{1,0:T(8,128)S(1)} custom-call(f32[160,2560]{1,0:T(8,128)S(1)} %get-tuple-element.41.kept0, f32[160,2560]{1,0:T(8,128)S(1)} %get-tuple-element.42.kept1, bf16[3232,128]{1,0:T(8,128)(2,1)S(1)} %collective-permute-done.4.p0, bf16[3232,128]{1,0:T(8,128)(2,1)S(1)} %collective-permute-done.5.p1, ...), custom_call_target="tpu_custom_call" | custom-call | tf_op jit(solution)/shard_map/own/pallas_call | solution.py:297
  79.7 2.1 %collective-permute-done.16.arr0 = bf16[1632,128]{1,0:T(8,128)(2,1)S(1)} collective-permute-done((bf16[1632,128]{1,0:T(8,128)(2,1)S(1)}, bf16[1632,128]{1,0:T(8,128)(2,1)S(1)}, u32[]{:S(2)}, u32[]{:S(2)}) %collective-permute-start.16) | collective-permute-done | bytes 417824 | tf_op jit(solution)/shard_map/ppermute | solution.py:128
  81.8 1.6 %collective-permute-done.17.arr1 = bf16[1632,128]{1,0:T(8,128)(2,1)S(1)} collective-permute-done((bf16[1632,128]{1,0:T(8,128)(2,1)S(1)}, bf16[1632,128]{1,0:T(8,128)(2,1)S(1)}, u32[]{:S(2)}, u32[]{:S(2)}) %collective-permute-start.17) | collective-permute-done | bytes 417824 | tf_op jit(solution)/shard_map/ppermute | solution.py:128
  83.5 0.3 last_far.1.rest_0_
  83.8 3.0 %collective-permute-start.20 = (bf16[168,640]{1,0:T(8,128)(2,1)S(1)}, bf16[168,640]{1,0:T(8,128)(2,1)S(1)}, u32[]{:S(2)}, u32[]{:S(2)}) collective-permute-start(bf16[168,640]{1,0:T(8,128)(2,1)S(1)} %last_far.1.rest_0_), channel_id=1, source_target_pairs={{0,64},{16,80},{32,96},{48,112},{64,0},{80,16},{96,32},{112,48},{1... | collective-permute-start | bytes 645128 | tf_op jit(solution)/shard_map/ppermute | solution.py:443
  86.8 0.7 last_near.1
  87.5 0.8 collective-permute-start.18
  88.3 0.3 last_mine.1.own0
  88.7 1.4 %collective-permute-done.20.own3 = bf16[168,640]{1,0:T(8,128)(2,1)S(1)} collective-permute-done((bf16[168,640]{1,0:T(8,128)(2,1)S(1)}, bf16[168,640]{1,0:T(8,128)(2,1)S(1)}, u32[]{:S(2)}, u32[]{:S(2)}) %collective-permute-start.20) | collective-permute-done | bytes 215072 | tf_op jit(solution)/shard_map/ppermute | solution.py:443
  90.1 3.4 %collective-permute-done.18.own1 = bf16[168,640]{1,0:T(8,128)(2,1)S(1)} collective-permute-done((bf16[168,640]{1,0:T(8,128)(2,1)S(1)}, bf16[168,640]{1,0:T(8,128)(2,1)S(1)}, u32[]{:S(2)}, u32[]{:S(2)}) %collective-permute-start.18) | collective-permute-done | bytes 215072 | tf_op jit(solution)/shard_map/ppermute | solution.py:128
  93.6 10.2 %collective-permute-start.21 = (bf16[4,168,384]{2,1,0:T(8,128)(2,1)S(1)}, bf16[4,168,384]{2,1,0:T(8,128)(2,1)S(1)}, u32[]{:S(2)}, u32[]{:S(2)}) collective-permute-start(bf16[4,168,384]{2,1,0:T(8,128)(2,1)S(1)} %pad_maximum_fusion), channel_id=1, source_target_pairs={{0,16},{16,0},{32,48},{48,32},{64,80},{80,64},{96,112},{112,96},{1... | collective-permute-start | bytes 1548296 | tf_op jit(solution)/shard_map/ppermute | solution.py:449
  103.8 1.5 %collective-permute-done.21.carr = bf16[4,168,384]{2,1,0:T(8,128)(2,1)S(1)} collective-permute-done((bf16[4,168,384]{2,1,0:T(8,128)(2,1)S(1)}, bf16[4,168,384]{2,1,0:T(8,128)(2,1)S(1)}, u32[]{:S(2)}, u32[]{:S(2)}) %collective-permute-start.21) | collective-permute-done | bytes 516128 | tf_op jit(solution)/shard_map/ppermute | solution.py:449
  105.3 1.7 %gram.1 = (f32[8,160,384]{2,1,0:T(8,128)S(1)}, f32[128,128]{1,0:T(8,128)S(1)}) custom-call(bf16[168,640]{1,0:T(8,128)(2,1)S(1)} %last_mine.1.own0, bf16[168,640]{1,0:T(8,128)(2,1)S(1)} %collective-permute-done.18.own1, bf16[168,640]{1,0:T(8,128)(2,1)S(1)} %collective-permute-done.19.own2, bf16[168,640]{1,0:T(8,128)(2,1)S(1)} %collective-permute-done.20.own3, ...), custom_call_target="tpu_custom_call" | custom-call | tf_op jit(solution)/shard_map/gram/pallas_call | solution.py:451
  107.0 13.6 %all_to_all.11 = f32[128,1,128]{2,1,0:T(1,128)S(1)} all-to-all(f32[128,1,128]{2,1,0:T(1,128)S(1)} %bitcast.13), channel_id=1, replica_groups=mesh['node'=8,'fsdp'=16] {'node','fsdp'}, dimensions={0} | all-to-all | bytes 131072 | tf_op jit(solution)/shard_map/all_to_all | solution.py:460
  120.6 1.6 %combine.1 = f32[160,320]{1,0:T(8,128)} custom-call(f32[8,160,384]{2,1,0:T(8,128)S(1)} %get-tuple-element.59.g_ref, f32[128,128]{1,0:T(8,128)S(1)} %bitcast.12), custom_call_target="tpu_custom_call" | custom-call | tf_op jit(solution)/shard_map/combine/pallas_call | solution.py:461
  (19 shorter events, 0.2 us)
Async XLA Ops:
  6.6 14.6 %collective-permute-start.8 = (bf16[3232,128]{1,0:T(8,128)(2,1)S(1)}, bf16[3232,128]{1,0:T(8,128)(2,1)S(1)}, u32[]{:S(2)}, u32[]{:S(2)}) collective-permute-start(bf16[3232,128]{1,0:T(8,128)(2,1)S(1)} %get-tuple-element.35.rest_0_), channel_id=1, source_target_pairs={{0,1},{1,0},{2,3},{3,2},{4,5},{5,4},{6,7},{7,6},{8,9},{9,8},{10,11... | collective-permute-start | bytes 2482184 | tf_op jit(solution)/shard_map/ppermute | solution.py:128
  10.0 13.9 %collective-permute-start.9 = (bf16[3232,128]{1,0:T(8,128)(2,1)S(1)}, bf16[3232,128]{1,0:T(8,128)(2,1)S(1)}, u32[]{:S(2)}, u32[]{:S(2)}) collective-permute-start(bf16[3232,128]{1,0:T(8,128)(2,1)S(1)} %get-tuple-element.36.rest_1_), channel_id=1, source_target_pairs={{0,4},{1,5},{2,6},{3,7},{4,0},{5,1},{6,2},{7,3},{8,12},{9,13},{10,... | collective-permute-start | bytes 2482184 | tf_op jit(solution)/shard_map/ppermute | solution.py:128
  16.0 12.6 %collective-permute-start = (bf16[3232,128]{1,0:T(8,128)(2,1)S(1)}, bf16[3232,128]{1,0:T(8,128)(2,1)S(1)}, u32[]{:S(2)}, u32[]{:S(2)}) collective-permute-start(bf16[3232,128]{1,0:T(8,128)(2,1)S(1)} %get-tuple-element.37.rest_0_), channel_id=1, source_target_pairs={{0,1},{1,0},{2,3},{3,2},{4,5},{5,4},{6,7},{7,6},{8,9},{9,8},{10,11... | collective-permute-start | bytes 2482184 | tf_op jit(solution)/shard_map/ppermute | solution.py:128
  16.3 16.4 %collective-permute-start.1 = (bf16[3232,128]{1,0:T(8,128)(2,1)S(1)}, bf16[3232,128]{1,0:T(8,128)(2,1)S(1)}, u32[]{:S(2)}, u32[]{:S(2)}) collective-permute-start(bf16[3232,128]{1,0:T(8,128)(2,1)S(1)} %get-tuple-element.38.rest_1_), channel_id=1, source_target_pairs={{0,4},{1,5},{2,6},{3,7},{4,0},{5,1},{6,2},{7,3},{8,12},{9,13},{10,... | collective-permute-start | bytes 2482184 | tf_op jit(solution)/shard_map/ppermute | solution.py:128
  18.6 26.5 %collective-permute-start.6 = (bf16[3232,128]{1,0:T(8,128)(2,1)S(1)}, bf16[3232,128]{1,0:T(8,128)(2,1)S(1)}, u32[]{:S(2)}, u32[]{:S(2)}) collective-permute-start(bf16[3232,128]{1,0:T(8,128)(2,1)S(1)} %get-tuple-element.45), channel_id=1, source_target_pairs={{0,1},{1,0},{2,3},{3,2},{4,5},{5,4},{6,7},{7,6},{8,9},{9,8},{10,11... | collective-permute-start | bytes 2482184 | tf_op jit(solution)/shard_map/ppermute | solution.py:128
  21.2 31.8 %collective-permute-start.7 = (bf16[3232,128]{1,0:T(8,128)(2,1)S(1)}, bf16[3232,128]{1,0:T(8,128)(2,1)S(1)}, u32[]{:S(2)}, u32[]{:S(2)}) collective-permute-start(bf16[3232,128]{1,0:T(8,128)(2,1)S(1)} %get-tuple-element.46), channel_id=1, source_target_pairs={{0,4},{1,5},{2,6},{3,7},{4,0},{5,1},{6,2},{7,3},{8,12},{9,13},{10,... | collective-permute-start | bytes 2482184 | tf_op jit(solution)/shard_map/ppermute | solution.py:128
  27.1 26.8 %collective-permute-start.10 = (bf16[3232,128]{1,0:T(8,128)(2,1)S(1)}, bf16[3232,128]{1,0:T(8,128)(2,1)S(1)}, u32[]{:S(2)}, u32[]{:S(2)}) collective-permute-start(bf16[3232,128]{1,0:T(8,128)(2,1)S(1)} %get-tuple-element.49), channel_id=1, source_target_pairs={{0,3},{1,2},{2,1},{3,0},{4,7},{5,6},{6,5},{7,4},{8,11},{9,10},{10,... | collective-permute-start | bytes 2482184 | tf_op jit(solution)/shard_map/ppermute | solution.py:128
  28.6 27.4 %collective-permute-start.11 = (bf16[3232,128]{1,0:T(8,128)(2,1)S(1)}, bf16[3232,128]{1,0:T(8,128)(2,1)S(1)}, u32[]{:S(2)}, u32[]{:S(2)}) collective-permute-start(bf16[3232,128]{1,0:T(8,128)(2,1)S(1)} %get-tuple-element.50), channel_id=1, source_target_pairs={{0,12},{1,13},{2,14},{3,15},{4,8},{5,9},{6,10},{7,11},{8,4},{9,5},... | collective-permute-start | bytes 2482184 | tf_op jit(solution)/shard_map/ppermute | solution.py:128
  35.0 22.4 %collective-permute-start.2 = (bf16[3232,128]{1,0:T(8,128)(2,1)S(1)}, bf16[3232,128]{1,0:T(8,128)(2,1)S(1)}, u32[]{:S(2)}, u32[]{:S(2)}) collective-permute-start(bf16[3232,128]{1,0:T(8,128)(2,1)S(1)} %get-tuple-element.39.rest_2_), channel_id=1, source_target_pairs={{0,1},{1,0},{2,3},{3,2},{4,5},{5,4},{6,7},{7,6},{8,9},{9,8},{10,11... | collective-permute-start | bytes 2482184 | tf_op jit(solution)/shard_map/ppermute | solution.py:128
  45.2 14.9 %collective-permute-start.3 = (bf16[3232,128]{1,0:T(8,128)(2,1)S(1)}, bf16[3232,128]{1,0:T(8,128)(2,1)S(1)}, u32[]{:S(2)}, u32[]{:S(2)}) collective-permute-start(bf16[3232,128]{1,0:T(8,128)(2,1)S(1)} %get-tuple-element.40.rest_3_), channel_id=1, source_target_pairs={{0,4},{1,5},{2,6},{3,7},{4,0},{5,1},{6,2},{7,3},{8,12},{9,13},{10,... | collective-permute-start | bytes 2482184 | tf_op jit(solution)/shard_map/ppermute | solution.py:128
  53.0 13.8 %collective-permute-start.4 = (bf16[3232,128]{1,0:T(8,128)(2,1)S(1)}, bf16[3232,128]{1,0:T(8,128)(2,1)S(1)}, u32[]{:S(2)}, u32[]{:S(2)}) collective-permute-start(bf16[3232,128]{1,0:T(8,128)(2,1)S(1)} %get-tuple-element.43), channel_id=1, source_target_pairs={{0,3},{1,2},{2,1},{3,0},{4,7},{5,6},{6,5},{7,4},{8,11},{9,10},{10,... | collective-permute-start | bytes 2482184 | tf_op jit(solution)/shard_map/ppermute | solution.py:128
  53.9 19.1 %collective-permute-start.5 = (bf16[3232,128]{1,0:T(8,128)(2,1)S(1)}, bf16[3232,128]{1,0:T(8,128)(2,1)S(1)}, u32[]{:S(2)}, u32[]{:S(2)}) collective-permute-start(bf16[3232,128]{1,0:T(8,128)(2,1)S(1)} %get-tuple-element.44), channel_id=1, source_target_pairs={{0,12},{1,13},{2,14},{3,15},{4,8},{5,9},{6,10},{7,11},{8,4},{9,5},... | collective-permute-start | bytes 2482184 | tf_op jit(solution)/shard_map/ppermute | solution.py:128
  57.3 15.7 %collective-permute-start.14 = (bf16[1632,128]{1,0:T(8,128)(2,1)S(1)}, bf16[1632,128]{1,0:T(8,128)(2,1)S(1)}, u32[]{:S(2)}, u32[]{:S(2)}) collective-permute-start(bf16[1632,128]{1,0:T(8,128)(2,1)S(1)} %get-tuple-element.53), channel_id=1, source_target_pairs={{0,4},{1,5},{2,6},{3,7},{4,0},{5,1},{6,2},{7,3},{8,12},{9,13},{10,... | collective-permute-start | bytes 1253384 | tf_op jit(solution)/shard_map/ppermute | solution.py:128
  57.4 15.6 %collective-permute-start.15 = (bf16[1632,128]{1,0:T(8,128)(2,1)S(1)}, bf16[1632,128]{1,0:T(8,128)(2,1)S(1)}, u32[]{:S(2)}, u32[]{:S(2)}) collective-permute-start(bf16[1632,128]{1,0:T(8,128)(2,1)S(1)} %get-tuple-element.54), channel_id=1, source_target_pairs={{0,1},{1,0},{2,3},{3,2},{4,5},{5,4},{6,7},{7,6},{8,9},{9,8},{10,11... | collective-permute-start | bytes 1253384 | tf_op jit(solution)/shard_map/ppermute | solution.py:128
  61.2 16.2 %collective-permute-start.12 = (bf16[1632,128]{1,0:T(8,128)(2,1)S(1)}, bf16[1632,128]{1,0:T(8,128)(2,1)S(1)}, u32[]{:S(2)}, u32[]{:S(2)}) collective-permute-start(bf16[1632,128]{1,0:T(8,128)(2,1)S(1)} %get-tuple-element.51), channel_id=1, source_target_pairs={{0,4},{1,5},{2,6},{3,7},{4,0},{5,1},{6,2},{7,3},{8,12},{9,13},{10,... | collective-permute-start | bytes 1253384 | tf_op jit(solution)/shard_map/ppermute | solution.py:128
  66.8 11.6 %collective-permute-start.13 = (bf16[1632,128]{1,0:T(8,128)(2,1)S(1)}, bf16[1632,128]{1,0:T(8,128)(2,1)S(1)}, u32[]{:S(2)}, u32[]{:S(2)}) collective-permute-start(bf16[1632,128]{1,0:T(8,128)(2,1)S(1)} %get-tuple-element.52), channel_id=1, source_target_pairs={{0,1},{1,0},{2,3},{3,2},{4,5},{5,4},{6,7},{7,6},{8,9},{9,8},{10,11... | collective-permute-start | bytes 1253384 | tf_op jit(solution)/shard_map/ppermute | solution.py:128
  74.9 7.0 %collective-permute-start.16 = (bf16[1632,128]{1,0:T(8,128)(2,1)S(1)}, bf16[1632,128]{1,0:T(8,128)(2,1)S(1)}, u32[]{:S(2)}, u32[]{:S(2)}) collective-permute-start(bf16[1632,128]{1,0:T(8,128)(2,1)S(1)} %get-tuple-element.55), channel_id=1, source_target_pairs={{0,12},{1,13},{2,14},{3,15},{4,8},{5,9},{6,10},{7,11},{8,4},{9,5},... | collective-permute-start | bytes 1253384 | tf_op jit(solution)/shard_map/ppermute | solution.py:128
  76.3 7.2 %collective-permute-start.17 = (bf16[1632,128]{1,0:T(8,128)(2,1)S(1)}, bf16[1632,128]{1,0:T(8,128)(2,1)S(1)}, u32[]{:S(2)}, u32[]{:S(2)}) collective-permute-start(bf16[1632,128]{1,0:T(8,128)(2,1)S(1)} %get-tuple-element.56), channel_id=1, source_target_pairs={{0,3},{1,2},{2,1},{3,0},{4,7},{5,6},{6,5},{7,4},{8,11},{9,10},{10,... | collective-permute-start | bytes 1253384 | tf_op jit(solution)/shard_map/ppermute | solution.py:128
  83.8 6.3 %collective-permute-start.20 = (bf16[168,640]{1,0:T(8,128)(2,1)S(1)}, bf16[168,640]{1,0:T(8,128)(2,1)S(1)}, u32[]{:S(2)}, u32[]{:S(2)}) collective-permute-start(bf16[168,640]{1,0:T(8,128)(2,1)S(1)} %last_far.1.rest_0_), channel_id=1, source_target_pairs={{0,64},{16,80},{32,96},{48,112},{64,0},{80,16},{96,32},{112,48},{1... | collective-permute-start | bytes 645128 | tf_op jit(solution)/shard_map/ppermute | solution.py:443
  87.5 6.0 %collective-permute-start.18 = (bf16[168,640]{1,0:T(8,128)(2,1)S(1)}, bf16[168,640]{1,0:T(8,128)(2,1)S(1)}, u32[]{:S(2)}, u32[]{:S(2)}) collective-permute-start(bf16[168,640]{1,0:T(8,128)(2,1)S(1)} %get-tuple-element.57.rest_0_), channel_id=1, source_target_pairs={{0,32},{1,33},{2,34},{3,35},{4,36},{5,37},{6,38},{7,39},{8,40},{9,... | collective-permute-start | bytes 645128 | tf_op jit(solution)/shard_map/ppermute | solution.py:128
  88.3 5.2 %collective-permute-start.19 = (bf16[168,640]{1,0:T(8,128)(2,1)S(1)}, bf16[168,640]{1,0:T(8,128)(2,1)S(1)}, u32[]{:S(2)}, u32[]{:S(2)}) collective-permute-start(bf16[168,640]{1,0:T(8,128)(2,1)S(1)} %get-tuple-element.58.rest_1_), channel_id=1, source_target_pairs={{0,96},{1,97},{2,98},{3,99},{4,100},{5,101},{6,102},{7,103},{8,104... | collective-permute-start | bytes 645128 | tf_op jit(solution)/shard_map/ppermute | solution.py:128
  93.6 11.7 %collective-permute-start.21 = (bf16[4,168,384]{2,1,0:T(8,128)(2,1)S(1)}, bf16[4,168,384]{2,1,0:T(8,128)(2,1)S(1)}, u32[]{:S(2)}, u32[]{:S(2)}) collective-permute-start(bf16[4,168,384]{2,1,0:T(8,128)(2,1)S(1)} %pad_maximum_fusion), channel_id=1, source_target_pairs={{0,16},{16,0},{32,48},{48,32},{64,80},{80,64},{96,112},{112,96},{1... | collective-permute-start | bytes 1548296 | tf_op jit(solution)/shard_map/ppermute | solution.py:449

commit v6 on v5

--- a/solution.py
+++ b/solution.py
@@ -278,11 +278,22 @@
         put.close()
 
 
-def q2_kernel(rows, tile, kept0, kept1, p0, p1, q0, q1, out0, out1):
-    for kept, p, q, out in ((kept0, p0, q0, out0), (kept1, p1, q1, out1)):
-        far, near, put = Reader(p, kept.shape[1], rows), Reader(q, kept.shape[1], rows), Writer(out)
-        for cols in parts_of(kept, tile):
-            put(kept[:rows, cols] + far(0, 1, cols) + near(0, 1, cols))
+def targets(early):
+    _, y, _, core = coordinates()
+    m1, m2 = masks(core)
+    return (y ^ 2, y ^ m1) if early else (y ^ m2, y)
+
+
+def q2_kernel(rows, early, kept0, kept1, p0, p1, q0, q1, *rest):
+    cols = kept0.shape[1]
+    tiles = cols // SIDE // LANES
+    for kept, p, q, out in ((kept0, p0, q0, rest[-2]), (kept1, p1, q1, rest[-1])):
+        far, near, put = Reader(p, cols, rows), Reader(q, cols, rows), Writer(out)
+        for target in targets(early):
+            for t in range(tiles):
+                tile = target * tiles + t
+                at = pl.ds(pl.multiple_of(tile * LANES, LANES), LANES)
+                put(kept[:rows, at] + far.dynamic(tile)[:rows] + near.dynamic(tile))
         put.close()
 
 
@@ -304,32 +315,34 @@
     )(*ins, *after)
 
 
-def last_kernel(rows, which, own, arr0, arr1, *rest):
-    _, y, _, core = coordinates()
-    m1, m2 = masks(core)
+def last_kernel(rows, early, pick, own, arr0, arr1, *rest):
     tiles = own.shape[1] // SIDE // LANES
-    targets = dict(far=(y ^ 2,), near=(y ^ m1, y ^ m2), mine=(y,))[which]
-    outs = rest[-len(targets) :]
-    readers = [Reader(a, own.shape[1], rows) for a in (arr0, arr1)]
-    for out, at in zip(outs, targets):
-        put = Writer(out)
-        for t in range(tiles):
-            tile = at * tiles + t
-            added = jnp.concatenate([read.dynamic(tile) for read in readers])
-            put(own[:, pl.ds(pl.multiple_of(tile * LANES, LANES), LANES)] + added)
-        put.close()
-
-
-def last(which, rows, own, arrivals, after=()):
-    count = 2 if which == "near" else 1
+    readers = [Reader(a, own.shape[1] // 2, rows) for a in (arr0, arr1)]
+    put = Writer(rest[-1])
+    for t in range(tiles):
+        at = (pick * tiles + t) * LANES
+        added = jnp.concatenate([read(0, 1, slice(at, at + LANES)) for read in readers])
+        tile = targets(early)[pick] * tiles + t
+        put(own[:, pl.ds(pl.multiple_of(tile * LANES, LANES), LANES)] + added)
+    put.close()
+
+
+def last(name, rows, early, pick, own, arrivals, after=()):
     return pl.pallas_call(
-        functools.partial(last_kernel, rows, which),
-        out_shape=[message(2 * rows, own.shape[1] // SIDE, True)] * count,
+        functools.partial(last_kernel, rows, early, pick),
+        out_shape=[message(2 * rows, own.shape[1] // SIDE, True)],
         in_specs=[VMEM] * 3 + [pl.BlockSpec(memory_space=pl.ANY)] * len(after),
-        out_specs=[VMEM] * count,
+        out_specs=[VMEM],
         compiler_params=params(12),
-        name="last_" + which,
+        name=name,
     )(own, *arrivals, *after)
+
+
+def cut_kernel(ref, *rest):
+    out = rest[-1]
+    wide = out.shape[1]
+    at = pl.ds(pl.multiple_of((ref.shape[1] - wide) * (1 - coordinates()[3]), LANES), wide)
+    out[...] = ref[:, at]
 
 
 def gram_kernel(rows, half, own0, own1, own2, own3, carr, g_ref, gram_ref):
@@ -434,18 +447,34 @@
     one = [message(rows, cols, False)] * 2
     q1_near = send(merge("q1_near", near_kernel, rows, 256, [*kept_near, *p2_near], one), False, True)
     q1_far = send(merge("q1_far", far_kernel, rows, 256, [*kept_near, *p2_near], one, p1b_far), False, True)
-    q2 = send(merge("q2", q2_kernel, rows, 256, [*kept_far, *p2_far, *q1_near], one), False, False)
-    own = merge("own", own_kernel, rows, 256, [*kept_far, *p2_far, *q1_far], [jax.ShapeDtypeStruct((2 * rows, cols), F32)])
-    far = last("far", rows, own[0], q2)
-    near = last("near", rows, own[0], q2, far)
-    mine = last("mine", rows, own[0], q2, near)[0]
-    far, (near1, near2) = far[0], near
+    half_of = [message(rows, cols // 2)] * 2
+    m9 = merge("q2_early", q2_kernel, rows, True, [*kept_far, *p2_far, *q1_near], half_of)
+    q2_early = send(m9, False, False)
+    q2_late = send(merge("q2_late", q2_kernel, rows, False, [*kept_far, *p2_far, *q1_near], half_of, m9), False, False)
+    own = merge("own", own_kernel, rows, 256, [*kept_far, *p2_far, *q1_far], [jax.ShapeDtypeStruct((2 * rows, cols), F32)])[0]
+    far = last("last_far", rows, True, 0, own, q2_early)
+    near1 = last("last_near1", rows, True, 1, own, q2_early, far)
+    near2 = last("last_near2", rows, False, 0, own, q2_late, near1)
+    mine = last("last_mine", rows, False, 1, own, q2_late, near2)[0]
+    far, near1, near2 = far[0], near1[0], near2[0]
     far = lax.ppermute(far, "node", [(i, i ^ 4) for i in range(2 * SIDE)])
     near1 = exchange(near1, "y", True)
     near2 = exchange(near2, "y", False)
     blocks = [mine, near1, near2, far]
-    start = (cols // SIDE - wide) * (1 - core)
-    across = jnp.stack([lax.dynamic_slice_in_dim(b, start, wide, axis=1) for b in blocks])
+    cuts, before = [], []
+    for name, k in (("far", 3), ("near1", 1), ("near2", 2), ("mine", 0)):
+        cut = pl.pallas_call(
+            cut_kernel,
+            out_shape=jax.ShapeDtypeStruct((blocks[0].shape[0], wide), BF16),
+            in_specs=[VMEM] + [pl.BlockSpec(memory_space=pl.ANY)] * len(before),
+            out_specs=VMEM,
+            compiler_params=params(12),
+            name="cut_" + name,
+        )(blocks[k], *before)
+        before = [cut] if name != "near2" else before
+        cuts.append(cut)
+    far_cut, near1_cut, near2_cut, mine_cut = cuts
+    across = jnp.stack([mine_cut, near1_cut, near2_cut, far_cut])
     carr = lax.ppermute(across, "node", [(i, i ^ 1) for i in range(2 * SIDE)])
     count = 2 * SIDE * SIDE * SIDE
     g, gram = pl.pallas_call(

time: 122 us -> 121 us (level)
  waiting for transfers between devices: 24.9 us -> 20.4 us
  blocking collectives: 13.6 us -> 15.7 us
    ppermute x20 -> x22, waiting for transfers between devices: 21.9 us -> 17.5 us  [exchange(): return lax.ppermute(array, ('node', 'fsdp'), pairing(axis, first))]
    all_to_all x1, blocking collectives: 13.6 us -> 15.7 us  [local(): sums = lax.all_to_all(gram, ('node', 'fsdp'), 0, 0, tiled=True)]
    ppermute x20 -> x22, starting transfers between devices: 35.9 us -> 36.7 us  [exchange(): return lax.ppermute(array, ('node', 'fsdp'), pairing(axis, first))]
    pallas_call x4 -> x5, Pallas kernels: 5.44 us -> 5.7 us  [merge(): pl.pallas_call(functools.partial(kernel, rows, tile), out_shape=outs, in_...]
  transfers between devices with their start and end apart: 22 -> 24, of which waited for: 11 -> 9; matrix products, arithmetic and copies ran while one was open for 0% -> 0% of each run, Pallas kernels for 20% -> 20%
where the time goes in v6:
time: 121 us
  starting transfers between devices  50.3 us (42%)
  Pallas kernels  34.6 us (29%)
  waiting for transfers between devices  20.4 us (17%)
  blocking collectives  15.7 us (13%)
    ppermute x22, starting transfers between devices, exchange(): return lax.ppermute(array, ('node', 'fsdp'), pairing(axis, first))  36.7 us
    pallas_call x7, Pallas kernels, product(): pl.pallas_call(functools.partial(product_kernel, which, rows, tile, coded...  17.7 us
    ppermute x22, waiting for transfers between devices, exchange(): return lax.ppermute(array, ('node', 'fsdp'), pairing(axis, first))  17.5 us
    all_to_all x1, blocking collectives, local(): sums = lax.all_to_all(gram, ('node', 'fsdp'), 0, 0, tiled=True)  15.7 us
    ppermute x1, starting transfers between devices, local(): carr = lax.ppermute(across, 'node', [(i, i ^ 1) for i in range(2 * SIDE)])  10.6 us
    pallas_call x1, Pallas kernels, first(): pl.pallas_call(functools.partial(first_kernel, rows, tile), out_shape=[xt...  6.57 us
    pallas_call x5, Pallas kernels, merge(): pl.pallas_call(functools.partial(kernel, rows, tile), out_shape=outs, in_...  5.7 us
    ppermute x1, starting transfers between devices, local(): far = lax.ppermute(far, 'node', [(i, i ^ 4) for i in range(2 * SIDE)])  2.98 us
  transfers between devices with their start and end apart: 24, of which 9 were waited for; matrix products, arithmetic and copies ran while one was open for 0% of the time, Pallas kernels for 20%

profile of v6, /device:TPU:1, one launch (start us, length us, event | category | flops | bytes accessed | tf_op | source)
XLA Modules:
  0.0 121.3 jit_solution(2768314155149092939)
XLA Ops:
  0.0 6.6 %p1a_near.1 = (bf16[2560,1024]{1,0:T(8,128)(2,1)S(1)}, bf16[1024,2560]{1,0:T(8,128)(2,1)S(1)}, bf16[3232,128]{1,0:T(8,128)(2,1)S(1)}, bf16[3232,128]{1,0:T(8,128)(2,1)S(1)}) custom-call(bf16[1024,2560]{1,0:T(8,128)(2,1)} %x_ref.1, bf16[1024,2560]{1,0:T(8,128)(2,1)} %dy_ref.1), custom_call_target="tpu_custom_call" | custom-call | tf_op jit(solution)/shard_map/p1a_near/pallas_call | solution.py:244
  6.6 3.4 %collective-permute-start.8 = (bf16[3232,128]{1,0:T(8,128)(2,1)S(1)}, bf16[3232,128]{1,0:T(8,128)(2,1)S(1)}, u32[]{:S(2)}, u32[]{:S(2)}) collective-permute-start(bf16[3232,128]{1,0:T(8,128)(2,1)S(1)} %get-tuple-element.35.rest_0_), channel_id=1, source_target_pairs={{0,1},{1,0},{2,3},{3,2},{4,5},{5,4},{6,7},{7,6},{8,9},{9,8},{10,11... | collective-permute-start | bytes 2482184 | tf_op jit(solution)/shard_map/ppermute | solution.py:128
  10.0 3.8 %collective-permute-start.9 = (bf16[3232,128]{1,0:T(8,128)(2,1)S(1)}, bf16[3232,128]{1,0:T(8,128)(2,1)S(1)}, u32[]{:S(2)}, u32[]{:S(2)}) collective-permute-start(bf16[3232,128]{1,0:T(8,128)(2,1)S(1)} %get-tuple-element.36.rest_1_), channel_id=1, source_target_pairs={{0,4},{1,5},{2,6},{3,7},{4,0},{5,1},{6,2},{7,3},{8,12},{9,13},{10,... | collective-permute-start | bytes 2482184 | tf_op jit(solution)/shard_map/ppermute | solution.py:128
  13.7 2.3 %p1a_far.1 = (bf16[3232,128]{1,0:T(8,128)(2,1)S(1)}, bf16[3232,128]{1,0:T(8,128)(2,1)S(1)}) custom-call(bf16[2560,1024]{1,0:T(8,128)(2,1)S(1)} %get-tuple-element.33.xt_ref, bf16[1024,2560]{1,0:T(8,128)(2,1)S(1)} %get-tuple-element.34.dy_ref, bf16[3232,128]{1,0:T(8,128)(2,1)S(1)} %get-tuple-element.35.rest_0_, bf16[3232,128]{1,0:T(8,128)(2,1)S(1)} %get-tuple-element.36.rest_1_), custom_call_target="tpu_custom_call" | custom-call | tf_op jit(solution)/shard_map/p1a_far/pallas_call | solution.py:230
  16.0 0.3 collective-permute-start
  16.3 2.3 %p1b_near.1 = (bf16[3232,128]{1,0:T(8,128)(2,1)S(1)}, bf16[3232,128]{1,0:T(8,128)(2,1)S(1)}) custom-call(bf16[2560,1024]{1,0:T(8,128)(2,1)S(1)} %get-tuple-element.33.xt_ref, bf16[1024,2560]{1,0:T(8,128)(2,1)S(1)} %get-tuple-element.34.dy_ref, bf16[3232,128]{1,0:T(8,128)(2,1)S(1)} %get-tuple-element.37.rest_0_, bf16[3232,128]{1,0:T(8,128)(2,1)S(1)} %get-tuple-element.38.rest_1_), custom_call_target="tpu_custom_call" | custom-call | tf_op jit(solution)/shard_map/p1b_near/pallas_call | solution.py:230
  18.6 2.5 %collective-permute-start.6 = (bf16[3232,128]{1,0:T(8,128)(2,1)S(1)}, bf16[3232,128]{1,0:T(8,128)(2,1)S(1)}, u32[]{:S(2)}, u32[]{:S(2)}) collective-permute-start(bf16[3232,128]{1,0:T(8,128)(2,1)S(1)} %get-tuple-element.45), channel_id=1, source_target_pairs={{0,1},{1,0},{2,3},{3,2},{4,5},{5,4},{6,7},{7,6},{8,9},{9,8},{10,11... | collective-permute-start | bytes 2482184 | tf_op jit(solution)/shard_map/ppermute | solution.py:128
  21.2 2.7 %collective-permute-start.7 = (bf16[3232,128]{1,0:T(8,128)(2,1)S(1)}, bf16[3232,128]{1,0:T(8,128)(2,1)S(1)}, u32[]{:S(2)}, u32[]{:S(2)}) collective-permute-start(bf16[3232,128]{1,0:T(8,128)(2,1)S(1)} %get-tuple-element.46), channel_id=1, source_target_pairs={{0,4},{1,5},{2,6},{3,7},{4,0},{5,1},{6,2},{7,3},{8,12},{9,13},{10,... | collective-permute-start | bytes 2482184 | tf_op jit(solution)/shard_map/ppermute | solution.py:128
  23.8 3.2 %p2_near.1 = (bf16[3232,128]{1,0:T(8,128)(2,1)S(1)}, bf16[3232,128]{1,0:T(8,128)(2,1)S(1)}) custom-call(bf16[2560,1024]{1,0:T(8,128)(2,1)S(1)} %get-tuple-element.33.xt_ref, bf16[1024,2560]{1,0:T(8,128)(2,1)S(1)} %get-tuple-element.34.dy_ref, bf16[3232,128]{1,0:T(8,128)(2,1)S(1)} %collective-permute-done.8.rest_0_.rest_2_, ...), custom_call_target="tpu_custom_call" | custom-call | tf_op jit(solution)/shard_map/p2_near/pallas_call | solution.py:230
  27.1 0.5 collective-permute-start.10
  27.5 1.1 collective-permute-done.rest_0_
  28.6 1.8 %collective-permute-start.11 = (bf16[3232,128]{1,0:T(8,128)(2,1)S(1)}, bf16[3232,128]{1,0:T(8,128)(2,1)S(1)}, u32[]{:S(2)}, u32[]{:S(2)}) collective-permute-start(bf16[3232,128]{1,0:T(8,128)(2,1)S(1)} %get-tuple-element.50), channel_id=1, source_target_pairs={{0,12},{1,13},{2,14},{3,15},{4,8},{5,9},{6,10},{7,11},{8,4},{9,5},... | collective-permute-start | bytes 2482184 | tf_op jit(solution)/shard_map/ppermute | solution.py:128
  30.5 2.2 %collective-permute-done.1.rest_1_ = bf16[3232,128]{1,0:T(8,128)(2,1)S(1)} collective-permute-done((bf16[3232,128]{1,0:T(8,128)(2,1)S(1)}, bf16[3232,128]{1,0:T(8,128)(2,1)S(1)}, u32[]{:S(2)}, u32[]{:S(2)}) %collective-permute-start.1) | collective-permute-done | bytes 827424 | tf_op jit(solution)/shard_map/ppermute | solution.py:128
  32.7 2.3 %p1b_far.1 = (bf16[3232,128]{1,0:T(8,128)(2,1)S(1)}, bf16[3232,128]{1,0:T(8,128)(2,1)S(1)}) custom-call(bf16[2560,1024]{1,0:T(8,128)(2,1)S(1)} %get-tuple-element.33.xt_ref, bf16[1024,2560]{1,0:T(8,128)(2,1)S(1)} %get-tuple-element.34.dy_ref, bf16[3232,128]{1,0:T(8,128)(2,1)S(1)} %collective-permute-done.rest_0_, ...), custom_call_target="tpu_custom_call" | custom-call | tf_op jit(solution)/shard_map/p1b_far/pallas_call | solution.py:230
  35.0 0.4 collective-permute-start.2
  35.4 9.8 %collective-permute-done.6.rest_0_.rest_2_ = bf16[3232,128]{1,0:T(8,128)(2,1)S(1)} collective-permute-done((bf16[3232,128]{1,0:T(8,128)(2,1)S(1)}, bf16[3232,128]{1,0:T(8,128)(2,1)S(1)}, u32[]{:S(2)}, u32[]{:S(2)}) %collective-permute-start.6) | collective-permute-done | bytes 827424 | tf_op jit(solution)/shard_map/ppermute | solution.py:128
  45.2 4.6 %collective-permute-start.3 = (bf16[3232,128]{1,0:T(8,128)(2,1)S(1)}, bf16[3232,128]{1,0:T(8,128)(2,1)S(1)}, u32[]{:S(2)}, u32[]{:S(2)}) collective-permute-start(bf16[3232,128]{1,0:T(8,128)(2,1)S(1)} %get-tuple-element.40.rest_3_), channel_id=1, source_target_pairs={{0,4},{1,5},{2,6},{3,7},{4,0},{5,1},{6,2},{7,3},{8,12},{9,13},{10,... | collective-permute-start | bytes 2482184 | tf_op jit(solution)/shard_map/ppermute | solution.py:128
  49.7 3.2 %p2_far.1 = (bf16[3232,128]{1,0:T(8,128)(2,1)S(1)}, bf16[3232,128]{1,0:T(8,128)(2,1)S(1)}) custom-call(bf16[2560,1024]{1,0:T(8,128)(2,1)S(1)} %get-tuple-element.33.xt_ref, bf16[1024,2560]{1,0:T(8,128)(2,1)S(1)} %get-tuple-element.34.dy_ref, bf16[3232,128]{1,0:T(8,128)(2,1)S(1)} %collective-permute-done.rest_0_, ...), custom_call_target="tpu_custom_call" | custom-call | tf_op jit(solution)/shard_map/p2_far/pallas_call | solution.py:230
  53.0 0.9 collective-permute-start.4
  53.9 2.2 %kept_near.1 = (f32[160,2560]{1,0:T(8,128)S(1)}, f32[160,2560]{1,0:T(8,128)S(1)}) custom-call(bf16[2560,1024]{1,0:T(8,128)(2,1)S(1)} %get-tuple-element.33.xt_ref, bf16[1024,2560]{1,0:T(8,128)(2,1)S(1)} %get-tuple-element.34.dy_ref, bf16[3232,128]{1,0:T(8,128)(2,1)S(1)} %collective-permute-done.6.rest_0_.rest_2_, ...), custom_call_target="tpu_custom_call" | custom-call | tf_op jit(solution)/shard_map/kept_near/pallas_call | solution.py:230
  56.1 1.2 q1_near.1
  57.4 2.5 %collective-permute-start.15 = (bf16[1632,128]{1,0:T(8,128)(2,1)S(1)}, bf16[1632,128]{1,0:T(8,128)(2,1)S(1)}, u32[]{:S(2)}, u32[]{:S(2)}) collective-permute-start(bf16[1632,128]{1,0:T(8,128)(2,1)S(1)} %get-tuple-element.54), channel_id=1, source_target_pairs={{0,1},{1,0},{2,3},{3,2},{4,5},{5,4},{6,7},{7,6},{8,9},{9,8},{10,11... | collective-permute-start | bytes 1253384 | tf_op jit(solution)/shard_map/ppermute | solution.py:128
  60.0 1.2 q1_far.1
  61.2 3.2 %collective-permute-start.12 = (bf16[1632,128]{1,0:T(8,128)(2,1)S(1)}, bf16[1632,128]{1,0:T(8,128)(2,1)S(1)}, u32[]{:S(2)}, u32[]{:S(2)}) collective-permute-start(bf16[1632,128]{1,0:T(8,128)(2,1)S(1)} %get-tuple-element.51), channel_id=1, source_target_pairs={{0,4},{1,5},{2,6},{3,7},{4,0},{5,1},{6,2},{7,3},{8,12},{9,13},{10,... | collective-permute-start | bytes 1253384 | tf_op jit(solution)/shard_map/ppermute | solution.py:128
  64.4 0.3 collective-permute-done.4.p0
  64.6 5.8 %collective-permute-start.13 = (bf16[1632,128]{1,0:T(8,128)(2,1)S(1)}, bf16[1632,128]{1,0:T(8,128)(2,1)S(1)}, u32[]{:S(2)}, u32[]{:S(2)}) collective-permute-start(bf16[1632,128]{1,0:T(8,128)(2,1)S(1)} %get-tuple-element.52), channel_id=1, source_target_pairs={{0,1},{1,0},{2,3},{3,2},{4,5},{5,4},{6,7},{7,6},{8,9},{9,8},{10,11... | collective-permute-start | bytes 1253384 | tf_op jit(solution)/shard_map/ppermute | solution.py:128
  70.5 2.2 %kept_far.1 = (f32[160,2560]{1,0:T(8,128)S(1)}, f32[160,2560]{1,0:T(8,128)S(1)}) custom-call(bf16[2560,1024]{1,0:T(8,128)(2,1)S(1)} %get-tuple-element.33.xt_ref, bf16[1024,2560]{1,0:T(8,128)(2,1)S(1)} %get-tuple-element.34.dy_ref, bf16[3232,128]{1,0:T(8,128)(2,1)S(1)} %collective-permute-done.2.rest_0_.rest_2_, ...), custom_call_target="tpu_custom_call" | custom-call | tf_op jit(solution)/shard_map/kept_far/pallas_call | solution.py:230
  72.7 1.1 q2_early.1
  73.7 1.7 %collective-permute-start.18 = (bf16[816,128]{1,0:T(8,128)(2,1)S(1)}, bf16[816,128]{1,0:T(8,128)(2,1)S(1)}, u32[]{:S(2)}, u32[]{:S(2)}) collective-permute-start(bf16[816,128]{1,0:T(8,128)(2,1)S(1)} %get-tuple-element.55.rest_0_), channel_id=1, source_target_pairs={{0,12},{1,13},{2,14},{3,15},{4,8},{5,9},{6,10},{7,11},{8,4},{9,5},... | collective-permute-start | bytes 626696 | tf_op jit(solution)/shard_map/ppermute | solution.py:128
  75.5 0.7 collective-permute-start.19
  76.2 1.0 q2_late.1
  77.2 0.7 collective-permute-start.16
  77.9 0.3 collective-permute-start.17
  78.2 1.3 %own.1 = f32[160,2560]{1,0:T(8,128)S(1)} custom-call(f32[160,2560]{1,0:T(8,128)S(1)} %get-tuple-element.41.kept0, f32[160,2560]{1,0:T(8,128)S(1)} %get-tuple-element.42.kept1, bf16[3232,128]{1,0:T(8,128)(2,1)S(1)} %collective-permute-done.4.p0, bf16[3232,128]{1,0:T(8,128)(2,1)S(1)} %collective-permute-done.5.p1, ...), custom_call_target="tpu_custom_call" | custom-call | tf_op jit(solution)/shard_map/own/pallas_call | solution.py:308
  79.5 0.6 collective-permute-done.19.arr1
  80.1 0.3 last_far.1.rest_0_
  80.4 3.0 %collective-permute-start.22 = (bf16[168,640]{1,0:T(8,128)(2,1)S(1)}, bf16[168,640]{1,0:T(8,128)(2,1)S(1)}, u32[]{:S(2)}, u32[]{:S(2)}) collective-permute-start(bf16[168,640]{1,0:T(8,128)(2,1)S(1)} %last_far.1.rest_0_), channel_id=1, source_target_pairs={{0,64},{16,80},{32,96},{48,112},{64,0},{80,16},{96,32},{112,48},{1... | collective-permute-start | bytes 645128 | tf_op jit(solution)/shard_map/ppermute | solution.py:460
  83.4 0.3 last_near1.1.rest_0_
  83.7 0.9 collective-permute-start.20
  84.6 0.3 last_near2.1.rest_0_
  85.0 0.3 last_mine.1.ref.own0
  85.3 1.4 %collective-permute-done.22.ref.own3 = bf16[168,640]{1,0:T(8,128)(2,1)S(1)} collective-permute-done((bf16[168,640]{1,0:T(8,128)(2,1)S(1)}, bf16[168,640]{1,0:T(8,128)(2,1)S(1)}, u32[]{:S(2)}, u32[]{:S(2)}) %collective-permute-start.22) | collective-permute-done | bytes 215072 | tf_op jit(solution)/shard_map/ppermute | solution.py:460
  86.7 3.3 %collective-permute-done.20.ref.own1 = bf16[168,640]{1,0:T(8,128)(2,1)S(1)} collective-permute-done((bf16[168,640]{1,0:T(8,128)(2,1)S(1)}, bf16[168,640]{1,0:T(8,128)(2,1)S(1)}, u32[]{:S(2)}, u32[]{:S(2)}) %collective-permute-start.20) | collective-permute-done | bytes 215072 | tf_op jit(solution)/shard_map/ppermute | solution.py:128
  90.2 10.6 %collective-permute-start.23 = (bf16[4,168,384]{2,1,0:T(8,128)(2,1)S(1)}, bf16[4,168,384]{2,1,0:T(8,128)(2,1)S(1)}, u32[]{:S(2)}, u32[]{:S(2)}) collective-permute-start(bf16[4,168,384]{2,1,0:T(8,128)(2,1)S(1)} %pad_maximum_fusion), channel_id=1, source_target_pairs={{0,16},{16,0},{32,48},{48,32},{64,80},{80,64},{96,112},{112,96},{1... | collective-permute-start | bytes 1548296 | tf_op jit(solution)/shard_map/ppermute | solution.py:478
  100.7 1.5 %collective-permute-done.23.carr = bf16[4,168,384]{2,1,0:T(8,128)(2,1)S(1)} collective-permute-done((bf16[4,168,384]{2,1,0:T(8,128)(2,1)S(1)}, bf16[4,168,384]{2,1,0:T(8,128)(2,1)S(1)}, u32[]{:S(2)}, u32[]{:S(2)}) %collective-permute-start.23) | collective-permute-done | bytes 516128 | tf_op jit(solution)/shard_map/ppermute | solution.py:478
  102.3 1.7 %gram.1 = (f32[8,160,384]{2,1,0:T(8,128)S(1)}, f32[128,128]{1,0:T(8,128)S(1)}) custom-call(bf16[168,640]{1,0:T(8,128)(2,1)S(1)} %last_mine.1.ref.own0, bf16[168,640]{1,0:T(8,128)(2,1)S(1)} %collective-permute-done.20.ref.own1, bf16[168,640]{1,0:T(8,128)(2,1)S(1)} %collective-permute-done.21.ref.own2, bf16[168,640]{1,0:T(8,128)(2,1)S(1)} %collective-permute-done.22.ref.own3, ...), custom_call_target="tpu_custom_call" | custom-call | tf_op jit(solution)/shard_map/gram/pallas_call | solution.py:480
  104.0 15.7 %all_to_all.11 = f32[128,1,128]{2,1,0:T(1,128)S(1)} all-to-all(f32[128,1,128]{2,1,0:T(1,128)S(1)} %bitcast.13), channel_id=1, replica_groups=mesh['node'=8,'fsdp'=16] {'node','fsdp'}, dimensions={0} | all-to-all | bytes 131072 | tf_op jit(solution)/shard_map/all_to_all | solution.py:489
  119.6 1.6 %combine.1 = f32[160,320]{1,0:T(8,128)} custom-call(f32[8,160,384]{2,1,0:T(8,128)S(1)} %get-tuple-element.59.g_ref, f32[128,128]{1,0:T(8,128)S(1)} %bitcast.12), custom_call_target="tpu_custom_call" | custom-call | tf_op jit(solution)/shard_map/combine/pallas_call | solution.py:490
  (25 shorter events, 0.6 us)
Async XLA Ops:
  6.6 14.6 %collective-permute-start.8 = (bf16[3232,128]{1,0:T(8,128)(2,1)S(1)}, bf16[3232,128]{1,0:T(8,128)(2,1)S(1)}, u32[]{:S(2)}, u32[]{:S(2)}) collective-permute-start(bf16[3232,128]{1,0:T(8,128)(2,1)S(1)} %get-tuple-element.35.rest_0_), channel_id=1, source_target_pairs={{0,1},{1,0},{2,3},{3,2},{4,5},{5,4},{6,7},{7,6},{8,9},{9,8},{10,11... | collective-permute-start | bytes 2482184 | tf_op jit(solution)/shard_map/ppermute | solution.py:128
  10.0 13.9 %collective-permute-start.9 = (bf16[3232,128]{1,0:T(8,128)(2,1)S(1)}, bf16[3232,128]{1,0:T(8,128)(2,1)S(1)}, u32[]{:S(2)}, u32[]{:S(2)}) collective-permute-start(bf16[3232,128]{1,0:T(8,128)(2,1)S(1)} %get-tuple-element.36.rest_1_), channel_id=1, source_target_pairs={{0,4},{1,5},{2,6},{3,7},{4,0},{5,1},{6,2},{7,3},{8,12},{9,13},{10,... | collective-permute-start | bytes 2482184 | tf_op jit(solution)/shard_map/ppermute | solution.py:128
  16.0 12.6 %collective-permute-start = (bf16[3232,128]{1,0:T(8,128)(2,1)S(1)}, bf16[3232,128]{1,0:T(8,128)(2,1)S(1)}, u32[]{:S(2)}, u32[]{:S(2)}) collective-permute-start(bf16[3232,128]{1,0:T(8,128)(2,1)S(1)} %get-tuple-element.37.rest_0_), channel_id=1, source_target_pairs={{0,1},{1,0},{2,3},{3,2},{4,5},{5,4},{6,7},{7,6},{8,9},{9,8},{10,11... | collective-permute-start | bytes 2482184 | tf_op jit(solution)/shard_map/ppermute | solution.py:128
  16.3 16.4 %collective-permute-start.1 = (bf16[3232,128]{1,0:T(8,128)(2,1)S(1)}, bf16[3232,128]{1,0:T(8,128)(2,1)S(1)}, u32[]{:S(2)}, u32[]{:S(2)}) collective-permute-start(bf16[3232,128]{1,0:T(8,128)(2,1)S(1)} %get-tuple-element.38.rest_1_), channel_id=1, source_target_pairs={{0,4},{1,5},{2,6},{3,7},{4,0},{5,1},{6,2},{7,3},{8,12},{9,13},{10,... | collective-permute-start | bytes 2482184 | tf_op jit(solution)/shard_map/ppermute | solution.py:128
  18.6 26.5 %collective-permute-start.6 = (bf16[3232,128]{1,0:T(8,128)(2,1)S(1)}, bf16[3232,128]{1,0:T(8,128)(2,1)S(1)}, u32[]{:S(2)}, u32[]{:S(2)}) collective-permute-start(bf16[3232,128]{1,0:T(8,128)(2,1)S(1)} %get-tuple-element.45), channel_id=1, source_target_pairs={{0,1},{1,0},{2,3},{3,2},{4,5},{5,4},{6,7},{7,6},{8,9},{9,8},{10,11... | collective-permute-start | bytes 2482184 | tf_op jit(solution)/shard_map/ppermute | solution.py:128
  21.2 31.8 %collective-permute-start.7 = (bf16[3232,128]{1,0:T(8,128)(2,1)S(1)}, bf16[3232,128]{1,0:T(8,128)(2,1)S(1)}, u32[]{:S(2)}, u32[]{:S(2)}) collective-permute-start(bf16[3232,128]{1,0:T(8,128)(2,1)S(1)} %get-tuple-element.46), channel_id=1, source_target_pairs={{0,4},{1,5},{2,6},{3,7},{4,0},{5,1},{6,2},{7,3},{8,12},{9,13},{10,... | collective-permute-start | bytes 2482184 | tf_op jit(solution)/shard_map/ppermute | solution.py:128
  27.1 26.8 %collective-permute-start.10 = (bf16[3232,128]{1,0:T(8,128)(2,1)S(1)}, bf16[3232,128]{1,0:T(8,128)(2,1)S(1)}, u32[]{:S(2)}, u32[]{:S(2)}) collective-permute-start(bf16[3232,128]{1,0:T(8,128)(2,1)S(1)} %get-tuple-element.49), channel_id=1, source_target_pairs={{0,3},{1,2},{2,1},{3,0},{4,7},{5,6},{6,5},{7,4},{8,11},{9,10},{10,... | collective-permute-start | bytes 2482184 | tf_op jit(solution)/shard_map/ppermute | solution.py:128
  28.6 27.4 %collective-permute-start.11 = (bf16[3232,128]{1,0:T(8,128)(2,1)S(1)}, bf16[3232,128]{1,0:T(8,128)(2,1)S(1)}, u32[]{:S(2)}, u32[]{:S(2)}) collective-permute-start(bf16[3232,128]{1,0:T(8,128)(2,1)S(1)} %get-tuple-element.50), channel_id=1, source_target_pairs={{0,12},{1,13},{2,14},{3,15},{4,8},{5,9},{6,10},{7,11},{8,4},{9,5},... | collective-permute-start | bytes 2482184 | tf_op jit(solution)/shard_map/ppermute | solution.py:128
  35.0 22.4 %collective-permute-start.2 = (bf16[3232,128]{1,0:T(8,128)(2,1)S(1)}, bf16[3232,128]{1,0:T(8,128)(2,1)S(1)}, u32[]{:S(2)}, u32[]{:S(2)}) collective-permute-start(bf16[3232,128]{1,0:T(8,128)(2,1)S(1)} %get-tuple-element.39.rest_2_), channel_id=1, source_target_pairs={{0,1},{1,0},{2,3},{3,2},{4,5},{5,4},{6,7},{7,6},{8,9},{9,8},{10,11... | collective-permute-start | bytes 2482184 | tf_op jit(solution)/shard_map/ppermute | solution.py:128
  45.2 14.9 %collective-permute-start.3 = (bf16[3232,128]{1,0:T(8,128)(2,1)S(1)}, bf16[3232,128]{1,0:T(8,128)(2,1)S(1)}, u32[]{:S(2)}, u32[]{:S(2)}) collective-permute-start(bf16[3232,128]{1,0:T(8,128)(2,1)S(1)} %get-tuple-element.40.rest_3_), channel_id=1, source_target_pairs={{0,4},{1,5},{2,6},{3,7},{4,0},{5,1},{6,2},{7,3},{8,12},{9,13},{10,... | collective-permute-start | bytes 2482184 | tf_op jit(solution)/shard_map/ppermute | solution.py:128
  53.0 11.7 %collective-permute-start.4 = (bf16[3232,128]{1,0:T(8,128)(2,1)S(1)}, bf16[3232,128]{1,0:T(8,128)(2,1)S(1)}, u32[]{:S(2)}, u32[]{:S(2)}) collective-permute-start(bf16[3232,128]{1,0:T(8,128)(2,1)S(1)} %get-tuple-element.43), channel_id=1, source_target_pairs={{0,3},{1,2},{2,1},{3,0},{4,7},{5,6},{6,5},{7,4},{8,11},{9,10},{10,... | collective-permute-start | bytes 2482184 | tf_op jit(solution)/shard_map/ppermute | solution.py:128
  53.9 18.7 %collective-permute-start.5 = (bf16[3232,128]{1,0:T(8,128)(2,1)S(1)}, bf16[3232,128]{1,0:T(8,128)(2,1)S(1)}, u32[]{:S(2)}, u32[]{:S(2)}) collective-permute-start(bf16[3232,128]{1,0:T(8,128)(2,1)S(1)} %get-tuple-element.44), channel_id=1, source_target_pairs={{0,12},{1,13},{2,14},{3,15},{4,8},{5,9},{6,10},{7,11},{8,4},{9,5},... | collective-permute-start | bytes 2482184 | tf_op jit(solution)/shard_map/ppermute | solution.py:128
  57.3 15.4 %collective-permute-start.14 = (bf16[1632,128]{1,0:T(8,128)(2,1)S(1)}, bf16[1632,128]{1,0:T(8,128)(2,1)S(1)}, u32[]{:S(2)}, u32[]{:S(2)}) collective-permute-start(bf16[1632,128]{1,0:T(8,128)(2,1)S(1)} %get-tuple-element.53), channel_id=1, source_target_pairs={{0,4},{1,5},{2,6},{3,7},{4,0},{5,1},{6,2},{7,3},{8,12},{9,13},{10,... | collective-permute-start | bytes 1253384 | tf_op jit(solution)/shard_map/ppermute | solution.py:128
  57.4 15.3 %collective-permute-start.15 = (bf16[1632,128]{1,0:T(8,128)(2,1)S(1)}, bf16[1632,128]{1,0:T(8,128)(2,1)S(1)}, u32[]{:S(2)}, u32[]{:S(2)}) collective-permute-start(bf16[1632,128]{1,0:T(8,128)(2,1)S(1)} %get-tuple-element.54), channel_id=1, source_target_pairs={{0,1},{1,0},{2,3},{3,2},{4,5},{5,4},{6,7},{7,6},{8,9},{9,8},{10,11... | collective-permute-start | bytes 1253384 | tf_op jit(solution)/shard_map/ppermute | solution.py:128
  61.2 16.7 %collective-permute-start.12 = (bf16[1632,128]{1,0:T(8,128)(2,1)S(1)}, bf16[1632,128]{1,0:T(8,128)(2,1)S(1)}, u32[]{:S(2)}, u32[]{:S(2)}) collective-permute-start(bf16[1632,128]{1,0:T(8,128)(2,1)S(1)} %get-tuple-element.51), channel_id=1, source_target_pairs={{0,4},{1,5},{2,6},{3,7},{4,0},{5,1},{6,2},{7,3},{8,12},{9,13},{10,... | collective-permute-start | bytes 1253384 | tf_op jit(solution)/shard_map/ppermute | solution.py:128
  64.6 13.6 %collective-permute-start.13 = (bf16[1632,128]{1,0:T(8,128)(2,1)S(1)}, bf16[1632,128]{1,0:T(8,128)(2,1)S(1)}, u32[]{:S(2)}, u32[]{:S(2)}) collective-permute-start(bf16[1632,128]{1,0:T(8,128)(2,1)S(1)} %get-tuple-element.52), channel_id=1, source_target_pairs={{0,1},{1,0},{2,3},{3,2},{4,5},{5,4},{6,7},{7,6},{8,9},{9,8},{10,11... | collective-permute-start | bytes 1253384 | tf_op jit(solution)/shard_map/ppermute | solution.py:128
  73.7 5.8 %collective-permute-start.18 = (bf16[816,128]{1,0:T(8,128)(2,1)S(1)}, bf16[816,128]{1,0:T(8,128)(2,1)S(1)}, u32[]{:S(2)}, u32[]{:S(2)}) collective-permute-start(bf16[816,128]{1,0:T(8,128)(2,1)S(1)} %get-tuple-element.55.rest_0_), channel_id=1, source_target_pairs={{0,12},{1,13},{2,14},{3,15},{4,8},{5,9},{6,10},{7,11},{8,4},{9,5},... | collective-permute-start | bytes 626696 | tf_op jit(solution)/shard_map/ppermute | solution.py:128
  75.5 4.7 %collective-permute-start.19 = (bf16[816,128]{1,0:T(8,128)(2,1)S(1)}, bf16[816,128]{1,0:T(8,128)(2,1)S(1)}, u32[]{:S(2)}, u32[]{:S(2)}) collective-permute-start(bf16[816,128]{1,0:T(8,128)(2,1)S(1)} %get-tuple-element.56.rest_1_), channel_id=1, source_target_pairs={{0,3},{1,2},{2,1},{3,0},{4,7},{5,6},{6,5},{7,4},{8,11},{9,10},{10,... | collective-permute-start | bytes 626696 | tf_op jit(solution)/shard_map/ppermute | solution.py:128
  77.2 7.3 %collective-permute-start.16 = (bf16[816,128]{1,0:T(8,128)(2,1)S(1)}, bf16[816,128]{1,0:T(8,128)(2,1)S(1)}, u32[]{:S(2)}, u32[]{:S(2)}) collective-permute-start(bf16[816,128]{1,0:T(8,128)(2,1)S(1)} %get-tuple-element.57), channel_id=1, source_target_pairs={{0,12},{1,13},{2,14},{3,15},{4,8},{5,9},{6,10},{7,11},{8,4},{9,5},... | collective-permute-start | bytes 626696 | tf_op jit(solution)/shard_map/ppermute | solution.py:128
  77.9 6.7 %collective-permute-start.17 = (bf16[816,128]{1,0:T(8,128)(2,1)S(1)}, bf16[816,128]{1,0:T(8,128)(2,1)S(1)}, u32[]{:S(2)}, u32[]{:S(2)}) collective-permute-start(bf16[816,128]{1,0:T(8,128)(2,1)S(1)} %get-tuple-element.58), channel_id=1, source_target_pairs={{0,3},{1,2},{2,1},{3,0},{4,7},{5,6},{6,5},{7,4},{8,11},{9,10},{10,... | collective-permute-start | bytes 626696 | tf_op jit(solution)/shard_map/ppermute | solution.py:128
  80.4 6.3 %collective-permute-start.22 = (bf16[168,640]{1,0:T(8,128)(2,1)S(1)}, bf16[168,640]{1,0:T(8,128)(2,1)S(1)}, u32[]{:S(2)}, u32[]{:S(2)}) collective-permute-start(bf16[168,640]{1,0:T(8,128)(2,1)S(1)} %last_far.1.rest_0_), channel_id=1, source_target_pairs={{0,64},{16,80},{32,96},{48,112},{64,0},{80,16},{96,32},{112,48},{1... | collective-permute-start | bytes 645128 | tf_op jit(solution)/shard_map/ppermute | solution.py:460
  83.7 6.3 %collective-permute-start.20 = (bf16[168,640]{1,0:T(8,128)(2,1)S(1)}, bf16[168,640]{1,0:T(8,128)(2,1)S(1)}, u32[]{:S(2)}, u32[]{:S(2)}) collective-permute-start(bf16[168,640]{1,0:T(8,128)(2,1)S(1)} %last_near1.1.rest_0_), channel_id=1, source_target_pairs={{0,32},{1,33},{2,34},{3,35},{4,36},{5,37},{6,38},{7,39},{8,40},{9,... | collective-permute-start | bytes 645128 | tf_op jit(solution)/shard_map/ppermute | solution.py:128
  84.9 5.2 %collective-permute-start.21 = (bf16[168,640]{1,0:T(8,128)(2,1)S(1)}, bf16[168,640]{1,0:T(8,128)(2,1)S(1)}, u32[]{:S(2)}, u32[]{:S(2)}) collective-permute-start(bf16[168,640]{1,0:T(8,128)(2,1)S(1)} %last_near2.1.rest_0_), channel_id=1, source_target_pairs={{0,96},{1,97},{2,98},{3,99},{4,100},{5,101},{6,102},{7,103},{8,104... | collective-permute-start | bytes 645128 | tf_op jit(solution)/shard_map/ppermute | solution.py:128
  90.2 12.1 %collective-permute-start.23 = (bf16[4,168,384]{2,1,0:T(8,128)(2,1)S(1)}, bf16[4,168,384]{2,1,0:T(8,128)(2,1)S(1)}, u32[]{:S(2)}, u32[]{:S(2)}) collective-permute-start(bf16[4,168,384]{2,1,0:T(8,128)(2,1)S(1)} %pad_maximum_fusion), channel_id=1, source_target_pairs={{0,16},{16,0},{32,48},{48,32},{64,80},{80,64},{96,112},{112,96},{1... | collective-permute-start | bytes 1548296 | tf_op jit(solution)/shard_map/ppermute | solution.py:478

commit v7 on v6

--- a/solution.py
+++ b/solution.py
@@ -10,7 +10,7 @@
 EPS = 1e-06
 POWER = 17
 TOP = 2.0 ** (124 / POWER)
-TINY = 2.0**-126
+TINY = 2.0**-118
 LANES = 128
 WIDE_ROWS = 8
 GROUP = 16
@@ -19,8 +19,8 @@
 
 
 def encode(values):
-    peak = jnp.max(jnp.abs(values), axis=0, keepdims=True).astype(BF16).astype(F32)
-    x = values * (TOP / jnp.maximum(peak, TINY))
+    peak = jnp.maximum(jnp.max(jnp.abs(values), axis=0, keepdims=True), TINY).astype(BF16).astype(F32)
+    x = values * (TOP / peak)
     x2 = x * x
     x4 = x2 * x2
     x8 = x4 * x4

time: 121 us -> 121 us (level)
  no operation moved by 1% of the time
where the time goes in v7:
time: 121 us
  starting transfers between devices  50.3 us (42%)
  Pallas kernels  34.6 us (29%)
  waiting for transfers between devices  20.5 us (17%)
  blocking collectives  15.7 us (13%)
    ppermute x22, starting transfers between devices, exchange(): return lax.ppermute(array, ('node', 'fsdp'), pairing(axis, first))  36.7 us
    pallas_call x7, Pallas kernels, product(): pl.pallas_call(functools.partial(product_kernel, which, rows, tile, coded...  17.7 us
    ppermute x22, waiting for transfers between devices, exchange(): return lax.ppermute(array, ('node', 'fsdp'), pairing(axis, first))  17.5 us
    all_to_all x1, blocking collectives, local(): sums = lax.all_to_all(gram, ('node', 'fsdp'), 0, 0, tiled=True)  15.7 us
    ppermute x1, starting transfers between devices, local(): carr = lax.ppermute(across, 'node', [(i, i ^ 1) for i in range(2 * SIDE)])  10.6 us
    pallas_call x1, Pallas kernels, first(): pl.pallas_call(functools.partial(first_kernel, rows, tile), out_shape=[xt...  6.57 us
    pallas_call x5, Pallas kernels, merge(): pl.pallas_call(functools.partial(kernel, rows, tile), out_shape=outs, in_...  5.7 us
    ppermute x1, starting transfers between devices, local(): far = lax.ppermute(far, 'node', [(i, i ^ 4) for i in range(2 * SIDE)])  2.99 us
  transfers between devices with their start and end apart: 24, of which 9 were waited for; matrix products, arithmetic and copies ran while one was open for 0% of the time, Pallas kernels for 20%

profile of v7, /device:TPU:1, one launch (start us, length us, event | category | flops | bytes accessed | tf_op | source)
XLA Modules:
  0.0 121.3 jit_solution(11153579122646114715)
XLA Ops:
  0.0 6.6 %p1a_near.1 = (bf16[2560,1024]{1,0:T(8,128)(2,1)S(1)}, bf16[1024,2560]{1,0:T(8,128)(2,1)S(1)}, bf16[3232,128]{1,0:T(8,128)(2,1)S(1)}, bf16[3232,128]{1,0:T(8,128)(2,1)S(1)}) custom-call(bf16[1024,2560]{1,0:T(8,128)(2,1)} %x_ref.1, bf16[1024,2560]{1,0:T(8,128)(2,1)} %dy_ref.1), custom_call_target="tpu_custom_call" | custom-call | tf_op jit(solution)/shard_map/p1a_near/pallas_call | solution.py:244
  6.6 3.4 %collective-permute-start.8 = (bf16[3232,128]{1,0:T(8,128)(2,1)S(1)}, bf16[3232,128]{1,0:T(8,128)(2,1)S(1)}, u32[]{:S(2)}, u32[]{:S(2)}) collective-permute-start(bf16[3232,128]{1,0:T(8,128)(2,1)S(1)} %get-tuple-element.35.rest_0_), channel_id=1, source_target_pairs={{0,1},{1,0},{2,3},{3,2},{4,5},{5,4},{6,7},{7,6},{8,9},{9,8},{10,11... | collective-permute-start | bytes 2482184 | tf_op jit(solution)/shard_map/ppermute | solution.py:128
  10.0 3.8 %collective-permute-start.9 = (bf16[3232,128]{1,0:T(8,128)(2,1)S(1)}, bf16[3232,128]{1,0:T(8,128)(2,1)S(1)}, u32[]{:S(2)}, u32[]{:S(2)}) collective-permute-start(bf16[3232,128]{1,0:T(8,128)(2,1)S(1)} %get-tuple-element.36.rest_1_), channel_id=1, source_target_pairs={{0,4},{1,5},{2,6},{3,7},{4,0},{5,1},{6,2},{7,3},{8,12},{9,13},{10,... | collective-permute-start | bytes 2482184 | tf_op jit(solution)/shard_map/ppermute | solution.py:128
  13.7 2.3 %p1a_far.1 = (bf16[3232,128]{1,0:T(8,128)(2,1)S(1)}, bf16[3232,128]{1,0:T(8,128)(2,1)S(1)}) custom-call(bf16[2560,1024]{1,0:T(8,128)(2,1)S(1)} %get-tuple-element.33.xt_ref, bf16[1024,2560]{1,0:T(8,128)(2,1)S(1)} %get-tuple-element.34.dy_ref, bf16[3232,128]{1,0:T(8,128)(2,1)S(1)} %get-tuple-element.35.rest_0_, bf16[3232,128]{1,0:T(8,128)(2,1)S(1)} %get-tuple-element.36.rest_1_), custom_call_target="tpu_custom_call" | custom-call | tf_op jit(solution)/shard_map/p1a_far/pallas_call | solution.py:230
  16.0 0.3 collective-permute-start
  16.3 2.3 %p1b_near.1 = (bf16[3232,128]{1,0:T(8,128)(2,1)S(1)}, bf16[3232,128]{1,0:T(8,128)(2,1)S(1)}) custom-call(bf16[2560,1024]{1,0:T(8,128)(2,1)S(1)} %get-tuple-element.33.xt_ref, bf16[1024,2560]{1,0:T(8,128)(2,1)S(1)} %get-tuple-element.34.dy_ref, bf16[3232,128]{1,0:T(8,128)(2,1)S(1)} %get-tuple-element.37.rest_0_, bf16[3232,128]{1,0:T(8,128)(2,1)S(1)} %get-tuple-element.38.rest_1_), custom_call_target="tpu_custom_call" | custom-call | tf_op jit(solution)/shard_map/p1b_near/pallas_call | solution.py:230
  18.6 2.6 %collective-permute-start.6 = (bf16[3232,128]{1,0:T(8,128)(2,1)S(1)}, bf16[3232,128]{1,0:T(8,128)(2,1)S(1)}, u32[]{:S(2)}, u32[]{:S(2)}) collective-permute-start(bf16[3232,128]{1,0:T(8,128)(2,1)S(1)} %get-tuple-element.45), channel_id=1, source_target_pairs={{0,1},{1,0},{2,3},{3,2},{4,5},{5,4},{6,7},{7,6},{8,9},{9,8},{10,11... | collective-permute-start | bytes 2482184 | tf_op jit(solution)/shard_map/ppermute | solution.py:128
  21.2 2.7 %collective-permute-start.7 = (bf16[3232,128]{1,0:T(8,128)(2,1)S(1)}, bf16[3232,128]{1,0:T(8,128)(2,1)S(1)}, u32[]{:S(2)}, u32[]{:S(2)}) collective-permute-start(bf16[3232,128]{1,0:T(8,128)(2,1)S(1)} %get-tuple-element.46), channel_id=1, source_target_pairs={{0,4},{1,5},{2,6},{3,7},{4,0},{5,1},{6,2},{7,3},{8,12},{9,13},{10,... | collective-permute-start | bytes 2482184 | tf_op jit(solution)/shard_map/ppermute | solution.py:128
  23.9 3.2 %p2_near.1 = (bf16[3232,128]{1,0:T(8,128)(2,1)S(1)}, bf16[3232,128]{1,0:T(8,128)(2,1)S(1)}) custom-call(bf16[2560,1024]{1,0:T(8,128)(2,1)S(1)} %get-tuple-element.33.xt_ref, bf16[1024,2560]{1,0:T(8,128)(2,1)S(1)} %get-tuple-element.34.dy_ref, bf16[3232,128]{1,0:T(8,128)(2,1)S(1)} %collective-permute-done.8.rest_0_.rest_2_, ...), custom_call_target="tpu_custom_call" | custom-call | tf_op jit(solution)/shard_map/p2_near/pallas_call | solution.py:230
  27.1 0.4 collective-permute-start.10
  27.5 1.1 collective-permute-done.rest_0_
  28.7 1.8 %collective-permute-start.11 = (bf16[3232,128]{1,0:T(8,128)(2,1)S(1)}, bf16[3232,128]{1,0:T(8,128)(2,1)S(1)}, u32[]{:S(2)}, u32[]{:S(2)}) collective-permute-start(bf16[3232,128]{1,0:T(8,128)(2,1)S(1)} %get-tuple-element.50), channel_id=1, source_target_pairs={{0,12},{1,13},{2,14},{3,15},{4,8},{5,9},{6,10},{7,11},{8,4},{9,5},... | collective-permute-start | bytes 2482184 | tf_op jit(solution)/shard_map/ppermute | solution.py:128
  30.5 2.2 %collective-permute-done.1.rest_1_ = bf16[3232,128]{1,0:T(8,128)(2,1)S(1)} collective-permute-done((bf16[3232,128]{1,0:T(8,128)(2,1)S(1)}, bf16[3232,128]{1,0:T(8,128)(2,1)S(1)}, u32[]{:S(2)}, u32[]{:S(2)}) %collective-permute-start.1) | collective-permute-done | bytes 827424 | tf_op jit(solution)/shard_map/ppermute | solution.py:128
  32.7 2.3 %p1b_far.1 = (bf16[3232,128]{1,0:T(8,128)(2,1)S(1)}, bf16[3232,128]{1,0:T(8,128)(2,1)S(1)}) custom-call(bf16[2560,1024]{1,0:T(8,128)(2,1)S(1)} %get-tuple-element.33.xt_ref, bf16[1024,2560]{1,0:T(8,128)(2,1)S(1)} %get-tuple-element.34.dy_ref, bf16[3232,128]{1,0:T(8,128)(2,1)S(1)} %collective-permute-done.rest_0_, ...), custom_call_target="tpu_custom_call" | custom-call | tf_op jit(solution)/shard_map/p1b_far/pallas_call | solution.py:230
  35.0 0.3 collective-permute-start.2
  35.3 9.8 %collective-permute-done.6.rest_0_.rest_2_ = bf16[3232,128]{1,0:T(8,128)(2,1)S(1)} collective-permute-done((bf16[3232,128]{1,0:T(8,128)(2,1)S(1)}, bf16[3232,128]{1,0:T(8,128)(2,1)S(1)}, u32[]{:S(2)}, u32[]{:S(2)}) %collective-permute-start.6) | collective-permute-done | bytes 827424 | tf_op jit(solution)/shard_map/ppermute | solution.py:128
  45.2 4.6 %collective-permute-start.3 = (bf16[3232,128]{1,0:T(8,128)(2,1)S(1)}, bf16[3232,128]{1,0:T(8,128)(2,1)S(1)}, u32[]{:S(2)}, u32[]{:S(2)}) collective-permute-start(bf16[3232,128]{1,0:T(8,128)(2,1)S(1)} %get-tuple-element.40.rest_3_), channel_id=1, source_target_pairs={{0,4},{1,5},{2,6},{3,7},{4,0},{5,1},{6,2},{7,3},{8,12},{9,13},{10,... | collective-permute-start | bytes 2482184 | tf_op jit(solution)/shard_map/ppermute | solution.py:128
  49.7 3.2 %p2_far.1 = (bf16[3232,128]{1,0:T(8,128)(2,1)S(1)}, bf16[3232,128]{1,0:T(8,128)(2,1)S(1)}) custom-call(bf16[2560,1024]{1,0:T(8,128)(2,1)S(1)} %get-tuple-element.33.xt_ref, bf16[1024,2560]{1,0:T(8,128)(2,1)S(1)} %get-tuple-element.34.dy_ref, bf16[3232,128]{1,0:T(8,128)(2,1)S(1)} %collective-permute-done.rest_0_, ...), custom_call_target="tpu_custom_call" | custom-call | tf_op jit(solution)/shard_map/p2_far/pallas_call | solution.py:230
  53.0 0.9 collective-permute-start.4
  53.9 2.2 %kept_near.1 = (f32[160,2560]{1,0:T(8,128)S(1)}, f32[160,2560]{1,0:T(8,128)S(1)}) custom-call(bf16[2560,1024]{1,0:T(8,128)(2,1)S(1)} %get-tuple-element.33.xt_ref, bf16[1024,2560]{1,0:T(8,128)(2,1)S(1)} %get-tuple-element.34.dy_ref, bf16[3232,128]{1,0:T(8,128)(2,1)S(1)} %collective-permute-done.6.rest_0_.rest_2_, ...), custom_call_target="tpu_custom_call" | custom-call | tf_op jit(solution)/shard_map/kept_near/pallas_call | solution.py:230
  56.1 1.1 q1_near.1
  57.4 2.5 %collective-permute-start.15 = (bf16[1632,128]{1,0:T(8,128)(2,1)S(1)}, bf16[1632,128]{1,0:T(8,128)(2,1)S(1)}, u32[]{:S(2)}, u32[]{:S(2)}) collective-permute-start(bf16[1632,128]{1,0:T(8,128)(2,1)S(1)} %get-tuple-element.54), channel_id=1, source_target_pairs={{0,1},{1,0},{2,3},{3,2},{4,5},{5,4},{6,7},{7,6},{8,9},{9,8},{10,11... | collective-permute-start | bytes 1253384 | tf_op jit(solution)/shard_map/ppermute | solution.py:128
  60.0 1.1 q1_far.1
  61.2 3.2 %collective-permute-start.12 = (bf16[1632,128]{1,0:T(8,128)(2,1)S(1)}, bf16[1632,128]{1,0:T(8,128)(2,1)S(1)}, u32[]{:S(2)}, u32[]{:S(2)}) collective-permute-start(bf16[1632,128]{1,0:T(8,128)(2,1)S(1)} %get-tuple-element.51), channel_id=1, source_target_pairs={{0,4},{1,5},{2,6},{3,7},{4,0},{5,1},{6,2},{7,3},{8,12},{9,13},{10,... | collective-permute-start | bytes 1253384 | tf_op jit(solution)/shard_map/ppermute | solution.py:128
  64.4 0.3 collective-permute-done.4.p0
  64.6 5.8 %collective-permute-start.13 = (bf16[1632,128]{1,0:T(8,128)(2,1)S(1)}, bf16[1632,128]{1,0:T(8,128)(2,1)S(1)}, u32[]{:S(2)}, u32[]{:S(2)}) collective-permute-start(bf16[1632,128]{1,0:T(8,128)(2,1)S(1)} %get-tuple-element.52), channel_id=1, source_target_pairs={{0,1},{1,0},{2,3},{3,2},{4,5},{5,4},{6,7},{7,6},{8,9},{9,8},{10,11... | collective-permute-start | bytes 1253384 | tf_op jit(solution)/shard_map/ppermute | solution.py:128
  70.4 2.2 %kept_far.1 = (f32[160,2560]{1,0:T(8,128)S(1)}, f32[160,2560]{1,0:T(8,128)S(1)}) custom-call(bf16[2560,1024]{1,0:T(8,128)(2,1)S(1)} %get-tuple-element.33.xt_ref, bf16[1024,2560]{1,0:T(8,128)(2,1)S(1)} %get-tuple-element.34.dy_ref, bf16[3232,128]{1,0:T(8,128)(2,1)S(1)} %collective-permute-done.2.rest_0_.rest_2_, ...), custom_call_target="tpu_custom_call" | custom-call | tf_op jit(solution)/shard_map/kept_far/pallas_call | solution.py:230
  72.6 1.1 q2_early.1
  73.7 1.7 %collective-permute-start.18 = (bf16[816,128]{1,0:T(8,128)(2,1)S(1)}, bf16[816,128]{1,0:T(8,128)(2,1)S(1)}, u32[]{:S(2)}, u32[]{:S(2)}) collective-permute-start(bf16[816,128]{1,0:T(8,128)(2,1)S(1)} %get-tuple-element.55.rest_0_), channel_id=1, source_target_pairs={{0,12},{1,13},{2,14},{3,15},{4,8},{5,9},{6,10},{7,11},{8,4},{9,5},... | collective-permute-start | bytes 626696 | tf_op jit(solution)/shard_map/ppermute | solution.py:128
  75.5 0.7 collective-permute-start.19
  76.2 1.0 q2_late.1
  77.2 0.7 collective-permute-start.16
  77.9 0.3 collective-permute-start.17
  78.2 1.3 %own.1 = f32[160,2560]{1,0:T(8,128)S(1)} custom-call(f32[160,2560]{1,0:T(8,128)S(1)} %get-tuple-element.41.kept0, f32[160,2560]{1,0:T(8,128)S(1)} %get-tuple-element.42.kept1, bf16[3232,128]{1,0:T(8,128)(2,1)S(1)} %collective-permute-done.4.p0, bf16[3232,128]{1,0:T(8,128)(2,1)S(1)} %collective-permute-done.5.p1, ...), custom_call_target="tpu_custom_call" | custom-call | tf_op jit(solution)/shard_map/own/pallas_call | solution.py:308
  79.5 0.6 collective-permute-done.19.arr1
  80.1 0.3 last_far.1.rest_0_
  80.4 3.0 %collective-permute-start.22 = (bf16[168,640]{1,0:T(8,128)(2,1)S(1)}, bf16[168,640]{1,0:T(8,128)(2,1)S(1)}, u32[]{:S(2)}, u32[]{:S(2)}) collective-permute-start(bf16[168,640]{1,0:T(8,128)(2,1)S(1)} %last_far.1.rest_0_), channel_id=1, source_target_pairs={{0,64},{16,80},{32,96},{48,112},{64,0},{80,16},{96,32},{112,48},{1... | collective-permute-start | bytes 645128 | tf_op jit(solution)/shard_map/ppermute | solution.py:460
  83.4 0.3 last_near1.1.rest_0_
  83.7 0.9 collective-permute-start.20
  84.6 0.3 last_near2.1.rest_0_
  85.0 0.3 last_mine.1.ref.own0
  85.3 1.4 %collective-permute-done.22.ref.own3 = bf16[168,640]{1,0:T(8,128)(2,1)S(1)} collective-permute-done((bf16[168,640]{1,0:T(8,128)(2,1)S(1)}, bf16[168,640]{1,0:T(8,128)(2,1)S(1)}, u32[]{:S(2)}, u32[]{:S(2)}) %collective-permute-start.22) | collective-permute-done | bytes 215072 | tf_op jit(solution)/shard_map/ppermute | solution.py:460
  86.7 3.3 %collective-permute-done.20.ref.own1 = bf16[168,640]{1,0:T(8,128)(2,1)S(1)} collective-permute-done((bf16[168,640]{1,0:T(8,128)(2,1)S(1)}, bf16[168,640]{1,0:T(8,128)(2,1)S(1)}, u32[]{:S(2)}, u32[]{:S(2)}) %collective-permute-start.20) | collective-permute-done | bytes 215072 | tf_op jit(solution)/shard_map/ppermute | solution.py:128
  90.2 10.6 %collective-permute-start.23 = (bf16[4,168,384]{2,1,0:T(8,128)(2,1)S(1)}, bf16[4,168,384]{2,1,0:T(8,128)(2,1)S(1)}, u32[]{:S(2)}, u32[]{:S(2)}) collective-permute-start(bf16[4,168,384]{2,1,0:T(8,128)(2,1)S(1)} %pad_maximum_fusion), channel_id=1, source_target_pairs={{0,16},{16,0},{32,48},{48,32},{64,80},{80,64},{96,112},{112,96},{1... | collective-permute-start | bytes 1548296 | tf_op jit(solution)/shard_map/ppermute | solution.py:478
  100.8 1.5 %collective-permute-done.23.carr = bf16[4,168,384]{2,1,0:T(8,128)(2,1)S(1)} collective-permute-done((bf16[4,168,384]{2,1,0:T(8,128)(2,1)S(1)}, bf16[4,168,384]{2,1,0:T(8,128)(2,1)S(1)}, u32[]{:S(2)}, u32[]{:S(2)}) %collective-permute-start.23) | collective-permute-done | bytes 516128 | tf_op jit(solution)/shard_map/ppermute | solution.py:478
  102.3 1.7 %gram.1 = (f32[8,160,384]{2,1,0:T(8,128)S(1)}, f32[128,128]{1,0:T(8,128)S(1)}) custom-call(bf16[168,640]{1,0:T(8,128)(2,1)S(1)} %last_mine.1.ref.own0, bf16[168,640]{1,0:T(8,128)(2,1)S(1)} %collective-permute-done.20.ref.own1, bf16[168,640]{1,0:T(8,128)(2,1)S(1)} %collective-permute-done.21.ref.own2, bf16[168,640]{1,0:T(8,128)(2,1)S(1)} %collective-permute-done.22.ref.own3, ...), custom_call_target="tpu_custom_call" | custom-call | tf_op jit(solution)/shard_map/gram/pallas_call | solution.py:480
  104.0 15.7 %all_to_all.11 = f32[128,1,128]{2,1,0:T(1,128)S(1)} all-to-all(f32[128,1,128]{2,1,0:T(1,128)S(1)} %bitcast.13), channel_id=1, replica_groups=mesh['node'=8,'fsdp'=16] {'node','fsdp'}, dimensions={0} | all-to-all | bytes 131072 | tf_op jit(solution)/shard_map/all_to_all | solution.py:489
  119.7 1.6 %combine.1 = f32[160,320]{1,0:T(8,128)} custom-call(f32[8,160,384]{2,1,0:T(8,128)S(1)} %get-tuple-element.59.g_ref, f32[128,128]{1,0:T(8,128)S(1)} %bitcast.12), custom_call_target="tpu_custom_call" | custom-call | tf_op jit(solution)/shard_map/combine/pallas_call | solution.py:490
  (25 shorter events, 0.6 us)
Async XLA Ops:
  6.6 14.6 %collective-permute-start.8 = (bf16[3232,128]{1,0:T(8,128)(2,1)S(1)}, bf16[3232,128]{1,0:T(8,128)(2,1)S(1)}, u32[]{:S(2)}, u32[]{:S(2)}) collective-permute-start(bf16[3232,128]{1,0:T(8,128)(2,1)S(1)} %get-tuple-element.35.rest_0_), channel_id=1, source_target_pairs={{0,1},{1,0},{2,3},{3,2},{4,5},{5,4},{6,7},{7,6},{8,9},{9,8},{10,11... | collective-permute-start | bytes 2482184 | tf_op jit(solution)/shard_map/ppermute | solution.py:128
  10.0 13.9 %collective-permute-start.9 = (bf16[3232,128]{1,0:T(8,128)(2,1)S(1)}, bf16[3232,128]{1,0:T(8,128)(2,1)S(1)}, u32[]{:S(2)}, u32[]{:S(2)}) collective-permute-start(bf16[3232,128]{1,0:T(8,128)(2,1)S(1)} %get-tuple-element.36.rest_1_), channel_id=1, source_target_pairs={{0,4},{1,5},{2,6},{3,7},{4,0},{5,1},{6,2},{7,3},{8,12},{9,13},{10,... | collective-permute-start | bytes 2482184 | tf_op jit(solution)/shard_map/ppermute | solution.py:128
  16.0 12.6 %collective-permute-start = (bf16[3232,128]{1,0:T(8,128)(2,1)S(1)}, bf16[3232,128]{1,0:T(8,128)(2,1)S(1)}, u32[]{:S(2)}, u32[]{:S(2)}) collective-permute-start(bf16[3232,128]{1,0:T(8,128)(2,1)S(1)} %get-tuple-element.37.rest_0_), channel_id=1, source_target_pairs={{0,1},{1,0},{2,3},{3,2},{4,5},{5,4},{6,7},{7,6},{8,9},{9,8},{10,11... | collective-permute-start | bytes 2482184 | tf_op jit(solution)/shard_map/ppermute | solution.py:128
  16.3 16.4 %collective-permute-start.1 = (bf16[3232,128]{1,0:T(8,128)(2,1)S(1)}, bf16[3232,128]{1,0:T(8,128)(2,1)S(1)}, u32[]{:S(2)}, u32[]{:S(2)}) collective-permute-start(bf16[3232,128]{1,0:T(8,128)(2,1)S(1)} %get-tuple-element.38.rest_1_), channel_id=1, source_target_pairs={{0,4},{1,5},{2,6},{3,7},{4,0},{5,1},{6,2},{7,3},{8,12},{9,13},{10,... | collective-permute-start | bytes 2482184 | tf_op jit(solution)/shard_map/ppermute | solution.py:128
  18.6 26.5 %collective-permute-start.6 = (bf16[3232,128]{1,0:T(8,128)(2,1)S(1)}, bf16[3232,128]{1,0:T(8,128)(2,1)S(1)}, u32[]{:S(2)}, u32[]{:S(2)}) collective-permute-start(bf16[3232,128]{1,0:T(8,128)(2,1)S(1)} %get-tuple-element.45), channel_id=1, source_target_pairs={{0,1},{1,0},{2,3},{3,2},{4,5},{5,4},{6,7},{7,6},{8,9},{9,8},{10,11... | collective-permute-start | bytes 2482184 | tf_op jit(solution)/shard_map/ppermute | solution.py:128
  21.2 31.8 %collective-permute-start.7 = (bf16[3232,128]{1,0:T(8,128)(2,1)S(1)}, bf16[3232,128]{1,0:T(8,128)(2,1)S(1)}, u32[]{:S(2)}, u32[]{:S(2)}) collective-permute-start(bf16[3232,128]{1,0:T(8,128)(2,1)S(1)} %get-tuple-element.46), channel_id=1, source_target_pairs={{0,4},{1,5},{2,6},{3,7},{4,0},{5,1},{6,2},{7,3},{8,12},{9,13},{10,... | collective-permute-start | bytes 2482184 | tf_op jit(solution)/shard_map/ppermute | solution.py:128
  27.1 26.8 %collective-permute-start.10 = (bf16[3232,128]{1,0:T(8,128)(2,1)S(1)}, bf16[3232,128]{1,0:T(8,128)(2,1)S(1)}, u32[]{:S(2)}, u32[]{:S(2)}) collective-permute-start(bf16[3232,128]{1,0:T(8,128)(2,1)S(1)} %get-tuple-element.49), channel_id=1, source_target_pairs={{0,3},{1,2},{2,1},{3,0},{4,7},{5,6},{6,5},{7,4},{8,11},{9,10},{10,... | collective-permute-start | bytes 2482184 | tf_op jit(solution)/shard_map/ppermute | solution.py:128
  28.7 27.4 %collective-permute-start.11 = (bf16[3232,128]{1,0:T(8,128)(2,1)S(1)}, bf16[3232,128]{1,0:T(8,128)(2,1)S(1)}, u32[]{:S(2)}, u32[]{:S(2)}) collective-permute-start(bf16[3232,128]{1,0:T(8,128)(2,1)S(1)} %get-tuple-element.50), channel_id=1, source_target_pairs={{0,12},{1,13},{2,14},{3,15},{4,8},{5,9},{6,10},{7,11},{8,4},{9,5},... | collective-permute-start | bytes 2482184 | tf_op jit(solution)/shard_map/ppermute | solution.py:128
  35.0 22.4 %collective-permute-start.2 = (bf16[3232,128]{1,0:T(8,128)(2,1)S(1)}, bf16[3232,128]{1,0:T(8,128)(2,1)S(1)}, u32[]{:S(2)}, u32[]{:S(2)}) collective-permute-start(bf16[3232,128]{1,0:T(8,128)(2,1)S(1)} %get-tuple-element.39.rest_2_), channel_id=1, source_target_pairs={{0,1},{1,0},{2,3},{3,2},{4,5},{5,4},{6,7},{7,6},{8,9},{9,8},{10,11... | collective-permute-start | bytes 2482184 | tf_op jit(solution)/shard_map/ppermute | solution.py:128
  45.2 14.9 %collective-permute-start.3 = (bf16[3232,128]{1,0:T(8,128)(2,1)S(1)}, bf16[3232,128]{1,0:T(8,128)(2,1)S(1)}, u32[]{:S(2)}, u32[]{:S(2)}) collective-permute-start(bf16[3232,128]{1,0:T(8,128)(2,1)S(1)} %get-tuple-element.40.rest_3_), channel_id=1, source_target_pairs={{0,4},{1,5},{2,6},{3,7},{4,0},{5,1},{6,2},{7,3},{8,12},{9,13},{10,... | collective-permute-start | bytes 2482184 | tf_op jit(solution)/shard_map/ppermute | solution.py:128
  53.0 11.7 %collective-permute-start.4 = (bf16[3232,128]{1,0:T(8,128)(2,1)S(1)}, bf16[3232,128]{1,0:T(8,128)(2,1)S(1)}, u32[]{:S(2)}, u32[]{:S(2)}) collective-permute-start(bf16[3232,128]{1,0:T(8,128)(2,1)S(1)} %get-tuple-element.43), channel_id=1, source_target_pairs={{0,3},{1,2},{2,1},{3,0},{4,7},{5,6},{6,5},{7,4},{8,11},{9,10},{10,... | collective-permute-start | bytes 2482184 | tf_op jit(solution)/shard_map/ppermute | solution.py:128
  53.9 18.7 %collective-permute-start.5 = (bf16[3232,128]{1,0:T(8,128)(2,1)S(1)}, bf16[3232,128]{1,0:T(8,128)(2,1)S(1)}, u32[]{:S(2)}, u32[]{:S(2)}) collective-permute-start(bf16[3232,128]{1,0:T(8,128)(2,1)S(1)} %get-tuple-element.44), channel_id=1, source_target_pairs={{0,12},{1,13},{2,14},{3,15},{4,8},{5,9},{6,10},{7,11},{8,4},{9,5},... | collective-permute-start | bytes 2482184 | tf_op jit(solution)/shard_map/ppermute | solution.py:128
  57.2 15.4 %collective-permute-start.14 = (bf16[1632,128]{1,0:T(8,128)(2,1)S(1)}, bf16[1632,128]{1,0:T(8,128)(2,1)S(1)}, u32[]{:S(2)}, u32[]{:S(2)}) collective-permute-start(bf16[1632,128]{1,0:T(8,128)(2,1)S(1)} %get-tuple-element.53), channel_id=1, source_target_pairs={{0,4},{1,5},{2,6},{3,7},{4,0},{5,1},{6,2},{7,3},{8,12},{9,13},{10,... | collective-permute-start | bytes 1253384 | tf_op jit(solution)/shard_map/ppermute | solution.py:128
  57.4 15.3 %collective-permute-start.15 = (bf16[1632,128]{1,0:T(8,128)(2,1)S(1)}, bf16[1632,128]{1,0:T(8,128)(2,1)S(1)}, u32[]{:S(2)}, u32[]{:S(2)}) collective-permute-start(bf16[1632,128]{1,0:T(8,128)(2,1)S(1)} %get-tuple-element.54), channel_id=1, source_target_pairs={{0,1},{1,0},{2,3},{3,2},{4,5},{5,4},{6,7},{7,6},{8,9},{9,8},{10,11... | collective-permute-start | bytes 1253384 | tf_op jit(solution)/shard_map/ppermute | solution.py:128
  61.2 16.7 %collective-permute-start.12 = (bf16[1632,128]{1,0:T(8,128)(2,1)S(1)}, bf16[1632,128]{1,0:T(8,128)(2,1)S(1)}, u32[]{:S(2)}, u32[]{:S(2)}) collective-permute-start(bf16[1632,128]{1,0:T(8,128)(2,1)S(1)} %get-tuple-element.51), channel_id=1, source_target_pairs={{0,4},{1,5},{2,6},{3,7},{4,0},{5,1},{6,2},{7,3},{8,12},{9,13},{10,... | collective-permute-start | bytes 1253384 | tf_op jit(solution)/shard_map/ppermute | solution.py:128
  64.6 13.5 %collective-permute-start.13 = (bf16[1632,128]{1,0:T(8,128)(2,1)S(1)}, bf16[1632,128]{1,0:T(8,128)(2,1)S(1)}, u32[]{:S(2)}, u32[]{:S(2)}) collective-permute-start(bf16[1632,128]{1,0:T(8,128)(2,1)S(1)} %get-tuple-element.52), channel_id=1, source_target_pairs={{0,1},{1,0},{2,3},{3,2},{4,5},{5,4},{6,7},{7,6},{8,9},{9,8},{10,11... | collective-permute-start | bytes 1253384 | tf_op jit(solution)/shard_map/ppermute | solution.py:128
  73.7 5.8 %collective-permute-start.18 = (bf16[816,128]{1,0:T(8,128)(2,1)S(1)}, bf16[816,128]{1,0:T(8,128)(2,1)S(1)}, u32[]{:S(2)}, u32[]{:S(2)}) collective-permute-start(bf16[816,128]{1,0:T(8,128)(2,1)S(1)} %get-tuple-element.55.rest_0_), channel_id=1, source_target_pairs={{0,12},{1,13},{2,14},{3,15},{4,8},{5,9},{6,10},{7,11},{8,4},{9,5},... | collective-permute-start | bytes 626696 | tf_op jit(solution)/shard_map/ppermute | solution.py:128
  75.5 4.7 %collective-permute-start.19 = (bf16[816,128]{1,0:T(8,128)(2,1)S(1)}, bf16[816,128]{1,0:T(8,128)(2,1)S(1)}, u32[]{:S(2)}, u32[]{:S(2)}) collective-permute-start(bf16[816,128]{1,0:T(8,128)(2,1)S(1)} %get-tuple-element.56.rest_1_), channel_id=1, source_target_pairs={{0,3},{1,2},{2,1},{3,0},{4,7},{5,6},{6,5},{7,4},{8,11},{9,10},{10,... | collective-permute-start | bytes 626696 | tf_op jit(solution)/shard_map/ppermute | solution.py:128
  77.2 7.3 %collective-permute-start.16 = (bf16[816,128]{1,0:T(8,128)(2,1)S(1)}, bf16[816,128]{1,0:T(8,128)(2,1)S(1)}, u32[]{:S(2)}, u32[]{:S(2)}) collective-permute-start(bf16[816,128]{1,0:T(8,128)(2,1)S(1)} %get-tuple-element.57), channel_id=1, source_target_pairs={{0,12},{1,13},{2,14},{3,15},{4,8},{5,9},{6,10},{7,11},{8,4},{9,5},... | collective-permute-start | bytes 626696 | tf_op jit(solution)/shard_map/ppermute | solution.py:128
  77.9 6.7 %collective-permute-start.17 = (bf16[816,128]{1,0:T(8,128)(2,1)S(1)}, bf16[816,128]{1,0:T(8,128)(2,1)S(1)}, u32[]{:S(2)}, u32[]{:S(2)}) collective-permute-start(bf16[816,128]{1,0:T(8,128)(2,1)S(1)} %get-tuple-element.58), channel_id=1, source_target_pairs={{0,3},{1,2},{2,1},{3,0},{4,7},{5,6},{6,5},{7,4},{8,11},{9,10},{10,... | collective-permute-start | bytes 626696 | tf_op jit(solution)/shard_map/ppermute | solution.py:128
  80.4 6.3 %collective-permute-start.22 = (bf16[168,640]{1,0:T(8,128)(2,1)S(1)}, bf16[168,640]{1,0:T(8,128)(2,1)S(1)}, u32[]{:S(2)}, u32[]{:S(2)}) collective-permute-start(bf16[168,640]{1,0:T(8,128)(2,1)S(1)} %last_far.1.rest_0_), channel_id=1, source_target_pairs={{0,64},{16,80},{32,96},{48,112},{64,0},{80,16},{96,32},{112,48},{1... | collective-permute-start | bytes 645128 | tf_op jit(solution)/shard_map/ppermute | solution.py:460
  83.7 6.3 %collective-permute-start.20 = (bf16[168,640]{1,0:T(8,128)(2,1)S(1)}, bf16[168,640]{1,0:T(8,128)(2,1)S(1)}, u32[]{:S(2)}, u32[]{:S(2)}) collective-permute-start(bf16[168,640]{1,0:T(8,128)(2,1)S(1)} %last_near1.1.rest_0_), channel_id=1, source_target_pairs={{0,32},{1,33},{2,34},{3,35},{4,36},{5,37},{6,38},{7,39},{8,40},{9,... | collective-permute-start | bytes 645128 | tf_op jit(solution)/shard_map/ppermute | solution.py:128
  84.9 5.2 %collective-permute-start.21 = (bf16[168,640]{1,0:T(8,128)(2,1)S(1)}, bf16[168,640]{1,0:T(8,128)(2,1)S(1)}, u32[]{:S(2)}, u32[]{:S(2)}) collective-permute-start(bf16[168,640]{1,0:T(8,128)(2,1)S(1)} %last_near2.1.rest_0_), channel_id=1, source_target_pairs={{0,96},{1,97},{2,98},{3,99},{4,100},{5,101},{6,102},{7,103},{8,104... | collective-permute-start | bytes 645128 | tf_op jit(solution)/shard_map/ppermute | solution.py:128
  90.2 12.1 %collective-permute-start.23 = (bf16[4,168,384]{2,1,0:T(8,128)(2,1)S(1)}, bf16[4,168,384]{2,1,0:T(8,128)(2,1)S(1)}, u32[]{:S(2)}, u32[]{:S(2)}) collective-permute-start(bf16[4,168,384]{2,1,0:T(8,128)(2,1)S(1)} %pad_maximum_fusion), channel_id=1, source_target_pairs={{0,16},{16,0},{32,48},{48,32},{64,80},{80,64},{96,112},{112,96},{1... | collective-permute-start | bytes 1548296 | tf_op jit(solution)/shard_map/ppermute | solution.py:478

commit v8 on v7

--- a/solution.py
+++ b/solution.py
@@ -345,20 +345,32 @@
     out[...] = ref[:, at]
 
 
-def gram_kernel(rows, half, own0, own1, own2, own3, carr, g_ref, gram_ref):
+def own_columns(half, wide, core):
+    start = (wide - half) * core
+    for t in range(wide // LANES):
+        lane = lax.broadcasted_iota(jnp.int32, (1, LANES), 1) + t * LANES
+        yield slice(t * LANES, (t + 1) * LANES), (lane >= start) & (lane < start + half)
+
+
+def held_kernel(rows, half, own0, own1, own2, own3, held_ref):
+    core = coordinates()[3]
+    wide = held_ref.shape[2]
+    for k, ref in enumerate((own0, own1, own2, own3)):
+        for cols, valid in own_columns(half, wide, core):
+            at = pl.ds(pl.multiple_of((ref.shape[1] - wide) * core + cols.start, LANES), LANES)
+            values = decode(ref[:rows, at], ref[rows : rows + 1, at].astype(F32))
+            held_ref[k, :, cols] = jnp.where(valid, values, 0.0)
+
+
+def gram_kernel(rows, half, held, carr, g_ref, gram_ref):
     _, y, _, core = coordinates()
     m1, m2 = masks(core)
     wide = g_ref.shape[2]
-    start = (wide - half) * core
-    lane = lax.broadcasted_iota(jnp.int32, (1, wide), 1)
-    valid = (lane >= start) & (lane < start + half)
-    at = pl.ds(pl.multiple_of((own0.shape[1] - wide) * core, LANES), wide)
-    sources = [(own0, 0, 0), (own1, m1, m2), (own2, m2, m1), (own3, 2, 2)]
-    for k, (ref, mask, mask_other) in enumerate(sources):
-        own = decode(ref[:rows, at], ref[rows : rows + 1, at].astype(F32))
-        g_ref[(y ^ mask) * 2 + core] = jnp.where(valid, own, 0.0)
-        other = decode(carr[k, :rows, :], carr[k, rows : rows + 1, :].astype(F32))
-        g_ref[(y ^ mask_other) * 2 + 1 - core] = jnp.where(valid, other, 0.0)
+    for k, (mask, mask_other) in enumerate(((0, 0), (m1, m2), (m2, m1), (2, 2))):
+        for cols, valid in own_columns(half, wide, core):
+            g_ref[(y ^ mask) * 2 + core, :, cols] = held[k, :, cols]
+            other = decode(carr[k, :rows, cols], carr[k, rows : rows + 1, cols].astype(F32))
+            g_ref[(y ^ mask_other) * 2 + 1 - core, :, cols] = jnp.where(valid, other, 0.0)
     nodes = g_ref.shape[0]
     pairs = [(i, j) for i in range(nodes) for j in range(i, nodes)]
 
@@ -477,6 +489,14 @@
     across = jnp.stack([mine_cut, near1_cut, near2_cut, far_cut])
     carr = lax.ppermute(across, "node", [(i, i ^ 1) for i in range(2 * SIDE)])
     count = 2 * SIDE * SIDE * SIDE
+    held = pl.pallas_call(
+        functools.partial(held_kernel, 2 * rows, half),
+        out_shape=jax.ShapeDtypeStruct((SIDE, 2 * rows, wide), F32),
+        in_specs=[VMEM] * SIDE,
+        out_specs=VMEM,
+        compiler_params=params(12),
+        name="held",
+    )(*blocks)
     g, gram = pl.pallas_call(
         functools.partial(gram_kernel, 2 * rows, half),
         out_shape=[
@@ -485,7 +505,7 @@
         ],
         compiler_params=params(12),
         name="gram",
-    )(*blocks, carr)
+    )(held, carr)
     sums = lax.all_to_all(gram, ("node", "fsdp"), 0, 0, tiled=True)
     return pl.pallas_call(
         functools.partial(combine_kernel, half),

time: 121 us -> 121 us (level)
  transfers between devices with their start and end apart: 24 -> 24, of which waited for: 9 -> 9; matrix products, arithmetic and copies ran while one was open for 0% -> 0% of each run, Pallas kernels for 20% -> 21%
where the time goes in v8:
time: 121 us
  starting transfers between devices  50.3 us (42%)
  Pallas kernels  34.7 us (29%)
  waiting for transfers between devices  20.1 us (17%)
  blocking collectives  15.7 us (13%)
    ppermute x22, starting transfers between devices, exchange(): return lax.ppermute(array, ('node', 'fsdp'), pairing(axis, first))  36.7 us
    pallas_call x7, Pallas kernels, product(): pl.pallas_call(functools.partial(product_kernel, which, rows, tile, coded...  17.7 us
    ppermute x22, waiting for transfers between devices, exchange(): return lax.ppermute(array, ('node', 'fsdp'), pairing(axis, first))  17.5 us
    all_to_all x1, blocking collectives, local(): sums = lax.all_to_all(gram, ('node', 'fsdp'), 0, 0, tiled=True)  15.7 us
    ppermute x1, starting transfers between devices, local(): carr = lax.ppermute(across, 'node', [(i, i ^ 1) for i in range(2 * SIDE)])  10.6 us
    pallas_call x1, Pallas kernels, first(): pl.pallas_call(functools.partial(first_kernel, rows, tile), out_shape=[xt...  6.57 us
    pallas_call x5, Pallas kernels, merge(): pl.pallas_call(functools.partial(kernel, rows, tile), out_shape=outs, in_...  5.7 us
    ppermute x1, starting transfers between devices, local(): far = lax.ppermute(far, 'node', [(i, i ^ 4) for i in range(2 * SIDE)])  2.99 us
  transfers between devices with their start and end apart: 24, of which 9 were waited for; matrix products, arithmetic and copies ran while one was open for 0% of the time, Pallas kernels for 21%

profile of v8, /device:TPU:1, one launch (start us, length us, event | category | flops | bytes accessed | tf_op | source)
XLA Modules:
  0.0 120.9 jit_solution(16583507883031938055)
XLA Ops:
  0.0 6.6 %p1a_near.1 = (bf16[2560,1024]{1,0:T(8,128)(2,1)S(1)}, bf16[1024,2560]{1,0:T(8,128)(2,1)S(1)}, bf16[3232,128]{1,0:T(8,128)(2,1)S(1)}, bf16[3232,128]{1,0:T(8,128)(2,1)S(1)}) custom-call(bf16[1024,2560]{1,0:T(8,128)(2,1)} %x_ref.1, bf16[1024,2560]{1,0:T(8,128)(2,1)} %dy_ref.1), custom_call_target="tpu_custom_call" | custom-call | tf_op jit(solution)/shard_map/p1a_near/pallas_call | solution.py:244
  6.6 3.4 %collective-permute-start.8 = (bf16[3232,128]{1,0:T(8,128)(2,1)S(1)}, bf16[3232,128]{1,0:T(8,128)(2,1)S(1)}, u32[]{:S(2)}, u32[]{:S(2)}) collective-permute-start(bf16[3232,128]{1,0:T(8,128)(2,1)S(1)} %get-tuple-element.35.rest_0_), channel_id=1, source_target_pairs={{0,1},{1,0},{2,3},{3,2},{4,5},{5,4},{6,7},{7,6},{8,9},{9,8},{10,11... | collective-permute-start | bytes 2482184 | tf_op jit(solution)/shard_map/ppermute | solution.py:128
  10.0 3.8 %collective-permute-start.9 = (bf16[3232,128]{1,0:T(8,128)(2,1)S(1)}, bf16[3232,128]{1,0:T(8,128)(2,1)S(1)}, u32[]{:S(2)}, u32[]{:S(2)}) collective-permute-start(bf16[3232,128]{1,0:T(8,128)(2,1)S(1)} %get-tuple-element.36.rest_1_), channel_id=1, source_target_pairs={{0,4},{1,5},{2,6},{3,7},{4,0},{5,1},{6,2},{7,3},{8,12},{9,13},{10,... | collective-permute-start | bytes 2482184 | tf_op jit(solution)/shard_map/ppermute | solution.py:128
  13.7 2.3 %p1a_far.1 = (bf16[3232,128]{1,0:T(8,128)(2,1)S(1)}, bf16[3232,128]{1,0:T(8,128)(2,1)S(1)}) custom-call(bf16[2560,1024]{1,0:T(8,128)(2,1)S(1)} %get-tuple-element.33.xt_ref, bf16[1024,2560]{1,0:T(8,128)(2,1)S(1)} %get-tuple-element.34.dy_ref, bf16[3232,128]{1,0:T(8,128)(2,1)S(1)} %get-tuple-element.35.rest_0_, bf16[3232,128]{1,0:T(8,128)(2,1)S(1)} %get-tuple-element.36.rest_1_), custom_call_target="tpu_custom_call" | custom-call | tf_op jit(solution)/shard_map/p1a_far/pallas_call | solution.py:230
  16.0 0.3 collective-permute-start
  16.3 2.3 %p1b_near.1 = (bf16[3232,128]{1,0:T(8,128)(2,1)S(1)}, bf16[3232,128]{1,0:T(8,128)(2,1)S(1)}) custom-call(bf16[2560,1024]{1,0:T(8,128)(2,1)S(1)} %get-tuple-element.33.xt_ref, bf16[1024,2560]{1,0:T(8,128)(2,1)S(1)} %get-tuple-element.34.dy_ref, bf16[3232,128]{1,0:T(8,128)(2,1)S(1)} %get-tuple-element.37.rest_0_, bf16[3232,128]{1,0:T(8,128)(2,1)S(1)} %get-tuple-element.38.rest_1_), custom_call_target="tpu_custom_call" | custom-call | tf_op jit(solution)/shard_map/p1b_near/pallas_call | solution.py:230
  18.6 2.6 %collective-permute-start.6 = (bf16[3232,128]{1,0:T(8,128)(2,1)S(1)}, bf16[3232,128]{1,0:T(8,128)(2,1)S(1)}, u32[]{:S(2)}, u32[]{:S(2)}) collective-permute-start(bf16[3232,128]{1,0:T(8,128)(2,1)S(1)} %get-tuple-element.45), channel_id=1, source_target_pairs={{0,1},{1,0},{2,3},{3,2},{4,5},{5,4},{6,7},{7,6},{8,9},{9,8},{10,11... | collective-permute-start | bytes 2482184 | tf_op jit(solution)/shard_map/ppermute | solution.py:128
  21.2 2.7 %collective-permute-start.7 = (bf16[3232,128]{1,0:T(8,128)(2,1)S(1)}, bf16[3232,128]{1,0:T(8,128)(2,1)S(1)}, u32[]{:S(2)}, u32[]{:S(2)}) collective-permute-start(bf16[3232,128]{1,0:T(8,128)(2,1)S(1)} %get-tuple-element.46), channel_id=1, source_target_pairs={{0,4},{1,5},{2,6},{3,7},{4,0},{5,1},{6,2},{7,3},{8,12},{9,13},{10,... | collective-permute-start | bytes 2482184 | tf_op jit(solution)/shard_map/ppermute | solution.py:128
  23.9 3.2 %p2_near.1 = (bf16[3232,128]{1,0:T(8,128)(2,1)S(1)}, bf16[3232,128]{1,0:T(8,128)(2,1)S(1)}) custom-call(bf16[2560,1024]{1,0:T(8,128)(2,1)S(1)} %get-tuple-element.33.xt_ref, bf16[1024,2560]{1,0:T(8,128)(2,1)S(1)} %get-tuple-element.34.dy_ref, bf16[3232,128]{1,0:T(8,128)(2,1)S(1)} %collective-permute-done.8.rest_0_.rest_2_, ...), custom_call_target="tpu_custom_call" | custom-call | tf_op jit(solution)/shard_map/p2_near/pallas_call | solution.py:230
  27.1 0.4 collective-permute-start.10
  27.5 1.1 collective-permute-done.rest_0_
  28.7 1.8 %collective-permute-start.11 = (bf16[3232,128]{1,0:T(8,128)(2,1)S(1)}, bf16[3232,128]{1,0:T(8,128)(2,1)S(1)}, u32[]{:S(2)}, u32[]{:S(2)}) collective-permute-start(bf16[3232,128]{1,0:T(8,128)(2,1)S(1)} %get-tuple-element.50), channel_id=1, source_target_pairs={{0,12},{1,13},{2,14},{3,15},{4,8},{5,9},{6,10},{7,11},{8,4},{9,5},... | collective-permute-start | bytes 2482184 | tf_op jit(solution)/shard_map/ppermute | solution.py:128
  30.5 2.2 %collective-permute-done.1.rest_1_ = bf16[3232,128]{1,0:T(8,128)(2,1)S(1)} collective-permute-done((bf16[3232,128]{1,0:T(8,128)(2,1)S(1)}, bf16[3232,128]{1,0:T(8,128)(2,1)S(1)}, u32[]{:S(2)}, u32[]{:S(2)}) %collective-permute-start.1) | collective-permute-done | bytes 827424 | tf_op jit(solution)/shard_map/ppermute | solution.py:128
  32.7 2.3 %p1b_far.1 = (bf16[3232,128]{1,0:T(8,128)(2,1)S(1)}, bf16[3232,128]{1,0:T(8,128)(2,1)S(1)}) custom-call(bf16[2560,1024]{1,0:T(8,128)(2,1)S(1)} %get-tuple-element.33.xt_ref, bf16[1024,2560]{1,0:T(8,128)(2,1)S(1)} %get-tuple-element.34.dy_ref, bf16[3232,128]{1,0:T(8,128)(2,1)S(1)} %collective-permute-done.rest_0_, ...), custom_call_target="tpu_custom_call" | custom-call | tf_op jit(solution)/shard_map/p1b_far/pallas_call | solution.py:230
  35.0 0.3 collective-permute-start.2
  35.3 9.8 %collective-permute-done.6.rest_0_.rest_2_ = bf16[3232,128]{1,0:T(8,128)(2,1)S(1)} collective-permute-done((bf16[3232,128]{1,0:T(8,128)(2,1)S(1)}, bf16[3232,128]{1,0:T(8,128)(2,1)S(1)}, u32[]{:S(2)}, u32[]{:S(2)}) %collective-permute-start.6) | collective-permute-done | bytes 827424 | tf_op jit(solution)/shard_map/ppermute | solution.py:128
  45.2 4.6 %collective-permute-start.3 = (bf16[3232,128]{1,0:T(8,128)(2,1)S(1)}, bf16[3232,128]{1,0:T(8,128)(2,1)S(1)}, u32[]{:S(2)}, u32[]{:S(2)}) collective-permute-start(bf16[3232,128]{1,0:T(8,128)(2,1)S(1)} %get-tuple-element.40.rest_3_), channel_id=1, source_target_pairs={{0,4},{1,5},{2,6},{3,7},{4,0},{5,1},{6,2},{7,3},{8,12},{9,13},{10,... | collective-permute-start | bytes 2482184 | tf_op jit(solution)/shard_map/ppermute | solution.py:128
  49.7 3.2 %p2_far.1 = (bf16[3232,128]{1,0:T(8,128)(2,1)S(1)}, bf16[3232,128]{1,0:T(8,128)(2,1)S(1)}) custom-call(bf16[2560,1024]{1,0:T(8,128)(2,1)S(1)} %get-tuple-element.33.xt_ref, bf16[1024,2560]{1,0:T(8,128)(2,1)S(1)} %get-tuple-element.34.dy_ref, bf16[3232,128]{1,0:T(8,128)(2,1)S(1)} %collective-permute-done.rest_0_, ...), custom_call_target="tpu_custom_call" | custom-call | tf_op jit(solution)/shard_map/p2_far/pallas_call | solution.py:230
  53.0 0.9 collective-permute-start.4
  53.9 2.2 %kept_near.1 = (f32[160,2560]{1,0:T(8,128)S(1)}, f32[160,2560]{1,0:T(8,128)S(1)}) custom-call(bf16[2560,1024]{1,0:T(8,128)(2,1)S(1)} %get-tuple-element.33.xt_ref, bf16[1024,2560]{1,0:T(8,128)(2,1)S(1)} %get-tuple-element.34.dy_ref, bf16[3232,128]{1,0:T(8,128)(2,1)S(1)} %collective-permute-done.6.rest_0_.rest_2_, ...), custom_call_target="tpu_custom_call" | custom-call | tf_op jit(solution)/shard_map/kept_near/pallas_call | solution.py:230
  56.1 1.1 q1_near.1
  57.4 2.5 %collective-permute-start.15 = (bf16[1632,128]{1,0:T(8,128)(2,1)S(1)}, bf16[1632,128]{1,0:T(8,128)(2,1)S(1)}, u32[]{:S(2)}, u32[]{:S(2)}) collective-permute-start(bf16[1632,128]{1,0:T(8,128)(2,1)S(1)} %get-tuple-element.54), channel_id=1, source_target_pairs={{0,1},{1,0},{2,3},{3,2},{4,5},{5,4},{6,7},{7,6},{8,9},{9,8},{10,11... | collective-permute-start | bytes 1253384 | tf_op jit(solution)/shard_map/ppermute | solution.py:128
  60.0 1.1 q1_far.1
  61.2 3.2 %collective-permute-start.12 = (bf16[1632,128]{1,0:T(8,128)(2,1)S(1)}, bf16[1632,128]{1,0:T(8,128)(2,1)S(1)}, u32[]{:S(2)}, u32[]{:S(2)}) collective-permute-start(bf16[1632,128]{1,0:T(8,128)(2,1)S(1)} %get-tuple-element.51), channel_id=1, source_target_pairs={{0,4},{1,5},{2,6},{3,7},{4,0},{5,1},{6,2},{7,3},{8,12},{9,13},{10,... | collective-permute-start | bytes 1253384 | tf_op jit(solution)/shard_map/ppermute | solution.py:128
  64.4 0.3 collective-permute-done.4.p0
  64.6 5.8 %collective-permute-start.13 = (bf16[1632,128]{1,0:T(8,128)(2,1)S(1)}, bf16[1632,128]{1,0:T(8,128)(2,1)S(1)}, u32[]{:S(2)}, u32[]{:S(2)}) collective-permute-start(bf16[1632,128]{1,0:T(8,128)(2,1)S(1)} %get-tuple-element.52), channel_id=1, source_target_pairs={{0,1},{1,0},{2,3},{3,2},{4,5},{5,4},{6,7},{7,6},{8,9},{9,8},{10,11... | collective-permute-start | bytes 1253384 | tf_op jit(solution)/shard_map/ppermute | solution.py:128
  70.4 2.2 %kept_far.1 = (f32[160,2560]{1,0:T(8,128)S(1)}, f32[160,2560]{1,0:T(8,128)S(1)}) custom-call(bf16[2560,1024]{1,0:T(8,128)(2,1)S(1)} %get-tuple-element.33.xt_ref, bf16[1024,2560]{1,0:T(8,128)(2,1)S(1)} %get-tuple-element.34.dy_ref, bf16[3232,128]{1,0:T(8,128)(2,1)S(1)} %collective-permute-done.2.rest_0_.rest_2_, ...), custom_call_target="tpu_custom_call" | custom-call | tf_op jit(solution)/shard_map/kept_far/pallas_call | solution.py:230
  72.6 1.1 q2_early.1
  73.7 1.7 %collective-permute-start.18 = (bf16[816,128]{1,0:T(8,128)(2,1)S(1)}, bf16[816,128]{1,0:T(8,128)(2,1)S(1)}, u32[]{:S(2)}, u32[]{:S(2)}) collective-permute-start(bf16[816,128]{1,0:T(8,128)(2,1)S(1)} %get-tuple-element.55.rest_0_), channel_id=1, source_target_pairs={{0,12},{1,13},{2,14},{3,15},{4,8},{5,9},{6,10},{7,11},{8,4},{9,5},... | collective-permute-start | bytes 626696 | tf_op jit(solution)/shard_map/ppermute | solution.py:128
  75.5 0.7 collective-permute-start.19
  76.2 1.0 q2_late.1
  77.2 0.7 collective-permute-start.16
  78.2 1.3 %own.1 = f32[160,2560]{1,0:T(8,128)S(1)} custom-call(f32[160,2560]{1,0:T(8,128)S(1)} %get-tuple-element.41.kept0, f32[160,2560]{1,0:T(8,128)S(1)} %get-tuple-element.42.kept1, bf16[3232,128]{1,0:T(8,128)(2,1)S(1)} %collective-permute-done.4.p0, bf16[3232,128]{1,0:T(8,128)(2,1)S(1)} %collective-permute-done.5.p1, ...), custom_call_target="tpu_custom_call" | custom-call | tf_op jit(solution)/shard_map/own/pallas_call | solution.py:308
  79.5 0.6 collective-permute-done.19.arr1
  80.1 0.3 last_far.1.rest_0_
  80.4 3.0 %collective-permute-start.22 = (bf16[168,640]{1,0:T(8,128)(2,1)S(1)}, bf16[168,640]{1,0:T(8,128)(2,1)S(1)}, u32[]{:S(2)}, u32[]{:S(2)}) collective-permute-start(bf16[168,640]{1,0:T(8,128)(2,1)S(1)} %last_far.1.rest_0_), channel_id=1, source_target_pairs={{0,64},{16,80},{32,96},{48,112},{64,0},{80,16},{96,32},{112,48},{1... | collective-permute-start | bytes 645128 | tf_op jit(solution)/shard_map/ppermute | solution.py:472
  83.4 0.3 last_near1.1.rest_0_
  83.7 0.9 collective-permute-start.20
  84.6 0.3 last_near2.1.rest_0_
  85.0 0.3 last_mine.1.own0.ref
  85.3 1.4 %collective-permute-done.22.own3.ref = bf16[168,640]{1,0:T(8,128)(2,1)S(1)} collective-permute-done((bf16[168,640]{1,0:T(8,128)(2,1)S(1)}, bf16[168,640]{1,0:T(8,128)(2,1)S(1)}, u32[]{:S(2)}, u32[]{:S(2)}) %collective-permute-start.22) | collective-permute-done | bytes 215072 | tf_op jit(solution)/shard_map/ppermute | solution.py:472
  86.7 3.3 %collective-permute-done.20.own1.ref = bf16[168,640]{1,0:T(8,128)(2,1)S(1)} collective-permute-done((bf16[168,640]{1,0:T(8,128)(2,1)S(1)}, bf16[168,640]{1,0:T(8,128)(2,1)S(1)}, u32[]{:S(2)}, u32[]{:S(2)}) %collective-permute-start.20) | collective-permute-done | bytes 215072 | tf_op jit(solution)/shard_map/ppermute | solution.py:128
  90.2 10.6 %collective-permute-start.23 = (bf16[4,168,384]{2,1,0:T(8,128)(2,1)S(1)}, bf16[4,168,384]{2,1,0:T(8,128)(2,1)S(1)}, u32[]{:S(2)}, u32[]{:S(2)}) collective-permute-start(bf16[4,168,384]{2,1,0:T(8,128)(2,1)S(1)} %pad_maximum_fusion), channel_id=1, source_target_pairs={{0,16},{16,0},{32,48},{48,32},{64,80},{80,64},{96,112},{112,96},{1... | collective-permute-start | bytes 1548296 | tf_op jit(solution)/shard_map/ppermute | solution.py:490
  100.8 0.4 held.1
  101.2 1.1 collective-permute-done.23.carr
  102.3 1.3 %gram.1 = (f32[8,160,384]{2,1,0:T(8,128)S(1)}, f32[128,128]{1,0:T(8,128)S(1)}) custom-call(f32[4,160,384]{2,1,0:T(8,128)S(1)} %held.1, bf16[4,168,384]{2,1,0:T(8,128)(2,1)S(1)} %collective-permute-done.23.carr), custom_call_target="tpu_custom_call" | custom-call | tf_op jit(solution)/shard_map/gram/pallas_call | solution.py:500
  103.7 15.7 %all_to_all.11 = f32[128,1,128]{2,1,0:T(1,128)S(1)} all-to-all(f32[128,1,128]{2,1,0:T(1,128)S(1)} %bitcast.13), channel_id=1, replica_groups=mesh['node'=8,'fsdp'=16] {'node','fsdp'}, dimensions={0} | all-to-all | bytes 131072 | tf_op jit(solution)/shard_map/all_to_all | solution.py:509
  119.3 1.6 %combine.1 = f32[160,320]{1,0:T(8,128)} custom-call(f32[8,160,384]{2,1,0:T(8,128)S(1)} %get-tuple-element.59.g_ref, f32[128,128]{1,0:T(8,128)S(1)} %bitcast.12), custom_call_target="tpu_custom_call" | custom-call | tf_op jit(solution)/shard_map/combine/pallas_call | solution.py:510
  (26 shorter events, 0.9 us)
Async XLA Ops:
  6.6 14.6 %collective-permute-start.8 = (bf16[3232,128]{1,0:T(8,128)(2,1)S(1)}, bf16[3232,128]{1,0:T(8,128)(2,1)S(1)}, u32[]{:S(2)}, u32[]{:S(2)}) collective-permute-start(bf16[3232,128]{1,0:T(8,128)(2,1)S(1)} %get-tuple-element.35.rest_0_), channel_id=1, source_target_pairs={{0,1},{1,0},{2,3},{3,2},{4,5},{5,4},{6,7},{7,6},{8,9},{9,8},{10,11... | collective-permute-start | bytes 2482184 | tf_op jit(solution)/shard_map/ppermute | solution.py:128
  10.0 13.9 %collective-permute-start.9 = (bf16[3232,128]{1,0:T(8,128)(2,1)S(1)}, bf16[3232,128]{1,0:T(8,128)(2,1)S(1)}, u32[]{:S(2)}, u32[]{:S(2)}) collective-permute-start(bf16[3232,128]{1,0:T(8,128)(2,1)S(1)} %get-tuple-element.36.rest_1_), channel_id=1, source_target_pairs={{0,4},{1,5},{2,6},{3,7},{4,0},{5,1},{6,2},{7,3},{8,12},{9,13},{10,... | collective-permute-start | bytes 2482184 | tf_op jit(solution)/shard_map/ppermute | solution.py:128
  16.0 12.6 %collective-permute-start = (bf16[3232,128]{1,0:T(8,128)(2,1)S(1)}, bf16[3232,128]{1,0:T(8,128)(2,1)S(1)}, u32[]{:S(2)}, u32[]{:S(2)}) collective-permute-start(bf16[3232,128]{1,0:T(8,128)(2,1)S(1)} %get-tuple-element.37.rest_0_), channel_id=1, source_target_pairs={{0,1},{1,0},{2,3},{3,2},{4,5},{5,4},{6,7},{7,6},{8,9},{9,8},{10,11... | collective-permute-start | bytes 2482184 | tf_op jit(solution)/shard_map/ppermute | solution.py:128
  16.3 16.4 %collective-permute-start.1 = (bf16[3232,128]{1,0:T(8,128)(2,1)S(1)}, bf16[3232,128]{1,0:T(8,128)(2,1)S(1)}, u32[]{:S(2)}, u32[]{:S(2)}) collective-permute-start(bf16[3232,128]{1,0:T(8,128)(2,1)S(1)} %get-tuple-element.38.rest_1_), channel_id=1, source_target_pairs={{0,4},{1,5},{2,6},{3,7},{4,0},{5,1},{6,2},{7,3},{8,12},{9,13},{10,... | collective-permute-start | bytes 2482184 | tf_op jit(solution)/shard_map/ppermute | solution.py:128
  18.6 26.5 %collective-permute-start.6 = (bf16[3232,128]{1,0:T(8,128)(2,1)S(1)}, bf16[3232,128]{1,0:T(8,128)(2,1)S(1)}, u32[]{:S(2)}, u32[]{:S(2)}) collective-permute-start(bf16[3232,128]{1,0:T(8,128)(2,1)S(1)} %get-tuple-element.45), channel_id=1, source_target_pairs={{0,1},{1,0},{2,3},{3,2},{4,5},{5,4},{6,7},{7,6},{8,9},{9,8},{10,11... | collective-permute-start | bytes 2482184 | tf_op jit(solution)/shard_map/ppermute | solution.py:128
  21.2 31.8 %collective-permute-start.7 = (bf16[3232,128]{1,0:T(8,128)(2,1)S(1)}, bf16[3232,128]{1,0:T(8,128)(2,1)S(1)}, u32[]{:S(2)}, u32[]{:S(2)}) collective-permute-start(bf16[3232,128]{1,0:T(8,128)(2,1)S(1)} %get-tuple-element.46), channel_id=1, source_target_pairs={{0,4},{1,5},{2,6},{3,7},{4,0},{5,1},{6,2},{7,3},{8,12},{9,13},{10,... | collective-permute-start | bytes 2482184 | tf_op jit(solution)/shard_map/ppermute | solution.py:128
  27.1 26.8 %collective-permute-start.10 = (bf16[3232,128]{1,0:T(8,128)(2,1)S(1)}, bf16[3232,128]{1,0:T(8,128)(2,1)S(1)}, u32[]{:S(2)}, u32[]{:S(2)}) collective-permute-start(bf16[3232,128]{1,0:T(8,128)(2,1)S(1)} %get-tuple-element.49), channel_id=1, source_target_pairs={{0,3},{1,2},{2,1},{3,0},{4,7},{5,6},{6,5},{7,4},{8,11},{9,10},{10,... | collective-permute-start | bytes 2482184 | tf_op jit(solution)/shard_map/ppermute | solution.py:128
  28.7 27.4 %collective-permute-start.11 = (bf16[3232,128]{1,0:T(8,128)(2,1)S(1)}, bf16[3232,128]{1,0:T(8,128)(2,1)S(1)}, u32[]{:S(2)}, u32[]{:S(2)}) collective-permute-start(bf16[3232,128]{1,0:T(8,128)(2,1)S(1)} %get-tuple-element.50), channel_id=1, source_target_pairs={{0,12},{1,13},{2,14},{3,15},{4,8},{5,9},{6,10},{7,11},{8,4},{9,5},... | collective-permute-start | bytes 2482184 | tf_op jit(solution)/shard_map/ppermute | solution.py:128
  35.0 22.4 %collective-permute-start.2 = (bf16[3232,128]{1,0:T(8,128)(2,1)S(1)}, bf16[3232,128]{1,0:T(8,128)(2,1)S(1)}, u32[]{:S(2)}, u32[]{:S(2)}) collective-permute-start(bf16[3232,128]{1,0:T(8,128)(2,1)S(1)} %get-tuple-element.39.rest_2_), channel_id=1, source_target_pairs={{0,1},{1,0},{2,3},{3,2},{4,5},{5,4},{6,7},{7,6},{8,9},{9,8},{10,11... | collective-permute-start | bytes 2482184 | tf_op jit(solution)/shard_map/ppermute | solution.py:128
  45.2 14.9 %collective-permute-start.3 = (bf16[3232,128]{1,0:T(8,128)(2,1)S(1)}, bf16[3232,128]{1,0:T(8,128)(2,1)S(1)}, u32[]{:S(2)}, u32[]{:S(2)}) collective-permute-start(bf16[3232,128]{1,0:T(8,128)(2,1)S(1)} %get-tuple-element.40.rest_3_), channel_id=1, source_target_pairs={{0,4},{1,5},{2,6},{3,7},{4,0},{5,1},{6,2},{7,3},{8,12},{9,13},{10,... | collective-permute-start | bytes 2482184 | tf_op jit(solution)/shard_map/ppermute | solution.py:128
  53.0 11.7 %collective-permute-start.4 = (bf16[3232,128]{1,0:T(8,128)(2,1)S(1)}, bf16[3232,128]{1,0:T(8,128)(2,1)S(1)}, u32[]{:S(2)}, u32[]{:S(2)}) collective-permute-start(bf16[3232,128]{1,0:T(8,128)(2,1)S(1)} %get-tuple-element.43), channel_id=1, source_target_pairs={{0,3},{1,2},{2,1},{3,0},{4,7},{5,6},{6,5},{7,4},{8,11},{9,10},{10,... | collective-permute-start | bytes 2482184 | tf_op jit(solution)/shard_map/ppermute | solution.py:128
  53.9 18.7 %collective-permute-start.5 = (bf16[3232,128]{1,0:T(8,128)(2,1)S(1)}, bf16[3232,128]{1,0:T(8,128)(2,1)S(1)}, u32[]{:S(2)}, u32[]{:S(2)}) collective-permute-start(bf16[3232,128]{1,0:T(8,128)(2,1)S(1)} %get-tuple-element.44), channel_id=1, source_target_pairs={{0,12},{1,13},{2,14},{3,15},{4,8},{5,9},{6,10},{7,11},{8,4},{9,5},... | collective-permute-start | bytes 2482184 | tf_op jit(solution)/shard_map/ppermute | solution.py:128
  57.2 15.4 %collective-permute-start.14 = (bf16[1632,128]{1,0:T(8,128)(2,1)S(1)}, bf16[1632,128]{1,0:T(8,128)(2,1)S(1)}, u32[]{:S(2)}, u32[]{:S(2)}) collective-permute-start(bf16[1632,128]{1,0:T(8,128)(2,1)S(1)} %get-tuple-element.53), channel_id=1, source_target_pairs={{0,4},{1,5},{2,6},{3,7},{4,0},{5,1},{6,2},{7,3},{8,12},{9,13},{10,... | collective-permute-start | bytes 1253384 | tf_op jit(solution)/shard_map/ppermute | solution.py:128
  57.4 15.3 %collective-permute-start.15 = (bf16[1632,128]{1,0:T(8,128)(2,1)S(1)}, bf16[1632,128]{1,0:T(8,128)(2,1)S(1)}, u32[]{:S(2)}, u32[]{:S(2)}) collective-permute-start(bf16[1632,128]{1,0:T(8,128)(2,1)S(1)} %get-tuple-element.54), channel_id=1, source_target_pairs={{0,1},{1,0},{2,3},{3,2},{4,5},{5,4},{6,7},{7,6},{8,9},{9,8},{10,11... | collective-permute-start | bytes 1253384 | tf_op jit(solution)/shard_map/ppermute | solution.py:128
  61.2 16.7 %collective-permute-start.12 = (bf16[1632,128]{1,0:T(8,128)(2,1)S(1)}, bf16[1632,128]{1,0:T(8,128)(2,1)S(1)}, u32[]{:S(2)}, u32[]{:S(2)}) collective-permute-start(bf16[1632,128]{1,0:T(8,128)(2,1)S(1)} %get-tuple-element.51), channel_id=1, source_target_pairs={{0,4},{1,5},{2,6},{3,7},{4,0},{5,1},{6,2},{7,3},{8,12},{9,13},{10,... | collective-permute-start | bytes 1253384 | tf_op jit(solution)/shard_map/ppermute | solution.py:128
  64.6 13.5 %collective-permute-start.13 = (bf16[1632,128]{1,0:T(8,128)(2,1)S(1)}, bf16[1632,128]{1,0:T(8,128)(2,1)S(1)}, u32[]{:S(2)}, u32[]{:S(2)}) collective-permute-start(bf16[1632,128]{1,0:T(8,128)(2,1)S(1)} %get-tuple-element.52), channel_id=1, source_target_pairs={{0,1},{1,0},{2,3},{3,2},{4,5},{5,4},{6,7},{7,6},{8,9},{9,8},{10,11... | collective-permute-start | bytes 1253384 | tf_op jit(solution)/shard_map/ppermute | solution.py:128
  73.7 5.8 %collective-permute-start.18 = (bf16[816,128]{1,0:T(8,128)(2,1)S(1)}, bf16[816,128]{1,0:T(8,128)(2,1)S(1)}, u32[]{:S(2)}, u32[]{:S(2)}) collective-permute-start(bf16[816,128]{1,0:T(8,128)(2,1)S(1)} %get-tuple-element.55.rest_0_), channel_id=1, source_target_pairs={{0,12},{1,13},{2,14},{3,15},{4,8},{5,9},{6,10},{7,11},{8,4},{9,5},... | collective-permute-start | bytes 626696 | tf_op jit(solution)/shard_map/ppermute | solution.py:128
  75.5 4.7 %collective-permute-start.19 = (bf16[816,128]{1,0:T(8,128)(2,1)S(1)}, bf16[816,128]{1,0:T(8,128)(2,1)S(1)}, u32[]{:S(2)}, u32[]{:S(2)}) collective-permute-start(bf16[816,128]{1,0:T(8,128)(2,1)S(1)} %get-tuple-element.56.rest_1_), channel_id=1, source_target_pairs={{0,3},{1,2},{2,1},{3,0},{4,7},{5,6},{6,5},{7,4},{8,11},{9,10},{10,... | collective-permute-start | bytes 626696 | tf_op jit(solution)/shard_map/ppermute | solution.py:128
  77.2 7.3 %collective-permute-start.16 = (bf16[816,128]{1,0:T(8,128)(2,1)S(1)}, bf16[816,128]{1,0:T(8,128)(2,1)S(1)}, u32[]{:S(2)}, u32[]{:S(2)}) collective-permute-start(bf16[816,128]{1,0:T(8,128)(2,1)S(1)} %get-tuple-element.57), channel_id=1, source_target_pairs={{0,12},{1,13},{2,14},{3,15},{4,8},{5,9},{6,10},{7,11},{8,4},{9,5},... | collective-permute-start | bytes 626696 | tf_op jit(solution)/shard_map/ppermute | solution.py:128
  77.9 6.7 %collective-permute-start.17 = (bf16[816,128]{1,0:T(8,128)(2,1)S(1)}, bf16[816,128]{1,0:T(8,128)(2,1)S(1)}, u32[]{:S(2)}, u32[]{:S(2)}) collective-permute-start(bf16[816,128]{1,0:T(8,128)(2,1)S(1)} %get-tuple-element.58), channel_id=1, source_target_pairs={{0,3},{1,2},{2,1},{3,0},{4,7},{5,6},{6,5},{7,4},{8,11},{9,10},{10,... | collective-permute-start | bytes 626696 | tf_op jit(solution)/shard_map/ppermute | solution.py:128
  80.4 6.3 %collective-permute-start.22 = (bf16[168,640]{1,0:T(8,128)(2,1)S(1)}, bf16[168,640]{1,0:T(8,128)(2,1)S(1)}, u32[]{:S(2)}, u32[]{:S(2)}) collective-permute-start(bf16[168,640]{1,0:T(8,128)(2,1)S(1)} %last_far.1.rest_0_), channel_id=1, source_target_pairs={{0,64},{16,80},{32,96},{48,112},{64,0},{80,16},{96,32},{112,48},{1... | collective-permute-start | bytes 645128 | tf_op jit(solution)/shard_map/ppermute | solution.py:472
  83.7 6.3 %collective-permute-start.20 = (bf16[168,640]{1,0:T(8,128)(2,1)S(1)}, bf16[168,640]{1,0:T(8,128)(2,1)S(1)}, u32[]{:S(2)}, u32[]{:S(2)}) collective-permute-start(bf16[168,640]{1,0:T(8,128)(2,1)S(1)} %last_near1.1.rest_0_), channel_id=1, source_target_pairs={{0,32},{1,33},{2,34},{3,35},{4,36},{5,37},{6,38},{7,39},{8,40},{9,... | collective-permute-start | bytes 645128 | tf_op jit(solution)/shard_map/ppermute | solution.py:128
  84.9 5.2 %collective-permute-start.21 = (bf16[168,640]{1,0:T(8,128)(2,1)S(1)}, bf16[168,640]{1,0:T(8,128)(2,1)S(1)}, u32[]{:S(2)}, u32[]{:S(2)}) collective-permute-start(bf16[168,640]{1,0:T(8,128)(2,1)S(1)} %last_near2.1.rest_0_), channel_id=1, source_target_pairs={{0,96},{1,97},{2,98},{3,99},{4,100},{5,101},{6,102},{7,103},{8,104... | collective-permute-start | bytes 645128 | tf_op jit(solution)/shard_map/ppermute | solution.py:128
  90.2 12.1 %collective-permute-start.23 = (bf16[4,168,384]{2,1,0:T(8,128)(2,1)S(1)}, bf16[4,168,384]{2,1,0:T(8,128)(2,1)S(1)}, u32[]{:S(2)}, u32[]{:S(2)}) collective-permute-start(bf16[4,168,384]{2,1,0:T(8,128)(2,1)S(1)} %pad_maximum_fusion), channel_id=1, source_target_pairs={{0,16},{16,0},{32,48},{48,32},{64,80},{80,64},{96,112},{112,96},{1... | collective-permute-start | bytes 1548296 | tf_op jit(solution)/shard_map/ppermute | solution.py:490

commit v9 on v8

--- a/solution.py
+++ b/solution.py
@@ -339,10 +339,15 @@
 
 
 def cut_kernel(ref, *rest):
-    out = rest[-1]
-    wide = out.shape[1]
+    cuts, out = rest[:-1], rest[-1]
+    wide = out.shape[-1]
     at = pl.ds(pl.multiple_of((ref.shape[1] - wide) * (1 - coordinates()[3]), LANES), wide)
-    out[...] = ref[:, at]
+    if len(cuts) < 3:
+        out[...] = ref[:, at]
+        return
+    out[2] = ref[:, at]
+    for k, held in zip((0, 1, 3), cuts):
+        out[k] = held[...]
 
 
 def own_columns(half, wide, core):
@@ -473,20 +478,20 @@
     near1 = exchange(near1, "y", True)
     near2 = exchange(near2, "y", False)
     blocks = [mine, near1, near2, far]
-    cuts, before = [], []
-    for name, k in (("far", 3), ("near1", 1), ("near2", 2), ("mine", 0)):
-        cut = pl.pallas_call(
+    def cut(name, block, before):
+        shape = (block.shape[0], wide)
+        return pl.pallas_call(
             cut_kernel,
-            out_shape=jax.ShapeDtypeStruct((blocks[0].shape[0], wide), BF16),
-            in_specs=[VMEM] + [pl.BlockSpec(memory_space=pl.ANY)] * len(before),
+            out_shape=jax.ShapeDtypeStruct(shape if len(before) < 3 else (SIDE, *shape), BF16),
+            in_specs=[VMEM] * (1 + len(before)),
             out_specs=VMEM,
             compiler_params=params(12),
             name="cut_" + name,
-        )(blocks[k], *before)
-        before = [cut] if name != "near2" else before
-        cuts.append(cut)
-    far_cut, near1_cut, near2_cut, mine_cut = cuts
-    across = jnp.stack([mine_cut, near1_cut, near2_cut, far_cut])
+        )(block, *before)
+
+    far_cut = cut("far", far, [])
+    near1_cut = cut("near1", near1, [far_cut])
+    across = cut("near2", near2, [cut("mine", mine, []), near1_cut, far_cut])
     carr = lax.ppermute(across, "node", [(i, i ^ 1) for i in range(2 * SIDE)])
     count = 2 * SIDE * SIDE * SIDE
     held = pl.pallas_call(

time: 121 us -> 121 us (level)
  no operation moved by 1% of the time
where the time goes in v9:
time: 121 us
  starting transfers between devices  50.3 us (42%)
  Pallas kernels  34.7 us (29%)
  waiting for transfers between devices  20 us (17%)
  blocking collectives  15.7 us (13%)
    ppermute x22, starting transfers between devices, exchange(): return lax.ppermute(array, ('node', 'fsdp'), pairing(axis, first))  36.7 us
    pallas_call x7, Pallas kernels, product(): pl.pallas_call(functools.partial(product_kernel, which, rows, tile, coded...  17.7 us
    ppermute x22, waiting for transfers between devices, exchange(): return lax.ppermute(array, ('node', 'fsdp'), pairing(axis, first))  17.5 us
    all_to_all x1, blocking collectives, local(): sums = lax.all_to_all(gram, ('node', 'fsdp'), 0, 0, tiled=True)  15.7 us
    ppermute x1, starting transfers between devices, local(): carr = lax.ppermute(across, 'node', [(i, i ^ 1) for i in range(2 * SIDE)])  10.6 us
    pallas_call x1, Pallas kernels, first(): pl.pallas_call(functools.partial(first_kernel, rows, tile), out_shape=[xt...  6.57 us
    pallas_call x5, Pallas kernels, merge(): pl.pallas_call(functools.partial(kernel, rows, tile), out_shape=outs, in_...  5.7 us
    ppermute x1, starting transfers between devices, local(): far = lax.ppermute(far, 'node', [(i, i ^ 4) for i in range(2 * SIDE)])  2.99 us
  transfers between devices with their start and end apart: 24, of which 9 were waited for; matrix products, arithmetic and copies ran while one was open for 0% of the time, Pallas kernels for 21%

profile of v9, /device:TPU:1, one launch (start us, length us, event | category | flops | bytes accessed | tf_op | source)
XLA Modules:
  0.0 120.9 jit_solution(9323611959162988561)
XLA Ops:
  0.0 6.6 %p1a_near.1 = (bf16[2560,1024]{1,0:T(8,128)(2,1)S(1)}, bf16[1024,2560]{1,0:T(8,128)(2,1)S(1)}, bf16[3232,128]{1,0:T(8,128)(2,1)S(1)}, bf16[3232,128]{1,0:T(8,128)(2,1)S(1)}) custom-call(bf16[1024,2560]{1,0:T(8,128)(2,1)} %x_ref.1, bf16[1024,2560]{1,0:T(8,128)(2,1)} %dy_ref.1), custom_call_target="tpu_custom_call" | custom-call | tf_op jit(solution)/shard_map/p1a_near/pallas_call | solution.py:244
  6.6 3.4 %collective-permute-start.8 = (bf16[3232,128]{1,0:T(8,128)(2,1)S(1)}, bf16[3232,128]{1,0:T(8,128)(2,1)S(1)}, u32[]{:S(2)}, u32[]{:S(2)}) collective-permute-start(bf16[3232,128]{1,0:T(8,128)(2,1)S(1)} %get-tuple-element.35.rest_0_), channel_id=1, source_target_pairs={{0,1},{1,0},{2,3},{3,2},{4,5},{5,4},{6,7},{7,6},{8,9},{9,8},{10,11... | collective-permute-start | bytes 2482184 | tf_op jit(solution)/shard_map/ppermute | solution.py:128
  10.0 3.8 %collective-permute-start.9 = (bf16[3232,128]{1,0:T(8,128)(2,1)S(1)}, bf16[3232,128]{1,0:T(8,128)(2,1)S(1)}, u32[]{:S(2)}, u32[]{:S(2)}) collective-permute-start(bf16[3232,128]{1,0:T(8,128)(2,1)S(1)} %get-tuple-element.36.rest_1_), channel_id=1, source_target_pairs={{0,4},{1,5},{2,6},{3,7},{4,0},{5,1},{6,2},{7,3},{8,12},{9,13},{10,... | collective-permute-start | bytes 2482184 | tf_op jit(solution)/shard_map/ppermute | solution.py:128
  13.7 2.3 %p1a_far.1 = (bf16[3232,128]{1,0:T(8,128)(2,1)S(1)}, bf16[3232,128]{1,0:T(8,128)(2,1)S(1)}) custom-call(bf16[2560,1024]{1,0:T(8,128)(2,1)S(1)} %get-tuple-element.33.xt_ref, bf16[1024,2560]{1,0:T(8,128)(2,1)S(1)} %get-tuple-element.34.dy_ref, bf16[3232,128]{1,0:T(8,128)(2,1)S(1)} %get-tuple-element.35.rest_0_, bf16[3232,128]{1,0:T(8,128)(2,1)S(1)} %get-tuple-element.36.rest_1_), custom_call_target="tpu_custom_call" | custom-call | tf_op jit(solution)/shard_map/p1a_far/pallas_call | solution.py:230
  16.0 0.3 collective-permute-start
  16.3 2.3 %p1b_near.1 = (bf16[3232,128]{1,0:T(8,128)(2,1)S(1)}, bf16[3232,128]{1,0:T(8,128)(2,1)S(1)}) custom-call(bf16[2560,1024]{1,0:T(8,128)(2,1)S(1)} %get-tuple-element.33.xt_ref, bf16[1024,2560]{1,0:T(8,128)(2,1)S(1)} %get-tuple-element.34.dy_ref, bf16[3232,128]{1,0:T(8,128)(2,1)S(1)} %get-tuple-element.37.rest_0_, bf16[3232,128]{1,0:T(8,128)(2,1)S(1)} %get-tuple-element.38.rest_1_), custom_call_target="tpu_custom_call" | custom-call | tf_op jit(solution)/shard_map/p1b_near/pallas_call | solution.py:230
  18.6 2.6 %collective-permute-start.6 = (bf16[3232,128]{1,0:T(8,128)(2,1)S(1)}, bf16[3232,128]{1,0:T(8,128)(2,1)S(1)}, u32[]{:S(2)}, u32[]{:S(2)}) collective-permute-start(bf16[3232,128]{1,0:T(8,128)(2,1)S(1)} %get-tuple-element.45), channel_id=1, source_target_pairs={{0,1},{1,0},{2,3},{3,2},{4,5},{5,4},{6,7},{7,6},{8,9},{9,8},{10,11... | collective-permute-start | bytes 2482184 | tf_op jit(solution)/shard_map/ppermute | solution.py:128
  21.2 2.7 %collective-permute-start.7 = (bf16[3232,128]{1,0:T(8,128)(2,1)S(1)}, bf16[3232,128]{1,0:T(8,128)(2,1)S(1)}, u32[]{:S(2)}, u32[]{:S(2)}) collective-permute-start(bf16[3232,128]{1,0:T(8,128)(2,1)S(1)} %get-tuple-element.46), channel_id=1, source_target_pairs={{0,4},{1,5},{2,6},{3,7},{4,0},{5,1},{6,2},{7,3},{8,12},{9,13},{10,... | collective-permute-start | bytes 2482184 | tf_op jit(solution)/shard_map/ppermute | solution.py:128
  23.9 3.2 %p2_near.1 = (bf16[3232,128]{1,0:T(8,128)(2,1)S(1)}, bf16[3232,128]{1,0:T(8,128)(2,1)S(1)}) custom-call(bf16[2560,1024]{1,0:T(8,128)(2,1)S(1)} %get-tuple-element.33.xt_ref, bf16[1024,2560]{1,0:T(8,128)(2,1)S(1)} %get-tuple-element.34.dy_ref, bf16[3232,128]{1,0:T(8,128)(2,1)S(1)} %collective-permute-done.8.rest_0_.rest_2_, ...), custom_call_target="tpu_custom_call" | custom-call | tf_op jit(solution)/shard_map/p2_near/pallas_call | solution.py:230
  27.1 0.4 collective-permute-start.10
  27.5 1.1 collective-permute-done.rest_0_
  28.7 1.8 %collective-permute-start.11 = (bf16[3232,128]{1,0:T(8,128)(2,1)S(1)}, bf16[3232,128]{1,0:T(8,128)(2,1)S(1)}, u32[]{:S(2)}, u32[]{:S(2)}) collective-permute-start(bf16[3232,128]{1,0:T(8,128)(2,1)S(1)} %get-tuple-element.50), channel_id=1, source_target_pairs={{0,12},{1,13},{2,14},{3,15},{4,8},{5,9},{6,10},{7,11},{8,4},{9,5},... | collective-permute-start | bytes 2482184 | tf_op jit(solution)/shard_map/ppermute | solution.py:128
  30.5 2.2 %collective-permute-done.1.rest_1_ = bf16[3232,128]{1,0:T(8,128)(2,1)S(1)} collective-permute-done((bf16[3232,128]{1,0:T(8,128)(2,1)S(1)}, bf16[3232,128]{1,0:T(8,128)(2,1)S(1)}, u32[]{:S(2)}, u32[]{:S(2)}) %collective-permute-start.1) | collective-permute-done | bytes 827424 | tf_op jit(solution)/shard_map/ppermute | solution.py:128
  32.7 2.3 %p1b_far.1 = (bf16[3232,128]{1,0:T(8,128)(2,1)S(1)}, bf16[3232,128]{1,0:T(8,128)(2,1)S(1)}) custom-call(bf16[2560,1024]{1,0:T(8,128)(2,1)S(1)} %get-tuple-element.33.xt_ref, bf16[1024,2560]{1,0:T(8,128)(2,1)S(1)} %get-tuple-element.34.dy_ref, bf16[3232,128]{1,0:T(8,128)(2,1)S(1)} %collective-permute-done.rest_0_, ...), custom_call_target="tpu_custom_call" | custom-call | tf_op jit(solution)/shard_map/p1b_far/pallas_call | solution.py:230
  35.0 0.3 collective-permute-start.2
  35.3 9.8 %collective-permute-done.6.rest_0_.rest_2_ = bf16[3232,128]{1,0:T(8,128)(2,1)S(1)} collective-permute-done((bf16[3232,128]{1,0:T(8,128)(2,1)S(1)}, bf16[3232,128]{1,0:T(8,128)(2,1)S(1)}, u32[]{:S(2)}, u32[]{:S(2)}) %collective-permute-start.6) | collective-permute-done | bytes 827424 | tf_op jit(solution)/shard_map/ppermute | solution.py:128
  45.2 4.6 %collective-permute-start.3 = (bf16[3232,128]{1,0:T(8,128)(2,1)S(1)}, bf16[3232,128]{1,0:T(8,128)(2,1)S(1)}, u32[]{:S(2)}, u32[]{:S(2)}) collective-permute-start(bf16[3232,128]{1,0:T(8,128)(2,1)S(1)} %get-tuple-element.40.rest_3_), channel_id=1, source_target_pairs={{0,4},{1,5},{2,6},{3,7},{4,0},{5,1},{6,2},{7,3},{8,12},{9,13},{10,... | collective-permute-start | bytes 2482184 | tf_op jit(solution)/shard_map/ppermute | solution.py:128
  49.7 3.2 %p2_far.1 = (bf16[3232,128]{1,0:T(8,128)(2,1)S(1)}, bf16[3232,128]{1,0:T(8,128)(2,1)S(1)}) custom-call(bf16[2560,1024]{1,0:T(8,128)(2,1)S(1)} %get-tuple-element.33.xt_ref, bf16[1024,2560]{1,0:T(8,128)(2,1)S(1)} %get-tuple-element.34.dy_ref, bf16[3232,128]{1,0:T(8,128)(2,1)S(1)} %collective-permute-done.rest_0_, ...), custom_call_target="tpu_custom_call" | custom-call | tf_op jit(solution)/shard_map/p2_far/pallas_call | solution.py:230
  53.0 0.9 collective-permute-start.4
  53.9 2.2 %kept_near.1 = (f32[160,2560]{1,0:T(8,128)S(1)}, f32[160,2560]{1,0:T(8,128)S(1)}) custom-call(bf16[2560,1024]{1,0:T(8,128)(2,1)S(1)} %get-tuple-element.33.xt_ref, bf16[1024,2560]{1,0:T(8,128)(2,1)S(1)} %get-tuple-element.34.dy_ref, bf16[3232,128]{1,0:T(8,128)(2,1)S(1)} %collective-permute-done.6.rest_0_.rest_2_, ...), custom_call_target="tpu_custom_call" | custom-call | tf_op jit(solution)/shard_map/kept_near/pallas_call | solution.py:230
  56.1 1.1 q1_near.1
  57.4 2.5 %collective-permute-start.15 = (bf16[1632,128]{1,0:T(8,128)(2,1)S(1)}, bf16[1632,128]{1,0:T(8,128)(2,1)S(1)}, u32[]{:S(2)}, u32[]{:S(2)}) collective-permute-start(bf16[1632,128]{1,0:T(8,128)(2,1)S(1)} %get-tuple-element.54), channel_id=1, source_target_pairs={{0,1},{1,0},{2,3},{3,2},{4,5},{5,4},{6,7},{7,6},{8,9},{9,8},{10,11... | collective-permute-start | bytes 1253384 | tf_op jit(solution)/shard_map/ppermute | solution.py:128
  60.0 1.1 q1_far.1
  61.2 3.2 %collective-permute-start.12 = (bf16[1632,128]{1,0:T(8,128)(2,1)S(1)}, bf16[1632,128]{1,0:T(8,128)(2,1)S(1)}, u32[]{:S(2)}, u32[]{:S(2)}) collective-permute-start(bf16[1632,128]{1,0:T(8,128)(2,1)S(1)} %get-tuple-element.51), channel_id=1, source_target_pairs={{0,4},{1,5},{2,6},{3,7},{4,0},{5,1},{6,2},{7,3},{8,12},{9,13},{10,... | collective-permute-start | bytes 1253384 | tf_op jit(solution)/shard_map/ppermute | solution.py:128
  64.4 0.3 collective-permute-done.4.p0
  64.6 5.8 %collective-permute-start.13 = (bf16[1632,128]{1,0:T(8,128)(2,1)S(1)}, bf16[1632,128]{1,0:T(8,128)(2,1)S(1)}, u32[]{:S(2)}, u32[]{:S(2)}) collective-permute-start(bf16[1632,128]{1,0:T(8,128)(2,1)S(1)} %get-tuple-element.52), channel_id=1, source_target_pairs={{0,1},{1,0},{2,3},{3,2},{4,5},{5,4},{6,7},{7,6},{8,9},{9,8},{10,11... | collective-permute-start | bytes 1253384 | tf_op jit(solution)/shard_map/ppermute | solution.py:128
  70.4 2.2 %kept_far.1 = (f32[160,2560]{1,0:T(8,128)S(1)}, f32[160,2560]{1,0:T(8,128)S(1)}) custom-call(bf16[2560,1024]{1,0:T(8,128)(2,1)S(1)} %get-tuple-element.33.xt_ref, bf16[1024,2560]{1,0:T(8,128)(2,1)S(1)} %get-tuple-element.34.dy_ref, bf16[3232,128]{1,0:T(8,128)(2,1)S(1)} %collective-permute-done.2.rest_0_.rest_2_, ...), custom_call_target="tpu_custom_call" | custom-call | tf_op jit(solution)/shard_map/kept_far/pallas_call | solution.py:230
  72.6 1.1 q2_early.1
  73.7 1.7 %collective-permute-start.18 = (bf16[816,128]{1,0:T(8,128)(2,1)S(1)}, bf16[816,128]{1,0:T(8,128)(2,1)S(1)}, u32[]{:S(2)}, u32[]{:S(2)}) collective-permute-start(bf16[816,128]{1,0:T(8,128)(2,1)S(1)} %get-tuple-element.55.rest_0_), channel_id=1, source_target_pairs={{0,12},{1,13},{2,14},{3,15},{4,8},{5,9},{6,10},{7,11},{8,4},{9,5},... | collective-permute-start | bytes 626696 | tf_op jit(solution)/shard_map/ppermute | solution.py:128
  75.5 0.7 collective-permute-start.19
  76.2 1.0 q2_late.1
  77.2 0.7 collective-permute-start.16
  78.2 1.3 %own.1 = f32[160,2560]{1,0:T(8,128)S(1)} custom-call(f32[160,2560]{1,0:T(8,128)S(1)} %get-tuple-element.41.kept0, f32[160,2560]{1,0:T(8,128)S(1)} %get-tuple-element.42.kept1, bf16[3232,128]{1,0:T(8,128)(2,1)S(1)} %collective-permute-done.4.p0, bf16[3232,128]{1,0:T(8,128)(2,1)S(1)} %collective-permute-done.5.p1, ...), custom_call_target="tpu_custom_call" | custom-call | tf_op jit(solution)/shard_map/own/pallas_call | solution.py:308
  79.5 0.6 collective-permute-done.19.arr1
  80.1 0.3 last_far.1.rest_0_
  80.4 3.0 %collective-permute-start.22 = (bf16[168,640]{1,0:T(8,128)(2,1)S(1)}, bf16[168,640]{1,0:T(8,128)(2,1)S(1)}, u32[]{:S(2)}, u32[]{:S(2)}) collective-permute-start(bf16[168,640]{1,0:T(8,128)(2,1)S(1)} %last_far.1.rest_0_), channel_id=1, source_target_pairs={{0,64},{16,80},{32,96},{48,112},{64,0},{80,16},{96,32},{112,48},{1... | collective-permute-start | bytes 645128 | tf_op jit(solution)/shard_map/ppermute | solution.py:477
  83.4 0.3 last_near1.1.rest_0_
  83.7 0.9 collective-permute-start.20
  84.6 0.3 last_near2.1.rest_0_
  85.0 0.3 last_mine.1.own0.ref
  85.3 1.4 %collective-permute-done.22.own3.ref = bf16[168,640]{1,0:T(8,128)(2,1)S(1)} collective-permute-done((bf16[168,640]{1,0:T(8,128)(2,1)S(1)}, bf16[168,640]{1,0:T(8,128)(2,1)S(1)}, u32[]{:S(2)}, u32[]{:S(2)}) %collective-permute-start.22) | collective-permute-done | bytes 215072 | tf_op jit(solution)/shard_map/ppermute | solution.py:477
  86.7 3.3 %collective-permute-done.20.own1.ref = bf16[168,640]{1,0:T(8,128)(2,1)S(1)} collective-permute-done((bf16[168,640]{1,0:T(8,128)(2,1)S(1)}, bf16[168,640]{1,0:T(8,128)(2,1)S(1)}, u32[]{:S(2)}, u32[]{:S(2)}) %collective-permute-start.20) | collective-permute-done | bytes 215072 | tf_op jit(solution)/shard_map/ppermute | solution.py:128
  90.1 10.6 %collective-permute-start.23 = (bf16[4,168,384]{2,1,0:T(8,128)(2,1)S(1)}, bf16[4,168,384]{2,1,0:T(8,128)(2,1)S(1)}, u32[]{:S(2)}, u32[]{:S(2)}) collective-permute-start(bf16[4,168,384]{2,1,0:T(8,128)(2,1)S(1)} %cut_near2.1), channel_id=1, source_target_pairs={{0,16},{16,0},{32,48},{48,32},{64,80},{80,64},{96,112},{112,96},{1... | collective-permute-start | bytes 1548296 | tf_op jit(solution)/shard_map/ppermute | solution.py:495
  100.7 0.4 held.1
  101.1 1.1 collective-permute-done.23.carr
  102.3 1.3 %gram.1 = (f32[8,160,384]{2,1,0:T(8,128)S(1)}, f32[128,128]{1,0:T(8,128)S(1)}) custom-call(f32[4,160,384]{2,1,0:T(8,128)S(1)} %held.1, bf16[4,168,384]{2,1,0:T(8,128)(2,1)S(1)} %collective-permute-done.23.carr), custom_call_target="tpu_custom_call" | custom-call | tf_op jit(solution)/shard_map/gram/pallas_call | solution.py:505
  103.6 15.7 %all_to_all.11 = f32[128,1,128]{2,1,0:T(1,128)S(1)} all-to-all(f32[128,1,128]{2,1,0:T(1,128)S(1)} %bitcast.5), channel_id=1, replica_groups=mesh['node'=8,'fsdp'=16] {'node','fsdp'}, dimensions={0} | all-to-all | bytes 131072 | tf_op jit(solution)/shard_map/all_to_all | solution.py:514
  119.3 1.6 %combine.1 = f32[160,320]{1,0:T(8,128)} custom-call(f32[8,160,384]{2,1,0:T(8,128)S(1)} %get-tuple-element.59.g_ref, f32[128,128]{1,0:T(8,128)S(1)} %bitcast.4), custom_call_target="tpu_custom_call" | custom-call | tf_op jit(solution)/shard_map/combine/pallas_call | solution.py:515
  (25 shorter events, 0.8 us)
Async XLA Ops:
  6.6 14.6 %collective-permute-start.8 = (bf16[3232,128]{1,0:T(8,128)(2,1)S(1)}, bf16[3232,128]{1,0:T(8,128)(2,1)S(1)}, u32[]{:S(2)}, u32[]{:S(2)}) collective-permute-start(bf16[3232,128]{1,0:T(8,128)(2,1)S(1)} %get-tuple-element.35.rest_0_), channel_id=1, source_target_pairs={{0,1},{1,0},{2,3},{3,2},{4,5},{5,4},{6,7},{7,6},{8,9},{9,8},{10,11... | collective-permute-start | bytes 2482184 | tf_op jit(solution)/shard_map/ppermute | solution.py:128
  10.0 13.9 %collective-permute-start.9 = (bf16[3232,128]{1,0:T(8,128)(2,1)S(1)}, bf16[3232,128]{1,0:T(8,128)(2,1)S(1)}, u32[]{:S(2)}, u32[]{:S(2)}) collective-permute-start(bf16[3232,128]{1,0:T(8,128)(2,1)S(1)} %get-tuple-element.36.rest_1_), channel_id=1, source_target_pairs={{0,4},{1,5},{2,6},{3,7},{4,0},{5,1},{6,2},{7,3},{8,12},{9,13},{10,... | collective-permute-start | bytes 2482184 | tf_op jit(solution)/shard_map/ppermute | solution.py:128
  16.0 12.6 %collective-permute-start = (bf16[3232,128]{1,0:T(8,128)(2,1)S(1)}, bf16[3232,128]{1,0:T(8,128)(2,1)S(1)}, u32[]{:S(2)}, u32[]{:S(2)}) collective-permute-start(bf16[3232,128]{1,0:T(8,128)(2,1)S(1)} %get-tuple-element.37.rest_0_), channel_id=1, source_target_pairs={{0,1},{1,0},{2,3},{3,2},{4,5},{5,4},{6,7},{7,6},{8,9},{9,8},{10,11... | collective-permute-start | bytes 2482184 | tf_op jit(solution)/shard_map/ppermute | solution.py:128
  16.3 16.4 %collective-permute-start.1 = (bf16[3232,128]{1,0:T(8,128)(2,1)S(1)}, bf16[3232,128]{1,0:T(8,128)(2,1)S(1)}, u32[]{:S(2)}, u32[]{:S(2)}) collective-permute-start(bf16[3232,128]{1,0:T(8,128)(2,1)S(1)} %get-tuple-element.38.rest_1_), channel_id=1, source_target_pairs={{0,4},{1,5},{2,6},{3,7},{4,0},{5,1},{6,2},{7,3},{8,12},{9,13},{10,... | collective-permute-start | bytes 2482184 | tf_op jit(solution)/shard_map/ppermute | solution.py:128
  18.6 26.5 %collective-permute-start.6 = (bf16[3232,128]{1,0:T(8,128)(2,1)S(1)}, bf16[3232,128]{1,0:T(8,128)(2,1)S(1)}, u32[]{:S(2)}, u32[]{:S(2)}) collective-permute-start(bf16[3232,128]{1,0:T(8,128)(2,1)S(1)} %get-tuple-element.45), channel_id=1, source_target_pairs={{0,1},{1,0},{2,3},{3,2},{4,5},{5,4},{6,7},{7,6},{8,9},{9,8},{10,11... | collective-permute-start | bytes 2482184 | tf_op jit(solution)/shard_map/ppermute | solution.py:128
  21.2 31.8 %collective-permute-start.7 = (bf16[3232,128]{1,0:T(8,128)(2,1)S(1)}, bf16[3232,128]{1,0:T(8,128)(2,1)S(1)}, u32[]{:S(2)}, u32[]{:S(2)}) collective-permute-start(bf16[3232,128]{1,0:T(8,128)(2,1)S(1)} %get-tuple-element.46), channel_id=1, source_target_pairs={{0,4},{1,5},{2,6},{3,7},{4,0},{5,1},{6,2},{7,3},{8,12},{9,13},{10,... | collective-permute-start | bytes 2482184 | tf_op jit(solution)/shard_map/ppermute | solution.py:128
  27.1 26.8 %collective-permute-start.10 = (bf16[3232,128]{1,0:T(8,128)(2,1)S(1)}, bf16[3232,128]{1,0:T(8,128)(2,1)S(1)}, u32[]{:S(2)}, u32[]{:S(2)}) collective-permute-start(bf16[3232,128]{1,0:T(8,128)(2,1)S(1)} %get-tuple-element.49), channel_id=1, source_target_pairs={{0,3},{1,2},{2,1},{3,0},{4,7},{5,6},{6,5},{7,4},{8,11},{9,10},{10,... | collective-permute-start | bytes 2482184 | tf_op jit(solution)/shard_map/ppermute | solution.py:128
  28.7 27.4 %collective-permute-start.11 = (bf16[3232,128]{1,0:T(8,128)(2,1)S(1)}, bf16[3232,128]{1,0:T(8,128)(2,1)S(1)}, u32[]{:S(2)}, u32[]{:S(2)}) collective-permute-start(bf16[3232,128]{1,0:T(8,128)(2,1)S(1)} %get-tuple-element.50), channel_id=1, source_target_pairs={{0,12},{1,13},{2,14},{3,15},{4,8},{5,9},{6,10},{7,11},{8,4},{9,5},... | collective-permute-start | bytes 2482184 | tf_op jit(solution)/shard_map/ppermute | solution.py:128
  35.0 22.4 %collective-permute-start.2 = (bf16[3232,128]{1,0:T(8,128)(2,1)S(1)}, bf16[3232,128]{1,0:T(8,128)(2,1)S(1)}, u32[]{:S(2)}, u32[]{:S(2)}) collective-permute-start(bf16[3232,128]{1,0:T(8,128)(2,1)S(1)} %get-tuple-element.39.rest_2_), channel_id=1, source_target_pairs={{0,1},{1,0},{2,3},{3,2},{4,5},{5,4},{6,7},{7,6},{8,9},{9,8},{10,11... | collective-permute-start | bytes 2482184 | tf_op jit(solution)/shard_map/ppermute | solution.py:128
  45.2 14.9 %collective-permute-start.3 = (bf16[3232,128]{1,0:T(8,128)(2,1)S(1)}, bf16[3232,128]{1,0:T(8,128)(2,1)S(1)}, u32[]{:S(2)}, u32[]{:S(2)}) collective-permute-start(bf16[3232,128]{1,0:T(8,128)(2,1)S(1)} %get-tuple-element.40.rest_3_), channel_id=1, source_target_pairs={{0,4},{1,5},{2,6},{3,7},{4,0},{5,1},{6,2},{7,3},{8,12},{9,13},{10,... | collective-permute-start | bytes 2482184 | tf_op jit(solution)/shard_map/ppermute | solution.py:128
  53.0 11.7 %collective-permute-start.4 = (bf16[3232,128]{1,0:T(8,128)(2,1)S(1)}, bf16[3232,128]{1,0:T(8,128)(2,1)S(1)}, u32[]{:S(2)}, u32[]{:S(2)}) collective-permute-start(bf16[3232,128]{1,0:T(8,128)(2,1)S(1)} %get-tuple-element.43), channel_id=1, source_target_pairs={{0,3},{1,2},{2,1},{3,0},{4,7},{5,6},{6,5},{7,4},{8,11},{9,10},{10,... | collective-permute-start | bytes 2482184 | tf_op jit(solution)/shard_map/ppermute | solution.py:128
  53.9 18.7 %collective-permute-start.5 = (bf16[3232,128]{1,0:T(8,128)(2,1)S(1)}, bf16[3232,128]{1,0:T(8,128)(2,1)S(1)}, u32[]{:S(2)}, u32[]{:S(2)}) collective-permute-start(bf16[3232,128]{1,0:T(8,128)(2,1)S(1)} %get-tuple-element.44), channel_id=1, source_target_pairs={{0,12},{1,13},{2,14},{3,15},{4,8},{5,9},{6,10},{7,11},{8,4},{9,5},... | collective-permute-start | bytes 2482184 | tf_op jit(solution)/shard_map/ppermute | solution.py:128
  57.2 15.4 %collective-permute-start.14 = (bf16[1632,128]{1,0:T(8,128)(2,1)S(1)}, bf16[1632,128]{1,0:T(8,128)(2,1)S(1)}, u32[]{:S(2)}, u32[]{:S(2)}) collective-permute-start(bf16[1632,128]{1,0:T(8,128)(2,1)S(1)} %get-tuple-element.53), channel_id=1, source_target_pairs={{0,4},{1,5},{2,6},{3,7},{4,0},{5,1},{6,2},{7,3},{8,12},{9,13},{10,... | collective-permute-start | bytes 1253384 | tf_op jit(solution)/shard_map/ppermute | solution.py:128
  57.4 15.3 %collective-permute-start.15 = (bf16[1632,128]{1,0:T(8,128)(2,1)S(1)}, bf16[1632,128]{1,0:T(8,128)(2,1)S(1)}, u32[]{:S(2)}, u32[]{:S(2)}) collective-permute-start(bf16[1632,128]{1,0:T(8,128)(2,1)S(1)} %get-tuple-element.54), channel_id=1, source_target_pairs={{0,1},{1,0},{2,3},{3,2},{4,5},{5,4},{6,7},{7,6},{8,9},{9,8},{10,11... | collective-permute-start | bytes 1253384 | tf_op jit(solution)/shard_map/ppermute | solution.py:128
  61.2 16.7 %collective-permute-start.12 = (bf16[1632,128]{1,0:T(8,128)(2,1)S(1)}, bf16[1632,128]{1,0:T(8,128)(2,1)S(1)}, u32[]{:S(2)}, u32[]{:S(2)}) collective-permute-start(bf16[1632,128]{1,0:T(8,128)(2,1)S(1)} %get-tuple-element.51), channel_id=1, source_target_pairs={{0,4},{1,5},{2,6},{3,7},{4,0},{5,1},{6,2},{7,3},{8,12},{9,13},{10,... | collective-permute-start | bytes 1253384 | tf_op jit(solution)/shard_map/ppermute | solution.py:128
  64.6 13.5 %collective-permute-start.13 = (bf16[1632,128]{1,0:T(8,128)(2,1)S(1)}, bf16[1632,128]{1,0:T(8,128)(2,1)S(1)}, u32[]{:S(2)}, u32[]{:S(2)}) collective-permute-start(bf16[1632,128]{1,0:T(8,128)(2,1)S(1)} %get-tuple-element.52), channel_id=1, source_target_pairs={{0,1},{1,0},{2,3},{3,2},{4,5},{5,4},{6,7},{7,6},{8,9},{9,8},{10,11... | collective-permute-start | bytes 1253384 | tf_op jit(solution)/shard_map/ppermute | solution.py:128
  73.7 5.8 %collective-permute-start.18 = (bf16[816,128]{1,0:T(8,128)(2,1)S(1)}, bf16[816,128]{1,0:T(8,128)(2,1)S(1)}, u32[]{:S(2)}, u32[]{:S(2)}) collective-permute-start(bf16[816,128]{1,0:T(8,128)(2,1)S(1)} %get-tuple-element.55.rest_0_), channel_id=1, source_target_pairs={{0,12},{1,13},{2,14},{3,15},{4,8},{5,9},{6,10},{7,11},{8,4},{9,5},... | collective-permute-start | bytes 626696 | tf_op jit(solution)/shard_map/ppermute | solution.py:128
  75.5 4.7 %collective-permute-start.19 = (bf16[816,128]{1,0:T(8,128)(2,1)S(1)}, bf16[816,128]{1,0:T(8,128)(2,1)S(1)}, u32[]{:S(2)}, u32[]{:S(2)}) collective-permute-start(bf16[816,128]{1,0:T(8,128)(2,1)S(1)} %get-tuple-element.56.rest_1_), channel_id=1, source_target_pairs={{0,3},{1,2},{2,1},{3,0},{4,7},{5,6},{6,5},{7,4},{8,11},{9,10},{10,... | collective-permute-start | bytes 626696 | tf_op jit(solution)/shard_map/ppermute | solution.py:128
  77.2 7.3 %collective-permute-start.16 = (bf16[816,128]{1,0:T(8,128)(2,1)S(1)}, bf16[816,128]{1,0:T(8,128)(2,1)S(1)}, u32[]{:S(2)}, u32[]{:S(2)}) collective-permute-start(bf16[816,128]{1,0:T(8,128)(2,1)S(1)} %get-tuple-element.57), channel_id=1, source_target_pairs={{0,12},{1,13},{2,14},{3,15},{4,8},{5,9},{6,10},{7,11},{8,4},{9,5},... | collective-permute-start | bytes 626696 | tf_op jit(solution)/shard_map/ppermute | solution.py:128
  77.9 6.7 %collective-permute-start.17 = (bf16[816,128]{1,0:T(8,128)(2,1)S(1)}, bf16[816,128]{1,0:T(8,128)(2,1)S(1)}, u32[]{:S(2)}, u32[]{:S(2)}) collective-permute-start(bf16[816,128]{1,0:T(8,128)(2,1)S(1)} %get-tuple-element.58), channel_id=1, source_target_pairs={{0,3},{1,2},{2,1},{3,0},{4,7},{5,6},{6,5},{7,4},{8,11},{9,10},{10,... | collective-permute-start | bytes 626696 | tf_op jit(solution)/shard_map/ppermute | solution.py:128
  80.4 6.3 %collective-permute-start.22 = (bf16[168,640]{1,0:T(8,128)(2,1)S(1)}, bf16[168,640]{1,0:T(8,128)(2,1)S(1)}, u32[]{:S(2)}, u32[]{:S(2)}) collective-permute-start(bf16[168,640]{1,0:T(8,128)(2,1)S(1)} %last_far.1.rest_0_), channel_id=1, source_target_pairs={{0,64},{16,80},{32,96},{48,112},{64,0},{80,16},{96,32},{112,48},{1... | collective-permute-start | bytes 645128 | tf_op jit(solution)/shard_map/ppermute | solution.py:477
  83.7 6.3 %collective-permute-start.20 = (bf16[168,640]{1,0:T(8,128)(2,1)S(1)}, bf16[168,640]{1,0:T(8,128)(2,1)S(1)}, u32[]{:S(2)}, u32[]{:S(2)}) collective-permute-start(bf16[168,640]{1,0:T(8,128)(2,1)S(1)} %last_near1.1.rest_0_), channel_id=1, source_target_pairs={{0,32},{1,33},{2,34},{3,35},{4,36},{5,37},{6,38},{7,39},{8,40},{9,... | collective-permute-start | bytes 645128 | tf_op jit(solution)/shard_map/ppermute | solution.py:128
  84.9 5.2 %collective-permute-start.21 = (bf16[168,640]{1,0:T(8,128)(2,1)S(1)}, bf16[168,640]{1,0:T(8,128)(2,1)S(1)}, u32[]{:S(2)}, u32[]{:S(2)}) collective-permute-start(bf16[168,640]{1,0:T(8,128)(2,1)S(1)} %last_near2.1.rest_0_), channel_id=1, source_target_pairs={{0,96},{1,97},{2,98},{3,99},{4,100},{5,101},{6,102},{7,103},{8,104... | collective-permute-start | bytes 645128 | tf_op jit(solution)/shard_map/ppermute | solution.py:128
  90.1 12.2 %collective-permute-start.23 = (bf16[4,168,384]{2,1,0:T(8,128)(2,1)S(1)}, bf16[4,168,384]{2,1,0:T(8,128)(2,1)S(1)}, u32[]{:S(2)}, u32[]{:S(2)}) collective-permute-start(bf16[4,168,384]{2,1,0:T(8,128)(2,1)S(1)} %cut_near2.1), channel_id=1, source_target_pairs={{0,16},{16,0},{32,48},{48,32},{64,80},{80,64},{96,112},{112,96},{1... | collective-permute-start | bytes 1548296 | tf_op jit(solution)/shard_map/ppermute | solution.py:495
